TPU v7x, 32 devices: a whole 2x2x4 slice. The times are simulated.
32 devices in a mesh: dp: 8 (over y, x, core), tensor: 4 (over z).
Axes of the slice: x: 2, y: 2, z: 4, core: 2. Of those that a mesh axis runs over, the one named last changes fastest.
Arguments:
- tokens: bfloat16 [28672, 768], P(('dp', 'tensor')), may hold values from -6 to 6
- gain_attn: float32 [768], P(('dp', 'tensor')), may hold values from 0.5 to 1.5
- w_query: bfloat16 [768, 768], P('dp', 'tensor'), may hold values from -0.3125 to 0.3125
- w_key: bfloat16 [768, 768], P('dp', 'tensor'), may hold values from -0.3125 to 0.3125
- w_value: bfloat16 [768, 768], P('dp', 'tensor'), may hold values from -0.21875 to 0.21875
- w_out: bfloat16 [768, 768], P('tensor', 'dp'), may hold values from -0.875 to 0.875
- gain_ffn: float32 [768], P(('dp', 'tensor')), may hold values from 0.5 to 1.5
- w_gate: bfloat16 [768, 2048], P('dp', 'tensor'), may hold values from -0.21875 to 0.21875
- w_up: bfloat16 [768, 2048], P('dp', 'tensor'), may hold values from -0.21875 to 0.21875
- w_down: bfloat16 [2048, 768], P('tensor', 'dp'), may hold values from -0.125 to 0.125
- segment_ids: int32 [28672], P('dp'), may hold values from 0 to 12, as said below
- parent_ids: int32 [28672], P('dp'), may hold values from 0 to 12, as said below
- positions: int32 [28672], P('dp'), may hold values from 0 to 2046, as said below
- cotangent: bfloat16 [28672, 768], P(('dp', 'tensor')), may hold values from -6 to 6
Outputs:
- mixed: bfloat16 [28672, 768], P(('dp', 'tensor'))
- grad_tokens: float32 [28672, 768], P(('dp', 'tensor'))
- grad_gain_attn: float32 [768], P(('dp', 'tensor'))
- grad_w_query: float32 [768, 768], P('dp', 'tensor')
- grad_w_key: float32 [768, 768], P('dp', 'tensor')
- grad_w_value: float32 [768, 768], P('dp', 'tensor')
- grad_w_out: float32 [768, 768], P('tensor', 'dp')
- grad_gain_ffn: float32 [768], P(('dp', 'tensor'))
- grad_w_gate: float32 [768, 2048], P('dp', 'tensor')
- grad_w_up: float32 [768, 2048], P('dp', 'tensor')
- grad_w_down: float32 [2048, 768], P('tensor', 'dp')
Inputs may be any that keep to these rules, and one draw needn't show every extreme that they name: `segment_ids`: each block of 3584 rows is one tree of 13 segments with distinct ids: a root of 512 tokens, 4 branches of 256 tokens under the root and 2 leaves of 256 tokens under each branch. A segment's tokens are contiguous and follow its parent's tokens. `parent_ids`: the id of the parent of the token's segment; on the root's tokens, the root's own id. `positions`: A tree's offset, 0 to 1023, plus the number of tokens before the token on its root-to-leaf path.
All inputs are finite; a program needn't handle non-finite values.
Results may differ from a plain program's by a relative error of at most 0.02.
Values may be sent and summed in bfloat16 or wider, within the bound.
No kernel may reach another device: no remote copies, remote signals or barrier semaphores. Data moves between devices by JAX's collectives and lax.ppermute only.
A program may use at most 192 MiB of HBM per device.

v0:
```python
import jax
import jax.numpy as jnp
from jax import lax
from jax.sharding import PartitionSpec as P

HEAD_DIM = 64
QBLOCK = 512


EPSILON = 1e-05
MASKED = -1e30
CONTRACT_ROWS = (((0,), (0,)), ((), ()))
CONTRACT_COLS = (((1,), (1,)), ((), ()))


def normalize(values, gain_vec):
    row_scale = lax.rsqrt(jnp.mean(values * values, axis=-1, keepdims=True) + EPSILON)
    return ((values * row_scale * gain_vec).astype(jnp.bfloat16), row_scale)


def norm_back(grad_out, values, row_scale, gain_vec):
    x_hat = values * row_scale
    scaled = grad_out * gain_vec
    grad_in = row_scale * (scaled - x_hat * jnp.mean(scaled * x_hat, axis=-1, keepdims=True))
    return (grad_in, jnp.sum(grad_out * x_hat, axis=0))


def tables(pos_ids):
    half_dim = HEAD_DIM // 2
    freq_table = jnp.exp(
        -jnp.log(10000.0) * (2.0 * jnp.arange(half_dim, dtype=jnp.float32) / HEAD_DIM)
    )
    freq_table = jnp.concatenate([freq_table, freq_table])
    angles = pos_ids.astype(jnp.float32)[:, None] * freq_table[None, :]
    return (jnp.cos(angles), jnp.sin(angles))


def rotate(values, cos_tab, sine_tab):
    half_dim = values.shape[-1] // 2
    turned = jnp.concatenate([-values[:, half_dim:], values[:, :half_dim]], axis=1)
    return values * cos_tab + turned * sine_tab


def rotate_back(grads, cos_tab, sine_tab):
    half_dim = grads.shape[-1] // 2
    sine_part = grads * sine_tab
    turned = jnp.concatenate([sine_part[:, half_dim:], -sine_part[:, :half_dim]], axis=1)
    return grads * cos_tab + turned


def block_scores(first_row, q_block, k_head, seg_ids, par_ids):
    row_index = first_row + jnp.arange(q_block.shape[0], dtype=jnp.int32)
    col_index = jnp.arange(seg_ids.shape[0], dtype=jnp.int32)
    seg_rows = lax.dynamic_slice_in_dim(seg_ids, first_row, q_block.shape[0], 0)
    par_rows = lax.dynamic_slice_in_dim(par_ids, first_row, q_block.shape[0], 0)
    causal = col_index[None, :] <= row_index[:, None]
    kinship = (
        (seg_ids[None, :] == seg_rows[:, None])
        | (seg_ids[None, :] == par_rows[:, None])
        | (par_ids == seg_ids)[None, :]
    )
    raw_score = lax.dot_general(q_block, k_head, CONTRACT_COLS, preferred_element_type=jnp.float32)
    return jnp.where(causal & kinship, raw_score * HEAD_DIM ** (-0.5), MASKED)


def head_forward(q_head, k_head, v_head, seg_ids, par_ids):
    row_count = q_head.shape[0]
    starts = jnp.arange(row_count // QBLOCK, dtype=jnp.int32) * QBLOCK

    def one_block(first_row):
        q_block = lax.dynamic_slice_in_dim(q_head, first_row, QBLOCK, 0)
        scores = block_scores(first_row, q_block, k_head, seg_ids, par_ids)
        row_top = jnp.max(scores, axis=1, keepdims=True)
        expo_vals = jnp.exp(scores - row_top)
        row_total = jnp.sum(expo_vals, axis=1, keepdims=True)
        prob_vals = (expo_vals / row_total).astype(jnp.bfloat16)
        out_block = jnp.dot(prob_vals, v_head, preferred_element_type=jnp.float32).astype(
            jnp.bfloat16
        )
        return (out_block, (row_top + jnp.log(row_total))[:, 0])

    block_outs, log_total = lax.map(one_block, starts)
    return (block_outs.reshape(row_count, HEAD_DIM), log_total.reshape(row_count))


def head_backward(q_head, k_head, v_head, grad_head, log_total, seg_ids, par_ids):
    row_count = q_head.shape[0]
    starts = jnp.arange(row_count // QBLOCK, dtype=jnp.int32) * QBLOCK

    def one_block(running, first_row):
        grad_keys, grad_values = running
        q_block = lax.dynamic_slice_in_dim(q_head, first_row, QBLOCK, 0)
        grad_block = lax.dynamic_slice_in_dim(grad_head, first_row, QBLOCK, 0)
        total_block = lax.dynamic_slice_in_dim(log_total, first_row, QBLOCK, 0)
        scores = block_scores(first_row, q_block, k_head, seg_ids, par_ids)
        prob_vals = jnp.exp(scores - total_block[:, None])
        grad_probs = lax.dot_general(
            grad_block, v_head, CONTRACT_COLS, preferred_element_type=jnp.float32
        )
        row_dot = jnp.sum(prob_vals * grad_probs, axis=1, keepdims=True)
        grad_raw = (prob_vals * (grad_probs - row_dot) * HEAD_DIM ** (-0.5)).astype(jnp.bfloat16)
        grad_query = jnp.dot(grad_raw, k_head, preferred_element_type=jnp.float32)
        grad_keys = grad_keys + lax.dot_general(
            grad_raw, q_block, CONTRACT_ROWS, preferred_element_type=jnp.float32
        )
        grad_values = grad_values + lax.dot_general(
            prob_vals.astype(jnp.bfloat16),
            grad_block,
            CONTRACT_ROWS,
            preferred_element_type=jnp.float32,
        )
        return ((grad_keys, grad_values), grad_query)

    zeros_init = jnp.zeros((row_count, HEAD_DIM), jnp.float32)
    (grad_keys, grad_values), grad_queries = lax.scan(one_block, (zeros_init, zeros_init), starts)
    return (grad_queries.reshape(row_count, HEAD_DIM), grad_keys, grad_values)


def gather_rows(values):
    return lax.all_gather(values, "tensor", axis=0, tiled=True)


def scatter_rows(term_fn, local_rows):
    return lax.psum_scatter(
        term_fn(jnp.int32(0), local_rows * lax.axis_size("tensor")).astype(jnp.bfloat16),
        "tensor",
        scatter_dimension=0,
        tiled=True,
    ).astype(jnp.float32)


def per_device(
    tokens,
    gain_attn,
    w_query,
    w_key,
    w_value,
    w_out,
    gain_ffn,
    w_gate,
    w_up,
    w_down,
    segment_ids,
    parent_ids,
    positions,
    cotangent,
):
    gain_one, gain_two = (
        lax.all_gather(gain_attn, ("dp", "tensor"), axis=0, tiled=True),
        lax.all_gather(gain_ffn, ("dp", "tensor"), axis=0, tiled=True),
    )
    fetched = (
        lax.all_gather(w_query, "dp", axis=0, tiled=True),
        lax.all_gather(w_key, "dp", axis=0, tiled=True),
        lax.all_gather(w_value, "dp", axis=0, tiled=True),
        lax.all_gather(w_out, "dp", axis=1, tiled=True),
        lax.all_gather(w_gate, "dp", axis=0, tiled=True),
        lax.all_gather(w_up, "dp", axis=0, tiled=True),
        lax.all_gather(w_down, "dp", axis=1, tiled=True),
    )
    query_full, key_full, value_full, out_full, gate_full, up_full, down_full = fetched
    local_rows = tokens.shape[0]
    x_local = tokens.astype(jnp.float32)
    normed_one, scale_one = normalize(x_local, gain_one)
    attn_in = gather_rows(normed_one)
    cos_tab, sine_tab = tables(positions)
    heads_dev = query_full.shape[1] // HEAD_DIM
    query_proj = jnp.dot(attn_in, query_full, preferred_element_type=jnp.float32)
    key_proj = jnp.dot(attn_in, key_full, preferred_element_type=jnp.float32)
    value_bf = jnp.dot(attn_in, value_full, preferred_element_type=jnp.float32).astype(jnp.bfloat16)
    query_heads = []
    key_heads = []
    head_outs = []
    head_totals = []
    for head_index in range(heads_dev):
        columns = slice(head_index * HEAD_DIM, (head_index + 1) * HEAD_DIM)
        q_rot = rotate(query_proj[:, columns], cos_tab, sine_tab).astype(jnp.bfloat16)
        k_rot = rotate(key_proj[:, columns], cos_tab, sine_tab).astype(jnp.bfloat16)
        out_head, total_head = head_forward(
            q_rot, k_rot, value_bf[:, columns], segment_ids, parent_ids
        )
        query_heads.append(q_rot)
        key_heads.append(k_rot)
        head_outs.append(out_head)
        head_totals.append(total_head)
    attn_out = jnp.concatenate(head_outs, axis=1)

    def attn_term(first_row, row_count):
        return jnp.dot(attn_out, out_full, preferred_element_type=jnp.float32)

    hidden_state = x_local + scatter_rows(attn_term, local_rows)
    normed_two, scale_two = normalize(hidden_state, gain_two)
    ffn_in = gather_rows(normed_two)
    gate_pre = jnp.dot(ffn_in, gate_full, preferred_element_type=jnp.float32)
    up_pre = jnp.dot(ffn_in, up_full, preferred_element_type=jnp.float32)
    sig_gate = jax.nn.sigmoid(gate_pre)
    silu_gate = gate_pre * sig_gate
    inner_act = (silu_gate * up_pre).astype(jnp.bfloat16)

    def down_term(first_row, row_count):
        return jnp.dot(inner_act, down_full, preferred_element_type=jnp.float32)

    result = hidden_state + scatter_rows(down_term, local_rows)
    fetched = (
        lax.all_gather(w_query, "dp", axis=0, tiled=True),
        lax.all_gather(w_key, "dp", axis=0, tiled=True),
        lax.all_gather(w_value, "dp", axis=0, tiled=True),
        lax.all_gather(w_out, "dp", axis=1, tiled=True),
        lax.all_gather(w_gate, "dp", axis=0, tiled=True),
        lax.all_gather(w_up, "dp", axis=0, tiled=True),
        lax.all_gather(w_down, "dp", axis=1, tiled=True),
    )
    query_full, key_full, value_full, out_full, gate_full, up_full, down_full = fetched
    grad_full = gather_rows(cotangent)
    grad_inner = lax.dot_general(
        grad_full, down_full, CONTRACT_COLS, preferred_element_type=jnp.float32
    )
    grad_down = lax.dot_general(
        inner_act, grad_full, CONTRACT_ROWS, preferred_element_type=jnp.float32
    )
    grad_gate_pre = (grad_inner * up_pre * sig_gate * (1.0 + gate_pre * (1.0 - sig_gate))).astype(
        jnp.bfloat16
    )
    grad_up_pre = (grad_inner * silu_gate).astype(jnp.bfloat16)
    grad_gate = lax.dot_general(
        ffn_in, grad_gate_pre, CONTRACT_ROWS, preferred_element_type=jnp.float32
    )
    grad_up = lax.dot_general(
        ffn_in, grad_up_pre, CONTRACT_ROWS, preferred_element_type=jnp.float32
    )

    def ffn_back_term(first_row, row_count):
        gate_part = lax.dot_general(
            grad_gate_pre, gate_full, CONTRACT_COLS, preferred_element_type=jnp.float32
        )
        up_part = lax.dot_general(
            grad_up_pre, up_full, CONTRACT_COLS, preferred_element_type=jnp.float32
        )
        return gate_part + up_part

    grad_normed_two = scatter_rows(ffn_back_term, local_rows)
    grad_hidden_norm, gain_two_term = norm_back(grad_normed_two, hidden_state, scale_two, gain_two)
    grad_hidden = cotangent.astype(jnp.float32) + grad_hidden_norm
    grad_attn_full = gather_rows(grad_hidden.astype(jnp.bfloat16))
    grad_attn_out = lax.dot_general(
        grad_attn_full, out_full, CONTRACT_COLS, preferred_element_type=jnp.float32
    ).astype(jnp.bfloat16)
    grad_out_weight = lax.dot_general(
        attn_out, grad_attn_full, CONTRACT_ROWS, preferred_element_type=jnp.float32
    )
    grad_query_heads = []
    grad_key_heads = []
    grad_value_heads = []
    for head_index in range(heads_dev):
        columns = slice(head_index * HEAD_DIM, (head_index + 1) * HEAD_DIM)
        grad_q_rot, grad_k_rot, grad_v_head = head_backward(
            query_heads[head_index],
            key_heads[head_index],
            value_bf[:, columns],
            grad_attn_out[:, columns],
            head_totals[head_index],
            segment_ids,
            parent_ids,
        )
        grad_query_heads.append(rotate_back(grad_q_rot, cos_tab, sine_tab).astype(jnp.bfloat16))
        grad_key_heads.append(rotate_back(grad_k_rot, cos_tab, sine_tab).astype(jnp.bfloat16))
        grad_value_heads.append(grad_v_head.astype(jnp.bfloat16))
    grad_query_proj = jnp.concatenate(grad_query_heads, axis=1)
    grad_key_proj = jnp.concatenate(grad_key_heads, axis=1)
    grad_value_proj = jnp.concatenate(grad_value_heads, axis=1)
    grad_query = lax.dot_general(
        attn_in, grad_query_proj, CONTRACT_ROWS, preferred_element_type=jnp.float32
    )
    grad_key = lax.dot_general(
        attn_in, grad_key_proj, CONTRACT_ROWS, preferred_element_type=jnp.float32
    )
    grad_value = lax.dot_general(
        attn_in, grad_value_proj, CONTRACT_ROWS, preferred_element_type=jnp.float32
    )

    def attn_back_term(first_row, row_count):
        query_part = lax.dot_general(
            grad_query_proj, query_full, CONTRACT_COLS, preferred_element_type=jnp.float32
        )
        key_part = lax.dot_general(
            grad_key_proj, key_full, CONTRACT_COLS, preferred_element_type=jnp.float32
        )
        value_part = lax.dot_general(
            grad_value_proj, value_full, CONTRACT_COLS, preferred_element_type=jnp.float32
        )
        return query_part + key_part + value_part

    grad_normed_one = scatter_rows(attn_back_term, local_rows)
    grad_in_norm, gain_one_term = norm_back(grad_normed_one, x_local, scale_one, gain_one)
    grad_tokens = grad_hidden + grad_in_norm
    weight_sums = (
        lax.psum_scatter(grad_query, "dp", scatter_dimension=0, tiled=True),
        lax.psum_scatter(grad_key, "dp", scatter_dimension=0, tiled=True),
        lax.psum_scatter(grad_value, "dp", scatter_dimension=0, tiled=True),
        lax.psum_scatter(grad_out_weight, "dp", scatter_dimension=1, tiled=True),
        lax.psum_scatter(grad_gate, "dp", scatter_dimension=0, tiled=True),
        lax.psum_scatter(grad_up, "dp", scatter_dimension=0, tiled=True),
        lax.psum_scatter(grad_down, "dp", scatter_dimension=1, tiled=True),
    )
    gain_sums = (
        lax.psum_scatter(gain_one_term, ("dp", "tensor"), scatter_dimension=0, tiled=True),
        lax.psum_scatter(gain_two_term, ("dp", "tensor"), scatter_dimension=0, tiled=True),
    )
    return (
        result.astype(jnp.bfloat16),
        grad_tokens,
        gain_sums[0],
        weight_sums[0],
        weight_sums[1],
        weight_sums[2],
        weight_sums[3],
        gain_sums[1],
        weight_sums[4],
        weight_sums[5],
        weight_sums[6],
    )


def solution(mesh):
    placed = (
        P(("dp", "tensor"), None),
        P(("dp", "tensor")),
        P("dp", "tensor"),
        P("dp", "tensor"),
        P("dp", "tensor"),
        P("tensor", "dp"),
        P(("dp", "tensor")),
        P("dp", "tensor"),
        P("dp", "tensor"),
        P("tensor", "dp"),
        P("dp"),
        P("dp"),
        P("dp"),
        P(("dp", "tensor"), None),
    )
    return jax.shard_map(
        per_device,
        mesh=mesh,
        in_specs=placed,
        out_specs=(
            P(("dp", "tensor"), None),
            P(("dp", "tensor"), None),
            P(("dp", "tensor")),
            P("dp", "tensor"),
            P("dp", "tensor"),
            P("dp", "tensor"),
            P("tensor", "dp"),
            P(("dp", "tensor")),
            P("dp", "tensor"),
            P("dp", "tensor"),
            P("tensor", "dp"),
        ),
        check_vma=False,
    )
```

profile of v0, /device:TPU:0, one launch (start us, length us, event | category | flops | bytes accessed | tf_op | source)
XLA Modules:
  0.0 2118.5 jit_solution(7777827139527649860)
XLA Ops:
  10.7 42.1 %all-reduce.5 = (f32[768]{0:T(1024)S(1)}, f32[768]{0:T(1024)}) all-reduce(f32[768]{0:T(1024)S(1)} %dynamic-update-slice, f32[768]{0:T(1024)S(1)} %dynamic-update-slice.1), channel_id=1, replica_groups=mesh['dp'=8,'tensor'=4] {'dp','tensor'}, use_global_device_ids=true, to_apply=%add | all-reduce | flops 1536 | bytes 12288
  55.9 11.6 all_gather.51
  67.5 8.7 all_gather.48
  76.2 9.5 all_gather.49
  85.7 8.7 all_gather.50
  94.4 63.8 %all-gather.5.cloned.1.call-done = bf16[3584,768]{1,0:T(8,128)(2,1)} async-done(((bf16[896,768]{1,0:T(8,128)(2,1)}), bf16[3584,768]{1,0:T(8,128)(2,1)}) %all-gather.5.cloned.1.call-update) | async-done | bytes 5505040 | tf_op jit(solution)/shard_map/all_gather | solution.py:120
  193.1 72.7 %while.89 = (s32[]{:T(128)}, bf16[7,512,64]{1,2,0:T(8,128)(2,1)S(1)}, f32[7,512]{1,0:T(8,128)S(1)}, s32[7]{0:T(128)S(1)}, s32[3584]{0:T(1024)S(1)}, /*index=5*/s...) while((s32[]{:T(128)}, ...), condition=%wide.region_12.13_spmd, body=%wide.region_9.12_spmd.sunk | while | flops 495484928 | bytes 23655124 | solution.py:82
  268.4 73.0 %while.88 = (s32[]{:T(128)}, bf16[7,512,64]{1,2,0:T(8,128)(2,1)S(1)}, f32[7,512]{1,0:T(8,128)S(1)}, s32[7]{0:T(128)S(1)}, s32[3584]{0:T(1024)S(1)}, /*index=5*/s...) while((s32[]{:T(128)}, ...), condition=%wide.region_8.9_spmd, body=%wide.region_5.8_spmd.sunk | while | flops 495484928 | bytes 23655124 | solution.py:82
  344.1 83.8 %while.87 = (s32[]{:T(128)}, bf16[7,512,64]{1,2,0:T(8,128)(2,1)S(1)}, f32[7,512]{1,0:T(8,128)S(1)}, s32[7]{0:T(128)S(1)}, s32[3584]{0:T(1024)S(1)}, /*index=5*/s...) while((s32[]{:T(128)}, ...), condition=%wide.region_4.5_spmd, body=%wide.region_1.4_spmd.sunk | while | flops 495484928 | bytes 23655124 | solution.py:82
  435.1 96.4 %reduce-scatter.14.cloned.1.call-done = bf16[896,768]{1,0:T(8,128)(2,1)} async-done(((bf16[3584,768]{1,0:T(8,128)(2,1)}), bf16[896,768]{1,0:T(8,128)(2,1)}) %reduce-scatter.14.cloned.1.call-update) | async-done | bytes 1376272 | tf_op jit(solution)/shard_map/reduce_scatter | solution.py:124
  535.9 11.4 all_gather.54
  547.3 11.3 all_gather.55
  558.5 10.8 all_gather.56
  569.4 68.9 %all-gather.7.cloned.1.call-done = bf16[3584,768]{1,0:T(8,128)(2,1)} async-done(((bf16[896,768]{1,0:T(8,128)(2,1)}), bf16[3584,768]{1,0:T(8,128)(2,1)}) %all-gather.7.cloned.1.call-update) | async-done | bytes 5505040 | tf_op jit(solution)/shard_map/all_gather | solution.py:120
  638.3 9.1 fusion.150
  652.6 87.9 %all-gather.9.cloned.1.call-done = bf16[3584,768]{1,0:T(8,128)(2,1)} async-done(((bf16[896,768]{1,0:T(8,128)(2,1)}), bf16[3584,768]{1,0:T(8,128)(2,1)}) %all-gather.9.cloned.1.call-update) | async-done | bytes 5505040 | tf_op jit(solution)/shard_map/all_gather | solution.py:120
  740.5 13.3 multiply_convert_fusion.3
  756.9 7.7 add_convert_fusion.1
  764.7 96.4 %reduce-scatter.18.cloned.1.call-done = bf16[896,768]{1,0:T(8,128)(2,1)} async-done(((bf16[3584,768]{1,0:T(8,128)(2,1)}), bf16[896,768]{1,0:T(8,128)(2,1)}) %reduce-scatter.18.cloned.1.call-update) | async-done | bytes 1376272 | tf_op jit(solution)/shard_map/reduce_scatter | solution.py:124
  867.6 102.1 %all-gather.11.cloned.1.call-done = bf16[3584,768]{1,0:T(8,128)(2,1)} async-done(((bf16[896,768]{1,0:T(8,128)(2,1)}), bf16[3584,768]{1,0:T(8,128)(2,1)}) %all-gather.11.cloned.1.call-update) | async-done | bytes 5505040 | tf_op jit(solution)/shard_map/all_gather | solution.py:120
  980.0 220.9 %while.90 = (s32[]{:T(128)}, f32[3584,64]{0,1:T(8,128)S(1)}, f32[3584,64]{0,1:T(8,128)}, f32[7,512,64]{1,0,2:T(8,128)}, s32[7]{0:T(128)S(1)}, /*index=5*/s32[358...) while((s32[]{:T(128)}, f32[3584,64]{0,1:T(8,128)S(1)}, ...), condition=%wide.region_20.21_spmd.clone, body=%wide.region_18.20_spmd.clone.sunk | while | flops 1204682752 | bytes 62114560 | solution.py:115
  986.0 7.4 multiply_reduce_fusion.7
  1017.4 7.4 multiply_reduce_fusion.7
  1049.0 7.4 multiply_reduce_fusion.7
  1080.6 7.4 multiply_reduce_fusion.7
  1112.2 7.4 multiply_reduce_fusion.7
  1143.7 7.4 multiply_reduce_fusion.7
  1175.3 7.4 multiply_reduce_fusion.7
  1205.0 211.9 %while.92 = (s32[]{:T(128)}, f32[3584,64]{0,1:T(8,128)S(1)}, f32[3584,64]{0,1:T(8,128)}, f32[7,512,64]{1,0,2:T(8,128)}, s32[7]{0:T(128)S(1)}, /*index=5*/s32[358...) while((s32[]{:T(128)}, f32[3584,64]{0,1:T(8,128)S(1)}, ...), condition=%wide.region_26.27_spmd.clone, body=%wide.region_24.26_spmd.clone.sunk | while | flops 1204682752 | bytes 65325880 | solution.py:115
  1211.5 7.1 multiply_reduce_fusion.9
  1241.6 7.1 multiply_reduce_fusion.9
  1271.8 7.1 multiply_reduce_fusion.9
  1302.1 7.1 multiply_reduce_fusion.9
  1332.3 7.1 multiply_reduce_fusion.9
  1362.6 7.1 multiply_reduce_fusion.9
  1392.8 7.1 multiply_reduce_fusion.9
  1420.8 216.9 %while.91 = (s32[]{:T(128)}, f32[3584,64]{0,1:T(8,128)S(1)}, f32[3584,64]{0,1:T(8,128)}, f32[7,512,64]{1,0,2:T(8,128)}, s32[7]{0:T(128)S(1)}, /*index=5*/s32[358...) while((s32[]{:T(128)}, f32[3584,64]{0,1:T(8,128)S(1)}, ...), condition=%wide.region_23.24_spmd.clone, body=%wide.region_21.23_spmd.clone.sunk | while | flops 1204682752 | bytes 65325880 | solution.py:115
  1427.8 7.1 multiply_reduce_fusion.8
  1458.6 7.1 multiply_reduce_fusion.8
  1470.7 5.2 convolution_add_fusion.15
  1489.6 7.1 multiply_reduce_fusion.8
  1501.7 5.2 convolution_add_fusion.15
  1520.6 7.1 multiply_reduce_fusion.8
  1532.7 5.2 convolution_add_fusion.15
  1551.5 7.1 multiply_reduce_fusion.8
  1563.7 5.2 convolution_add_fusion.15
  1582.5 7.1 multiply_reduce_fusion.8
  1613.5 7.1 multiply_reduce_fusion.8
  1657.2 5.8 fusion.128
  1663.1 6.8 add_convert_fusion
  1671.1 7.5 convolution_convert_fusion
  1678.7 7.9 fusion.154
  1686.9 7.9 fusion.152
  1694.9 7.8 fusion.153
  1720.4 46.1 %reduce-scatter.20.cloned.1.call-done = bf16[896,768]{1,0:T(8,128)(2,1)} async-done(((bf16[3584,768]{1,0:T(8,128)(2,1)}), bf16[896,768]{1,0:T(8,128)(2,1)}) %reduce-scatter.20.cloned.1.call-update) | async-done | bytes 1376272 | tf_op jit(solution)/shard_map/reduce_scatter | solution.py:124
  1769.0 47.3 %all-reduce.4 = (f32[768]{0:T(1024)S(1)}, f32[768]{0:T(1024)S(1)}) all-reduce(f32[768]{0:T(1024)S(1)} %get-tuple-element.985, f32[768]{0:T(1024)S(1)} %copy-done.78), channel_id=6, replica_groups=mesh['dp'=8,'tensor'=4] {'dp','tensor'}, use_global_device_ids=true, to_apply=%region_30.31.clone | all-reduce | flops 1536 | bytes 12288
  1817.5 51.0 %reduce-scatter.16.cloned.1.call-done = bf16[896,768]{1,0:T(8,128)(2,1)} async-done(((bf16[3584,768]{1,0:T(8,128)(2,1)}), bf16[896,768]{1,0:T(8,128)(2,1)}) %reduce-scatter.16.cloned.1.call-update) | async-done | bytes 1376272 | tf_op jit(solution)/shard_map/reduce_scatter | solution.py:124
  1868.5 5.3 fusion.66
  1873.8 37.3 %reduce-scatter.32.cloned.1.call-done = f32[512,96]{0,1:T(8,128)} async-done(((f32[512,768]{0,1:T(8,128)}), f32[512,96]{0,1:T(8,128)}) %reduce-scatter.32.cloned.1.call-update) | async-done | bytes 196624 | tf_op jit(solution)/shard_map/reduce_scatter | solution.py:303
  1911.1 42.4 %reduce-scatter.28.cloned.1.call-done = f32[96,512]{1,0:T(8,128)} async-done(((f32[768,512]{1,0:T(8,128)}), f32[96,512]{1,0:T(8,128)}) %reduce-scatter.28.cloned.1.call-update) | async-done | bytes 196624 | tf_op jit(solution)/shard_map/reduce_scatter | solution.py:301
  1953.5 42.2 %reduce-scatter.30.cloned.1.call-done = f32[96,512]{1,0:T(8,128)} async-done(((f32[768,512]{1,0:T(8,128)}), f32[96,512]{1,0:T(8,128)}) %reduce-scatter.30.cloned.1.call-update) | async-done | bytes 196624 | tf_op jit(solution)/shard_map/reduce_scatter | solution.py:302
  1995.7 38.7 %reduce-scatter.26.cloned.1.call-done = f32[96,192]{1,0:T(8,128)} async-done(((f32[768,192]{1,0:T(8,128)}), f32[96,192]{1,0:T(8,128)}) %reduce-scatter.26.cloned.1.call-update) | async-done | bytes 73744 | tf_op jit(solution)/shard_map/reduce_scatter | solution.py:299
  2034.4 38.6 %reduce-scatter.24.cloned.1.call-done = f32[96,192]{1,0:T(8,128)} async-done(((f32[768,192]{1,0:T(8,128)}), f32[96,192]{1,0:T(8,128)}) %reduce-scatter.24.cloned.1.call-update) | async-done | bytes 73744 | tf_op jit(solution)/shard_map/reduce_scatter | solution.py:298
  2073.0 38.6 %reduce-scatter.22.cloned.1.call-done = f32[96,192]{1,0:T(8,128)} async-done(((f32[768,192]{1,0:T(8,128)}), f32[96,192]{1,0:T(8,128)}) %reduce-scatter.22.cloned.1.call-update) | async-done | bytes 73744 | tf_op jit(solution)/shard_map/reduce_scatter | solution.py:297
  (813 shorter events, 755.3 us)
Async XLA Ops:
  7.2 48.5 %copy-start.55 = (s32[3584]{0:T(1024)S(1)}, s32[3584]{0:T(1024)}, u32[]{:S(2)}) copy-start(s32[3584]{0:T(1024)} %param.37) | copy-start | bytes 43012
  7.2 48.5 %copy-start.54 = (s32[3584]{0:T(1024)S(1)}, s32[3584]{0:T(1024)}, u32[]{:S(2)}) copy-start(s32[3584]{0:T(1024)} %param.36) | copy-start | bytes 43012
  7.2 48.5 %copy-start.77 = (s32[3584]{0:T(1024)S(1)}, s32[3584]{0:T(1024)}, u32[]{:S(2)}) copy-start(s32[3584]{0:T(1024)} %param.38) | copy-start | bytes 43012
  7.2 48.5 %copy-start.72 = (bf16[192,96]{1,0:T(8,128)(2,1)S(1)}, bf16[192,96]{1,0:T(8,128)(2,1)}, u32[]{:S(2)}) copy-start(bf16[192,96]{1,0:T(8,128)(2,1)} %param.31) | copy-start | bytes 110596
  7.2 60.3 %copy-start.69 = (bf16[96,192]{1,0:T(8,128)(2,1)S(1)}, bf16[96,192]{1,0:T(8,128)(2,1)}, u32[]{:S(2)}) copy-start(bf16[96,192]{1,0:T(8,128)(2,1)} %param.28) | copy-start | bytes 110596
  7.2 68.9 %copy-start.70 = (bf16[96,192]{1,0:T(8,128)(2,1)S(1)}, bf16[96,192]{1,0:T(8,128)(2,1)}, u32[]{:S(2)}) copy-start(bf16[96,192]{1,0:T(8,128)(2,1)} %param.29) | copy-start | bytes 110596
  7.2 78.4 %copy-start.71 = (bf16[96,192]{1,0:T(8,128)(2,1)S(1)}, bf16[96,192]{1,0:T(8,128)(2,1)}, u32[]{:S(2)}) copy-start(bf16[96,192]{1,0:T(8,128)(2,1)} %param.30) | copy-start | bytes 110596
  7.2 151.0 %all-gather.5.cloned.1.call-start = ((), (), s32[]{:S(2)}) async-start(), calls=%async_computation.11 | async-start | bytes 6881280 | tf_op jit(solution)/shard_map/all_gather | solution.py:120
  9.0 67.1 %copy-start.61 = (f32[896]{0:T(1024)}, f32[896]{0:T(1024)S(1)}, u32[]{:S(2)}) copy-start(f32[896]{0:T(1024)S(1)} %add_rsqrt_fusion.1) | copy-start | bytes 10756
  55.6 476.0 %reduce-scatter.14.cloned.1.call-start = ((), (), s32[]{:S(2)}) async-start(), calls=%async_computation.12 | async-start | bytes 6881280 | tf_op jit(solution)/shard_map/reduce_scatter | solution.py:124
  55.8 131.0 %copy-start.52 = (f32[3584]{0:T(1024)}, f32[3584]{0:T(1024)S(1)}, u32[]{:S(2)}) copy-start(f32[3584]{0:T(1024)S(1)} %convert_element_type.155) | copy-start | bytes 43012
  76.2 90.6 %copy-start.27 = (bf16[768,192]{1,0:T(8,128)(2,1)}, bf16[768,192]{1,0:T(8,128)(2,1)S(1)}, u32[]{:S(2)}) copy-start(bf16[768,192]{1,0:T(8,128)(2,1)S(1)} %all_gather.48) | copy-start | bytes 884740
  85.7 96.4 %copy-start.29 = (bf16[768,192]{1,0:T(8,128)(2,1)}, bf16[768,192]{1,0:T(8,128)(2,1)S(1)}, u32[]{:S(2)}) copy-start(bf16[768,192]{1,0:T(8,128)(2,1)S(1)} %all_gather.49) | copy-start | bytes 884740
  94.3 68.4 %copy-start.24 = (bf16[768,192]{1,0:T(8,128)(2,1)}, bf16[768,192]{1,0:T(8,128)(2,1)S(1)}, u32[]{:S(2)}) copy-start(bf16[768,192]{1,0:T(8,128)(2,1)S(1)} %all_gather.50) | copy-start | bytes 884740
  94.4 92.4 %copy-start.79 = (f32[64]{0:T(128)}, f32[64]{0:T(128)S(1)}, u32[]{:S(2)}) copy-start(f32[64]{0:T(128)S(1)} %pad_maximum_fusion.9) | copy-start | bytes 772
  344.1 85.7 %copy-start.34 = (bf16[7,8,8,512]{3,2,0,1:T(8,128)(2,1)S(1)}, bf16[7,8,8,512]{3,2,0,1:T(8,128)(2,1)}, u32[]{:S(2)}) copy-start(bf16[7,8,8,512]{3,2,0,1:T(8,128)(2,1)} %copy.123) | copy-start | bytes 1376260
  435.1 96.5 %copy-start = (bf16[896,768]{1,0:T(8,128)(2,1)S(1)}, bf16[896,768]{1,0:T(8,128)(2,1)}, u32[]{:S(2)}) copy-start(bf16[896,768]{1,0:T(8,128)(2,1)} %param.26) | copy-start | bytes 4128772
  435.1 98.5 %copy-start.67 = (f32[768]{0:T(1024)S(1)}, f32[768]{0:T(1024)}, u32[]{:S(2)}) copy-start(f32[768]{0:T(1024)} %get-tuple-element.1128) | copy-start | bytes 9220
  435.1 203.2 %all-gather.7.cloned.1.call-start = ((), (), s32[]{:S(2)}) async-start(), calls=%async_computation.13 | async-start | bytes 6881280 | tf_op jit(solution)/shard_map/all_gather | solution.py:120
  533.6 330.9 %copy-start.56 = (f32[896]{0:T(1024)}, f32[896]{0:T(1024)S(1)}, u32[]{:S(2)}) copy-start(f32[896]{0:T(1024)S(1)} %add_rsqrt_fusion) | copy-start | bytes 10756
  533.6 13.7 copy-start.59
  533.6 24.9 %copy-start.60 = (bf16[512,96]{0,1:T(8,128)(2,1)S(1)}, bf16[512,96]{0,1:T(8,128)(2,1)}, u32[]{:S(2)}) copy-start(bf16[512,96]{0,1:T(8,128)(2,1)} %param.35) | copy-start | bytes 294916
  535.2 205.3 %all-gather.9.cloned.1.call-start = ((), (), s32[]{:S(2)}) async-start(), calls=%async_computation.15 | async-start | bytes 6881280 | tf_op jit(solution)/shard_map/all_gather | solution.py:120
  535.8 325.3 %reduce-scatter.18.cloned.1.call-start = ((), (), s32[]{:S(2)}) async-start(), calls=%async_computation.16 | async-start | bytes 6881280 | tf_op jit(solution)/shard_map/reduce_scatter | solution.py:124
  638.3 9.2 copy-start.50
  638.3 9.2 copy-start.81
  740.5 13.4 copy-start.51
  764.7 205.0 %all-gather.11.cloned.1.call-start = ((), (), s32[]{:S(2)}) async-start(), calls=%async_computation.17 | async-start | bytes 6881280 | tf_op jit(solution)/shard_map/all_gather | solution.py:120
  866.6 852.1 %reduce-scatter.34.cloned.1.call-start = ((), (), s32[]{:S(2)}) async-start(), calls=%async_computation.25 | async-start | bytes 884736
  867.6 108.0 %copy-start.23 = (bf16[3584,192]{0,1:T(8,128)(2,1)S(1)}, bf16[3584,192]{0,1:T(8,128)(2,1)}, u32[]{:S(2)}) copy-start(bf16[3584,192]{0,1:T(8,128)(2,1)} %copy-done.22) | copy-start | bytes 4128772
  969.7 5.9 copy-start.17
  978.8 787.7 %reduce-scatter.20.cloned.1.call-start = ((), (), s32[]{:S(2)}) async-start(), calls=%async_computation.18 | async-start | bytes 6881280 | tf_op jit(solution)/shard_map/reduce_scatter | solution.py:124
  1205.0 215.8 %copy-start.2 = (f32[3584,64]{0,1:T(8,128)S(1)}, f32[3584,64]{0,1:T(8,128)}, u32[]{:S(2)}) copy-start(f32[3584,64]{0,1:T(8,128)} %custom-call.2) | copy-start | bytes 2752516
  1637.7 5.6 copy-start.4
  1637.7 5.6 copy-start.20
  1637.8 5.6 copy-start.53
  1637.8 5.6 copy-start.80
  1651.9 5.2 copy-start.42
  1651.9 5.2 copy-start.44
  1657.2 5.9 copy-start.25
  1657.2 5.9 copy-start.31
  1657.2 5.9 copy-start.32
  1657.2 5.9 copy-start.33
  1670.0 198.5 %reduce-scatter.16.cloned.1.call-start = ((), (), s32[]{:S(2)}) async-start(), calls=%async_computation.14 | async-start | bytes 6881280 | tf_op jit(solution)/shard_map/reduce_scatter | solution.py:124
  1678.6 232.5 %reduce-scatter.32.cloned.1.call-start = ((), (), s32[]{:S(2)}) async-start(), calls=%async_computation.24 | async-start | bytes 1769472 | tf_op jit(solution)/shard_map/reduce_scatter | solution.py:303
  1686.6 266.9 %reduce-scatter.28.cloned.1.call-start = ((), (), s32[]{:S(2)}) async-start(), calls=%async_computation.22 | async-start | bytes 1769472 | tf_op jit(solution)/shard_map/reduce_scatter | solution.py:301
  1694.8 300.9 %reduce-scatter.30.cloned.1.call-start = ((), (), s32[]{:S(2)}) async-start(), calls=%async_computation.23 | async-start | bytes 1769472 | tf_op jit(solution)/shard_map/reduce_scatter | solution.py:302
  1702.8 5.4 copy-start.43
  1702.8 5.4 copy-start.45
  1702.8 5.4 copy-start.47
  1702.8 331.6 %reduce-scatter.26.cloned.1.call-start = ((), (), s32[]{:S(2)}) async-start(), calls=%async_computation.21 | async-start | bytes 884736 | tf_op jit(solution)/shard_map/reduce_scatter | solution.py:299
  1708.0 5.4 copy-start.37
  1708.0 5.4 copy-start.39
  1708.0 5.4 copy-start.41
  1708.1 364.9 %reduce-scatter.24.cloned.1.call-start = ((), (), s32[]{:S(2)}) async-start(), calls=%async_computation.20 | async-start | bytes 884736 | tf_op jit(solution)/shard_map/reduce_scatter | solution.py:298
  1713.3 398.2 %reduce-scatter.22.cloned.1.call-start = ((), (), s32[]{:S(2)}) async-start(), calls=%async_computation.19 | async-start | bytes 884736 | tf_op jit(solution)/shard_map/reduce_scatter | solution.py:297
  1713.4 53.2 %copy-start.1 = (bf16[896,768]{1,0:T(8,128)(2,1)S(1)}, bf16[896,768]{1,0:T(8,128)(2,1)}, u32[]{:S(2)}) copy-start(bf16[896,768]{1,0:T(8,128)(2,1)} %param.26) | copy-start | bytes 4128772
  1713.4 53.1 %copy-start.62 = (f32[896]{0:T(1024)S(1)}, f32[896]{0:T(1024)}, u32[]{:S(2)}) copy-start(f32[896]{0:T(1024)} %copy-done.61) | copy-start | bytes 10756
  1713.4 53.1 %copy-start.74 = (f32[768]{0:T(1024)S(1)}, f32[768]{0:T(1024)}, u32[]{:S(2)}) copy-start(f32[768]{0:T(1024)} %copy-done.73) | copy-start | bytes 9220
  1718.6 50.4 %copy-start.78 = (f32[768]{0:T(1024)S(1)}, f32[768]{0:T(1024)}, u32[]{:S(2)}) copy-start(f32[768]{0:T(1024)} %get-tuple-element.983) | copy-start | bytes 9220
  1718.6 149.9 %copy-start.6 = (bf16[896,768]{1,0:T(8,128)(2,1)S(1)}, bf16[896,768]{1,0:T(8,128)(2,1)}, u32[]{:S(2)}) copy-start(bf16[896,768]{1,0:T(8,128)(2,1)} %reduce-scatter.14.cloned.1.call-done) | copy-start | bytes 4128772
  1718.6 149.9 %copy-start.57 = (f32[896]{0:T(1024)S(1)}, f32[896]{0:T(1024)}, u32[]{:S(2)}) copy-start(f32[896]{0:T(1024)} %copy-done.56) | copy-start | bytes 10756
  1718.6 149.9 %copy-start.68 = (f32[768]{0:T(1024)S(1)}, f32[768]{0:T(1024)}, u32[]{:S(2)}) copy-start(f32[768]{0:T(1024)} %get-tuple-element.1128) | copy-start | bytes 9220
  1718.6 149.9 %copy-start.76 = (f32[896]{0:T(1024)S(1)}, f32[896]{0:T(1024)}, u32[]{:S(2)}) copy-start(f32[896]{0:T(1024)} %copy-done.75) | copy-start | bytes 10756
  (58 other events, 192.8 us)
Sparse Core Ops, SparseCore 0:
  55.7 102.4 all-gather.4
  435.2 96.3 reduce-scatter.13
  535.4 102.9 all-gather.6
  639.7 100.7 all-gather.8
  764.8 96.3 reduce-scatter.17
  866.7 102.8 all-gather.10
  979.0 33.3 reduce-scatter.33
  1670.1 96.4 reduce-scatter.19
  1768.9 99.5 reduce-scatter.15
  1872.2 38.8 reduce-scatter.31
  1915.0 38.4 reduce-scatter.27
  1957.2 38.4 reduce-scatter.29
  1999.4 34.9 reduce-scatter.25
  2038.0 34.9 reduce-scatter.23
  2076.6 34.9 reduce-scatter.21
where the time goes:
time: 2130 us; the launch traced here: 2120 us
  waiting for transfers between devices  851 us (40%)
  matrix products  640 us (30%)
  other arithmetic  205 us (10%)
  blocking collectives  161 us (8%)
  local copies, waits for them, and re-layouts  160 us (8%)
  loops' own time  84.9 us (4%)
    all_gather x4, waiting for transfers between devices, gather_rows(): return lax.all_gather(values, 'tensor', axis=0, tiled=True)  323 us
    reduce_scatter x4, waiting for transfers between devices, scatter_rows(): lax.psum_scatter(term_fn(jnp.int32(0), local_rows * lax.axis_size('tensor...  290 us
    dot_general x42, matrix products, block_scores(): lax.dot_general(q_block, k_head, CONTRACT_COLS, preferred_element_type=jn...  239 us
    dot_general x21, matrix products, one_block(): lax.dot_general(prob_vals.astype(jnp.bfloat16), grad_block, CONTRACT_ROWS...  107 us
    convert_element_type x21, other arithmetic, one_block(): (prob_vals * (grad_probs - row_dot) * HEAD_DIM ** (-0.5)).astype(jnp.bflo...  106 us
    unnamed x2, blocking collectives  89.4 us
    dynamic_update_slice x42, local copies, waits for them, and re-layouts, head_backward(): lax.scan(one_block, (zeros_init, zeros_init), starts)  81.6 us
    dot_general x21, matrix products, one_block(): lax.dot_general(grad_block, v_head, CONTRACT_COLS, preferred_element_type...  53.9 us
  transfers between devices with their start and end apart: 15, of which 14 were waited for; matrix products, arithmetic and copies ran while one was open for 34% of the time, Pallas kernels for 0%

commit v1 on v0

v1 whole, which is shorter than its diff:
```python
import functools

import jax
import jax.numpy as jnp
from jax import lax
from jax.experimental import pallas as pl
from jax.experimental.pallas import tpu as pltpu
from jax.sharding import PartitionSpec as P

HEAD_DIM = 64
BLOCK = 256
TILE = 128
ROOT = 512
KEYS = 1024
EPSILON = 1e-05
MASKED = -1e30
VMEM = 60 * 1024 * 1024
F32 = jnp.float32
BF16 = jnp.bfloat16
ROWS = (((0,), (0,)), ((), ()))
COLS = (((1,), (1,)), ((), ()))


def dot(a, b, dims=(((1,), (0,)), ((), ()))):
    return lax.dot_general(a, b, dims, preferred_element_type=F32)


def half_turn(u):
    lane = lax.broadcasted_iota(jnp.int32, u.shape, 1)
    return jnp.where(lane % HEAD_DIM < HEAD_DIM // 2, pltpu.roll(u, 96, 1), pltpu.roll(u, 32, 1))


def proj_kernel(x_ref, xl_ref, gain_ref, wq_ref, wk_ref, wv_ref, cos_ref, sin_ref, cosl_ref, sinl_ref,
                a_ref, k_ref, v_ref, q_ref):
    def normed(ref):
        x = ref[...].astype(F32)
        scale = lax.rsqrt(jnp.mean(x * x, axis=-1, keepdims=True) + EPSILON)
        return (x * scale * gain_ref[...]).astype(BF16)

    def rotated(u, cos, sin, out_ref, factor):
        for c in range(u.shape[1] // 128):
            part = u[:, c * 128:(c + 1) * 128]
            r = (part * cos + half_turn(part) * sin).astype(BF16)
            out_ref[:, c * 128:(c + 1) * 128] = r * factor if factor is not None else r

    a = normed(x_ref)
    a_ref[...] = a
    rotated(dot(a, wk_ref[...]), cos_ref[...], sin_ref[...], k_ref, None)
    v_ref[...] = dot(a, wv_ref[...]).astype(BF16)
    al = normed(xl_ref)
    rotated(dot(al, wq_ref[...]), cosl_ref[...], sinl_ref[...], q_ref, jnp.asarray(HEAD_DIM ** -0.5, BF16))


def project(x_full, x_loc, gain, w_all, cos, sin, cos_l, sin_l):
    rows, d = x_full.shape
    loc = x_loc.shape[0]
    steps = loc // TILE
    big = rows // steps

    def tiles(n, w):
        return pl.BlockSpec((n, w), lambda i: (i, 0))

    def weight(j):
        return pl.BlockSpec((d, d), lambda i: (0, j))

    return pl.pallas_call(
        proj_kernel,
        grid=(steps,),
        in_specs=[tiles(big, d), tiles(TILE, d), pl.BlockSpec((1, d), lambda i: (0, 0)),
                  weight(0), weight(1), weight(2),
                  tiles(big, 128), tiles(big, 128), tiles(TILE, 128), tiles(TILE, 128)],
        out_specs=[tiles(big, d), tiles(big, d), tiles(big, d), tiles(TILE, d)],
        out_shape=[jax.ShapeDtypeStruct((rows, d), BF16)] * 3 + [jax.ShapeDtypeStruct((loc, d), BF16)],
        compiler_params=pltpu.CompilerParams(vmem_limit_bytes=VMEM),
        name="project",
    )(x_full, x_loc, gain, w_all, w_all, w_all, cos, sin, cos_l, sin_l)


def fill_bias(meta_ref, bias_ref, keys_axis):
    shape = bias_ref.shape[1:]

    def one(i, carry):
        sub, leaf = meta_ref[i, 0], meta_ref[i, 1]
        key = lax.broadcasted_iota(jnp.int32, shape, keys_axis)
        row = lax.broadcasted_iota(jnp.int32, shape, 1 - keys_axis)
        in_root = sub < ROOT // TILE
        root_top = jnp.where(in_root, sub * TILE, ROOT)
        own_top = jnp.where(in_root, -ROOT, (sub % 2) * TILE)
        root_ok = (key < ROOT) & (key <= row + root_top)
        parent_ok = (key >= ROOT) & (key < ROOT + jnp.where(leaf > 0, BLOCK, 0))
        own_ok = (key >= ROOT + BLOCK) & (key - (ROOT + BLOCK) <= row + own_top)
        bias_ref[i] = jnp.where(root_ok | parent_ok | own_ok, 0.0, MASKED).astype(F32)
        return carry

    lax.fori_loop(0, bias_ref.shape[0], one, 0)


def half_masks():
    lane = lax.broadcasted_iota(jnp.int32, (TILE, 128), 1)
    return lane < HEAD_DIM


def fwd_kernel(meta_ref, q_ref, k_ref, v_ref, o_ref, l_ref, bias_ref):
    @pl.when(pl.program_id(0) == 0)
    def _():
        fill_bias(meta_ref, bias_ref, 1)

    low = half_masks()

    def one(i, carry):
        row = pl.multiple_of(i * TILE, TILE)
        par = pl.multiple_of(meta_ref[i, 2], BLOCK)
        own = pl.multiple_of(meta_ref[i, 3], TILE)
        q = q_ref[pl.ds(row, TILE), :]
        spans = ((pl.ds(0, ROOT), 0, ROOT), (pl.ds(par, BLOCK), ROOT, BLOCK), (pl.ds(own, BLOCK), ROOT + BLOCK, BLOCK))
        outs = []
        logs = []
        for head in range(2):
            qh = jnp.where(low if head == 0 else ~low, q, jnp.zeros_like(q))
            s = [dot(qh, k_ref[sl, :], COLS) + bias_ref[i, :, at:at + n] for sl, at, n in spans]
            top = functools.reduce(jnp.maximum, [jnp.max(part, axis=1, keepdims=True) for part in s])
            e = [jnp.exp(part - top) for part in s]
            total = sum(jnp.sum(part, axis=1, keepdims=True) for part in e)
            acc = sum(dot(part.astype(BF16), v_ref[sl, :]) for part, (sl, _, _) in zip(e, spans))
            outs.append(acc / total)
            logs.append(top + jnp.log(total))
        o_ref[pl.ds(row, TILE), :] = jnp.where(low, outs[0], outs[1]).astype(BF16)
        both = jnp.where(low, logs[0], logs[1]).T
        l_ref[0, :, pl.ds(row, TILE)] = both[60:68, :]
        return carry

    lax.fori_loop(0, q_ref.shape[0] // TILE, one, 0)


def attend(meta, q, k, v):
    loc, d = q.shape
    rows = k.shape[0]
    pairs = d // 128
    pair = lambda n: pl.BlockSpec((n, 128), lambda p: (0, p))
    return pl.pallas_call(
        fwd_kernel,
        grid=(pairs,),
        in_specs=[pl.BlockSpec(memory_space=pltpu.SMEM), pair(loc), pair(rows), pair(rows)],
        out_specs=[pair(loc), pl.BlockSpec((1, 8, loc), lambda p: (p, 0, 0))],
        out_shape=[jax.ShapeDtypeStruct((loc, d), BF16), jax.ShapeDtypeStruct((pairs, 8, loc), F32)],
        scratch_shapes=[pltpu.VMEM((loc // TILE, TILE, KEYS), F32)],
        compiler_params=pltpu.CompilerParams(vmem_limit_bytes=VMEM),
        name="attend",
    )(meta, q, k, v)


def bwd_kernel(meta_ref, q_ref, k_ref, v_ref, do_ref, o_ref, l_ref, cos_ref, sin_ref, cosl_ref, sinl_ref,
               dq_ref, dk_ref, dv_ref, bias_ref, dk_acc, dv_acc):
    @pl.when(pl.program_id(0) == 0)
    def _():
        fill_bias(meta_ref, bias_ref, 0)

    low = half_masks()
    dk_acc[...] = jnp.zeros_like(dk_acc)
    dv_acc[...] = jnp.zeros_like(dv_acc)

    def one(i, carry):
        row = pl.multiple_of(i * TILE, TILE)
        par = pl.multiple_of(meta_ref[i, 2], BLOCK)
        own = pl.multiple_of(meta_ref[i, 3], TILE)
        here = pl.ds(row, TILE)
        q = q_ref[here, :]
        do = do_ref[here, :]
        dots = (do.astype(F32) * o_ref[here, :].astype(F32)).T
        spans = ((pl.ds(0, ROOT), 0, ROOT), (pl.ds(par, BLOCK), ROOT, BLOCK), (pl.ds(own, BLOCK), ROOT + BLOCK, BLOCK))
        dqs = []
        for head in range(2):
            keep = low if head == 0 else ~low
            qh = jnp.where(keep, q, jnp.zeros_like(q))
            doh = jnp.where(keep, do, jnp.zeros_like(do))
            log = l_ref[0, 3 + head:4 + head, here]
            row_dot = jnp.sum(dots[head * HEAD_DIM:(head + 1) * HEAD_DIM, :], axis=0, keepdims=True)
            dq = jnp.zeros((TILE, 128), F32)
            for sl, at, n in spans:
                kk = k_ref[sl, :]
                s = dot(kk, qh, COLS) + bias_ref[i, at:at + n, :]
                p = jnp.exp(s - log)
                dp = dot(v_ref[sl, :], doh, COLS)
                ds = (p * (dp - row_dot)).astype(BF16)
                dv_acc[sl, :] += dot(p.astype(BF16), doh)
                dk_acc[sl, :] += dot(ds, qh)
                dq += dot(ds, kk, ROWS)
            dqs.append(dq)
        dq = jnp.where(low, dqs[0], dqs[1]) * HEAD_DIM ** -0.5
        dq_ref[here, :] = (dq * cosl_ref[here, :] - half_turn(dq) * sinl_ref[here, :]).astype(BF16)
        return carry

    lax.fori_loop(0, q_ref.shape[0] // TILE, one, 0)

    def last(j, carry):
        here = pl.ds(pl.multiple_of(j * BLOCK, BLOCK), BLOCK)
        dk = dk_acc[here, :]
        dk_ref[here, :] = (dk * cos_ref[here, :] - half_turn(dk) * sin_ref[here, :]).astype(BF16)
        dv_ref[here, :] = dv_acc[here, :].astype(BF16)
        return carry

    lax.fori_loop(0, k_ref.shape[0] // BLOCK, last, 0)


def attend_back(meta, q, k, v, do, o, logs, cos, sin, cos_l, sin_l):
    loc, d = q.shape
    rows = k.shape[0]
    pairs = d // 128
    pair = lambda n: pl.BlockSpec((n, 128), lambda p: (0, p))
    whole = lambda n: pl.BlockSpec((n, 128), lambda p: (0, 0))
    return pl.pallas_call(
        bwd_kernel,
        grid=(pairs,),
        in_specs=[pl.BlockSpec(memory_space=pltpu.SMEM), pair(loc), pair(rows), pair(rows), pair(loc), pair(loc),
                  pl.BlockSpec((1, 8, loc), lambda p: (p, 0, 0)), whole(rows), whole(rows), whole(loc), whole(loc)],
        out_specs=[pair(loc), pair(rows), pair(rows)],
        out_shape=[jax.ShapeDtypeStruct((loc, d), BF16)] + [jax.ShapeDtypeStruct((rows, d), BF16)] * 2,
        scratch_shapes=[pltpu.VMEM((loc // TILE, KEYS, TILE), F32), pltpu.VMEM((rows, 128), F32), pltpu.VMEM((rows, 128), F32)],
        compiler_params=pltpu.CompilerParams(vmem_limit_bytes=VMEM),
        name="attend_back",
    )(meta, q, k, v, do, o, logs, cos, sin, cos_l, sin_l)


def tables(pos):
    half = HEAD_DIM // 2
    freq = jnp.exp(-jnp.log(10000.0) * (2.0 * jnp.arange(half, dtype=F32) / HEAD_DIM))
    angle = pos.astype(F32)[:, None] * jnp.concatenate([freq, freq, freq, freq])[None, :]
    sign = jnp.where(jnp.arange(2 * HEAD_DIM) % HEAD_DIM < half, -1.0, 1.0).astype(F32)
    return jnp.cos(angle), jnp.sin(angle) * sign[None, :]


def norm_back(grad_out, x_hat, scale, gain):
    scaled = grad_out * gain
    return scale * (scaled - x_hat * jnp.mean(scaled * x_hat, axis=-1, keepdims=True))


def per_device(tokens, gain_attn, w_query, w_key, w_value, w_out, gain_ffn, w_gate, w_up, w_down,
               segment_ids, parent_ids, positions, cotangent):
    loc, d = tokens.shape
    t_size = lax.axis_size("tensor")
    t_at = lax.axis_index("tensor")
    rows = loc * t_size
    ff = w_gate.shape[1] * t_size

    gains = jnp.zeros((8, 128), F32)
    own_gain = gain_attn.shape[0]
    gains = gains.at[0, :own_gain].set(gain_attn).at[1, :own_gain].set(gain_ffn)
    gains = lax.all_gather(gains, ("dp", "tensor"), axis=0, tiled=False)
    gain_one = gains[:, 0, :own_gain].reshape(1, d)
    gain_two = gains[:, 1, :own_gain].reshape(1, d)

    x_full = lax.all_gather(tokens, "tensor", axis=0, tiled=True)

    parts = (w_query, w_key, w_value, w_out.T, w_gate, w_up, w_down.T)
    pack = jnp.concatenate(parts, axis=1)
    pack = lax.all_gather(pack, "tensor", axis=0, tiled=False)
    cuts = []
    at = 0
    for part in parts:
        n = part.shape[1]
        cuts.append(jnp.swapaxes(pack[:, :, at:at + n], 0, 1).reshape(part.shape[0], n * t_size))
        at += n
    w_qkv = lax.all_gather(jnp.concatenate(cuts[:3], axis=1), "dp", axis=0, tiled=True)
    w_rest = lax.all_gather(jnp.concatenate(cuts[3:], axis=1), "dp", axis=0, tiled=True)
    out_t = w_rest[:, :d]
    gate = w_rest[:, d:d + ff]
    up = w_rest[:, d + ff:d + 2 * ff]
    down_t = w_rest[:, d + 2 * ff:]

    seg = segment_ids[::BLOCK]
    par = parent_ids[::BLOCK]
    sub = t_at * (loc // TILE) + jnp.arange(loc // TILE, dtype=jnp.int32)
    block = sub // 2
    my_par = par[block]
    parent = jnp.argmax(seg[None, :] == my_par[:, None], axis=1).astype(jnp.int32)
    leaf = ((my_par != seg[0]) & (block >= 2)).astype(jnp.int32)
    meta = jnp.stack([sub, leaf, parent * BLOCK * leaf, block * BLOCK], axis=1)

    cos, sin = tables(positions)
    cos_l = lax.dynamic_slice_in_dim(cos, t_at * loc, loc, 0)
    sin_l = lax.dynamic_slice_in_dim(sin, t_at * loc, loc, 0)

    a_full, k, v, q = project(x_full, tokens, gain_one, w_qkv, cos, sin, cos_l, sin_l)
    o, logs = attend(meta, q, k, v)

    x = tokens.astype(F32)
    scale_one = lax.rsqrt(jnp.mean(x * x, axis=-1, keepdims=True) + EPSILON)
    h = x + dot(o, out_t, COLS)
    scale_two = lax.rsqrt(jnp.mean(h * h, axis=-1, keepdims=True) + EPSILON)
    c_hat = h * scale_two
    c = (c_hat * gain_two).astype(BF16)
    g = dot(c, gate)
    u = dot(c, up)
    sig = jax.nn.sigmoid(g)
    silu = g * sig
    m = (silu * u).astype(BF16)
    mixed = (h + dot(m, down_t, COLS)).astype(BF16)

    dm = dot(cotangent, down_t)
    dg = (dm * u * sig * (1.0 + g * (1.0 - sig))).astype(BF16)
    du = (dm * silu).astype(BF16)
    g_down = dot(cotangent, m, ROWS)
    g_gate = dot(c, dg, ROWS)
    g_up = dot(c, du, ROWS)
    dc = dot(dg, gate, COLS) + dot(du, up, COLS)
    gain_two_sum = jnp.sum(dc * c_hat, axis=0)
    dh = cotangent.astype(F32) + norm_back(dc, c_hat, scale_two, gain_two)
    dhb = dh.astype(BF16)
    do = dot(dhb, out_t).astype(BF16)
    g_out = dot(dhb, o, ROWS)
    rest = jnp.concatenate([g_out.astype(BF16), g_gate.astype(BF16), g_up.astype(BF16), g_down.astype(BF16)], axis=1)

    def owners(grads, widths):
        mine = lax.psum_scatter(grads, "dp", scatter_dimension=0, tiled=True)
        pieces = []
        at = 0
        for n in widths:
            pieces.append(jnp.swapaxes(mine[:, at:at + n].reshape(mine.shape[0], t_size, n // t_size), 0, 1))
            at += n
        packed = jnp.concatenate(pieces, axis=2)
        total = lax.psum_scatter(packed, "tensor", scatter_dimension=0, tiled=False).astype(F32)
        outs = []
        at = 0
        for n in widths:
            outs.append(total[:, at:at + n // t_size])
            at += n // t_size
        return outs

    r_out, r_gate, r_up, r_down = owners(rest, (d, ff, ff, ff))

    dq, dk, dv = attend_back(meta, q, k, v, do, o, logs, cos, sin, cos_l, sin_l)
    w_q, w_k, w_v = w_qkv[:, :d], w_qkv[:, d:2 * d], w_qkv[:, 2 * d:]
    da_part = (dot(dk, w_k, COLS) + dot(dv, w_v, COLS)).astype(BF16)
    da_sum = lax.psum_scatter(da_part, "tensor", scatter_dimension=0, tiled=True)
    a_loc = lax.dynamic_slice_in_dim(a_full, t_at * loc, loc, 0)
    g_qkv = jnp.concatenate([dot(a_loc, dq, ROWS).astype(BF16), dot(a_full, dk, ROWS).astype(BF16),
                             dot(a_full, dv, ROWS).astype(BF16)], axis=1)
    r_q, r_k, r_v = owners(g_qkv, (d, d, d))
    da = da_sum.astype(F32) + dot(dq, w_q, COLS)
    x_hat = x * scale_one
    grad_tokens = dh + norm_back(da, x_hat, scale_one, gain_one)
    gain_one_sum = jnp.sum(da * x_hat, axis=0)
    sums = lax.psum(jnp.stack([gain_one_sum, gain_two_sum]), ("dp", "tensor"))
    at = (lax.axis_index("dp") * t_size + t_at) * own_gain
    mine = lax.dynamic_slice_in_dim(sums, at, own_gain, 1)
    return (mixed, grad_tokens, mine[0], r_q, r_k, r_v, r_out.T, mine[1], r_gate, r_up, r_down.T)


def solution(mesh):
    rows = P(("dp", "tensor"), None)
    gain = P(("dp", "tensor"))
    wide = P("dp", "tensor")
    tall = P("tensor", "dp")
    return jax.shard_map(
        per_device,
        mesh=mesh,
        in_specs=(rows, gain, wide, wide, wide, tall, gain, wide, wide, tall, P("dp"), P("dp"), P("dp"), rows),
        out_specs=(rows, rows, gain, wide, wide, wide, tall, gain, wide, wide, tall),
        check_vma=False,
    )
```

time: 2130 us -> 736 us (0.35)
  waiting for transfers between devices: 851 us -> 262 us
  matrix products: 640 us -> 107 us
  other arithmetic: 205 us -> 22.9 us
  Pallas kernels: 0 us -> 147 us
  local copies, waits for them, and re-layouts: 160 us -> 63.7 us
  loops' own time: 84.9 us -> 0 us
  blocking collectives: 161 us -> 112 us
    dot_general x167 -> x18, matrix products: 637 us -> 107 us  [dot(): return lax.dot_general(a, b, dims, preferred_element_type=F32)]
    reduce_scatter x10 -> x3, waiting for transfers between devices: 528 us -> 54.9 us  [the longest x1 54.7 us: owners(): mine = lax.psum_scatter(grads, 'dp', scatter_dimension=0, tiled=True)]
    all_gather x4, waiting for transfers between devices: 323 us -> 98.4 us  [the longest x1 42.4 us: per_device(): pack = lax.all_gather(pack, 'tensor', axis=0, tiled=False)]
    pallas_call x0 -> x3, Pallas kernels: none -> 147 us  [the longest x1 90.7 us: attend_back(): pl.pallas_call(bwd_kernel, grid=(pairs,), in_specs=[pl.BlockSpec(memory_s...]
    convert_element_type x32 -> x5, other arithmetic: 133 us -> 2.25 us  [the longest x2 1.94 us: owners(): lax.psum_scatter(packed, 'tensor', scatter_dimension=0, tiled=False)]
    unnamed x16 -> x11, waiting for transfers between devices: 0.77 us -> 109 us
    unnamed x2 -> x0, blocking collectives: 89.4 us -> none
    another operation x6 -> x0, loops' own time: 84.9 us -> none  [the longest x3 42.5 us: head_backward(): lax.scan(one_block, (zeros_init, zeros_init), starts)]
  transfers between devices with their start and end apart: 15 -> 9, of which waited for: 14 -> 8; matrix products, arithmetic and copies ran while one was open for 34% -> 17% of each run, Pallas kernels for 0% -> 8%
where the time goes in v1:
time: 736 us; the launch traced here: 731 us
  waiting for transfers between devices  262 us (36%)
  Pallas kernels  147 us (20%)
  blocking collectives  112 us (15%)
  matrix products  107 us (15%)
  local copies, waits for them, and re-layouts  63.7 us (9%)
  other arithmetic  22.9 us (3%)
  between operations  14.7 us (2%)
    unnamed x11, waiting for transfers between devices  109 us
    dot_general x18, matrix products, dot(): return lax.dot_general(a, b, dims, preferred_element_type=F32)  107 us
    pallas_call x1, Pallas kernels, attend_back(): pl.pallas_call(bwd_kernel, grid=(pairs,), in_specs=[pl.BlockSpec(memory_s...  90.7 us
    all_gather x1, blocking collectives, per_device(): gains = lax.all_gather(gains, ('dp', 'tensor'), axis=0, tiled=False)  69.9 us
    reduce_scatter x1, waiting for transfers between devices, owners(): mine = lax.psum_scatter(grads, 'dp', scatter_dimension=0, tiled=True)  54.7 us
    all_gather x1, waiting for transfers between devices, per_device(): pack = lax.all_gather(pack, 'tensor', axis=0, tiled=False)  42.4 us
    psum x1, blocking collectives, per_device(): sums = lax.psum(jnp.stack([gain_one_sum, gain_two_sum]), ('dp', 'tensor'))  42.1 us
    pallas_call x1, Pallas kernels, attend(): pl.pallas_call(fwd_kernel, grid=(pairs,), in_specs=[pl.BlockSpec(memory_s...  39.1 us
  transfers between devices with their start and end apart: 9, of which 8 were waited for; matrix products, arithmetic and copies ran while one was open for 17% of the time, Pallas kernels for 8%

profile of v1, /device:TPU:0, one launch (start us, length us, event | category | flops | bytes accessed | tf_op | source)
XLA Modules:
  0.0 730.6 jit_solution(69037357627027192)
XLA Ops:
  7.2 0.9 copy.116
  8.1 2.0 concatenate.28
  10.9 42.4 %all-gather.12.cloned.1.call-done = bf16[384,2304]{1,0:T(8,128)(2,1)} async-done(((bf16[96,2304]{1,0:T(8,128)(2,1)}), bf16[384,2304]{1,0:T(8,128)(2,1)}) %all-gather.12.cloned.1.call-update) | async-done | bytes 1769488 | tf_op jit(solution)/shard_map/all_gather | solution.py:256
  53.3 1.5 fusion.48
  58.4 1.1 pad_maximum_fusion.2
  64.2 69.9 %all_gather.26 = f32[32,8,128]{2,1,0:T(8,128)S(1)} all-gather(f32[1,8,128]{2,1,0:T(8,128)S(1)} %scatter.9), channel_id=1, replica_groups=mesh['dp'=8,'tensor'=4] {'dp','tensor'}, dimensions={0}, use_global_device_ids=true | all-gather | bytes 135168 | tf_op jit(solution)/shard_map/all_gather | solution.py:248
  134.9 2.6 copy.125
  138.3 6.4 fusion.27
  144.8 1.2 copy-done.2
  146.0 1.0 constant_dynamic-slice_fusion.1
  147.0 11.5 %all-gather.6.cloned.1.call-done.x_ref = bf16[3584,768]{1,0:T(8,128)(2,1)} async-done(((bf16[896,768]{1,0:T(8,128)(2,1)}), bf16[3584,768]{1,0:T(8,128)(2,1)}) %all-gather.6.cloned.1.call-update) | async-done | bytes 5505040 | tf_op jit(solution)/shard_map/all_gather | solution.py:252
  158.5 35.0 %all-gather.8.cloned.1.call-done.wq_ref.wk_ref.wv_ref = bf16[768,2304]{1,0:T(8,128)(2,1)} async-done(((bf16[96,2304]{1,0:T(8,128)(2,1)}), bf16[768,2304]{1,0:T(8,128)(2,1)}) %all-gather.8.cloned.1.call-update) | async-done | bytes 3538960 | tf_op jit(solution)/shard_map/all_gather | solution.py:263
  193.5 17.5 %project.1 = (bf16[3584,768]{1,0:T(8,128)(2,1)}, bf16[3584,768]{1,0:T(8,128)(2,1)}, bf16[3584,768]{1,0:T(8,128)(2,1)}, bf16[896,768]{1,0:T(8,128)(2,1)}) custom-call(bf16[3584,768]{1,0:T(8,128)(2,1)} %all-gather.6.cloned.1.call-done.x_ref, bf16[896,768]{1,0:T(8,128)(2,1)} %xl_ref.1, f32[1,768]{1,0:T(1,128)} %reshape_squeeze.4.gain_ref, ...), custom_call_target="tpu_custom_call" | custom-call | tf_op jit(solution)/shard_map/project/pallas_call | solution.py:66
  211.1 39.1 %attend.1 = (bf16[896,768]{1,0:T(8,128)(2,1)}, f32[6,8,896]{2,1,0:T(8,128)}) custom-call(s32[7,4]{1,0:T(8,128)} %pad_add_fusion.meta_ref, bf16[896,768]{1,0:T(8,128)(2,1)} %get-tuple-element.46.q_ref, bf16[3584,768]{1,0:T(8,128)(2,1)} %get-tuple-element.47.k_ref, bf16[3584,768]{1,0:T(8,128)(2,1)} %get-tuple-element.48.v_ref), custom_call_target="tpu_custom_call" | custom-call | tf_op jit(solution)/shard_map/attend/pallas_call | solution.py:140
  250.2 9.5 %all-gather.10.cloned.1.call-done = bf16[768,6912]{1,0:T(8,128)(2,1)} async-done(((bf16[96,6912]{1,0:T(8,128)(2,1)}), bf16[768,6912]{1,0:T(8,128)(2,1)}) %all-gather.10.cloned.1.call-update) | async-done | bytes 10616848 | tf_op jit(solution)/shard_map/all_gather | solution.py:264
  259.7 3.3 multiply_reduce_fusion.2
  263.3 2.2 copy-done.21
  266.0 5.5 fusion.9
  271.5 5.3 fusion.19
  276.8 11.2 %fusion.2 = (bf16[896,2048]{1,0:T(8,128)(2,1)S(1)}, bf16[896,2048]{1,0:T(8,128)(2,1)}, bf16[896,2048]{1,0:T(8,128)(2,1)}) fusion(f32[2048,896]{0,1:T(8,128)} %fusion.9, f32[896,2048]{1,0:T(8,128)} %fusion.19, bf16[896,768]{0,1:T(8,128)(2,1)S(1)} %multiply_convert_fusion.1, bf16[768,6912]{1,0:T(8,128)(2,1)S(1)} %copy-done.21), kind=kOutput, calls=%fused_computation.7 | convolution fusion | flops 2846097408 | bytes 30212096 | tf_op jit(solution)/shard_map/dot_general | solution.py:25
  288.0 6.8 fusion.13
  294.9 4.4 multiply_reduce_fusion
  300.0 2.4 convolution_convert_fusion.3.do_ref
  302.4 90.7 %attend_back.1 = (bf16[896,768]{1,0:T(8,128)(2,1)}, bf16[3584,768]{1,0:T(8,128)(2,1)}, bf16[3584,768]{1,0:T(8,128)(2,1)}) custom-call(s32[7,4]{1,0:T(8,128)} %pad_add_fusion.meta_ref, bf16[896,768]{1,0:T(8,128)(2,1)} %get-tuple-element.46.q_ref, bf16[3584,768]{1,0:T(8,128)(2,1)} %get-tuple-element.47.k_ref, bf16[3584,768]{1,0:T(8,128)(2,1)} %get-tuple-element.48.v_ref, ...), custom_call_target="tpu_custom_call" | custom-call | tf_op jit(solution)/shard_map/attend_back/pallas_call | solution.py:211
  393.1 8.8 %convolution_convert_fusion.5 = bf16[768,768]{0,1:T(8,128)(2,1)S(1)} fusion(bf16[3584,768]{1,0:T(8,128)(2,1)} %get-tuple-element.54, bf16[3584,768]{1,0:T(8,128)(2,1)} %get-tuple-element.52), kind=kOutput, calls=%fused_computation.54 | convolution fusion | flops 4228448256 | bytes 12189696 | tf_op jit(solution)/shard_map/dot_general | solution.py:25
  402.0 4.6 convolution_convert_fusion.6
  406.6 1.4 convolution_convert_fusion.7
  408.5 4.0 copy.151
  412.8 1.5 copy-done.7
  414.3 3.8 convolution_convert_fusion.4
  418.0 1.6 copy.135
  419.6 6.5 convolution_convert_fusion.1
  426.2 3.6 convolution_convert_fusion.2
  429.8 3.7 fusion.8
  433.6 4.6 pad_maximum_fusion
  438.2 1.9 copy-done
  440.2 9.7 %fusion.36 = f32[3584,768]{1,0:T(8,128)} fusion(bf16[3584,768]{1,0:T(8,128)(2,1)} %get-tuple-element.51, bf16[768,2304]{1,0:T(8,128)(2,1)S(1)} %copy-done), kind=kOutput, calls=%fused_computation.61 | convolution fusion | flops 4227858432 | bytes 17694720 | tf_op jit(solution)/shard_map/dot_general | solution.py:25
  449.8 10.9 %reduce-scatter.18.cloned.1.call-done = bf16[96,2304]{1,0:T(8,128)(2,1)} async-done(((bf16[768,2304]{1,0:T(8,128)(2,1)}), bf16[96,2304]{1,0:T(8,128)(2,1)}) %reduce-scatter.18.cloned.1.call-update) | async-done | bytes 442384
  460.7 1.8 fusion.51
  462.6 1.7 copy.162
  464.3 1.7 copy.133
  466.0 1.7 copy.161
  467.7 1.7 copy.132
  469.5 1.7 copy.160
  471.2 1.8 copy.131
  473.0 2.3 pad_maximum_fusion.3
  475.3 13.4 %add_convert_fusion = bf16[3584,768]{1,0:T(8,128)(2,1)} fusion(f32[3584,768]{1,0:T(8,128)} %fusion.36, bf16[3584,768]{1,0:T(8,128)(2,1)} %get-tuple-element.52, bf16[768,2304]{1,0:T(8,128)(2,1)S(1)} %copy-done), kind=kOutput, calls=%fused_computation.1 | convolution fusion | flops 4233363456 | bytes 23199744 | tf_op jit(solution)/shard_map/dot_general | solution.py:25
  489.7 1.9 fusion.26
  491.6 54.7 %reduce-scatter.12.cloned.1.call-done = bf16[96,6912]{1,0:T(8,128)(2,1)} async-done(((bf16[768,6912]{1,0:T(8,128)(2,1)}), bf16[96,6912]{1,0:T(8,128)(2,1)}) %reduce-scatter.12.cloned.1.call-update) | async-done | bytes 1327120 | tf_op jit(solution)/shard_map/reduce_scatter | solution.py:314
  546.3 1.6 slice.199
  547.9 1.8 reshape.265
  549.7 1.6 copy.180
  551.3 1.3 fusion.50
  555.0 3.8 concatenate.35
  558.8 8.4 %add_convert_fusion.1 = bf16[896,768]{0,1:T(8,128)(2,1)} fusion(f32[896,768]{0,1:T(8,128)} %copy-done.9, bf16[896,2048]{1,0:T(8,128)(2,1)} %get-tuple-element.107, bf16[768,6912]{1,0:T(8,128)(2,1)} %all-gather.10.cloned.1.call-done), kind=kOutput, calls=%fused_computation.45 | convolution fusion | flops 2819948544 | bytes 10944512 | tf_op jit(solution)/shard_map/dot_general | solution.py:25
  567.3 2.5 copy.140
  570.0 0.9 bitcast_convert_fusion.1
  571.7 97.1 %reduce-scatter.16.cloned.1.call-done = bf16[896,768]{1,0:T(8,128)(2,1)} async-done(((bf16[3584,768]{1,0:T(8,128)(2,1)}), bf16[896,768]{1,0:T(8,128)(2,1)}) %reduce-scatter.16.cloned.1.call-update) | async-done | bytes 1376272
  668.8 2.5 copy.150
  671.3 4.1 fusion.25
  676.1 2.2 copy.141
  678.3 42.1 %psum.7 = f32[2,768]{1,0:T(2,128)S(1)} all-reduce(f32[2,768]{1,0:T(2,128)S(1)} %pad_maximum_fusion.5), channel_id=1, replica_groups=mesh['dp'=8,'tensor'=4] {'dp','tensor'}, use_global_device_ids=true, to_apply=%region_8.9 | all-reduce | flops 1536 | bytes 12288 | tf_op jit(solution)/shard_map/psum | solution.py:343
  721.0 1.0 bitcast_convert_fusion
  722.1 1.0 slice_bitcast_fusion
  (132 shorter events, 19.3 us)
Async XLA Ops:
  7.2 46.1 %all-gather.12.cloned.1.call-start = ((), (), s32[]{:S(2)}) async-start(), calls=%async_computation.11 | async-start | bytes 2211840 | tf_op jit(solution)/shard_map/all_gather | solution.py:256
  10.1 148.4 %all-gather.6.cloned.1.call-start = ((), (), s32[]{:S(2)}) async-start(), calls=%async_computation.5 | async-start | bytes 6881280 | tf_op jit(solution)/shard_map/all_gather | solution.py:252
  10.8 182.7 %all-gather.8.cloned.1.call-start = ((), (), s32[]{:S(2)}) async-start(), calls=%async_computation.6 | async-start | bytes 3981312 | tf_op jit(solution)/shard_map/all_gather | solution.py:263
  53.3 3.6 copy-start.11
  56.8 202.9 %all-gather.10.cloned.1.call-start = ((), (), s32[]{:S(2)}) async-start(), calls=%async_computation.7 | async-start | bytes 11943936 | tf_op jit(solution)/shard_map/all_gather | solution.py:264
  58.1 1.5 copy-start.5
  59.5 4.4 copy-start.19
  59.5 4.4 copy-start.20
  59.5 75.3 %copy-start.17 = (s32[3584]{0:T(1024)S(1)}, s32[3584]{0:T(1024)}, u32[]{:S(2)}) copy-start(s32[3584]{0:T(1024)} %param.30) | copy-start | bytes 43012
  59.6 401.2 %reduce-scatter.18.cloned.1.call-start = ((), (), s32[]{:S(2)}) async-start(), calls=%async_computation.13 | async-start | bytes 3981312
  60.5 199.2 %copy-start.3 = (bf16[896,768]{0,1:T(8,128)(2,1)}, bf16[896,768]{0,1:T(8,128)(2,1)S(1)}, u32[]{:S(2)}) copy-start(bf16[896,768]{0,1:T(8,128)(2,1)S(1)} %copy.113) | copy-start | bytes 4128772
  144.7 1.2 copy-start.2
  144.8 48.8 %copy-start.1 = (f32[3584,128]{1,0:T(8,128)}, f32[3584,128]{1,0:T(8,128)S(1)}, u32[]{:S(2)}) copy-start(f32[3584,128]{1,0:T(8,128)S(1)} %get-tuple-element.128.sin_ref) | copy-start | bytes 5505028
  259.7 5.8 copy-start.21
  263.0 36.3 %copy-start.9 = (f32[896,768]{0,1:T(8,128)}, f32[896,768]{0,1:T(8,128)S(1)}, u32[]{:S(2)}) copy-start(f32[896,768]{0,1:T(8,128)S(1)} %get-tuple-element.133) | copy-start | bytes 8257540
  263.0 3.1 copy-start.12
  266.0 10.8 %copy-start.14 = (bf16[896,768]{0,1:T(8,128)(2,1)}, bf16[896,768]{0,1:T(8,128)(2,1)S(1)}, u32[]{:S(2)}) copy-start(bf16[896,768]{0,1:T(8,128)(2,1)S(1)} %multiply_convert_fusion.1) | copy-start | bytes 4128772
  288.0 6.8 copy-start.24
  294.9 4.5 copy-start.10
  300.0 2.4 copy-start.6
  302.4 99.5 %slice-start = ((s8[5505024]{0:T(1024)(128)(4,1)}), s8[1310720]{0:T(1024)(128)(4,1)S(1)}, s32[]{:S(2)}) async-start(s8[5505024]{0:T(1024)(128)(4,1)} %bitcast.140), calls=%async_computation.14 | async-start | bytes 2621440
  393.1 8.9 %copy-start.22 = (bf16[3584,768]{1,0:T(8,128)(2,1)S(1)}, bf16[3584,768]{1,0:T(8,128)(2,1)}, u32[]{:S(2)}) copy-start(bf16[3584,768]{1,0:T(8,128)(2,1)} %get-tuple-element.51) | copy-start | bytes 16515076
  393.1 8.9 %slice-start.1 = ((s8[5505024]{0:T(1024)(128)(4,1)}), s8[4194304]{0:T(1024)(128)(4,1)S(1)}, s32[]{:S(2)}) async-start(s8[5505024]{0:T(1024)(128)(4,1)} %bitcast.140), calls=%async_computation.15 | async-start | bytes 8388608
  402.0 4.6 copy-start.23
  412.5 1.8 copy-start.7
  412.5 133.8 %reduce-scatter.12.cloned.1.call-start = ((), (), s32[]{:S(2)}) async-start(), calls=%async_computation.9 | async-start | bytes 11943936 | tf_op jit(solution)/shard_map/reduce_scatter | solution.py:314
  419.6 6.5 copy-start.15
  419.6 6.5 copy-start.25
  426.1 3.7 copy-start.13
  426.2 3.7 copy-start.26
  438.2 2.0 copy-start
  438.2 131.8 %reduce-scatter.10.cloned.1.call-start = ((), (), s32[]{:S(2)}) async-start(), calls=%async_computation.8 | async-start | bytes 614400 | tf_op jit(solution)/shard_map/reduce_scatter | solution.py:321
  475.3 193.5 %reduce-scatter.16.cloned.1.call-start = ((), (), s32[]{:S(2)}) async-start(), calls=%async_computation.12 | async-start | bytes 6881280
  488.7 232.3 %reduce-scatter.14.cloned.1.call-start = ((), (), s32[]{:S(2)}) async-start(), calls=%async_computation.10 | async-start | bytes 1720320 | tf_op jit(solution)/shard_map/reduce_scatter | solution.py:321
  567.3 2.5 copy-start.18
  567.3 104.0 %copy-start.16 = (f32[768]{0:T(1024)S(1)}, f32[768]{0:T(1024)}, u32[]{:S(2)}) copy-start(f32[768]{0:T(1024)} %mul.206) | copy-start | bytes 9220
  671.3 4.1 copy-start.4
  671.3 4.1 copy-start.8
Sparse Core Ops, SparseCore 0:
  10.2 43.0 all-gather.11
  54.8 103.6 all-gather.5
  161.0 32.5 all-gather.7
  195.8 63.8 all-gather.9
  412.6 48.0 reduce-scatter.17
  464.1 82.2 reduce-scatter.11
  548.6 21.2 reduce-scatter.9
  572.4 96.3 reduce-scatter.15
  671.2 33.1 reduce-scatter.13

commit v2 on v1

v2 whole, which is shorter than its diff:
```python
import functools

import jax
import jax.numpy as jnp
from jax import lax
from jax.experimental import pallas as pl
from jax.experimental.pallas import tpu as pltpu
from jax.sharding import PartitionSpec as P

HEAD_DIM = 64
BLOCK = 256
TILE = 128
ROOT = 512
BRANCHES = 4
SLOTS = BRANCHES * BLOCK
FAR = ROOT + SLOTS
EARLY = ROOT + BLOCK
GAIN_LANES = 128
EPSILON = 1e-05
MASKED = -1e30
VMEM = 60 * 1024 * 1024
F32 = jnp.float32
BF16 = jnp.bfloat16
PLAIN = (((1,), (0,)), ((), ()))
ROWS = (((0,), (0,)), ((), ()))
COLS = (((1,), (1,)), ((), ()))


def dot(a, b, dims=PLAIN):
    return lax.dot_general(a, b, dims, preferred_element_type=F32)


def cost(us):
    return pl.CostEstimate(flops=int(us * 3e7), bytes_accessed=0, transcendentals=0)


def params():
    return pltpu.CompilerParams(vmem_limit_bytes=VMEM)


def half_turn(u):
    lane = lax.broadcasted_iota(jnp.int32, u.shape, 1)
    return jnp.where(lane % HEAD_DIM < HEAD_DIM // 2, pltpu.roll(u, 96, 1), pltpu.roll(u, 32, 1))


SMEM = pl.BlockSpec(memory_space=pltpu.SMEM)
ANY = pl.BlockSpec(memory_space=pl.ANY)


def after(count, kernel):
    return lambda *refs: kernel(*refs[count:])


def fixed(shape):
    return pl.BlockSpec(shape, lambda i: (0,) * len(shape), pipeline_mode=pl.Buffered(1))


def tiled(n, w):
    return pl.BlockSpec((n, w), lambda i: (i, 0))


def pair(n):
    return pl.BlockSpec((n, 128), lambda p: (0, p))


def aligned(row, n, unit=TILE):
    return pl.ds(pl.multiple_of(row, unit), n)


def shape(n, w, kind):
    return jax.ShapeDtypeStruct((n, w), kind)


def inv_rms(x):
    return lax.rsqrt(jnp.mean(x * x, axis=-1, keepdims=True) + EPSILON)


def plan_kernel(tiles, blocks, at_ref, seg_ref, par_ref, meta_ref, slot_ref):
    t = at_ref[0]
    first = ROOT // BLOCK
    root = seg_ref[0]
    seg = [seg_ref[b * BLOCK] for b in range(blocks)]
    par = [par_ref[b * BLOCK] for b in range(blocks)]
    rank = []
    count = jnp.int32(0)
    for b in range(blocks):
        rank.append(count)
        if b >= first:
            count = count + (par[b] == root).astype(jnp.int32)
    for beta in range(BRANCHES):
        at = jnp.int32(0)
        for b in range(first, blocks):
            at = jnp.where((par[b] == root) & (rank[b] == beta), b, at)
        for half in range(2):
            sub = 2 * at + half
            h = 2 * beta + half
            slot_ref[h, 0] = sub // tiles
            slot_ref[h, 1] = sub % tiles
            slot_ref[h, 2] = sub
            for j in range(3, 8):
                slot_ref[h, j] = 0
    for i in range(8):
        sub = t * tiles + min(i, tiles - 1)
        block = sub // 2
        mine = par_ref[block * BLOCK]
        leaf = ((mine != root) & (block >= first)).astype(jnp.int32)
        slot = jnp.int32(0)
        for b in range(first, blocks):
            slot = jnp.where((seg[b] == mine) & (par[b] == root), rank[b], slot)
        given = jnp.int32(-1)
        for h in range(2, 2 * BRANCHES):
            given = jnp.where((slot_ref[h, 2] == sub) & (t > 0), (h - 2) * TILE, given)
        meta_ref[i, 0] = sub
        meta_ref[i, 1] = leaf
        meta_ref[i, 2] = slot * leaf * BLOCK
        meta_ref[i, 3] = block * BLOCK - t * tiles * TILE + TILE
        meta_ref[i, 4] = given
        meta_ref[i, 5] = t
        meta_ref[i, 6] = jnp.where(t == 0, (slot_ref[2, 0] == 0).astype(jnp.int32), 0)
        meta_ref[i, 7] = 0


def plan(t_at, seg, par, tiles):
    out = jax.ShapeDtypeStruct((8, 8), jnp.int32)
    return pl.pallas_call(
        functools.partial(plan_kernel, tiles, seg.shape[0] // BLOCK),
        in_specs=[SMEM] * 3,
        out_specs=[SMEM] * 2,
        out_shape=[out, out],
        name="plan",
    )(t_at.reshape(1), seg, par)


def normed(x, gain):
    return (x * inv_rms(x) * gain).astype(BF16)


def rotated(u, cos, sin, out_ref, rows, factor):
    for c in range(u.shape[1] // 128):
        part = u[:, c * 128:(c + 1) * 128]
        r = (part * cos + half_turn(part) * sin).astype(BF16)
        out_ref[rows, c * 128:(c + 1) * 128] = r * factor if factor is not None else r


def line_kernel(out_ref, parts):
    n = (parts[0].shape[1] - GAIN_LANES) // 4
    for j in range(4):
        for r, part in enumerate(parts):
            out_ref[:, (j * len(parts) + r) * n:(j * len(parts) + r + 1) * n] = part[:, j * n:(j + 1) * n]
    out_ref[:, 4 * n * len(parts):] = sum(part[:, 4 * n:] for part in parts)


def line(deps, parts):
    rows, wide = parts[0].shape
    out = (rows, (wide - GAIN_LANES) * len(parts) + GAIN_LANES)
    return pl.pallas_call(
        after(len(deps), lambda *refs: line_kernel(refs[-1], refs[:-1])),
        grid=(1,),
        in_specs=[ANY] * len(deps) + [fixed(one.shape) for one in parts],
        out_specs=fixed(out),
        out_shape=shape(*out, BF16),
        compiler_params=params(),
        cost_estimate=cost(2),
        name="line",
    )(*deps, *parts)


def join_kernel(ins, out_ref):
    at = 0
    for part in ins:
        out_ref[:, at:at + part.shape[1]] = part[...]
        at += part.shape[1]


def join(deps, *parts):
    out = (parts[0].shape[0], sum(part.shape[1] for part in parts))
    return pl.pallas_call(
        after(len(deps), lambda *refs: join_kernel(refs[:-1], refs[-1])),
        grid=(1,),
        in_specs=[ANY] * len(deps) + [fixed(one.shape) for one in parts],
        out_specs=fixed(out),
        out_shape=shape(*out, BF16),
        compiler_params=params(),
        cost_estimate=cost(2),
        name="join",
    )(*deps, *parts)


def meet_kernel(kept_ref, kept_gain, away_ref, out_ref):
    d = kept_ref.shape[2]
    out_ref[:, :, :d] = (kept_ref[...].astype(F32) + away_ref[:, :, :d].astype(F32)).astype(BF16)
    out_ref[:, :, d:] = (kept_gain[...].astype(F32) + away_ref[:, :, d:].astype(F32)).astype(BF16)


def meet(deps, kept, kept_gain, away):
    chips = kept.shape[0]
    block = lambda one: pl.BlockSpec((1,) + one.shape[1:], lambda i: (i, 0, 0))
    return pl.pallas_call(
        after(len(deps), meet_kernel),
        grid=(chips,),
        in_specs=[ANY] * len(deps) + [block(one) for one in (kept, kept_gain, away)],
        out_specs=block(away),
        out_shape=jax.ShapeDtypeStruct(away.shape, BF16),
        compiler_params=params(),
        cost_estimate=cost(3),
        name="meet",
    )(*deps, kept, kept_gain, away)


def own_kernel(count, at_ref, x_ref, cos_ref, sin_ref, *refs):
    pieces, (w_ref, gain_ref, a_ref, q_ref, k_ref, v_ref) = refs[:count], refs[count:]
    d = x_ref.shape[1]
    t, dp = at_ref[0], at_ref[1]
    step = pl.program_id(0)

    @pl.when(step == 0)
    def _():
        cols = []
        for m, piece in enumerate(pieces):
            rows = piece.shape[0]
            w_ref[aligned((dp ^ m) * rows if count > 1 else 0, rows, 8), :] = piece[:, :4 * d]
        for j in range(count):
            row = jnp.zeros((pieces[0].shape[0], GAIN_LANES), F32)
            for m, piece in enumerate(pieces):
                row = jnp.where((dp ^ m) == j if count > 1 else True, piece[:, 4 * d:].astype(F32), row)
            cols.append(row)
        table = jnp.concatenate(cols, axis=0).T
        gain_ref[...] = jnp.zeros_like(gain_ref)
        gain_ref[0:1, :] = table[0:1, :] + table[1:2, :] + table[2:3, :]
        gain_ref[1:2, :] = table[3:4, :] + table[4:5, :] + table[5:6, :]

    n = x_ref.shape[0]
    here = aligned(t * (n * pl.num_programs(0)) + step * n, n, 16)
    cos, sin = cos_ref[here, :], sin_ref[here, :]
    a = normed(x_ref[...].astype(F32), gain_ref[0:1, :])
    a_ref[...] = a
    rotated(dot(a, w_ref[:, :d]), cos, sin, q_ref, slice(None), jnp.asarray(HEAD_DIM ** -0.5, BF16))
    rotated(dot(a, w_ref[:, d:2 * d]), cos, sin, k_ref, slice(None), None)
    v_ref[...] = dot(a, w_ref[:, 2 * d:3 * d]).astype(BF16)


def project_own(deps, at, x, tab, pieces):
    loc, d = x.shape
    n = loc // 2
    return pl.pallas_call(
        after(len(deps), functools.partial(own_kernel, len(pieces))),
        grid=(2,),
        in_specs=[ANY] * len(deps) + [SMEM, tiled(n, d), fixed(tab[0].shape), fixed(tab[0].shape)] + [fixed(one.shape) for one in pieces],
        out_specs=[pl.BlockSpec((d, 4 * d), lambda i: (0, 0)), pl.BlockSpec((8, d), lambda i: (0, 0))] + [tiled(n, d)] * 4,
        out_shape=[shape(d, 4 * d, BF16), shape(8, d, F32)] + [shape(loc, d, BF16)] * 4,
        compiler_params=params(),
        cost_estimate=cost(10),
        name="project_own",
    )(*deps, at, x, *tab, *pieces)


def near_rows_kernel(at_ref, x_ref, r1_ref, r2_ref, r3_ref, f1_ref, gain_ref, wk_ref, wv_ref, cos_ref, sin_ref,
                     x_out, a_ref, k_ref, v_ref):
    t = at_ref[0]
    loc = x_ref.shape[0]
    root = pl.ds(0, ROOT)
    edge = pl.ds(ROOT, TILE)

    @pl.when(t == 0)
    def _():
        x_out[root, :] = x_ref[root, :]

    for at, ref in ((1, r1_ref), (2, r2_ref), (3, r3_ref)):
        @pl.when(t == at)
        def _():
            x_out[root, :] = ref[...]

    x_out[edge, :] = f1_ref[f1_ref.shape[0] - TILE:, :]

    a = normed(x_out[...].astype(F32), gain_ref[0:1, :])
    a_ref[...] = a
    k = dot(a, wk_ref[...])
    back = aligned(jnp.maximum(t * loc - TILE, 0), TILE)
    rotated(k[:ROOT], cos_ref[root, :], sin_ref[root, :], k_ref, root, None)
    rotated(k[ROOT:], cos_ref[back, :], sin_ref[back, :], k_ref, edge, None)
    v_ref[...] = dot(a, wv_ref[...]).astype(BF16)


def weight(d, j):
    return pl.BlockSpec((d, d), lambda i: (0, j), pipeline_mode=pl.Buffered(1))


def project_near(at, x, r1, r2, r3, f1, gains, w, tab):
    d = x.shape[1]
    n = ROOT + TILE
    return pl.pallas_call(
        near_rows_kernel,
        grid=(1,),
        in_specs=[SMEM] + [fixed(one.shape) for one in (x, r1, r2, r3, f1, gains)] + [weight(d, 1), weight(d, 2)]
        + [fixed(one.shape) for one in tab],
        out_specs=[fixed((n, d))] * 4,
        out_shape=[shape(n, d, BF16)] * 4,
        compiler_params=params(),
        cost_estimate=cost(5),
        name="project_near",
    )(at, x, r1, r2, r3, f1, gains, w, w, *tab)


def far_rows_kernel(meta_ref, slot_ref, x_ref, a1_ref, a2_ref, a3_ref, b1_ref, b2_ref, b3_ref, gain_ref, wk_ref, wv_ref, cos_ref, sin_ref,
                    x_out, a_ref, k_ref, v_ref):
    t = meta_ref[0, 5]
    for h in range(2 * BRANCHES):
        owner, at = slot_ref[h, 0], slot_ref[h, 1]
        rows = aligned(at * TILE, TILE)
        head = aligned(jnp.minimum(at * TILE, ROOT - TILE), TILE)
        back = aligned(jnp.maximum(at * TILE - ROOT, 0), TILE)
        to = pl.ds(h * TILE, TILE)

        @pl.when(owner > t)
        def _():
            x_out[to, :] = jnp.zeros((TILE, x_out.shape[1]), BF16)

        @pl.when(owner == t)
        def _():
            x_out[to, :] = x_ref[rows, :]

        for hop, a_from, b_from in ((1, a1_ref, b1_ref), (2, a2_ref, b2_ref), (3, a3_ref, b3_ref)):
            @pl.when((owner + hop == t) & (at < ROOT // TILE))
            def _():
                x_out[to, :] = a_from[head, :]

            @pl.when((owner + hop == t) & (at >= ROOT // TILE))
            def _():
                x_out[to, :] = b_from[back, :]

    a = normed(x_out[...].astype(F32), gain_ref[0:1, :])
    a_ref[...] = a
    k = dot(a, wk_ref[...])
    for h in range(2 * BRANCHES):
        back = aligned(slot_ref[h, 2] * TILE, TILE)
        rotated(k[h * TILE:(h + 1) * TILE], cos_ref[back, :], sin_ref[back, :], k_ref, pl.ds(h * TILE, TILE), None)
    v_ref[...] = dot(a, wv_ref[...]).astype(BF16)


def project_far(meta, slots, x, ups, gains, w, tab):
    d = x.shape[1]
    return pl.pallas_call(
        far_rows_kernel,
        grid=(1,),
        in_specs=[SMEM, SMEM] + [fixed(one.shape) for one in (x, *ups, gains)] + [weight(d, 1), weight(d, 2)]
        + [fixed(one.shape) for one in tab],
        out_specs=[fixed((SLOTS, d))] * 4,
        out_shape=[shape(SLOTS, d, BF16)] * 4,
        compiler_params=params(),
        cost_estimate=cost(7),
        name="project_far",
    )(meta, slots, x, *ups, gains, w, w, *tab)


def fill_bias(root_ref, own_ref, keys_axis):
    for ref in (root_ref, own_ref):
        if ref is None:
            continue
        key = lax.broadcasted_iota(jnp.int32, ref.shape[1:], keys_axis)
        row = lax.broadcasted_iota(jnp.int32, ref.shape[1:], 1 - keys_axis)
        for s in range(ref.shape[0]):
            ref[s] = jnp.where(key <= row + s * TILE, 0.0, MASKED).astype(F32)


def low_half():
    return lax.broadcasted_iota(jnp.int32, (TILE, 128), 1) < HEAD_DIM


def tile_of(meta_ref, i):
    return (meta_ref[i, 0], meta_ref[i, 1], aligned(meta_ref[i, 2], BLOCK), aligned(meta_ref[i, 3], BLOCK),
            aligned(i * TILE, TILE))


def line_up(to_ref, near_ref, own_ref):
    loc = own_ref.shape[0]
    to_ref[pl.ds(0, TILE), :] = near_ref[pl.ds(ROOT, TILE), :]
    to_ref[pl.ds(TILE, loc), :] = own_ref[...]
    to_ref[pl.ds(TILE + loc, TILE), :] = jnp.zeros((TILE, 128), to_ref.dtype)


def attend_near_kernel(meta_ref, q_ref, kn_ref, vn_ref, k_ref, v_ref, acc_ref, top_ref, sum_ref, root_ref, own_ref, ko_ref, vo_ref):
    @pl.when(pl.program_id(0) == 0)
    def _():
        fill_bias(root_ref, own_ref, 1)

    line_up(ko_ref, kn_ref, k_ref)
    line_up(vo_ref, vn_ref, v_ref)
    low = low_half()
    root = pl.ds(0, ROOT)

    def one(i, carry):
        sub, leaf, par, own, here = tile_of(meta_ref, i)
        q = q_ref[here, :]

        def soft(spans):
            outs = []
            for head in range(2):
                qh = jnp.where(low if head == 0 else ~low, q, jnp.zeros_like(q))
                s = [dot(qh, kk, COLS) if b is None else dot(qh, kk, COLS) + b for kk, _, b in spans]
                top = functools.reduce(jnp.maximum, [jnp.max(part, axis=1, keepdims=True) for part in s])
                e = [jnp.exp(part - top) for part in s]
                total = sum(jnp.sum(part, axis=1, keepdims=True) for part in e)
                acc = sum(dot(part.astype(BF16), vv) for part, (_, vv, _) in zip(e, spans))
                outs.append((acc, top, total))
            acc_ref[here, :] = jnp.where(low, outs[0][0], outs[1][0])
            top_ref[here, :] = jnp.where(low, outs[0][1], outs[1][1])
            sum_ref[here, :] = jnp.where(low, outs[0][2], outs[1][2])

        @pl.when(sub < ROOT // TILE)
        def _():
            soft([(kn_ref[root, :], vn_ref[root, :], root_ref[sub])])

        @pl.when(sub >= ROOT // TILE)
        def _():
            soft([(kn_ref[root, :], vn_ref[root, :], None), (ko_ref[own, :], vo_ref[own, :], own_ref[sub % 2])])

        return carry

    lax.fori_loop(0, acc_ref.shape[0] // TILE, one, 0)


def bias_scratch(keys_axis):
    def one(n):
        return pltpu.VMEM((n // TILE,) + ((n, TILE) if keys_axis == 0 else (TILE, n)), F32)
    return one(ROOT), one(BLOCK)


def line_scratch(loc, kind):
    return pltpu.VMEM((loc + 2 * TILE, 128), kind)


def attend_near(meta, q, near, own):
    loc, d = q.shape
    n = ROOT + TILE
    return pl.pallas_call(
        attend_near_kernel,
        grid=(d // 128,),
        in_specs=[SMEM, pair(loc), pair(n), pair(n), pair(loc), pair(loc)],
        out_specs=[pair(loc)] * 3,
        out_shape=[shape(loc, d, F32)] * 3,
        scratch_shapes=[*bias_scratch(1), line_scratch(loc, BF16), line_scratch(loc, BF16)],
        compiler_params=params(),
        cost_estimate=cost(30),
        name="attend_near",
    )(meta, q, *near, *own)


def attend_far_kernel(meta_ref, q_ref, ks_ref, vs_ref, acc_ref, top_ref, sum_ref, o_ref, l_ref):
    low = low_half()

    def one(i, carry):
        sub, leaf, par, own, here = tile_of(meta_ref, i)
        acc, tops, sums = acc_ref[here, :], top_ref[here, :], sum_ref[here, :]

        def finish(acc, top, total):
            o_ref[here, :] = (acc / total).astype(BF16)
            l_ref[0, :, here] = (top + jnp.log(total)).T[60:68, :]

        @pl.when(leaf == 0)
        def _():
            finish(acc, tops, sums)

        @pl.when(leaf > 0)
        def _():
            q = q_ref[here, :]
            kk, vv = ks_ref[par, :], vs_ref[par, :]
            outs = []
            for head in range(2):
                qh = jnp.where(low if head == 0 else ~low, q, jnp.zeros_like(q))
                old = tops[:, head * HEAD_DIM:head * HEAD_DIM + 1]
                s = dot(qh, kk, COLS)
                top = jnp.maximum(jnp.max(s, axis=1, keepdims=True), old)
                e = jnp.exp(s - top)
                outs.append((dot(e.astype(BF16), vv), top, jnp.sum(e, axis=1, keepdims=True)))
            new, top, total = (jnp.where(low, outs[0][j], outs[1][j]) for j in range(3))
            fade = jnp.exp(tops - top)
            finish(acc * fade + new, top, sums * fade + total)

        return carry

    lax.fori_loop(0, o_ref.shape[0] // TILE, one, 0)


def log_spec(loc):
    return pl.BlockSpec((1, 8, loc), lambda p: (p, 0, 0))


def attend_far(meta, q, far, acc, top, total):
    loc, d = q.shape
    return pl.pallas_call(
        attend_far_kernel,
        grid=(d // 128,),
        in_specs=[SMEM, pair(loc), pair(SLOTS), pair(SLOTS), pair(loc), pair(loc), pair(loc)],
        out_specs=[pair(loc), log_spec(loc)],
        out_shape=[shape(loc, d, BF16), jax.ShapeDtypeStruct((d // 128, 8, loc), F32)],
        compiler_params=params(),
        cost_estimate=cost(11),
        name="attend_far",
    )(meta, q, *far, acc, top, total)


def split_cores(core, got, kept_ref, away_ref, where):
    @pl.when(core == 0)
    def _():
        kept_ref[where] = got[:, 0]
        away_ref[where] = got[:, 1]

    @pl.when(core == 1)
    def _():
        kept_ref[where] = got[:, 1]
        away_ref[where] = got[:, 0]


def ffn_kernel(at_ref, x_ref, o_ref, ct_ref, gain_ref, wo_ref, w_ref,
               mixed_ref, do_ref, dhb_ref, dh_ref, sum_ref, kept_ref, away_ref, c_s, m_s, dg_s, du_s, ct_t, c_t):
    step = pl.program_id(0)
    loc, d = ct_ref.shape
    n = x_ref.shape[0]
    parts, hid = m_s.shape[0], m_s.shape[2]

    def slab(t, j):
        return w_ref[:, t, :, j * hid:(j + 1) * hid].reshape(d, hid)

    @pl.when(step < loc // n)
    def _():
        here = aligned(step * n, n, 16)
        ct = ct_ref[here, :]
        h = x_ref[...].astype(F32) + dot(o_ref[...], wo_ref[...], COLS)
        scale = inv_rms(h)
        c_hat = h * scale
        gain = gain_ref[1:2, :]
        c = (c_hat * gain).astype(BF16)
        c_s[here, :] = c
        y = h
        dc = jnp.zeros_like(h)
        for t in range(parts):
            g = dot(c, slab(t, 0))
            u = dot(c, slab(t, 1))
            dm = dot(ct, slab(t, 2))
            sig = jax.nn.sigmoid(g)
            silu = g * sig
            m = (silu * u).astype(BF16)
            dg = (dm * u * (sig * (1.0 + g * (1.0 - sig)))).astype(BF16)
            du = (dm * silu).astype(BF16)
            y = y + dot(m, slab(t, 2), COLS)
            dc = dc + dot(dg, slab(t, 0), COLS) + dot(du, slab(t, 1), COLS)
            m_s[t, here, :] = m
            dg_s[t, here, :] = dg
            du_s[t, here, :] = du
        mixed_ref[...] = y.astype(BF16)
        part = jnp.sum(dc * c_hat, axis=0, keepdims=True)

        @pl.when(step == 0)
        def _():
            sum_ref[...] = jnp.zeros_like(sum_ref)

        sum_ref[0:1, :] += part
        scaled = dc * gain
        dh = ct.astype(F32) + scale * (scaled - c_hat * jnp.mean(scaled * c_hat, axis=-1, keepdims=True))
        dh_ref[...] = dh
        dhb = dh.astype(BF16)
        dhb_ref[...] = dhb
        do_ref[...] = dot(dhb, wo_ref[...]).astype(BF16)

    @pl.when(step == loc // n)
    def _():
        ct_t[...] = ct_ref[...].T
        c_t[...] = c_s[...].T

    @pl.when(step >= loc // n)
    def _():
        t = step - loc // n
        for j, (left, right) in enumerate(((c_t, dg_s), (c_t, du_s), (ct_t, m_s))):
            got = dot(left[...], right[t]).astype(BF16)
            chips, _, rows, _ = kept_ref.shape
            split_cores(at_ref[1] % 2, got.reshape(chips, 2, rows, hid), kept_ref, away_ref,
                        (slice(None), 0, slice(None), slice(j * hid, (j + 1) * hid)))


def feed_forward(at_core, x, o, ct, gains, w, rest):
    loc, d = x.shape
    dp, parts, rows, wide = rest.shape
    hid = wide // 3
    steps = 2
    n = loc // steps
    at = lambda i: (jnp.minimum(i, steps - 1), 0)
    tile = pl.BlockSpec((n, d), at)
    grads = pl.BlockSpec((dp // 2, 1, rows, wide), lambda i: (0, jnp.maximum(i - steps, 0), 0, 0))
    return pl.pallas_call(
        ffn_kernel,
        grid=(steps + parts,),
        in_specs=[SMEM, tile, tile, fixed((loc, d)), fixed((8, d)), weight(d, 3), fixed(rest.shape)],
        out_specs=[tile, tile, tile, tile, pl.BlockSpec((8, d), lambda i: (0, 0)), grads, grads],
        out_shape=[shape(loc, d, BF16), shape(loc, d, BF16), shape(loc, d, BF16), shape(loc, d, F32), shape(8, d, F32)]
        + [jax.ShapeDtypeStruct((dp // 2, parts, rows, wide), BF16)] * 2,
        scratch_shapes=[pltpu.VMEM((loc, d), BF16)] + [pltpu.VMEM((parts, loc, hid), BF16)] * 3 + [pltpu.VMEM((d, loc), BF16)] * 2,
        compiler_params=params(),
        cost_estimate=cost(40),
        name="feed_forward",
    )(at_core, x, o, ct, gains, w, rest)


def unrotate(w, cos, sin):
    return w * cos - half_turn(w) * sin


def back_setup(low, q_ref, do_ref, o_ref, l_ref, here):
    q, do = q_ref[here, :], do_ref[here, :]
    dots = (do.astype(F32) * o_ref[here, :].astype(F32)).T
    heads = []
    for head in range(2):
        keep = low if head == 0 else ~low
        heads.append((jnp.where(keep, q, jnp.zeros_like(q)), jnp.where(keep, do, jnp.zeros_like(do)),
                      l_ref[0, 3 + head:4 + head, here],
                      jnp.sum(dots[head * HEAD_DIM:(head + 1) * HEAD_DIM, :], axis=0, keepdims=True)))
    return heads


def back_span(low, heads, kk, vv, bias, acc, dk_acc, dv_acc):
    dqs = []
    for qh, doh, log, row_dot in heads:
        s = dot(kk, qh, COLS)
        if bias is not None:
            s = s + bias
        p = jnp.exp(s - log)
        dp = dot(vv, doh, COLS)
        ds = (p * (dp - row_dot)).astype(BF16)
        dv_acc[acc, :] += dot(p.astype(BF16), doh)
        dk_acc[acc, :] += dot(ds, qh)
        dqs.append(dot(ds, kk, ROWS))
    return jnp.where(low, dqs[0], dqs[1])


def back_far_kernel(meta_ref, slot_ref, q_ref, do_ref, o_ref, l_ref, kn_ref, vn_ref, ks_ref, vs_ref, cos_ref, sin_ref,
                    dq_ref, dk_ref, dv_ref, root_ref, dk_acc, dv_acc):
    @pl.when(pl.program_id(0) == 0)
    def _():
        fill_bias(root_ref, None, 0)

    low = low_half()
    root = pl.ds(0, ROOT)
    for ref in (dk_acc, dv_acc):
        ref[...] = jnp.zeros_like(ref)

    def one(i, carry):
        sub, leaf, par, own, here = tile_of(meta_ref, i)
        heads = back_setup(low, q_ref, do_ref, o_ref, l_ref, here)

        @pl.when(sub < ROOT // TILE)
        def _():
            dq_ref[here, :] = back_span(low, heads, kn_ref[root, :], vn_ref[root, :], root_ref[sub], root, dk_acc, dv_acc)

        @pl.when(sub >= ROOT // TILE)
        def _():
            dq_ref[here, :] = back_span(low, heads, kn_ref[root, :], vn_ref[root, :], None, root, dk_acc, dv_acc)

        @pl.when(leaf > 0)
        def _():
            acc = aligned(meta_ref[i, 2] + ROOT, BLOCK, BLOCK)
            dq_ref[here, :] += back_span(low, heads, ks_ref[par, :], vs_ref[par, :], None, acc, dk_acc, dv_acc)

        return carry

    lax.fori_loop(0, do_ref.shape[0] // TILE, one, 0)
    dk_ref[root, :] = unrotate(dk_acc[root, :], cos_ref[root, :], sin_ref[root, :]).astype(BF16)
    for h in range(2 * BRANCHES):
        at, back = pl.ds(ROOT + h * TILE, TILE), aligned(slot_ref[h, 2] * TILE, TILE)
        dk_ref[at, :] = unrotate(dk_acc[at, :], cos_ref[back, :], sin_ref[back, :]).astype(BF16)
    dv_ref[...] = dv_acc[...].astype(BF16)


def back_far(meta, slots, q, do, o, logs, near, far, tab):
    loc, d = do.shape
    n = ROOT + TILE
    return pl.pallas_call(
        back_far_kernel,
        grid=(d // 128,),
        in_specs=[SMEM, SMEM, pair(loc), pair(loc), pair(loc), log_spec(loc), pair(n), pair(n), pair(SLOTS), pair(SLOTS)]
        + [fixed(one.shape) for one in tab],
        out_specs=[pair(loc), pair(FAR), pair(FAR)],
        out_shape=[shape(loc, d, F32), shape(FAR, d, BF16), shape(FAR, d, BF16)],
        scratch_shapes=[bias_scratch(0)[0], pltpu.VMEM((FAR, 128), F32), pltpu.VMEM((FAR, 128), F32)],
        compiler_params=params(),
        cost_estimate=cost(50),
        name="back_far",
    )(meta, slots, q, do, o, logs, *near, *far, *tab)


def back_near_kernel(meta_ref, q_ref, do_ref, o_ref, l_ref, kn_ref, vn_ref, k_ref, v_ref, cos_ref, sin_ref, part_ref,
                     dq_ref, dk_ref, dv_ref, dke_ref, dve_ref, own_ref, ko_ref, vo_ref, dk_acc, dv_acc):
    @pl.when(pl.program_id(0) == 0)
    def _():
        fill_bias(None, own_ref, 0)

    line_up(ko_ref, kn_ref, k_ref)
    line_up(vo_ref, vn_ref, v_ref)
    low = low_half()
    loc = do_ref.shape[0]
    t = meta_ref[0, 5]
    for ref in (dk_acc, dv_acc):
        ref[...] = jnp.zeros_like(ref)

    def one(i, carry):
        sub, leaf, par, own, here = tile_of(meta_ref, i)
        back = aligned(sub * TILE, TILE)

        def put(dq):
            dq_ref[here, :] = unrotate(dq * HEAD_DIM ** -0.5, cos_ref[back, :], sin_ref[back, :]).astype(BF16)

        @pl.when(sub < ROOT // TILE)
        def _():
            put(part_ref[here, :])

        @pl.when(sub >= ROOT // TILE)
        def _():
            heads = back_setup(low, q_ref, do_ref, o_ref, l_ref, here)
            put(part_ref[here, :] + back_span(low, heads, ko_ref[own, :], vo_ref[own, :], own_ref[sub % 2], own, dk_acc, dv_acc))

        return carry

    lax.fori_loop(0, loc // TILE, one, 0)
    edge, mine = pl.ds(0, TILE), pl.ds(TILE, loc)
    before = aligned(jnp.maximum(t * loc - TILE, 0), TILE)
    here = aligned(t * loc, loc)
    dke_ref[...] = unrotate(dk_acc[edge, :], cos_ref[before, :], sin_ref[before, :]).astype(BF16)
    dve_ref[...] = dv_acc[edge, :].astype(BF16)
    dk_ref[...] = unrotate(dk_acc[mine, :], cos_ref[here, :], sin_ref[here, :]).astype(BF16)
    dv_ref[...] = dv_acc[mine, :].astype(BF16)


def back_near(deps, meta, q, do, o, logs, near, own, tab, dq_part):
    loc, d = do.shape
    n = ROOT + TILE
    return pl.pallas_call(
        after(len(deps), back_near_kernel),
        grid=(d // 128,),
        in_specs=[ANY] * len(deps) + [SMEM, pair(loc), pair(loc), pair(loc), log_spec(loc), pair(n), pair(n), pair(loc), pair(loc)]
        + [fixed(one.shape) for one in tab] + [pair(loc)],
        out_specs=[pair(loc)] * 3 + [pair(TILE)] * 2,
        out_shape=[shape(loc, d, BF16)] * 3 + [shape(TILE, d, BF16)] * 2,
        scratch_shapes=[bias_scratch(0)[1], line_scratch(loc, BF16), line_scratch(loc, BF16), line_scratch(loc, F32),
                        line_scratch(loc, F32)],
        compiler_params=params(),
        cost_estimate=cost(25),
        name="back_near",
    )(*deps, meta, q, do, o, logs, *near, *own, *tab, dq_part)


def spread_kernel(dk_ref, dv_ref, xn_ref, xs_ref, wk_ref, wv_ref, early_ref, late_ref, sum_ref):
    step = pl.program_id(0)
    da = dot(dk_ref[...], wk_ref[...], COLS) + dot(dv_ref[...], wv_ref[...], COLS)

    @pl.when(step < EARLY // BLOCK)
    def _():
        early_ref[...] = da.astype(BF16)

    @pl.when(step >= EARLY // BLOCK)
    def _():
        late_ref[...] = da.astype(BF16)

    x = jnp.where(step < ROOT // BLOCK, xn_ref[...], xs_ref[...]).astype(F32)

    @pl.when(step == 0)
    def _():
        sum_ref[...] = jnp.zeros_like(sum_ref)

    sum_ref[0:1, :] += jnp.sum(da * (x * inv_rms(x)), axis=0, keepdims=True)


def spread(deps, dk, dv, x_near, x_slot, w):
    d = w.shape[0]
    near, early = ROOT // BLOCK, EARLY // BLOCK
    at = lambda f: pl.BlockSpec((BLOCK, d), lambda i: (f(i), 0))
    return pl.pallas_call(
        after(len(deps), spread_kernel),
        grid=(FAR // BLOCK,),
        in_specs=[ANY] * len(deps) + [at(lambda i: i), at(lambda i: i), at(lambda i: jnp.minimum(i, near - 1)), at(lambda i: jnp.maximum(i - near, 0)),
                  weight(d, 1), weight(d, 2)],
        out_specs=[at(lambda i: jnp.minimum(i, early - 1)), at(lambda i: jnp.maximum(i - early, 0)),
                   pl.BlockSpec((8, d), lambda i: (0, 0))],
        out_shape=[shape(EARLY, d, BF16), shape(FAR - EARLY, d, BF16), shape(8, d, F32)],
        compiler_params=params(),
        cost_estimate=cost(6),
        name="spread",
    )(*deps, dk, dv, x_near, x_slot, w, w)


def own_back_kernel(x_ref, xe_ref, dq_ref, dk_ref, dv_ref, dke_ref, dve_ref, wq_ref, wk_ref, wv_ref, da_ref, edge_ref, sum_ref):
    step = pl.program_id(0)
    wk, wv = wk_ref[...], wv_ref[...]

    def gain_part(da, x):
        x = x.astype(F32)
        return jnp.sum(da * (x * inv_rms(x)), axis=0, keepdims=True)

    @pl.when(step == 0)
    def _():
        edge = dot(dke_ref[...], wk, COLS) + dot(dve_ref[...], wv, COLS)
        edge_ref[...] = edge.astype(BF16)
        sum_ref[...] = jnp.zeros_like(sum_ref)
        sum_ref[0:1, :] = gain_part(edge, xe_ref[pl.ds(ROOT, TILE), :])

    da = dot(dq_ref[...], wq_ref[...], COLS) + dot(dk_ref[...], wk, COLS) + dot(dv_ref[...], wv, COLS)
    da_ref[...] = da
    sum_ref[0:1, :] += gain_part(da, x_ref[...])


def own_back(deps, x, x_near, dq, dk, dv, dke, dve, w):
    loc, d = x.shape
    n = loc // 2
    return pl.pallas_call(
        after(len(deps), own_back_kernel),
        grid=(2,),
        in_specs=[ANY] * len(deps) + [tiled(n, d), fixed(x_near.shape), tiled(n, d), tiled(n, d), tiled(n, d), fixed((TILE, d)), fixed((TILE, d)),
                  weight(d, 0), weight(d, 1), weight(d, 2)],
        out_specs=[tiled(n, d), pl.BlockSpec((TILE, d), lambda i: (0, 0)), pl.BlockSpec((8, d), lambda i: (0, 0))],
        out_shape=[shape(loc, d, F32), shape(TILE, d, BF16), shape(8, d, F32)],
        compiler_params=params(),
        cost_estimate=cost(6),
        name="own_back",
    )(*deps, x, x_near, dq, dk, dv, dke, dve, w, w, w)


def weights_kernel(at_ref, s1_ref, s2_ref, s3_ref, a_ref, an_ref, as_ref, dhb_ref, dq_ref, dk_ref, dv_ref, dkf_ref, dvf_ref,
                   dke_ref, dve_ref, o_ref, kept_ref, away_ref, kept_gain, away_gain):
    step = pl.program_id(0)
    core = at_ref[1] % 2
    chips, rows, d = kept_ref.shape

    def put(total, kept, away):
        split_cores(core, total.astype(BF16).reshape(chips, 2, rows, total.shape[1]), kept, away, (slice(None),) * 3)

    def keyed(own, far, edge):
        root, tail = pl.ds(0, ROOT), pl.ds(ROOT, TILE)
        return (dot(a_ref[...], own[...], ROWS) + dot(an_ref[root, :], far[root, :], ROWS)
                + dot(as_ref[...], far[pl.ds(ROOT, SLOTS), :], ROWS) + dot(an_ref[tail, :], edge[...], ROWS))

    @pl.when(step == 0)
    def _():
        line = lax.broadcasted_iota(jnp.int32, (GAIN_LANES, d), 0)
        table = jnp.where(line == 0, s1_ref[0:1, :] + s2_ref[0:1, :], jnp.where(line == 1, s3_ref[0:1, :], 0.0))
        put(table.T, kept_gain, away_gain)
        put(dot(a_ref[...], dq_ref[...], ROWS), kept_ref, away_ref)

    @pl.when(step == 1)
    def _():
        put(keyed(dk_ref, dkf_ref, dke_ref), kept_ref, away_ref)

    @pl.when(step == 2)
    def _():
        put(keyed(dv_ref, dvf_ref, dve_ref), kept_ref, away_ref)

    @pl.when(step == 3)
    def _():
        put(dot(dhb_ref[...], o_ref[...], ROWS), kept_ref, away_ref)


def weight_sums(deps, at, sums, a_own, a_near, a_slot, dhb, dq, dk, dv, dkf, dvf, dke, dve, o, dp):
    loc, d = a_own.shape
    chips, rows = dp // 2, d // dp
    arrays = (*sums, a_own, a_near, a_slot, dhb, dq, dk, dv, dkf, dvf, dke, dve, o)
    out = pl.BlockSpec((chips, rows, d), lambda i: (0, 0, i))
    gain = pl.BlockSpec((chips, rows, GAIN_LANES), lambda i: (0, 0, 0))
    return pl.pallas_call(
        after(len(deps), weights_kernel),
        grid=(4,),
        in_specs=[ANY] * len(deps) + [SMEM] + [fixed(one.shape) for one in arrays],
        out_specs=[out, out, gain, gain],
        out_shape=[jax.ShapeDtypeStruct((chips, rows, 4 * d), BF16)] * 2 + [jax.ShapeDtypeStruct((chips, rows, GAIN_LANES), BF16)] * 2,
        compiler_params=params(),
        cost_estimate=cost(14),
        name="weight_sums",
    )(*deps, at, *arrays)


def finish_kernel(meta_ref, da_ref, dh_ref, x_ref, gain_ref, early_ref, late_ref, low_ref, edge_ref, out_ref):
    t = meta_ref[0, 5]
    tiles = x_ref.shape[0] // TILE

    def one(i, carry):
        here = aligned(i * TILE, TILE)
        given = meta_ref[i, 4]
        x = x_ref[here, :].astype(F32)
        scale = inv_rms(x)
        x_hat = x * scale
        gain = gain_ref[0:1, :]
        da = da_ref[here, :]
        none = jnp.zeros((TILE, x.shape[1]), F32)
        late = late_ref[aligned(jnp.maximum(given, 0), TILE), :].astype(F32)
        early = early_ref[aligned(jnp.minimum(i * TILE, EARLY - TILE), TILE), :].astype(F32)
        da = da + jnp.where(given >= 0, late, none)
        da = da + jnp.where((t == 0) & (i < EARLY // TILE), early, none)
        last = i == tiles - 1
        da = da + jnp.where(last & (meta_ref[0, 6] > 0), low_ref[...].astype(F32), none)
        da = da + jnp.where(last & (t % 2 == 0), edge_ref[...].astype(F32), none)
        scaled = da * gain
        out_ref[here, :] = dh_ref[here, :] + scale * (scaled - x_hat * jnp.mean(scaled * x_hat, axis=-1, keepdims=True))
        return carry

    lax.fori_loop(0, tiles, one, 0)


def finish(meta, da, dh, x, gains, early, late, low, edge):
    loc, d = x.shape
    arrays = (da, dh, x, gains, early, late, low, edge)
    return pl.pallas_call(
        finish_kernel,
        grid=(1,),
        in_specs=[SMEM] + [fixed(one.shape) for one in arrays],
        out_specs=fixed((loc, d)),
        out_shape=shape(loc, d, F32),
        compiler_params=params(),
        cost_estimate=cost(6),
        name="finish",
    )(meta, *arrays)


def tables(pos):
    half = HEAD_DIM // 2
    freq = jnp.exp(-jnp.log(10000.0) * (2.0 * jnp.arange(half, dtype=F32) / HEAD_DIM))
    angle = pos.astype(F32)[:, None] * jnp.concatenate([freq, freq, freq, freq])[None, :]
    sign = jnp.where(jnp.arange(2 * HEAD_DIM) % HEAD_DIM < half, -1.0, 1.0).astype(F32)
    return jnp.cos(angle), jnp.sin(angle) * sign[None, :]


def swap(x, axis, mask):
    return lax.ppermute(x, axis, [(i, i ^ mask) for i in range(lax.axis_size(axis))])


def send(x, *pairs):
    return lax.ppermute(x, "tensor", list(pairs))


def three(g):
    high = lax.reduce_precision(g, 8, 7)
    mid = lax.reduce_precision(g - high, 8, 7)
    return [high.astype(BF16), mid.astype(BF16), (g - high - mid).astype(BF16)]


def total_kernel(own_ref, *refs):
    ins, out_ref = refs[:-1], refs[-1]
    out_ref[...] = sum((one[...].astype(F32) for one in ins), own_ref[...].astype(F32)).astype(BF16)


def total(deps, *parts):
    one = fixed(parts[0].shape)
    return pl.pallas_call(
        after(len(deps), total_kernel),
        grid=(1,),
        in_specs=[ANY] * len(deps) + [one] * len(parts),
        out_specs=one,
        out_shape=jax.ShapeDtypeStruct(parts[0].shape, BF16),
        compiler_params=params(),
        cost_estimate=cost(3),
        name="total",
    )(*deps, *parts)


def meet_chips(deps, part, chip):
    blocks = [lax.dynamic_index_in_dim(part, chip ^ m, 0, keepdims=False) for m in range(part.shape[0])]
    moved = [swap(block, "dp", 2 * m) for m, block in enumerate(blocks) if m]
    return total(deps, blocks[0], *moved)


def per_device(tokens, gain_attn, w_query, w_key, w_value, w_out, gain_ffn, w_gate, w_up, w_down,
               segment_ids, parent_ids, positions, cotangent):
    loc, d = tokens.shape
    t_size, t_at = lax.axis_size("tensor"), lax.axis_index("tensor")
    d_size, d_at = lax.axis_size("dp"), lax.axis_index("dp")
    tiles = loc // TILE
    own_gain = gain_attn.shape[0]
    rows, hid = w_gate.shape
    n = w_query.shape[1]
    at = jnp.stack([t_at, d_at]).astype(jnp.int32)

    up = [(i, i + 1) for i in range(t_size - 1)]
    a1 = send(tokens[:ROOT], *up)
    gain_cols = jnp.stack(three(gain_attn) + three(gain_ffn), axis=1)
    gain_cols = lax.dynamic_update_slice(jnp.zeros((rows, GAIN_LANES), BF16), gain_cols, (t_at * own_gain, 0))
    pack = jnp.concatenate([w_query, w_key, w_value, w_out.T, gain_cols], axis=1)
    others = [pack] + [swap(pack, "tensor", m) for m in range(1, t_size)]
    lined = line((a1,), others)
    a2 = send(a1, *up[1:])
    pieces = [None] * d_size
    for m in range(0, d_size, 2):
        pieces[m] = swap(lined, "dp", m) if m else lined
    ready = (a2, *(pieces[m] for m in range(2, d_size, 2)))
    rest = join(ready, w_gate, w_up, w_down.T)
    b1 = send(join(ready, tokens[ROOT:]), *up)
    a3 = send(a2, *up[2:])
    for m in range(0, d_size, 2):
        pieces[m + 1] = swap(pieces[m], "dp", 1)
    if rows % 16:
        whole = jnp.zeros((d_size * rows, lined.shape[1]), BF16)
        for m in range(d_size):
            whole = lax.dynamic_update_slice_in_dim(whole, pieces[m], (d_at ^ m) * rows, 0)
        pieces = [whole]
    rest = lax.all_gather(rest, ("dp", "tensor"), axis=0, tiled=False).reshape(d_size, t_size, rows, 3 * hid)
    meta, slots = plan(at[:1], segment_ids, parent_ids, tiles)
    tab = tables(positions)
    w, gains, a_own, q, k_own, v_own = project_own((), at, tokens, tab, pieces)
    front = join((a3, k_own), tokens[ROOT:])
    b2 = send(front, (0, 2), (1, 3))
    b3 = send(front, (0, 3))
    x_near, a_near, k_near, v_near = project_near(at, tokens, a1, a2, a3, b1, gains, w, tab)
    near, own = (k_near, v_near), (k_own, v_own)
    acc, top, weight_sum = attend_near(meta, q, near, own)
    x_slot, a_slot, k_slot, v_slot = project_far(meta, slots, tokens, (a1, a2, a3, b1, b2, b3), gains, w, tab)
    far = (k_slot, v_slot)
    o, logs = attend_far(meta, q, far, acc, top, weight_sum)

    mixed, do, dhb, dh, ffn_sum, kept, away = feed_forward(at, tokens, o, cotangent, gains, w, rest)
    chip = d_at // 2
    away = swap(away, "dp", 1)
    dq_part, dk_far, dv_far = back_far(meta, slots, q, do, o, logs, near, far, tab)
    rest_part = (kept.astype(F32) + away.astype(F32)).astype(BF16)
    early, late, far_sum = spread((rest_part,), dk_far, dv_far, x_near, x_slot, w)
    rest_sum = meet_chips((), rest_part, chip)
    late_in = send(late, (3, 2))
    early_in = send(early, (3, 2), (1, 0))
    dq, dk, dv, dke, dve = back_near((early, late), meta, q, do, o, logs, near, own, tab, dq_part)
    late = late + late_in
    early = early + early_in
    late_in = send(late, (2, 1))
    early_in = send(early, (2, 0))
    da, edge, own_sum = own_back((rest_sum, late, early), tokens, x_near, dq, dk, dv, dke, dve, w)
    kept, away, kept_gain, away_gain = weight_sums(
        (late_in, early), at, (far_sum, own_sum, ffn_sum), a_own, a_near, a_slot, dhb, dq, dk, dv, dk_far, dv_far, dke, dve, o, d_size)
    edge = send(edge, (1, 0), (3, 2))
    away = swap(jnp.concatenate([away, away_gain], axis=2), "dp", 1)
    part = meet((), kept, kept_gain, away)
    late = late + late_in
    early = early + early_in
    low_edge = send(late[:TILE], (1, 0))
    grad_tokens = finish(meta, da, dh, tokens, gains, early, late, low_edge, edge)
    rest_sum = join((part,), rest_sum.reshape(t_size * rows, 3 * hid)).reshape(rest_sum.shape)
    rest_owned = lax.dynamic_index_in_dim(rest_sum, t_at, 0, keepdims=False).astype(F32)
    for m in range(1, t_size):
        rest_owned = rest_owned + swap(lax.dynamic_index_in_dim(rest_sum, t_at ^ m, 0, keepdims=False), "tensor", m).astype(F32)
    summed = meet_chips((early_in,), part, chip)

    def share(m):
        return jnp.concatenate([summed[:, j * d + m * n:j * d + (m + 1) * n] for j in range(4)] + [summed[:, 4 * d:]], axis=1)

    owned = share(0).astype(F32)
    for m in range(1, t_size):
        owned = owned + swap(share(m), "tensor", m).astype(F32)
    gain_sums = lax.dynamic_slice(owned, (t_at * own_gain, 4 * n), (own_gain, GAIN_LANES))
    return (mixed, grad_tokens, gain_sums[:, 0], owned[:, :n], owned[:, n:2 * n], owned[:, 2 * n:3 * n], owned[:, 3 * n:4 * n].T,
            gain_sums[:, 1], rest_owned[:, :hid], rest_owned[:, hid:2 * hid], rest_owned[:, 2 * hid:].T)


def solution(mesh):
    rows = P(("dp", "tensor"), None)
    gain = P(("dp", "tensor"))
    wide = P("dp", "tensor")
    tall = P("tensor", "dp")
    return jax.shard_map(
        per_device,
        mesh=mesh,
        in_specs=(rows, gain, wide, wide, wide, tall, gain, wide, wide, tall, P("dp"), P("dp"), P("dp"), rows),
        out_specs=(rows, rows, gain, wide, wide, wide, tall, gain, wide, wide, tall),
        check_vma=False,
    )
```

time: 736 us -> 582 us (0.79)
  waiting for transfers between devices: 262 us -> 121 us
  starting transfers between devices: 0.83 us -> 125 us
  blocking collectives: 112 us -> 0 us
  matrix products: 107 us -> 0 us
  Pallas kernels: 147 us -> 254 us
  local copies, waits for them, and re-layouts: 63.7 us -> 28.5 us
    ppermute x0 -> x36, starting transfers between devices: none -> 125 us  [the longest x24 98.2 us: swap(): lax.ppermute(x, axis, [(i, i ^ mask) for i in range(lax.axis_size(axis))])]
    ppermute x0 -> x36, waiting for transfers between devices: none -> 110 us  [the longest x24 79.3 us: swap(): lax.ppermute(x, axis, [(i, i ^ mask) for i in range(lax.axis_size(axis))])]
    unnamed x11 -> x1, waiting for transfers between devices: 109 us -> 0.02 us
    pallas_call x3 -> x21, Pallas kernels: 147 us -> 254 us  [the longest x1 45.3 us: feed_forward(): pl.pallas_call(ffn_kernel, grid=(steps + parts,), in_specs=[SMEM, tile, t...]
    dot_general x18 -> x0, matrix products: 107 us -> none  [dot(): return lax.dot_general(a, b, dims, preferred_element_type=F32)]
    all_gather x4 -> x1, waiting for transfers between devices: 98.4 us -> 10.3 us  [per_device(): lax.all_gather(rest, ('dp', 'tensor'), axis=0, tiled=False)]
    all_gather x1 -> x0, blocking collectives: 69.9 us -> none  [per_device(): gains = lax.all_gather(gains, ('dp', 'tensor'), axis=0, tiled=False)]
    reduce_scatter x3 -> x0, waiting for transfers between devices: 54.9 us -> none  [the longest x1 54.7 us: owners(): mine = lax.psum_scatter(grads, 'dp', scatter_dimension=0, tiled=True)]
  transfers between devices with their start and end apart: 9 -> 37, of which waited for: 8 -> 15; matrix products, arithmetic and copies ran while one was open for 17% -> 5% of each run, Pallas kernels for 8% -> 31%
where the time goes in v2:
time: 582 us; the launch traced here: 573 us
  Pallas kernels  254 us (44%)
  starting transfers between devices  125 us (21%)
  waiting for transfers between devices  121 us (21%)
  other arithmetic  29 us (5%)
  local copies, waits for them, and re-layouts  28.5 us (5%)
  between operations  14.9 us (3%)
    ppermute x24, starting transfers between devices, swap(): lax.ppermute(x, axis, [(i, i ^ mask) for i in range(lax.axis_size(axis))])  98.2 us
    ppermute x24, waiting for transfers between devices, swap(): lax.ppermute(x, axis, [(i, i ^ mask) for i in range(lax.axis_size(axis))])  79.3 us
    pallas_call x1, Pallas kernels, feed_forward(): pl.pallas_call(ffn_kernel, grid=(steps + parts,), in_specs=[SMEM, tile, t...  45.3 us
    pallas_call x1, Pallas kernels, back_far(): pl.pallas_call(back_far_kernel, grid=(d // 128,), in_specs=[SMEM, SMEM, p...  44.1 us
    pallas_call x1, Pallas kernels, attend_near(): pl.pallas_call(attend_near_kernel, grid=(d // 128,), in_specs=[SMEM, pair...  34.2 us
    ppermute x12, waiting for transfers between devices, send(): return lax.ppermute(x, 'tensor', list(pairs))  31 us
    ppermute x12, starting transfers between devices, send(): return lax.ppermute(x, 'tensor', list(pairs))  27.1 us
    pallas_call x1, Pallas kernels, back_near(): pl.pallas_call(after(len(deps), back_near_kernel), grid=(d // 128,), in_s...  23.6 us
  transfers between devices with their start and end apart: 37, of which 15 were waited for; matrix products, arithmetic and copies ran while one was open for 5% of the time, Pallas kernels for 31%

profile of v2, /device:TPU:0, one launch (start us, length us, event | category | flops | bytes accessed | tf_op | source)
XLA Modules:
  0.0 572.7 jit_solution(16302309575609554513)
XLA Ops:
  8.4 5.0 collective-permute-start
  16.6 1.6 collective-permute-start.1
  19.3 1.8 collective-permute-start.3
  21.0 10.3 %collective-permute-done.refs_0_.a1_ref.r1_ref = bf16[512,768]{1,0:T(8,128)(2,1)S(1)} collective-permute-done((bf16[512,768]{1,0:T(8,128)(2,1)S(1)}, bf16[512,768]{1,0:T(8,128)(2,1)S(1)}, u32[]{:S(2)}, u32[]{:S(2)}) %collective-permute-start) | collective-permute-done | bytes 786464 | tf_op jit(solution)/shard_map/ppermute | solution.py:931
  32.0 3.0 collective-permute-done.1.refs_2_
  35.0 3.7 collective-permute-done.2.refs_3_
  38.7 2.6 collective-permute-done.3.refs_4_
  42.0 2.2 line.1.refs_4_
  44.1 2.4 collective-permute-start.9
  47.6 14.5 %collective-permute-done.9.refs_10_.refs_3_ = bf16[96,3200]{1,0:T(8,128)(2,1)S(1)} collective-permute-done((bf16[96,3200]{1,0:T(8,128)(2,1)}, bf16[96,3200]{1,0:T(8,128)(2,1)S(1)}, u32[]{:S(2)}, u32[]{:S(2)}) %collective-permute-start.9) | collective-permute-done | bytes 614432 | tf_op jit(solution)/shard_map/ppermute | solution.py:927
  62.1 11.1 %collective-permute-done.5.refs_6_.refs_1_ = bf16[96,3200]{1,0:T(8,128)(2,1)S(1)} collective-permute-done((bf16[96,3200]{1,0:T(8,128)(2,1)}, bf16[96,3200]{1,0:T(8,128)(2,1)S(1)}, u32[]{:S(2)}, u32[]{:S(2)}) %collective-permute-start.5) | collective-permute-done | bytes 614432 | tf_op jit(solution)/shard_map/ppermute | solution.py:927
  74.5 1.7 join.6
  78.1 8.3 %fusion = (f32[3584,128]{1,0:T(8,128)}, f32[3584,128]{1,0:T(8,128)}) fusion(f32[128]{0:T(128)S(1)} %get-tuple-element.179, f32[128]{0:T(128)S(1)} %get-tuple-element.180, f32[3584]{0:T(1024)S(1)} %convert_element_type.57), kind=kLoop, calls=%fused_computation.4 | loop fusion | flops 917504 | bytes 3685376 | tf_op jit(solution)/shard_map/mul | solution.py:923
  86.4 1.9 slice.93.refs_4_.refs_2_
  88.3 1.9 join.4
  90.3 7.2 %collective-permute-start.13 = (bf16[384,768]{1,0:T(8,128)(2,1)}, bf16[384,768]{1,0:T(8,128)(2,1)S(1)}, u32[]{:S(2)}, u32[]{:S(2)}) collective-permute-start(bf16[384,768]{1,0:T(8,128)(2,1)} %join.4), channel_id=1, source_target_pairs={{0,1},{1,2},{2,3},{4,5},{5,6},{6,7},{8,9},{9,10},{10,11},{12,13},{... | collective-permute-start | bytes 1769480 | tf_op jit(solution)/shard_map/ppermute | solution.py:931
  99.2 11.2 %project_own.1 = (bf16[768,3072]{1,0:T(8,128)(2,1)}, f32[8,768]{1,0:T(8,128)}, bf16[896,768]{1,0:T(8,128)(2,1)}, bf16[896,768]{1,0:T(8,128)(2,1)}, bf16[896,768]{1,0:T(8,128)(2,1)}, /*index=5*/bf16[896,768]{1,0:T(8,128)(2,1)}) custom-call(s32[2]{0:T(128)} %pad_add_fusion.refs_0_.at_ref.refs_2_, bf16[896,768]{1,0:T(8,128)(2,1)} %x_ref.7, ...), custom_call_target="tpu_custom_call" | custom-call | flops 300000000 | tf_op jit(solution)/shard_map/project_own/pallas_call | solution.py:245
  111.3 1.9 join.5
  113.3 4.4 collective-permute-start.14
  117.7 1.3 collective-permute-start.15
  119.0 2.2 plan.1
  122.0 7.2 %project_near.1 = (bf16[640,768]{1,0:T(8,128)(2,1)}, bf16[640,768]{1,0:T(8,128)(2,1)}, bf16[640,768]{1,0:T(8,128)(2,1)}, bf16[640,768]{1,0:T(8,128)(2,1)}) custom-call(s32[2]{0:T(128)} %pad_add_fusion.refs_0_.at_ref.refs_2_, bf16[896,768]{1,0:T(8,128)(2,1)} %x_ref.7, bf16[512,768]{1,0:T(8,128)(2,1)} %copy-done.5, bf16[512,768]{1,0:T(8,128)(2,1)} %copy-done.2, ...), custom_call_target="tpu_custom_call" | custom-call | flops 150000000 | tf_op jit(solution)/shard_map/project_near/pallas_call | solution.py:291
  129.3 34.2 %attend_near.1 = (f32[896,768]{1,0:T(8,128)}, f32[896,768]{1,0:T(8,128)}, f32[896,768]{1,0:T(8,128)}) custom-call(s32[8,8]{1,0:T(8,128)} %get-tuple-element.57.meta_ref.refs_2_, bf16[896,768]{1,0:T(8,128)(2,1)} %get-tuple-element.58.q_ref.refs_3_, bf16[640,768]{1,0:T(8,128)(2,1)} %get-tuple-element.65.kn_ref.refs_7_, ...), custom_call_target="tpu_custom_call" | custom-call | flops 900000000 | tf_op jit(solution)/shard_map/attend_near/pallas_call | solution.py:435
  164.5 10.2 %project_far.1 = (bf16[1024,768]{1,0:T(8,128)(2,1)}, bf16[1024,768]{1,0:T(8,128)(2,1)}, bf16[1024,768]{1,0:T(8,128)(2,1)}, bf16[1024,768]{1,0:T(8,128)(2,1)}) custom-call(s32[8,8]{1,0:T(8,128)} %get-tuple-element.57.meta_ref.refs_2_, s32[8,8]{1,0:T(8,128)} %get-tuple-element.59.slot_ref, bf16[896,768]{1,0:T(8,128)(2,1)} %x_ref.7, ...), custom_call_target="tpu_custom_call" | custom-call | flops 210000000 | tf_op jit(solution)/shard_map/project_far/pallas_call | solution.py:342
  174.8 9.2 %attend_far.1 = (bf16[896,768]{1,0:T(8,128)(2,1)}, f32[6,8,896]{2,1,0:T(8,128)}) custom-call(s32[8,8]{1,0:T(8,128)} %get-tuple-element.57.meta_ref.refs_2_, bf16[896,768]{1,0:T(8,128)(2,1)} %get-tuple-element.58.q_ref.refs_3_, bf16[1024,768]{1,0:T(8,128)(2,1)} %get-tuple-element.63.ks_ref, bf16[1024,768]{1,0:T(8,128)(2,1)} %get-tuple-element.64.vs_ref, ...), custom_call_target="tpu_custom_call" | custom-call | flops 330000000 | tf_op jit(solution)/shard_map/attend_far/pallas_call | solution.py:490
  184.0 10.3 %all-gather.3.cloned.1.call-done = bf16[3072,1536]{1,0:T(8,128)(2,1)} async-done(((bf16[96,1536]{1,0:T(8,128)(2,1)}), bf16[3072,1536]{1,0:T(8,128)(2,1)}) %all-gather.3.cloned.1.call-update) | async-done | bytes 9437200 | tf_op jit(solution)/shard_map/all_gather | solution.py:998
  194.2 45.3 %feed_forward.1 = (bf16[896,768]{1,0:T(8,128)(2,1)}, bf16[896,768]{1,0:T(8,128)(2,1)}, bf16[896,768]{1,0:T(8,128)(2,1)}, f32[896,768]{1,0:T(8,128)}, f32[8,768]{...) custom-call(s32[2]{0:T(128)} %pad_add_fusion.refs_0_.at_ref.refs_2_, ...), custom_call_target="tpu_custom_call" | custom-call | flops 1200000000 | tf_op jit(solution)/shard_map/feed_forward/pallas_call | solution.py:589
  239.8 44.1 %back_far.1 = (f32[896,768]{1,0:T(8,128)}, bf16[1536,768]{1,0:T(8,128)(2,1)}, bf16[1536,768]{1,0:T(8,128)(2,1)}) custom-call(s32[8,8]{1,0:T(8,128)} %get-tuple-element.57.meta_ref.refs_2_, s32[8,8]{1,0:T(8,128)} %get-tuple-element.59.slot_ref, bf16[896,768]{1,0:T(8,128)(2,1)} %get-tuple-element.58.q_ref.refs_3_, ...), custom_call_target="tpu_custom_call" | custom-call | flops 1500000000 | tf_op jit(solution)/shard_map/back_far/pallas_call | solution.py:675
  284.0 7.4 %add_convert_fusion.refs_0_ = bf16[4,4,96,1536]{3,2,1,0:T(8,128)(2,1)} fusion(bf16[4,4,96,1536]{3,2,1,0:T(8,128)(2,1)} %collective-permute-done.16, bf16[4,4,96,1536]{3,2,1,0:T(8,128)(2,1)} %get-tuple-element.73), kind=kLoop, calls=%fused_computation | loop fusion | flops 9437184 | bytes 14155776 | tf_op jit(solution)/shard_map/convert_element_type | solution.py:1016
  291.4 10.2 %spread.1 = (bf16[768,768]{1,0:T(8,128)(2,1)}, bf16[768,768]{1,0:T(8,128)(2,1)}, f32[8,768]{1,0:T(8,128)}) custom-call(bf16[4,4,96,1536]{3,2,1,0:T(8,128)(2,1)} %add_convert_fusion.refs_0_, bf16[1536,768]{1,0:T(8,128)(2,1)} %get-tuple-element.77.refs_1_.refs_13_, bf16[1536,768]{1,0:T(8,128)(2,1)} %get-tuple-element.78.refs_2_.refs_14_, ...), custom_call_target="tpu_custom_call" | custom-call | flops 180000000 | tf_op jit(solution)/shard_map/spread/pallas_call | solution.py:774
  302.3 1.4 collective-permute-start.21
  303.8 4.5 dynamic-slice_bitcast_fusion
  308.3 1.4 collective-permute-start.17
  309.7 3.8 collective-permute-start.18
  313.5 1.5 collective-permute-start.19
  315.3 1.7 collective-permute-start.23
  317.0 23.6 %back_near.1 = (bf16[896,768]{1,0:T(8,128)(2,1)}, bf16[896,768]{1,0:T(8,128)(2,1)}, bf16[896,768]{1,0:T(8,128)(2,1)}, bf16[128,768]{1,0:T(8,128)(2,1)}, bf16[128,768]{1,0:T(8,128)(2,1)}) custom-call(bf16[768,768]{1,0:T(8,128)(2,1)} %get-tuple-element.82.refs_0_, bf16[768,768]{1,0:T(8,128)(2,1)} %get-tuple-element.81.refs_1_, ...), custom_call_target="tpu_custom_call" | custom-call | flops 750000000 | tf_op jit(solution)/shard_map/back_near/pallas_call | solution.py:734
  340.7 1.6 collective-permute-done.21
  342.2 2.6 add.87.refs_2_.refs_1_
  344.8 20.0 %collective-permute-done.18.refs_2_ = bf16[4,96,1536]{2,1,0:T(8,128)(2,1)} collective-permute-done((bf16[4,96,1536]{2,1,0:T(8,128)(2,1)}, bf16[4,96,1536]{2,1,0:T(8,128)(2,1)}, u32[]{:S(2)}, u32[]{:S(2)}) %collective-permute-start.18) | collective-permute-done | bytes 1179680 | tf_op jit(solution)/shard_map/ppermute | solution.py:927
  364.8 1.9 collective-permute-done.19.refs_3_
  366.7 4.0 total.2.refs_0_
  370.7 9.5 %own_back.1 = (f32[896,768]{1,0:T(8,128)}, bf16[128,768]{1,0:T(8,128)(2,1)}, f32[8,768]{1,0:T(8,128)}) custom-call(bf16[4,96,1536]{2,1,0:T(8,128)(2,1)} %total.2.refs_0_, bf16[768,768]{1,0:T(8,128)(2,1)} %copy-done.3, bf16[768,768]{1,0:T(8,128)(2,1)} %add.87.refs_2_.refs_1_, bf16[896,768]{1,0:T(8,128)(2,1)} %x_ref.7, ...), custom_call_target="tpu_custom_call" | custom-call | flops 180000000 | tf_op jit(solution)/shard_map/own_back/pallas_call | solution.py:811
  380.2 17.9 %weight_sums.1 = (bf16[4,96,3072]{2,1,0:T(8,128)(2,1)}, bf16[4,96,3072]{2,1,0:T(8,128)(2,1)}, bf16[4,96,128]{2,1,0:T(8,128)(2,1)}, bf16[4,96,128]{2,1,0:T(8,128)(2,1)}) custom-call(bf16[768,768]{1,0:T(8,128)(2,1)} %collective-permute-done.23.refs_0_, bf16[768,768]{1,0:T(8,128)(2,1)} %add.87.refs_2_.refs_1_, s32[2]{0:T(128)} %pad_add_fusion.refs_0_.at_ref.refs_2_, ...), custom_call_target="tpu_custom_call" | custom-call | flops 420000000 | tf_op jit(solution)/shard_map/weight_sums/pallas_call | solution.py:864
  398.1 3.5 pad_maximum_fusion
  401.6 1.3 collective-permute-start.22
  402.9 1.3 collective-permute-start.25
  404.2 1.6 add.89.late_ref
  406.8 1.3 collective-permute-start.24
  408.1 4.8 meet.1.refs_0_
  412.9 2.5 join.7
  415.4 1.9 dynamic-slice_bitcast_fusion.10
  417.3 34.3 %collective-permute-start.33 = (bf16[96,1536]{1,0:T(8,128)(2,1)S(1)}, bf16[96,1536]{1,0:T(8,128)(2,1)S(1)}, u32[]{:S(2)}, u32[]{:S(2)}) collective-permute-start(bf16[96,1536]{1,0:T(8,128)(2,1)S(1)} %get-tuple-element.146), channel_id=1, source_target_pairs={{0,1},{1,0},{2,3},{3,2},{4,5},{5,4},{6,7},{7,6},{8,9},{9,8},{10,11... | collective-permute-start | bytes 884744 | tf_op jit(solution)/shard_map/ppermute | solution.py:927
  451.7 39.9 %collective-permute-start.34 = (bf16[96,1536]{1,0:T(8,128)(2,1)}, bf16[96,1536]{1,0:T(8,128)(2,1)}, u32[]{:S(2)}, u32[]{:S(2)}) collective-permute-start(bf16[96,1536]{1,0:T(8,128)(2,1)} %get-tuple-element.148), channel_id=1, source_target_pairs={{0,2},{1,3},{2,0},{3,1},{4,6},{5,7},{6,4},{7,5},{8,10},{9,11},{10,... | collective-permute-start | bytes 884744 | tf_op jit(solution)/shard_map/ppermute | solution.py:927
  491.6 1.5 dynamic-slice_bitcast_fusion.4
  493.1 19.2 %collective-permute-done.22.refs_0_ = bf16[768,768]{1,0:T(8,128)(2,1)} collective-permute-done((bf16[768,768]{1,0:T(8,128)(2,1)S(1)}, bf16[768,768]{1,0:T(8,128)(2,1)}, u32[]{:S(2)}, u32[]{:S(2)}) %collective-permute-start.22) | collective-permute-done | bytes 1179680 | tf_op jit(solution)/shard_map/ppermute | solution.py:931
  516.5 2.6 add.88.early_ref
  519.1 7.7 %finish.1 = f32[896,768]{1,0:T(8,128)} custom-call(s32[8,8]{1,0:T(8,128)} %get-tuple-element.57.meta_ref.refs_2_, f32[896,768]{1,0:T(8,128)} %get-tuple-element.89.da_ref, f32[896,768]{1,0:T(8,128)} %get-tuple-element.90.dh_ref, bf16[896,768]{1,0:T(8,128)(2,1)} %x_ref.7, f32[8,768]{1,0:T(8,128)} %get-tuple-element.61.gain_ref, ...), custom_call_target="tpu_custom_call" | custom-call | flops 180000000 | tf_op jit(solution)/shard_map/finish/pallas_call | solution.py:906
  526.8 1.3 fusion.2
  529.2 12.9 %collective-permute-done.28.refs_3_ = bf16[96,3200]{1,0:T(8,128)(2,1)S(1)} collective-permute-done((bf16[96,3200]{1,0:T(8,128)(2,1)}, bf16[96,3200]{1,0:T(8,128)(2,1)S(1)}, u32[]{:S(2)}, u32[]{:S(2)}) %collective-permute-start.28) | collective-permute-done | bytes 614432 | tf_op jit(solution)/shard_map/ppermute | solution.py:927
  543.0 2.8 total.3
  545.8 1.4 fusion.11
  549.4 4.4 collective-permute-start.32
  555.1 8.2 %collective-permute-done.31 = bf16[96,896]{1,0:T(8,128)(2,1)S(1)} collective-permute-done((bf16[96,896]{1,0:T(8,128)(2,1)S(1)}, bf16[96,896]{1,0:T(8,128)(2,1)S(1)}, u32[]{:S(2)}, u32[]{:S(2)}) %collective-permute-start.31) | collective-permute-done | bytes 172064 | tf_op jit(solution)/shard_map/ppermute | solution.py:927
  (127 shorter events, 29.8 us)
Async XLA Ops:
  7.2 187.1 %all-gather.3.cloned.1.call-start = ((), (), s32[]{:S(2)}) async-start(), calls=%async_computation | async-start | bytes 9732096 | tf_op jit(solution)/shard_map/all_gather | solution.py:998
  8.4 22.9 %collective-permute-start = (bf16[512,768]{1,0:T(8,128)(2,1)S(1)}, bf16[512,768]{1,0:T(8,128)(2,1)S(1)}, u32[]{:S(2)}, u32[]{:S(2)}) collective-permute-start(bf16[512,768]{1,0:T(8,128)(2,1)S(1)} %slice.92), channel_id=1, source_target_pairs={{0,1},{1,2},{2,3},{4,5},{5,6},{6,7},{8,9},{9,10},{10,11},{12,13},{... | collective-permute-start | bytes 2359304 | tf_op jit(solution)/shard_map/ppermute | solution.py:931
  16.6 24.7 %copy-start.15 = (bf16[96,896]{1,0:T(8,128)(2,1)}, bf16[96,896]{1,0:T(8,128)(2,1)S(1)}, u32[]{:S(2)}) copy-start(bf16[96,896]{1,0:T(8,128)(2,1)S(1)} %concatenate.23.refs_1_) | copy-start | bytes 516100
  16.6 18.4 %collective-permute-start.1 = (bf16[96,896]{1,0:T(8,128)(2,1)S(1)}, bf16[96,896]{1,0:T(8,128)(2,1)S(1)}, u32[]{:S(2)}, u32[]{:S(2)}) collective-permute-start(bf16[96,896]{1,0:T(8,128)(2,1)S(1)} %concatenate.23.refs_1_), channel_id=1, source_target_pairs={{0,1},{1,0},{2,3},{3,2},{4,5},{5,4},{6,7},{7,6},{8,9},{9,8},{10,11... | collective-permute-start | bytes 516104 | tf_op jit(solution)/shard_map/ppermute | solution.py:927
  18.2 20.5 %collective-permute-start.2 = (bf16[96,896]{1,0:T(8,128)(2,1)S(1)}, bf16[96,896]{1,0:T(8,128)(2,1)S(1)}, u32[]{:S(2)}, u32[]{:S(2)}) collective-permute-start(bf16[96,896]{1,0:T(8,128)(2,1)S(1)} %concatenate.23.refs_1_), channel_id=1, source_target_pairs={{0,2},{1,3},{2,0},{3,1},{4,6},{5,7},{6,4},{7,5},{8,10},{9,11},{10,... | collective-permute-start | bytes 516104 | tf_op jit(solution)/shard_map/ppermute | solution.py:927
  19.3 22.0 %collective-permute-start.3 = (bf16[96,896]{1,0:T(8,128)(2,1)S(1)}, bf16[96,896]{1,0:T(8,128)(2,1)S(1)}, u32[]{:S(2)}, u32[]{:S(2)}) collective-permute-start(bf16[96,896]{1,0:T(8,128)(2,1)S(1)} %concatenate.23.refs_1_), channel_id=1, source_target_pairs={{0,3},{1,2},{2,1},{3,0},{4,7},{5,6},{6,5},{7,4},{8,11},{9,10},{10,... | collective-permute-start | bytes 516104 | tf_op jit(solution)/shard_map/ppermute | solution.py:927
  31.3 10.0 %copy-start.5 = (bf16[512,768]{1,0:T(8,128)(2,1)}, bf16[512,768]{1,0:T(8,128)(2,1)S(1)}, u32[]{:S(2)}) copy-start(bf16[512,768]{1,0:T(8,128)(2,1)S(1)} %collective-permute-done.refs_0_.a1_ref.r1_ref) | copy-start | bytes 2359300
  31.3 41.9 %collective-permute-start.11 = (bf16[512,768]{1,0:T(8,128)(2,1)S(1)}, bf16[512,768]{1,0:T(8,128)(2,1)S(1)}, u32[]{:S(2)}, u32[]{:S(2)}) collective-permute-start(bf16[512,768]{1,0:T(8,128)(2,1)S(1)} %collective-permute-done.refs_0_.a1_ref.r1_ref), channel_id=1, source_target_pairs={{1,2},{2,3},{5,6},{6,7},{9,10},{10,11},{13,14},{14,15},{17,18},{18... | collective-permute-start | bytes 2359304 | tf_op jit(solution)/shard_map/ppermute | solution.py:931
  35.0 6.3 %copy-start.25 = (bf16[96,896]{1,0:T(8,128)(2,1)}, bf16[96,896]{1,0:T(8,128)(2,1)S(1)}, u32[]{:S(2)}) copy-start(bf16[96,896]{1,0:T(8,128)(2,1)S(1)} %collective-permute-done.1.refs_2_) | copy-start | bytes 516100
  38.7 2.6 copy-start.26
  44.1 32.1 %copy-start.28 = (s32[3584]{0:T(1024)S(1)}, s32[3584]{0:T(1024)}, u32[]{:S(2)}) copy-start(s32[3584]{0:T(1024)} %param.26) | copy-start | bytes 43012
  44.1 17.9 %collective-permute-start.9 = (bf16[96,3200]{1,0:T(8,128)(2,1)}, bf16[96,3200]{1,0:T(8,128)(2,1)S(1)}, u32[]{:S(2)}, u32[]{:S(2)}) collective-permute-start(bf16[96,3200]{1,0:T(8,128)(2,1)} %line.1.refs_4_), channel_id=1, source_target_pairs={{0,24},{4,28},{8,16},{12,20},{16,8},{20,12},{24,0},{28,4},{1,25},{... | collective-permute-start | bytes 1843208 | tf_op jit(solution)/shard_map/ppermute | solution.py:927
  46.6 26.6 %collective-permute-start.5 = (bf16[96,3200]{1,0:T(8,128)(2,1)}, bf16[96,3200]{1,0:T(8,128)(2,1)S(1)}, u32[]{:S(2)}, u32[]{:S(2)}) collective-permute-start(bf16[96,3200]{1,0:T(8,128)(2,1)} %line.1.refs_4_), channel_id=1, source_target_pairs={{0,8},{4,12},{8,0},{12,4},{16,24},{20,28},{24,16},{28,20},{1,9},{5... | collective-permute-start | bytes 1843208 | tf_op jit(solution)/shard_map/ppermute | solution.py:927
  47.1 26.1 %collective-permute-start.7 = (bf16[96,3200]{1,0:T(8,128)(2,1)}, bf16[96,3200]{1,0:T(8,128)(2,1)S(1)}, u32[]{:S(2)}, u32[]{:S(2)}) collective-permute-start(bf16[96,3200]{1,0:T(8,128)(2,1)} %line.1.refs_4_), channel_id=1, source_target_pairs={{0,16},{4,20},{8,24},{12,28},{16,0},{20,4},{24,8},{28,12},{1,17},{... | collective-permute-start | bytes 1843208 | tf_op jit(solution)/shard_map/ppermute | solution.py:927
  62.1 11.1 %copy-start.8 = (bf16[96,3200]{1,0:T(8,128)(2,1)}, bf16[96,3200]{1,0:T(8,128)(2,1)S(1)}, u32[]{:S(2)}) copy-start(bf16[96,3200]{1,0:T(8,128)(2,1)S(1)} %collective-permute-done.9.refs_10_.refs_3_) | copy-start | bytes 1843204
  73.2 0.8 copy-start.9
  73.2 1.1 copy-start.10
  73.2 1.3 copy-start.2
  73.2 3.2 copy-start.13
  76.4 13.9 %collective-permute-start.4 = (bf16[96,3200]{1,0:T(8,128)(2,1)S(1)}, bf16[96,3200]{1,0:T(8,128)(2,1)S(1)}, u32[]{:S(2)}, u32[]{:S(2)}) collective-permute-start(bf16[96,3200]{1,0:T(8,128)(2,1)S(1)} %copy-done.13), channel_id=1, source_target_pairs={{0,4},{4,0},{8,12},{12,8},{16,20},{20,16},{24,28},{28,24},{1,5},{5... | collective-permute-start | bytes 1843208 | tf_op jit(solution)/shard_map/ppermute | solution.py:927
  76.4 21.7 %collective-permute-start.10 = (bf16[96,3200]{1,0:T(8,128)(2,1)}, bf16[96,3200]{1,0:T(8,128)(2,1)S(1)}, u32[]{:S(2)}, u32[]{:S(2)}) collective-permute-start(bf16[96,3200]{1,0:T(8,128)(2,1)} %copy-done.8), channel_id=1, source_target_pairs={{0,4},{4,0},{8,12},{12,8},{16,20},{20,16},{24,28},{28,24},{1,5},{5... | collective-permute-start | bytes 1843208 | tf_op jit(solution)/shard_map/ppermute | solution.py:927
  76.9 21.2 %collective-permute-start.6 = (bf16[96,3200]{1,0:T(8,128)(2,1)}, bf16[96,3200]{1,0:T(8,128)(2,1)S(1)}, u32[]{:S(2)}, u32[]{:S(2)}) collective-permute-start(bf16[96,3200]{1,0:T(8,128)(2,1)} %copy-done.9), channel_id=1, source_target_pairs={{0,4},{4,0},{8,12},{12,8},{16,20},{20,16},{24,28},{28,24},{1,5},{5... | collective-permute-start | bytes 1843208 | tf_op jit(solution)/shard_map/ppermute | solution.py:927
  77.0 21.1 %collective-permute-start.8 = (bf16[96,3200]{1,0:T(8,128)(2,1)}, bf16[96,3200]{1,0:T(8,128)(2,1)}, u32[]{:S(2)}, u32[]{:S(2)}) collective-permute-start(bf16[96,3200]{1,0:T(8,128)(2,1)} %copy-done.10), channel_id=1, source_target_pairs={{0,4},{4,0},{8,12},{12,8},{16,20},{20,16},{24,28},{28,24},{1,5},{5... | collective-permute-start | bytes 1843208 | tf_op jit(solution)/shard_map/ppermute | solution.py:927
  77.4 33.0 %collective-permute-start.12 = (bf16[512,768]{1,0:T(8,128)(2,1)}, bf16[512,768]{1,0:T(8,128)(2,1)S(1)}, u32[]{:S(2)}, u32[]{:S(2)}) collective-permute-start(bf16[512,768]{1,0:T(8,128)(2,1)} %copy-done.2), channel_id=1, source_target_pairs={{2,3},{6,7},{10,11},{14,15},{18,19},{22,23},{26,27},{30,31}} | collective-permute-start | bytes 2359304 | tf_op jit(solution)/shard_map/ppermute | solution.py:931
  90.3 7.8 %copy-start.16 = (bf16[96,3200]{1,0:T(8,128)(2,1)}, bf16[96,3200]{1,0:T(8,128)(2,1)S(1)}, u32[]{:S(2)}) copy-start(bf16[96,3200]{1,0:T(8,128)(2,1)S(1)} %collective-permute-done.4.refs_5_) | copy-start | bytes 1843204
  90.3 30.9 %collective-permute-start.13 = (bf16[384,768]{1,0:T(8,128)(2,1)}, bf16[384,768]{1,0:T(8,128)(2,1)S(1)}, u32[]{:S(2)}, u32[]{:S(2)}) collective-permute-start(bf16[384,768]{1,0:T(8,128)(2,1)} %join.4), channel_id=1, source_target_pairs={{0,1},{1,2},{2,3},{4,5},{5,6},{6,7},{8,9},{9,10},{10,11},{12,13},{... | collective-permute-start | bytes 1769480 | tf_op jit(solution)/shard_map/ppermute | solution.py:931
  98.1 0.8 copy-start.17
  98.1 1.1 copy-start.18
  110.4 0.9 copy-start.6
  113.3 50.3 %collective-permute-start.14 = (bf16[384,768]{1,0:T(8,128)(2,1)}, bf16[384,768]{1,0:T(8,128)(2,1)S(1)}, u32[]{:S(2)}, u32[]{:S(2)}) collective-permute-start(bf16[384,768]{1,0:T(8,128)(2,1)} %join.5), channel_id=1, source_target_pairs={{0,2},{1,3},{4,6},{5,7},{8,10},{9,11},{12,14},{13,15},{16,18},{17,... | collective-permute-start | bytes 1769480 | tf_op jit(solution)/shard_map/ppermute | solution.py:931
  117.7 45.8 %collective-permute-start.15 = (bf16[384,768]{1,0:T(8,128)(2,1)}, bf16[384,768]{1,0:T(8,128)(2,1)S(1)}, u32[]{:S(2)}, u32[]{:S(2)}) collective-permute-start(bf16[384,768]{1,0:T(8,128)(2,1)} %join.5), channel_id=1, source_target_pairs={{0,3},{4,7},{8,11},{12,15},{16,19},{20,23},{24,27},{28,31}} | collective-permute-start | bytes 1769480 | tf_op jit(solution)/shard_map/ppermute | solution.py:931
  121.2 0.8 copy-start.14
  163.5 0.8 copy-start.21
  163.5 1.0 copy-start.22
  239.5 44.4 %collective-permute-start.16 = (bf16[4,4,96,1536]{3,2,1,0:T(8,128)(2,1)}, bf16[4,4,96,1536]{3,2,1,0:T(8,128)(2,1)}, u32[]{:S(2)}, u32[]{:S(2)}) collective-permute-start(bf16[4,4,96,1536]{3,2,1,0:T(8,128)(2,1)} %get-tuple-element.74), channel_id=1, source_target_pairs={{0,4},{4,0},{8,12},{12,8},{16,20},{20,16},{24,28},{28,24},{1,5},{5... | collective-permute-start | bytes 14155784 | tf_op jit(solution)/shard_map/ppermute | solution.py:927
  301.6 13.4 %collective-permute-start.20 = (bf16[768,768]{1,0:T(8,128)(2,1)}, bf16[768,768]{1,0:T(8,128)(2,1)S(1)}, u32[]{:S(2)}, u32[]{:S(2)}) collective-permute-start(bf16[768,768]{1,0:T(8,128)(2,1)} %get-tuple-element.81.refs_1_), channel_id=1, source_target_pairs={{3,2},{7,6},{11,10},{15,14},{19,18},{23,22},{27,26},{31,30}} | collective-permute-start | bytes 3538952 | tf_op jit(solution)/shard_map/ppermute | solution.py:931
  302.3 12.7 %copy-start.12 = (bf16[768,768]{1,0:T(8,128)(2,1)S(1)}, bf16[768,768]{1,0:T(8,128)(2,1)}, u32[]{:S(2)}) copy-start(bf16[768,768]{1,0:T(8,128)(2,1)} %get-tuple-element.81.refs_1_) | copy-start | bytes 3538948
  302.3 39.9 %collective-permute-start.21 = (bf16[768,768]{1,0:T(8,128)(2,1)}, bf16[768,768]{1,0:T(8,128)(2,1)}, u32[]{:S(2)}, u32[]{:S(2)}) collective-permute-start(bf16[768,768]{1,0:T(8,128)(2,1)} %get-tuple-element.82.refs_0_), channel_id=1, source_target_pairs={{3,2},{1,0},{7,6},{5,4},{11,10},{9,8},{15,14},{13,12},{19,18},{17,... | collective-permute-start | bytes 3538952 | tf_op jit(solution)/shard_map/ppermute | solution.py:931
  308.3 36.5 %collective-permute-start.17 = (bf16[4,96,1536]{2,1,0:T(8,128)(2,1)}, bf16[4,96,1536]{2,1,0:T(8,128)(2,1)}, u32[]{:S(2)}, u32[]{:S(2)}) collective-permute-start(bf16[4,96,1536]{2,1,0:T(8,128)(2,1)} %get-tuple-element.140), channel_id=1, source_target_pairs={{0,8},{4,12},{8,0},{12,4},{16,24},{20,28},{24,16},{28,20},{1,9},{5... | collective-permute-start | bytes 3538952 | tf_op jit(solution)/shard_map/ppermute | solution.py:927
  309.7 55.0 %collective-permute-start.18 = (bf16[4,96,1536]{2,1,0:T(8,128)(2,1)}, bf16[4,96,1536]{2,1,0:T(8,128)(2,1)}, u32[]{:S(2)}, u32[]{:S(2)}) collective-permute-start(bf16[4,96,1536]{2,1,0:T(8,128)(2,1)} %get-tuple-element.139), channel_id=1, source_target_pairs={{0,16},{4,20},{8,24},{12,28},{16,0},{20,4},{24,8},{28,12},{1,17},{... | collective-permute-start | bytes 3538952 | tf_op jit(solution)/shard_map/ppermute | solution.py:927
  313.5 53.1 %collective-permute-start.19 = (bf16[4,96,1536]{2,1,0:T(8,128)(2,1)}, bf16[4,96,1536]{2,1,0:T(8,128)(2,1)}, u32[]{:S(2)}, u32[]{:S(2)}) collective-permute-start(bf16[4,96,1536]{2,1,0:T(8,128)(2,1)} %get-tuple-element.138), channel_id=1, source_target_pairs={{0,24},{4,28},{8,16},{12,20},{16,8},{20,12},{24,0},{28,4},{1,25},{... | collective-permute-start | bytes 3538952 | tf_op jit(solution)/shard_map/ppermute | solution.py:927
  315.3 25.4 %copy-start.3 = (bf16[768,768]{1,0:T(8,128)(2,1)}, bf16[768,768]{1,0:T(8,128)(2,1)S(1)}, u32[]{:S(2)}) copy-start(bf16[768,768]{1,0:T(8,128)(2,1)S(1)} %add.86.refs_1_) | copy-start | bytes 3538948
  315.3 64.9 %collective-permute-start.23 = (bf16[768,768]{1,0:T(8,128)(2,1)S(1)}, bf16[768,768]{1,0:T(8,128)(2,1)}, u32[]{:S(2)}, u32[]{:S(2)}) collective-permute-start(bf16[768,768]{1,0:T(8,128)(2,1)S(1)} %add.86.refs_1_), channel_id=1, source_target_pairs={{2,1},{6,5},{10,9},{14,13},{18,17},{22,21},{26,25},{30,29}} | collective-permute-start | bytes 3538952 | tf_op jit(solution)/shard_map/ppermute | solution.py:931
  317.0 25.2 %copy-start.11 = (bf16[768,768]{1,0:T(8,128)(2,1)S(1)}, bf16[768,768]{1,0:T(8,128)(2,1)}, u32[]{:S(2)}) copy-start(bf16[768,768]{1,0:T(8,128)(2,1)} %get-tuple-element.82.refs_0_) | copy-start | bytes 3538948
  398.1 3.5 copy-start.1
  398.1 6.1 %copy-start.4 = (bf16[768,768]{1,0:T(8,128)(2,1)S(1)}, bf16[768,768]{1,0:T(8,128)(2,1)}, u32[]{:S(2)}) copy-start(bf16[768,768]{1,0:T(8,128)(2,1)} %copy-done.3) | copy-start | bytes 3538948
  401.6 6.5 %collective-permute-start.26 = (bf16[4,96,3200]{2,1,0:T(8,128)(2,1)}, bf16[4,96,3200]{2,1,0:T(8,128)(2,1)}, u32[]{:S(2)}, u32[]{:S(2)}) collective-permute-start(bf16[4,96,3200]{2,1,0:T(8,128)(2,1)} %pad_maximum_fusion), channel_id=1, source_target_pairs={{0,4},{4,0},{8,12},{12,8},{16,20},{20,16},{24,28},{28,24},{1,5},{5... | collective-permute-start | bytes 7372808 | tf_op jit(solution)/shard_map/ppermute | solution.py:927
  401.6 110.7 %collective-permute-start.22 = (bf16[768,768]{1,0:T(8,128)(2,1)S(1)}, bf16[768,768]{1,0:T(8,128)(2,1)}, u32[]{:S(2)}, u32[]{:S(2)}) collective-permute-start(bf16[768,768]{1,0:T(8,128)(2,1)S(1)} %copy-done.1), channel_id=1, source_target_pairs={{2,0},{6,4},{10,8},{14,12},{18,16},{22,20},{26,24},{30,28}} | collective-permute-start | bytes 3538952 | tf_op jit(solution)/shard_map/ppermute | solution.py:931
  402.9 88.7 %collective-permute-start.25 = (bf16[128,768]{1,0:T(8,128)(2,1)}, bf16[128,768]{1,0:T(8,128)(2,1)}, u32[]{:S(2)}, u32[]{:S(2)}) collective-permute-start(bf16[128,768]{1,0:T(8,128)(2,1)} %get-tuple-element.91), channel_id=1, source_target_pairs={{1,0},{3,2},{5,4},{7,6},{9,8},{11,10},{13,12},{15,14},{17,16},{19,... | collective-permute-start | bytes 589832 | tf_op jit(solution)/shard_map/ppermute | solution.py:931
  405.7 1.0 copy-start.7
  406.8 106.8 %collective-permute-start.24 = (bf16[128,768]{1,0:T(8,128)(2,1)S(1)}, bf16[128,768]{1,0:T(8,128)(2,1)}, u32[]{:S(2)}, u32[]{:S(2)}) collective-permute-start(bf16[128,768]{1,0:T(8,128)(2,1)S(1)} %slice.121), channel_id=1, source_target_pairs={{1,0},{5,4},{9,8},{13,12},{17,16},{21,20},{25,24},{29,28}} | collective-permute-start | bytes 589832 | tf_op jit(solution)/shard_map/ppermute | solution.py:931
  412.9 78.7 %copy-start = (bf16[4,96,3200]{2,1,0:T(8,128)(2,1)S(1)}, bf16[4,96,3200]{2,1,0:T(8,128)(2,1)}, u32[]{:S(2)}) copy-start(bf16[4,96,3200]{2,1,0:T(8,128)(2,1)} %meet.1.refs_0_) | copy-start | bytes 7372804
  417.3 97.3 %collective-permute-start.33 = (bf16[96,1536]{1,0:T(8,128)(2,1)S(1)}, bf16[96,1536]{1,0:T(8,128)(2,1)S(1)}, u32[]{:S(2)}, u32[]{:S(2)}) collective-permute-start(bf16[96,1536]{1,0:T(8,128)(2,1)S(1)} %get-tuple-element.146), channel_id=1, source_target_pairs={{0,1},{1,0},{2,3},{3,2},{4,5},{5,4},{6,7},{7,6},{8,9},{9,8},{10,11... | collective-permute-start | bytes 884744 | tf_op jit(solution)/shard_map/ppermute | solution.py:927
  451.7 75.1 %collective-permute-start.34 = (bf16[96,1536]{1,0:T(8,128)(2,1)}, bf16[96,1536]{1,0:T(8,128)(2,1)}, u32[]{:S(2)}, u32[]{:S(2)}) collective-permute-start(bf16[96,1536]{1,0:T(8,128)(2,1)} %get-tuple-element.148), channel_id=1, source_target_pairs={{0,2},{1,3},{2,0},{3,1},{4,6},{5,7},{6,4},{7,5},{8,10},{9,11},{10,... | collective-permute-start | bytes 884744 | tf_op jit(solution)/shard_map/ppermute | solution.py:927
  491.6 35.2 %collective-permute-start.35 = (bf16[96,1536]{1,0:T(8,128)(2,1)S(1)}, bf16[96,1536]{1,0:T(8,128)(2,1)}, u32[]{:S(2)}, u32[]{:S(2)}) collective-permute-start(bf16[96,1536]{1,0:T(8,128)(2,1)S(1)} %get-tuple-element.147), channel_id=1, source_target_pairs={{0,3},{1,2},{2,1},{3,0},{4,7},{5,6},{6,5},{7,4},{8,11},{9,10},{10,... | collective-permute-start | bytes 884744 | tf_op jit(solution)/shard_map/ppermute | solution.py:927
  512.3 17.0 %collective-permute-start.27 = (bf16[96,3200]{1,0:T(8,128)(2,1)}, bf16[96,3200]{1,0:T(8,128)(2,1)S(1)}, u32[]{:S(2)}, u32[]{:S(2)}) collective-permute-start(bf16[96,3200]{1,0:T(8,128)(2,1)} %get-tuple-element.144), channel_id=1, source_target_pairs={{0,8},{4,12},{8,0},{12,4},{16,24},{20,28},{24,16},{28,20},{1,9},{5... | collective-permute-start | bytes 1843208 | tf_op jit(solution)/shard_map/ppermute | solution.py:927
  513.6 28.6 %collective-permute-start.28 = (bf16[96,3200]{1,0:T(8,128)(2,1)}, bf16[96,3200]{1,0:T(8,128)(2,1)S(1)}, u32[]{:S(2)}, u32[]{:S(2)}) collective-permute-start(bf16[96,3200]{1,0:T(8,128)(2,1)} %get-tuple-element.143), channel_id=1, source_target_pairs={{0,16},{4,20},{8,24},{12,28},{16,0},{20,4},{24,8},{28,12},{1,17},{... | collective-permute-start | bytes 1843208 | tf_op jit(solution)/shard_map/ppermute | solution.py:927
  515.4 26.8 %collective-permute-start.29 = (bf16[96,3200]{1,0:T(8,128)(2,1)}, bf16[96,3200]{1,0:T(8,128)(2,1)}, u32[]{:S(2)}, u32[]{:S(2)}) collective-permute-start(bf16[96,3200]{1,0:T(8,128)(2,1)} %get-tuple-element.142), channel_id=1, source_target_pairs={{0,24},{4,28},{8,16},{12,20},{16,8},{20,12},{24,0},{28,4},{1,25},{... | collective-permute-start | bytes 1843208 | tf_op jit(solution)/shard_map/ppermute | solution.py:927
  519.1 7.7 %copy-start.24 = (bf16[96,1536]{1,0:T(8,128)(2,1)S(1)}, bf16[96,1536]{1,0:T(8,128)(2,1)}, u32[]{:S(2)}) copy-start(bf16[96,1536]{1,0:T(8,128)(2,1)} %copy-done.23) | copy-start | bytes 884740
  529.2 12.9 %copy-start.19 = (bf16[96,3200]{1,0:T(8,128)(2,1)}, bf16[96,3200]{1,0:T(8,128)(2,1)S(1)}, u32[]{:S(2)}) copy-start(bf16[96,3200]{1,0:T(8,128)(2,1)S(1)} %collective-permute-done.27.refs_2_) | copy-start | bytes 1843204
  542.2 0.8 copy-start.20
  549.0 6.1 %collective-permute-start.30 = (bf16[96,896]{1,0:T(8,128)(2,1)S(1)}, bf16[96,896]{1,0:T(8,128)(2,1)S(1)}, u32[]{:S(2)}, u32[]{:S(2)}) collective-permute-start(bf16[96,896]{1,0:T(8,128)(2,1)S(1)} %concatenate.26), channel_id=1, source_target_pairs={{0,1},{1,0},{2,3},{3,2},{4,5},{5,4},{6,7},{7,6},{8,9},{9,8},{10,11... | collective-permute-start | bytes 516104 | tf_op jit(solution)/shard_map/ppermute | solution.py:927
  549.2 14.1 %collective-permute-start.31 = (bf16[96,896]{1,0:T(8,128)(2,1)S(1)}, bf16[96,896]{1,0:T(8,128)(2,1)S(1)}, u32[]{:S(2)}, u32[]{:S(2)}) collective-permute-start(bf16[96,896]{1,0:T(8,128)(2,1)S(1)} %concatenate.27), channel_id=1, source_target_pairs={{0,2},{1,3},{2,0},{3,1},{4,6},{5,7},{6,4},{7,5},{8,10},{9,11},{10,... | collective-permute-start | bytes 516104 | tf_op jit(solution)/shard_map/ppermute | solution.py:927
  549.4 13.9 %collective-permute-start.32 = (bf16[96,896]{1,0:T(8,128)(2,1)S(1)}, bf16[96,896]{1,0:T(8,128)(2,1)S(1)}, u32[]{:S(2)}, u32[]{:S(2)}) collective-permute-start(bf16[96,896]{1,0:T(8,128)(2,1)S(1)} %pad_maximum_fusion.1), channel_id=1, source_target_pairs={{0,3},{1,2},{2,1},{3,0},{4,7},{5,6},{6,5},{7,4},{8,11},{9,10},{10,... | collective-permute-start | bytes 516104 | tf_op jit(solution)/shard_map/ppermute | solution.py:927
  (2 other events, 1.4 us)
Sparse Core Ops, SparseCore 0:
  76.4 117.8 all-gather.2

commit v3 on v2

--- a/solution.py
+++ b/solution.py
@@ -186,25 +186,119 @@
     )(*deps, *parts)
 
 
-def meet_kernel(kept_ref, kept_gain, away_ref, out_ref):
-    d = kept_ref.shape[2]
-    out_ref[:, :, :d] = (kept_ref[...].astype(F32) + away_ref[:, :, :d].astype(F32)).astype(BF16)
-    out_ref[:, :, d:] = (kept_gain[...].astype(F32) + away_ref[:, :, d:].astype(F32)).astype(BF16)
-
-
-def meet(deps, kept, kept_gain, away):
-    chips = kept.shape[0]
-    block = lambda one: pl.BlockSpec((1,) + one.shape[1:], lambda i: (i, 0, 0))
-    return pl.pallas_call(
-        after(len(deps), meet_kernel),
-        grid=(chips,),
-        in_specs=[ANY] * len(deps) + [block(one) for one in (kept, kept_gain, away)],
-        out_specs=block(away),
-        out_shape=jax.ShapeDtypeStruct(away.shape, BF16),
-        compiler_params=params(),
-        cost_estimate=cost(3),
+def begin_kernel(x_ref, *refs):
+    ins, rest_ref, front_ref = refs[:-2], refs[-2], refs[-1]
+    join_kernel(ins, rest_ref)
+    front_ref[...] = x_ref[ROOT:, :]
+
+
+def begin(deps, x, *parts):
+    outs = ((parts[0].shape[0], sum(part.shape[1] for part in parts)), (x.shape[0] - ROOT, x.shape[1]))
+    return pl.pallas_call(
+        after(len(deps), begin_kernel),
+        grid=(1,),
+        in_specs=[ANY] * len(deps) + [fixed(one.shape) for one in (x, *parts)],
+        out_specs=[fixed(one) for one in outs],
+        out_shape=[shape(*one, BF16) for one in outs],
+        compiler_params=params(),
+        cost_estimate=cost(2),
+        name="begin",
+    )(*deps, x, *parts)
+
+
+def cores_kernel(at_ref, kept_ref, away_ref, *outs):
+    chip = at_ref[1] // 2
+    for m, out_ref in enumerate(outs):
+        out_ref[0] = (kept_ref[chip ^ m, 0].astype(F32) + away_ref[chip ^ m, 0].astype(F32)).astype(BF16)
+
+
+def meet_rest(at, kept, away):
+    chips, parts, rows, wide = kept.shape
+    block = pl.BlockSpec((chips, 1, rows, wide), lambda i: (0, i, 0, 0))
+    out = pl.BlockSpec((1, rows, wide), lambda i: (i, 0, 0))
+    return pl.pallas_call(
+        cores_kernel,
+        grid=(parts,),
+        in_specs=[SMEM, block, block],
+        out_specs=[out] * chips,
+        out_shape=[jax.ShapeDtypeStruct((parts, rows, wide), BF16)] * chips,
+        compiler_params=params(),
+        cost_estimate=cost(5),
+        name="meet_rest",
+    )(at, kept, away)
+
+
+def meet_kernel(count, at_ref, *refs):
+    ins, outs = refs[:2 * count], refs[2 * count:]
+    chip = at_ref[1] // 2
+    for m, out_ref in enumerate(outs):
+        at = 0
+        for kept, away in zip(ins[:count], ins[count:]):
+            n = kept.shape[2]
+            out_ref[:, at:at + n] = (kept[chip ^ m].astype(F32) + away[chip ^ m].astype(F32)).astype(BF16)
+            at += n
+
+
+def meet(deps, at, kept, away):
+    chips, rows, _ = kept[0].shape
+    ins = (*kept, *away)
+    out = (rows, sum(one.shape[2] for one in kept))
+    return pl.pallas_call(
+        after(len(deps), functools.partial(meet_kernel, len(kept))),
+        grid=(1,),
+        in_specs=[ANY] * len(deps) + [SMEM] + [fixed(one.shape) for one in ins],
+        out_specs=[fixed(out)] * chips,
+        out_shape=[shape(*out, BF16)] * chips,
+        compiler_params=params(),
+        cost_estimate=cost(4),
         name="meet",
-    )(*deps, kept, kept_gain, away)
+    )(*deps, at, *ins)
+
+
+def fold_kernel(at_ref, *refs):
+    ins, (keep_ref, send_ref) = refs[:-2], refs[-2:]
+    t = at_ref[0]
+    half = keep_ref.shape[0]
+    for r in range(2 * half):
+        got = sum((one[t ^ r].astype(F32) for one in ins[1:]), ins[0][t ^ r].astype(F32)).astype(BF16)
+        if r < half:
+            keep_ref[r] = got
+        else:
+            send_ref[r - half] = got
+
+
+def fold(at, *blocks):
+    parts, rows, wide = blocks[0].shape
+    out = (parts // 2, rows, wide)
+    return pl.pallas_call(
+        fold_kernel,
+        grid=(1,),
+        in_specs=[SMEM] + [fixed(one.shape) for one in blocks],
+        out_specs=[fixed(out)] * 2,
+        out_shape=[jax.ShapeDtypeStruct(out, BF16)] * 2,
+        compiler_params=params(),
+        cost_estimate=cost(4),
+        name="fold",
+    )(at, *blocks)
+
+
+def middle_kernel(keep_ref, got_ref, mine_ref, send_ref):
+    for r, out_ref in enumerate((mine_ref, send_ref)):
+        out_ref[...] = (keep_ref[r].astype(F32) + got_ref[r].astype(F32)).astype(BF16)
+
+
+def middle(deps, keep, got):
+    out = keep.shape[1:]
+    return pl.pallas_call(
+        after(len(deps), middle_kernel),
+        grid=(1,),
+        in_specs=[ANY] * len(deps) + [fixed(keep.shape)] * 2,
+        out_specs=[fixed(out)] * 2,
+        out_shape=[shape(*out, BF16)] * 2,
+        compiler_params=params(),
+        cost_estimate=cost(2),
+        name="middle",
+    )(*deps, keep, got)
 
 
 def own_kernel(count, at_ref, x_ref, cos_ref, sin_ref, *refs):
@@ -357,13 +451,27 @@
         if ref is None:
             continue
         key = lax.broadcasted_iota(jnp.int32, ref.shape[1:], keys_axis)
-        row = lax.broadcasted_iota(jnp.int32, ref.shape[1:], 1 - keys_axis)
+        row = lax.broadcasted_iota(jnp.int32, ref.shape[1:], 1 - keys_axis) % TILE
         for s in range(ref.shape[0]):
             ref[s] = jnp.where(key <= row + s * TILE, 0.0, MASKED).astype(F32)
 
 
 def low_half():
     return lax.broadcasted_iota(jnp.int32, (TILE, 128), 1) < HEAD_DIM
+
+
+def both(low, x):
+    none = jnp.zeros_like(x)
+    return jnp.concatenate([jnp.where(low, x, none), jnp.where(low, none, x)], axis=0)
+
+
+def diagonal(x):
+    return jnp.concatenate([x[:HEAD_DIM, :TILE], x[HEAD_DIM:, TILE:]], axis=0)
+
+
+def per_half(row):
+    upper = lax.broadcasted_iota(jnp.int32, (128, TILE), 0) < HEAD_DIM
+    return jnp.where(upper, row[:, :TILE], row[:, TILE:])
 
 
 def tile_of(meta_ref, i):
@@ -378,50 +486,62 @@
     to_ref[pl.ds(TILE + loc, TILE), :] = jnp.zeros((TILE, 128), to_ref.dtype)
 
 
-def attend_near_kernel(meta_ref, q_ref, kn_ref, vn_ref, k_ref, v_ref, acc_ref, top_ref, sum_ref, root_ref, own_ref, ko_ref, vo_ref):
+def soften(q, spans):
+    s = [dot(kk, q, COLS) if b is None else dot(kk, q, COLS) + b for kk, _, b in spans]
+    top = functools.reduce(jnp.maximum, [jnp.max(part, axis=0, keepdims=True) for part in s])
+    return s, top
+
+
+def weigh(s, top, spans):
+    e = [jnp.exp(part - top) for part in s]
+    total = sum(jnp.sum(part, axis=0, keepdims=True) for part in e)
+    return diagonal(sum(dot(vt, part.astype(BF16)) for part, (_, vt, _) in zip(e, spans))), total
+
+
+def attend_near_kernel(meta_ref, q_ref, kn_ref, vn_ref, k_ref, v_ref, acc_ref, stat_ref, root_ref, own_ref, ko_ref, vo_ref, vr_ref):
     @pl.when(pl.program_id(0) == 0)
     def _():
-        fill_bias(root_ref, own_ref, 1)
-
+        fill_bias(root_ref, own_ref, 0)
+
+    loc = q_ref.shape[0]
     line_up(ko_ref, kn_ref, k_ref)
-    line_up(vo_ref, vn_ref, v_ref)
+    root = pl.ds(0, ROOT)
+    vr_ref[...] = vn_ref[root, :].T
+    vo_ref[:, :TILE] = vn_ref[pl.ds(ROOT, TILE), :].T
+    vo_ref[:, TILE:TILE + loc] = v_ref[...].T
+    vo_ref[:, TILE + loc:] = jnp.zeros((128, TILE), BF16)
     low = low_half()
-    root = pl.ds(0, ROOT)
-
-    def one(i, carry):
+    stat_ref[...] = jnp.zeros_like(stat_ref)
+
+    def one(i, rooted):
         sub, leaf, par, own, here = tile_of(meta_ref, i)
-        q = q_ref[here, :]
-
-        def soft(spans):
-            outs = []
-            for head in range(2):
-                qh = jnp.where(low if head == 0 else ~low, q, jnp.zeros_like(q))
-                s = [dot(qh, kk, COLS) if b is None else dot(qh, kk, COLS) + b for kk, _, b in spans]
-                top = functools.reduce(jnp.maximum, [jnp.max(part, axis=1, keepdims=True) for part in s])
-                e = [jnp.exp(part - top) for part in s]
-                total = sum(jnp.sum(part, axis=1, keepdims=True) for part in e)
-                acc = sum(dot(part.astype(BF16), vv) for part, (_, vv, _) in zip(e, spans))
-                outs.append((acc, top, total))
-            acc_ref[here, :] = jnp.where(low, outs[0][0], outs[1][0])
-            top_ref[here, :] = jnp.where(low, outs[0][1], outs[1][1])
-            sum_ref[here, :] = jnp.where(low, outs[0][2], outs[1][2])
-
-        @pl.when(sub < ROOT // TILE)
-        def _():
-            soft([(kn_ref[root, :], vn_ref[root, :], root_ref[sub])])
-
-        @pl.when(sub >= ROOT // TILE)
-        def _():
-            soft([(kn_ref[root, :], vn_ref[root, :], None), (ko_ref[own, :], vo_ref[own, :], own_ref[sub % 2])])
-
-        return carry
-
-    lax.fori_loop(0, acc_ref.shape[0] // TILE, one, 0)
+        q = both(low, q_ref[here, :])
+        spans = [(kn_ref[root, :], vr_ref[...], root_ref[i] if rooted else None)]
+        if not rooted:
+            spans.append((ko_ref[own, :], vo_ref[:, own], own_ref[sub % 2]))
+        s, top = soften(q, spans)
+        acc, total = weigh(s, top, spans)
+        acc_ref[:, here] = acc
+        for h in range(2):
+            stat_ref[0, h:h + 1, here] = top[:, h * TILE:(h + 1) * TILE]
+            stat_ref[0, 2 + h:3 + h, here] = total[:, h * TILE:(h + 1) * TILE]
+
+    tiles = loc // TILE
+
+    @pl.when(meta_ref[0, 0] > 0)
+    def _():
+        for i in range(tiles):
+            one(i, False)
+
+    @pl.when(meta_ref[0, 0] == 0)
+    def _():
+        for i in range(tiles):
+            one(i, i < ROOT // TILE)
 
 
 def bias_scratch(keys_axis):
     def one(n):
-        return pltpu.VMEM((n // TILE,) + ((n, TILE) if keys_axis == 0 else (TILE, n)), F32)
+        return pltpu.VMEM((n // TILE,) + ((n, 2 * TILE) if keys_axis == 0 else (2 * TILE, n)), F32)
     return one(ROOT), one(BLOCK)
 
 
@@ -436,67 +556,54 @@
         attend_near_kernel,
         grid=(d // 128,),
         in_specs=[SMEM, pair(loc), pair(n), pair(n), pair(loc), pair(loc)],
-        out_specs=[pair(loc)] * 3,
-        out_shape=[shape(loc, d, F32)] * 3,
-        scratch_shapes=[*bias_scratch(1), line_scratch(loc, BF16), line_scratch(loc, BF16)],
-        compiler_params=params(),
-        cost_estimate=cost(30),
+        out_specs=[pl.BlockSpec((128, loc), lambda p: (p, 0)), log_spec(loc)],
+        out_shape=[shape(d, loc, F32), jax.ShapeDtypeStruct((d // 128, 8, loc), F32)],
+        scratch_shapes=[*bias_scratch(0), line_scratch(loc, BF16), pltpu.VMEM((128, loc + 2 * TILE), BF16), pltpu.VMEM((128, ROOT), BF16)],
+        compiler_params=params(),
+        cost_estimate=cost(20),
         name="attend_near",
     )(meta, q, *near, *own)
 
 
-def attend_far_kernel(meta_ref, q_ref, ks_ref, vs_ref, acc_ref, top_ref, sum_ref, o_ref, l_ref):
+def attend_far_kernel(meta_ref, q_ref, ks_ref, vs_ref, acc_ref, stat_ref, o_ref, l_ref, vt_ref):
     low = low_half()
-
-    def one(i, carry):
+    vt_ref[...] = vs_ref[...].T
+    l_ref[...] = jnp.zeros_like(l_ref)
+    for i in range(o_ref.shape[0] // TILE):
         sub, leaf, par, own, here = tile_of(meta_ref, i)
-        acc, tops, sums = acc_ref[here, :], top_ref[here, :], sum_ref[here, :]
-
-        def finish(acc, top, total):
-            o_ref[here, :] = (acc / total).astype(BF16)
-            l_ref[0, :, here] = (top + jnp.log(total)).T[60:68, :]
-
-        @pl.when(leaf == 0)
-        def _():
-            finish(acc, tops, sums)
-
-        @pl.when(leaf > 0)
-        def _():
-            q = q_ref[here, :]
-            kk, vv = ks_ref[par, :], vs_ref[par, :]
-            outs = []
-            for head in range(2):
-                qh = jnp.where(low if head == 0 else ~low, q, jnp.zeros_like(q))
-                old = tops[:, head * HEAD_DIM:head * HEAD_DIM + 1]
-                s = dot(qh, kk, COLS)
-                top = jnp.maximum(jnp.max(s, axis=1, keepdims=True), old)
-                e = jnp.exp(s - top)
-                outs.append((dot(e.astype(BF16), vv), top, jnp.sum(e, axis=1, keepdims=True)))
-            new, top, total = (jnp.where(low, outs[0][j], outs[1][j]) for j in range(3))
-            fade = jnp.exp(tops - top)
-            finish(acc * fade + new, top, sums * fade + total)
-
-        return carry
-
-    lax.fori_loop(0, o_ref.shape[0] // TILE, one, 0)
+        stat = stat_ref[0, :, here]
+        old = jnp.concatenate([stat[0:1], stat[1:2]], axis=1)
+        old_total = jnp.concatenate([stat[2:3], stat[3:4]], axis=1)
+        spans = [(ks_ref[par, :], vt_ref[:, par], jnp.where(leaf > 0, 0.0, MASKED).astype(F32))]
+        s, top = soften(both(low, q_ref[here, :]), spans)
+        top = jnp.maximum(top, old)
+        new, total = weigh(s, top, spans)
+        fade = jnp.exp(old - top)
+        total = old_total * fade + total
+        out = (acc_ref[:, here] * per_half(fade) + new) / per_half(total)
+        o_ref[here, :] = out.T.astype(BF16)
+        log = top + jnp.log(total)
+        for h in range(2):
+            l_ref[0, h:h + 1, here] = log[:, h * TILE:(h + 1) * TILE]
 
 
 def log_spec(loc):
     return pl.BlockSpec((1, 8, loc), lambda p: (p, 0, 0))
 
 
-def attend_far(meta, q, far, acc, top, total):
+def attend_far(meta, q, far, acc, stat):
     loc, d = q.shape
     return pl.pallas_call(
         attend_far_kernel,
         grid=(d // 128,),
-        in_specs=[SMEM, pair(loc), pair(SLOTS), pair(SLOTS), pair(loc), pair(loc), pair(loc)],
+        in_specs=[SMEM, pair(loc), pair(SLOTS), pair(SLOTS), pl.BlockSpec((128, loc), lambda p: (p, 0)), log_spec(loc)],
         out_specs=[pair(loc), log_spec(loc)],
         out_shape=[shape(loc, d, BF16), jax.ShapeDtypeStruct((d // 128, 8, loc), F32)],
-        compiler_params=params(),
-        cost_estimate=cost(11),
+        scratch_shapes=[pltpu.VMEM((128, SLOTS), BF16)],
+        compiler_params=params(),
+        cost_estimate=cost(9),
         name="attend_far",
-    )(meta, q, *far, acc, top, total)
+    )(meta, q, *far, acc, stat)
 
 
 def split_cores(core, got, kept_ref, away_ref, where):
@@ -605,34 +712,27 @@
 
 
 def back_setup(low, q_ref, do_ref, o_ref, l_ref, here):
-    q, do = q_ref[here, :], do_ref[here, :]
+    do = do_ref[here, :]
     dots = (do.astype(F32) * o_ref[here, :].astype(F32)).T
-    heads = []
-    for head in range(2):
-        keep = low if head == 0 else ~low
-        heads.append((jnp.where(keep, q, jnp.zeros_like(q)), jnp.where(keep, do, jnp.zeros_like(do)),
-                      l_ref[0, 3 + head:4 + head, here],
-                      jnp.sum(dots[head * HEAD_DIM:(head + 1) * HEAD_DIM, :], axis=0, keepdims=True)))
-    return heads
-
-
-def back_span(low, heads, kk, vv, bias, acc, dk_acc, dv_acc):
-    dqs = []
-    for qh, doh, log, row_dot in heads:
-        s = dot(kk, qh, COLS)
-        if bias is not None:
-            s = s + bias
-        p = jnp.exp(s - log)
-        dp = dot(vv, doh, COLS)
-        ds = (p * (dp - row_dot)).astype(BF16)
-        dv_acc[acc, :] += dot(p.astype(BF16), doh)
-        dk_acc[acc, :] += dot(ds, qh)
-        dqs.append(dot(ds, kk, ROWS))
-    return jnp.where(low, dqs[0], dqs[1])
+    row_dot = [jnp.sum(dots[h * HEAD_DIM:(h + 1) * HEAD_DIM, :], axis=0, keepdims=True) for h in range(2)]
+    log = [l_ref[0, h:h + 1, here] for h in range(2)]
+    return both(low, q_ref[here, :]), both(low, do), jnp.concatenate(log, axis=1), jnp.concatenate(row_dot, axis=1)
+
+
+def back_span(setup, kk, vv, kt, bias, acc, dk_acc, dv_acc):
+    q, do, log, row_dot = setup
+    s = dot(kk, q, COLS)
+    if bias is not None:
+        s = s + bias
+    p = jnp.exp(s - log)
+    ds = (p * (dot(vv, do, COLS) - row_dot)).astype(BF16)
+    dv_acc[acc, :] += dot(p.astype(BF16), do)
+    dk_acc[acc, :] += dot(ds, q)
+    return diagonal(dot(kt, ds))
 
 
 def back_far_kernel(meta_ref, slot_ref, q_ref, do_ref, o_ref, l_ref, kn_ref, vn_ref, ks_ref, vs_ref, cos_ref, sin_ref,
-                    dq_ref, dk_ref, dv_ref, root_ref, dk_acc, dv_acc):
+                    dq_ref, dk_ref, dv_ref, root_ref, krt_ref, kst_ref, dk_acc, dv_acc):
     @pl.when(pl.program_id(0) == 0)
     def _():
         fill_bias(root_ref, None, 0)
@@ -641,27 +741,30 @@
     root = pl.ds(0, ROOT)
     for ref in (dk_acc, dv_acc):
         ref[...] = jnp.zeros_like(ref)
-
-    def one(i, carry):
+    krt_ref[...] = kn_ref[root, :].T
+    kst_ref[...] = ks_ref[...].T
+    tiles = do_ref.shape[0] // TILE
+
+    def one(i, rooted):
         sub, leaf, par, own, here = tile_of(meta_ref, i)
-        heads = back_setup(low, q_ref, do_ref, o_ref, l_ref, here)
-
-        @pl.when(sub < ROOT // TILE)
-        def _():
-            dq_ref[here, :] = back_span(low, heads, kn_ref[root, :], vn_ref[root, :], root_ref[sub], root, dk_acc, dv_acc)
-
-        @pl.when(sub >= ROOT // TILE)
-        def _():
-            dq_ref[here, :] = back_span(low, heads, kn_ref[root, :], vn_ref[root, :], None, root, dk_acc, dv_acc)
-
-        @pl.when(leaf > 0)
-        def _():
+        setup = back_setup(low, q_ref, do_ref, o_ref, l_ref, here)
+        dq = back_span(setup, kn_ref[root, :], vn_ref[root, :], krt_ref[...], root_ref[i] if rooted else None, root, dk_acc, dv_acc)
+        if not rooted:
             acc = aligned(meta_ref[i, 2] + ROOT, BLOCK, BLOCK)
-            dq_ref[here, :] += back_span(low, heads, ks_ref[par, :], vs_ref[par, :], None, acc, dk_acc, dv_acc)
-
-        return carry
-
-    lax.fori_loop(0, do_ref.shape[0] // TILE, one, 0)
+            hide = jnp.where(leaf > 0, 0.0, MASKED).astype(F32)
+            dq = dq + back_span(setup, ks_ref[par, :], vs_ref[par, :], kst_ref[:, par], hide, acc, dk_acc, dv_acc)
+        dq_ref[:, here] = dq
+
+    @pl.when(meta_ref[0, 0] > 0)
+    def _():
+        for i in range(tiles):
+            one(i, False)
+
+    @pl.when(meta_ref[0, 0] == 0)
+    def _():
+        for i in range(tiles):
+            one(i, i < ROOT // TILE)
+
     dk_ref[root, :] = unrotate(dk_acc[root, :], cos_ref[root, :], sin_ref[root, :]).astype(BF16)
     for h in range(2 * BRANCHES):
         at, back = pl.ds(ROOT + h * TILE, TILE), aligned(slot_ref[h, 2] * TILE, TILE)
@@ -669,6 +772,10 @@
     dv_ref[...] = dv_acc[...].astype(BF16)
 
 
+def turned(loc):
+    return pl.BlockSpec((128, loc), lambda p: (p, 0))
+
+
 def back_far(meta, slots, q, do, o, logs, near, far, tab):
     loc, d = do.shape
     n = ROOT + TILE
@@ -677,9 +784,10 @@
         grid=(d // 128,),
         in_specs=[SMEM, SMEM, pair(loc), pair(loc), pair(loc), log_spec(loc), pair(n), pair(n), pair(SLOTS), pair(SLOTS)]
         + [fixed(one.shape) for one in tab],
-        out_specs=[pair(loc), pair(FAR), pair(FAR)],
-        out_shape=[shape(loc, d, F32), shape(FAR, d, BF16), shape(FAR, d, BF16)],
-        scratch_shapes=[bias_scratch(0)[0], pltpu.VMEM((FAR, 128), F32), pltpu.VMEM((FAR, 128), F32)],
+        out_specs=[turned(loc), pair(FAR), pair(FAR)],
+        out_shape=[shape(d, loc, F32), shape(FAR, d, BF16), shape(FAR, d, BF16)],
+        scratch_shapes=[bias_scratch(0)[0], pltpu.VMEM((128, ROOT), BF16), pltpu.VMEM((128, SLOTS), BF16),
+                        pltpu.VMEM((FAR, 128), F32), pltpu.VMEM((FAR, 128), F32)],
         compiler_params=params(),
         cost_estimate=cost(50),
         name="back_far",
@@ -687,38 +795,39 @@
 
 
 def back_near_kernel(meta_ref, q_ref, do_ref, o_ref, l_ref, kn_ref, vn_ref, k_ref, v_ref, cos_ref, sin_ref, part_ref,
-                     dq_ref, dk_ref, dv_ref, dke_ref, dve_ref, own_ref, ko_ref, vo_ref, dk_acc, dv_acc):
+                     dq_ref, dk_ref, dv_ref, dke_ref, dve_ref, own_ref, ko_ref, vo_ref, kt_ref, dk_acc, dv_acc):
     @pl.when(pl.program_id(0) == 0)
     def _():
         fill_bias(None, own_ref, 0)
 
     line_up(ko_ref, kn_ref, k_ref)
     line_up(vo_ref, vn_ref, v_ref)
+    kt_ref[...] = ko_ref[...].T
     low = low_half()
     loc = do_ref.shape[0]
     t = meta_ref[0, 5]
     for ref in (dk_acc, dv_acc):
         ref[...] = jnp.zeros_like(ref)
 
-    def one(i, carry):
+    def one(i, rooted):
         sub, leaf, par, own, here = tile_of(meta_ref, i)
+        dq = part_ref[:, here]
+        if not rooted:
+            setup = back_setup(low, q_ref, do_ref, o_ref, l_ref, here)
+            dq = dq + back_span(setup, ko_ref[own, :], vo_ref[own, :], kt_ref[:, own], own_ref[sub % 2], own, dk_acc, dv_acc)
         back = aligned(sub * TILE, TILE)
-
-        def put(dq):
-            dq_ref[here, :] = unrotate(dq * HEAD_DIM ** -0.5, cos_ref[back, :], sin_ref[back, :]).astype(BF16)
-
-        @pl.when(sub < ROOT // TILE)
-        def _():
-            put(part_ref[here, :])
-
-        @pl.when(sub >= ROOT // TILE)
-        def _():
-            heads = back_setup(low, q_ref, do_ref, o_ref, l_ref, here)
-            put(part_ref[here, :] + back_span(low, heads, ko_ref[own, :], vo_ref[own, :], own_ref[sub % 2], own, dk_acc, dv_acc))
-
-        return carry
-
-    lax.fori_loop(0, loc // TILE, one, 0)
+        dq_ref[here, :] = unrotate(dq.T * HEAD_DIM ** -0.5, cos_ref[back, :], sin_ref[back, :]).astype(BF16)
+
+    @pl.when(t > 0)
+    def _():
+        for i in range(loc // TILE):
+            one(i, False)
+
+    @pl.when(t == 0)
+    def _():
+        for i in range(loc // TILE):
+            one(i, i < ROOT // TILE)
+
     edge, mine = pl.ds(0, TILE), pl.ds(TILE, loc)
     before = aligned(jnp.maximum(t * loc - TILE, 0), TILE)
     here = aligned(t * loc, loc)
@@ -735,11 +844,11 @@
         after(len(deps), back_near_kernel),
         grid=(d // 128,),
         in_specs=[ANY] * len(deps) + [SMEM, pair(loc), pair(loc), pair(loc), log_spec(loc), pair(n), pair(n), pair(loc), pair(loc)]
-        + [fixed(one.shape) for one in tab] + [pair(loc)],
+        + [fixed(one.shape) for one in tab] + [turned(loc)],
         out_specs=[pair(loc)] * 3 + [pair(TILE)] * 2,
         out_shape=[shape(loc, d, BF16)] * 3 + [shape(TILE, d, BF16)] * 2,
-        scratch_shapes=[bias_scratch(0)[1], line_scratch(loc, BF16), line_scratch(loc, BF16), line_scratch(loc, F32),
-                        line_scratch(loc, F32)],
+        scratch_shapes=[bias_scratch(0)[1], line_scratch(loc, BF16), line_scratch(loc, BF16),
+                        pltpu.VMEM((128, loc + 2 * TILE), BF16), line_scratch(loc, F32), line_scratch(loc, F32)],
         compiler_params=params(),
         cost_estimate=cost(25),
         name="back_near",
@@ -821,59 +930,63 @@
     )(*deps, x, x_near, dq, dk, dv, dke, dve, w, w, w)
 
 
-def weights_kernel(at_ref, s1_ref, s2_ref, s3_ref, a_ref, an_ref, as_ref, dhb_ref, dq_ref, dk_ref, dv_ref, dkf_ref, dvf_ref,
-                   dke_ref, dve_ref, o_ref, kept_ref, away_ref, kept_gain, away_gain):
-    step = pl.program_id(0)
-    core = at_ref[1] % 2
-    chips, rows, d = kept_ref.shape
-
-    def put(total, kept, away):
-        split_cores(core, total.astype(BF16).reshape(chips, 2, rows, total.shape[1]), kept, away, (slice(None),) * 3)
-
-    def keyed(own, far, edge):
-        root, tail = pl.ds(0, ROOT), pl.ds(ROOT, TILE)
-        return (dot(a_ref[...], own[...], ROWS) + dot(an_ref[root, :], far[root, :], ROWS)
-                + dot(as_ref[...], far[pl.ds(ROOT, SLOTS), :], ROWS) + dot(an_ref[tail, :], edge[...], ROWS))
+def spill(core, got, kept_ref, away_ref):
+    chips, rows, _ = kept_ref.shape
+    split_cores(core, got.astype(BF16).reshape(chips, 2, rows, got.shape[1]), kept_ref, away_ref, (slice(None),) * 3)
+
+
+def keyed(a_ref, an_ref, as_ref, own, far, edge):
+    root, tail = pl.ds(0, ROOT), pl.ds(ROOT, TILE)
+    return (dot(a_ref[...], own[...], ROWS) + dot(an_ref[root, :], far[root, :], ROWS)
+            + dot(as_ref[...], far[pl.ds(ROOT, SLOTS), :], ROWS) + dot(an_ref[tail, :], edge[...], ROWS))
+
+
+def first_kernel(at_ref, s1_ref, s2_ref, s3_ref, a_ref, dq_ref, dhb_ref, o_ref, kept_ref, away_ref, kept_gain, away_gain):
+    step, core = pl.program_id(0), at_ref[1] % 2
 
     @pl.when(step == 0)
     def _():
-        line = lax.broadcasted_iota(jnp.int32, (GAIN_LANES, d), 0)
+        line = lax.broadcasted_iota(jnp.int32, (GAIN_LANES, a_ref.shape[1]), 0)
         table = jnp.where(line == 0, s1_ref[0:1, :] + s2_ref[0:1, :], jnp.where(line == 1, s3_ref[0:1, :], 0.0))
-        put(table.T, kept_gain, away_gain)
-        put(dot(a_ref[...], dq_ref[...], ROWS), kept_ref, away_ref)
+        spill(core, table.T, kept_gain, away_gain)
+        spill(core, dot(a_ref[...], dq_ref[...], ROWS), kept_ref, away_ref)
 
     @pl.when(step == 1)
     def _():
-        put(keyed(dk_ref, dkf_ref, dke_ref), kept_ref, away_ref)
-
-    @pl.when(step == 2)
-    def _():
-        put(keyed(dv_ref, dvf_ref, dve_ref), kept_ref, away_ref)
-
-    @pl.when(step == 3)
-    def _():
-        put(dot(dhb_ref[...], o_ref[...], ROWS), kept_ref, away_ref)
-
-
-def weight_sums(deps, at, sums, a_own, a_near, a_slot, dhb, dq, dk, dv, dkf, dvf, dke, dve, o, dp):
-    loc, d = a_own.shape
+        spill(core, dot(dhb_ref[...], o_ref[...], ROWS), kept_ref, away_ref)
+
+
+def second_kernel(at_ref, a_ref, an_ref, as_ref, dk_ref, dv_ref, dkf_ref, dvf_ref, dke_ref, dve_ref, kept_ref, away_ref):
+    step, core = pl.program_id(0), at_ref[1] % 2
+
+    @pl.when(step == 0)
+    def _():
+        spill(core, keyed(a_ref, an_ref, as_ref, dk_ref, dkf_ref, dke_ref), kept_ref, away_ref)
+
+    @pl.when(step == 1)
+    def _():
+        spill(core, keyed(a_ref, an_ref, as_ref, dv_ref, dvf_ref, dve_ref), kept_ref, away_ref)
+
+
+def weight_sums(kernel, deps, at, arrays, dp, gains):
+    d = arrays[-1].shape[1]
     chips, rows = dp // 2, d // dp
-    arrays = (*sums, a_own, a_near, a_slot, dhb, dq, dk, dv, dkf, dvf, dke, dve, o)
-    out = pl.BlockSpec((chips, rows, d), lambda i: (0, 0, i))
-    gain = pl.BlockSpec((chips, rows, GAIN_LANES), lambda i: (0, 0, 0))
-    return pl.pallas_call(
-        after(len(deps), weights_kernel),
-        grid=(4,),
+    widths = [(2 * d, pl.BlockSpec((chips, rows, d), lambda i: (0, 0, i)))] * 2
+    if gains:
+        widths += [(GAIN_LANES, pl.BlockSpec((chips, rows, GAIN_LANES), lambda i: (0, 0, 0)))] * 2
+    return pl.pallas_call(
+        after(len(deps), kernel),
+        grid=(2,),
         in_specs=[ANY] * len(deps) + [SMEM] + [fixed(one.shape) for one in arrays],
-        out_specs=[out, out, gain, gain],
-        out_shape=[jax.ShapeDtypeStruct((chips, rows, 4 * d), BF16)] * 2 + [jax.ShapeDtypeStruct((chips, rows, GAIN_LANES), BF16)] * 2,
-        compiler_params=params(),
-        cost_estimate=cost(14),
+        out_specs=[spec for _, spec in widths],
+        out_shape=[jax.ShapeDtypeStruct((chips, rows, wide), BF16) for wide, _ in widths],
+        compiler_params=params(),
+        cost_estimate=cost(8),
         name="weight_sums",
     )(*deps, at, *arrays)
 
 
-def finish_kernel(meta_ref, da_ref, dh_ref, x_ref, gain_ref, early_ref, late_ref, low_ref, edge_ref, out_ref):
+def finish_kernel(meta_ref, da_ref, dh_ref, x_ref, gain_ref, early2_ref, late2_ref, early_ref, late_ref, edge_ref, out_ref):
     t = meta_ref[0, 5]
     tiles = x_ref.shape[0] // TILE
 
@@ -886,13 +999,13 @@
         gain = gain_ref[0:1, :]
         da = da_ref[here, :]
         none = jnp.zeros((TILE, x.shape[1]), F32)
-        late = late_ref[aligned(jnp.maximum(given, 0), TILE), :].astype(F32)
-        early = early_ref[aligned(jnp.minimum(i * TILE, EARLY - TILE), TILE), :].astype(F32)
+        slot = jnp.maximum(given, 0)
+        late = late_ref[aligned(slot, TILE), :].astype(F32) + late2_ref[aligned(slot, TILE), :].astype(F32)
+        front = aligned(jnp.minimum(i * TILE, EARLY - TILE), TILE)
+        early = early_ref[front, :].astype(F32) + early2_ref[front, :].astype(F32)
         da = da + jnp.where(given >= 0, late, none)
         da = da + jnp.where((t == 0) & (i < EARLY // TILE), early, none)
-        last = i == tiles - 1
-        da = da + jnp.where(last & (meta_ref[0, 6] > 0), low_ref[...].astype(F32), none)
-        da = da + jnp.where(last & (t % 2 == 0), edge_ref[...].astype(F32), none)
+        da = da + jnp.where((i == tiles - 1) & (t % 2 == 0), edge_ref[...].astype(F32), none)
         scaled = da * gain
         out_ref[here, :] = dh_ref[here, :] + scale * (scaled - x_hat * jnp.mean(scaled * x_hat, axis=-1, keepdims=True))
         return carry
@@ -900,19 +1013,19 @@
     lax.fori_loop(0, tiles, one, 0)
 
 
-def finish(meta, da, dh, x, gains, early, late, low, edge):
+def finish(deps, meta, da, dh, x, gains, early2, late2, early, late, edge):
     loc, d = x.shape
-    arrays = (da, dh, x, gains, early, late, low, edge)
-    return pl.pallas_call(
-        finish_kernel,
+    arrays = (da, dh, x, gains, early2, late2, early, late, edge)
+    return pl.pallas_call(
+        after(len(deps), finish_kernel),
         grid=(1,),
-        in_specs=[SMEM] + [fixed(one.shape) for one in arrays],
+        in_specs=[ANY] * len(deps) + [SMEM] + [fixed(one.shape) for one in arrays],
         out_specs=fixed((loc, d)),
         out_shape=shape(loc, d, F32),
         compiler_params=params(),
         cost_estimate=cost(6),
         name="finish",
-    )(meta, *arrays)
+    )(*deps, meta, *arrays)
 
 
 def tables(pos):
@@ -956,10 +1069,8 @@
     )(*deps, *parts)
 
 
-def meet_chips(deps, part, chip):
-    blocks = [lax.dynamic_index_in_dim(part, chip ^ m, 0, keepdims=False) for m in range(part.shape[0])]
-    moved = [swap(block, "dp", 2 * m) for m, block in enumerate(blocks) if m]
-    return total(deps, blocks[0], *moved)
+def meet_chips(deps, blocks):
+    return total(deps, blocks[0], *(swap(block, "dp", 2 * m) for m, block in enumerate(blocks) if m))
 
 
 def per_device(tokens, gain_attn, w_query, w_key, w_value, w_out, gain_ffn, w_gate, w_up, w_down,
@@ -979,14 +1090,16 @@
     gain_cols = lax.dynamic_update_slice(jnp.zeros((rows, GAIN_LANES), BF16), gain_cols, (t_at * own_gain, 0))
     pack = jnp.concatenate([w_query, w_key, w_value, w_out.T, gain_cols], axis=1)
     others = [pack] + [swap(pack, "tensor", m) for m in range(1, t_size)]
-    lined = line((a1,), others)
+    meta, slots = plan(at[:1], segment_ids, parent_ids, tiles)
+    tab = tables(positions)
+    lined = line((a1, *tab), others)
     a2 = send(a1, *up[1:])
     pieces = [None] * d_size
     for m in range(0, d_size, 2):
         pieces[m] = swap(lined, "dp", m) if m else lined
     ready = (a2, *(pieces[m] for m in range(2, d_size, 2)))
-    rest = join(ready, w_gate, w_up, w_down.T)
-    b1 = send(join(ready, tokens[ROOT:]), *up)
+    rest, front = begin(ready, tokens, w_gate, w_up, w_down.T)
+    b1 = send(front, *up)
     a3 = send(a2, *up[2:])
     for m in range(0, d_size, 2):
         pieces[m + 1] = swap(pieces[m], "dp", 1)
@@ -996,57 +1109,56 @@
             whole = lax.dynamic_update_slice_in_dim(whole, pieces[m], (d_at ^ m) * rows, 0)
         pieces = [whole]
     rest = lax.all_gather(rest, ("dp", "tensor"), axis=0, tiled=False).reshape(d_size, t_size, rows, 3 * hid)
-    meta, slots = plan(at[:1], segment_ids, parent_ids, tiles)
-    tab = tables(positions)
     w, gains, a_own, q, k_own, v_own = project_own((), at, tokens, tab, pieces)
     front = join((a3, k_own), tokens[ROOT:])
     b2 = send(front, (0, 2), (1, 3))
     b3 = send(front, (0, 3))
     x_near, a_near, k_near, v_near = project_near(at, tokens, a1, a2, a3, b1, gains, w, tab)
     near, own = (k_near, v_near), (k_own, v_own)
-    acc, top, weight_sum = attend_near(meta, q, near, own)
+    acc, stat = attend_near(meta, q, near, own)
     x_slot, a_slot, k_slot, v_slot = project_far(meta, slots, tokens, (a1, a2, a3, b1, b2, b3), gains, w, tab)
     far = (k_slot, v_slot)
-    o, logs = attend_far(meta, q, far, acc, top, weight_sum)
+    o, logs = attend_far(meta, q, far, acc, stat)
 
     mixed, do, dhb, dh, ffn_sum, kept, away = feed_forward(at, tokens, o, cotangent, gains, w, rest)
-    chip = d_at // 2
     away = swap(away, "dp", 1)
     dq_part, dk_far, dv_far = back_far(meta, slots, q, do, o, logs, near, far, tab)
-    rest_part = (kept.astype(F32) + away.astype(F32)).astype(BF16)
-    early, late, far_sum = spread((rest_part,), dk_far, dv_far, x_near, x_slot, w)
-    rest_sum = meet_chips((), rest_part, chip)
-    late_in = send(late, (3, 2))
+    rest_blocks = meet_rest(at, kept, away)
+    early, late, far_sum = spread((rest_blocks[0],), dk_far, dv_far, x_near, x_slot, w)
+    keep, away = fold(at, rest_blocks[0], *(swap(block, "dp", 2 * m) for m, block in enumerate(rest_blocks) if m))
     early_in = send(early, (3, 2), (1, 0))
-    dq, dk, dv, dke, dve = back_near((early, late), meta, q, do, o, logs, near, own, tab, dq_part)
-    late = late + late_in
-    early = early + early_in
+    dq, dk, dv, dke, dve = back_near((early,), meta, q, do, o, logs, near, own, tab, dq_part)
+    late_in = send(join((dq,), late), (3, 2))
+    early = total((dq,), early, early_in)
+    early_in = send(early, (2, 0))
+    da, edge, own_sum = own_back((early,), tokens, x_near, dq, dk, dv, dke, dve, w)
+    kept_a, away_a, kept_gain, away_gain = weight_sums(
+        first_kernel, (keep,), at, (far_sum, own_sum, ffn_sum, a_own, dq, dhb, o), d_size, True)
+    away_a = swap(jnp.concatenate([away_a, away_gain], axis=2), "dp", 1)
+    late = total((dq,), late, late_in)
     late_in = send(late, (2, 1))
-    early_in = send(early, (2, 0))
-    da, edge, own_sum = own_back((rest_sum, late, early), tokens, x_near, dq, dk, dv, dke, dve, w)
-    kept, away, kept_gain, away_gain = weight_sums(
-        (late_in, early), at, (far_sum, own_sum, ffn_sum), a_own, a_near, a_slot, dhb, dq, dk, dv, dk_far, dv_far, dke, dve, o, d_size)
-    edge = send(edge, (1, 0), (3, 2))
-    away = swap(jnp.concatenate([away, away_gain], axis=2), "dp", 1)
-    part = meet((), kept, kept_gain, away)
-    late = late + late_in
-    early = early + early_in
-    low_edge = send(late[:TILE], (1, 0))
-    grad_tokens = finish(meta, da, dh, tokens, gains, early, late, low_edge, edge)
-    rest_sum = join((part,), rest_sum.reshape(t_size * rows, 3 * hid)).reshape(rest_sum.shape)
-    rest_owned = lax.dynamic_index_in_dim(rest_sum, t_at, 0, keepdims=False).astype(F32)
-    for m in range(1, t_size):
-        rest_owned = rest_owned + swap(lax.dynamic_index_in_dim(rest_sum, t_at ^ m, 0, keepdims=False), "tensor", m).astype(F32)
-    summed = meet_chips((early_in,), part, chip)
+    kept_b, away_b = weight_sums(
+        second_kernel, (keep, late, early_in), at, (a_own, a_near, a_slot, dk, dv, dk_far, dv_far, dke, dve), d_size, False)
+    away = swap(away, "tensor", 2)
+    away_b = swap(away_b, "dp", 1)
+    kept_a = jnp.concatenate([kept_a, kept_gain], axis=2)
+    blocks = meet((), at, (kept_a, kept_b), (away_a, away_b))
+    summed = meet_chips((late_in,), blocks)
+    mine, away = middle((summed,), keep, away)
+    rest_owned = mine.astype(F32) + swap(away, "tensor", 1).astype(F32)
+    crossing = (slots[2, 0] == 0) & (t_at == 1)
+    edge = send(edge + jnp.where(crossing, late[:TILE] + late_in[:TILE], jnp.zeros_like(edge)), (1, 0), (3, 2))
+    grad_tokens = finish((summed,), meta, da, dh, tokens, gains, early, late, early_in, late_in, edge)
+    starts = (0, d, 2 * d + GAIN_LANES, 3 * d + GAIN_LANES)
 
     def share(m):
-        return jnp.concatenate([summed[:, j * d + m * n:j * d + (m + 1) * n] for j in range(4)] + [summed[:, 4 * d:]], axis=1)
+        return jnp.concatenate([summed[:, at + m * n:at + (m + 1) * n] for at in starts] + [summed[:, 2 * d:2 * d + GAIN_LANES]], axis=1)
 
     owned = share(0).astype(F32)
     for m in range(1, t_size):
         owned = owned + swap(share(m), "tensor", m).astype(F32)
     gain_sums = lax.dynamic_slice(owned, (t_at * own_gain, 4 * n), (own_gain, GAIN_LANES))
-    return (mixed, grad_tokens, gain_sums[:, 0], owned[:, :n], owned[:, n:2 * n], owned[:, 2 * n:3 * n], owned[:, 3 * n:4 * n].T,
+    return (mixed, grad_tokens, gain_sums[:, 0], owned[:, :n], owned[:, 2 * n:3 * n], owned[:, 3 * n:4 * n], owned[:, n:2 * n].T,
             gain_sums[:, 1], rest_owned[:, :hid], rest_owned[:, hid:2 * hid], rest_owned[:, 2 * hid:].T)
 
 

time: 582 us -> 481 us (0.83)
  starting transfers between devices: 125 us -> 78.4 us
  waiting for transfers between devices: 121 us -> 104 us
  Pallas kernels: 254 us -> 239 us
  other arithmetic: 29 us -> 15.2 us
  local copies, waits for them, and re-layouts: 28.5 us -> 21.8 us
    ppermute x24, starting transfers between devices: 98.2 us -> 45 us  [swap(): lax.ppermute(x, axis, [(i, i ^ mask) for i in range(lax.axis_size(axis))])]
    ppermute x24, waiting for transfers between devices: 79.3 us -> 61.5 us  [swap(): lax.ppermute(x, axis, [(i, i ^ mask) for i in range(lax.axis_size(axis))])]
    pallas_call x1, Pallas kernels: 44.1 us -> 27.3 us  [back_far(): pl.pallas_call(back_far_kernel, grid=(d // 128,), in_specs=[SMEM, SMEM, p...]
    pallas_call x3 -> x8, Pallas kernels: 30.4 us -> 47.2 us  [the longest x2 20.1 us: weight_sums(): pl.pallas_call(after(len(deps), kernel), grid=(2,), in_specs=[ANY] * len(...]
    pallas_call x1, Pallas kernels: 34.2 us -> 22.3 us  [attend_near(): pl.pallas_call(attend_near_kernel, grid=(d // 128,), in_specs=[SMEM, pair...]
    pallas_call x1, Pallas kernels: 23.6 us -> 14.4 us  [back_near(): pl.pallas_call(after(len(deps), back_near_kernel), grid=(d // 128,), in_s...]
    squeeze x3 -> x0, local copies, waits for them, and re-layouts: 7.99 us -> none  [the longest x2 6.07 us: meet_chips(): lax.dynamic_index_in_dim(part, chip ^ m, 0, keepdims=False)]
    convert_element_type x1 -> x0, other arithmetic: 7.42 us -> none  [per_device(): rest_part = (kept.astype(F32) + away.astype(F32)).astype(BF16)]
  transfers between devices with their start and end apart: 37 -> 36, of which waited for: 15 -> 11; matrix products, arithmetic and copies ran while one was open for 5% -> 5% of each run, Pallas kernels for 31% -> 37%
where the time goes in v3:
time: 481 us; the launch traced here: 474 us
  Pallas kernels  239 us (50%)
  waiting for transfers between devices  104 us (22%)
  starting transfers between devices  78.4 us (16%)
  local copies, waits for them, and re-layouts  21.8 us (5%)
  between operations  15.7 us (3%)
  other arithmetic  15.2 us (3%)
    ppermute x24, waiting for transfers between devices, swap(): lax.ppermute(x, axis, [(i, i ^ mask) for i in range(lax.axis_size(axis))])  61.5 us
    pallas_call x1, Pallas kernels, feed_forward(): pl.pallas_call(ffn_kernel, grid=(steps + parts,), in_specs=[SMEM, tile, t...  45.7 us
    ppermute x24, starting transfers between devices, swap(): lax.ppermute(x, axis, [(i, i ^ mask) for i in range(lax.axis_size(axis))])  45 us
    ppermute x11, starting transfers between devices, send(): return lax.ppermute(x, 'tensor', list(pairs))  33.4 us
    pallas_call x1, Pallas kernels, back_far(): pl.pallas_call(back_far_kernel, grid=(d // 128,), in_specs=[SMEM, SMEM, p...  27.3 us
    ppermute x11, waiting for transfers between devices, send(): return lax.ppermute(x, 'tensor', list(pairs))  27.2 us
    pallas_call x1, Pallas kernels, attend_near(): pl.pallas_call(attend_near_kernel, grid=(d // 128,), in_specs=[SMEM, pair...  22.3 us
    pallas_call x2, Pallas kernels, weight_sums(): pl.pallas_call(after(len(deps), kernel), grid=(2,), in_specs=[ANY] * len(...  20.1 us
  transfers between devices with their start and end apart: 36, of which 11 were waited for; matrix products, arithmetic and copies ran while one was open for 5% of the time, Pallas kernels for 37%

profile of v3, /device:TPU:0, one launch (start us, length us, event | category | flops | bytes accessed | tf_op | source)
XLA Modules:
  0.0 474.0 jit_solution(4918650643089806047)
XLA Ops:
  7.3 1.2 slice.96
  8.5 5.0 %collective-permute-start = (bf16[512,768]{1,0:T(8,128)(2,1)S(1)}, bf16[512,768]{1,0:T(8,128)(2,1)S(1)}, u32[]{:S(2)}, u32[]{:S(2)}) collective-permute-start(bf16[512,768]{1,0:T(8,128)(2,1)S(1)} %slice.96), channel_id=1, source_target_pairs={{0,1},{1,2},{2,3},{4,5},{5,6},{6,7},{8,9},{9,10},{10,11},{12,13},{... | collective-permute-start | bytes 2359304 | tf_op jit(solution)/shard_map/ppermute | solution.py:1044
  14.4 1.6 collective-permute-start.1
  16.0 1.1 collective-permute-start.2
  17.1 1.8 collective-permute-start.3
  19.0 12.4 %collective-permute-done.refs_0_.a1_ref.r1_ref = bf16[512,768]{1,0:T(8,128)(2,1)S(1)} collective-permute-done((bf16[512,768]{1,0:T(8,128)(2,1)S(1)}, bf16[512,768]{1,0:T(8,128)(2,1)S(1)}, u32[]{:S(2)}, u32[]{:S(2)}) %collective-permute-start) | collective-permute-done | bytes 786464 | tf_op jit(solution)/shard_map/ppermute | solution.py:1044
  32.1 8.3 %fusion = (f32[3584,128]{1,0:T(8,128)}, f32[3584,128]{1,0:T(8,128)}) fusion(f32[128]{0:T(128)S(1)} %get-tuple-element.199, f32[128]{0:T(128)S(1)} %get-tuple-element.200, f32[3584]{0:T(1024)S(1)} %convert_element_type.39), kind=kLoop, calls=%fused_computation.2 | loop fusion | flops 917504 | bytes 3685376 | tf_op jit(solution)/shard_map/mul | solution.py:1036
  42.0 2.2 line.1.refs_4_
  44.2 1.5 collective-permute-start.5
  45.7 1.5 collective-permute-start.7
  47.7 13.5 %collective-permute-done.5.refs_6_.refs_1_ = bf16[96,3200]{1,0:T(8,128)(2,1)S(1)} collective-permute-done((bf16[96,3200]{1,0:T(8,128)(2,1)}, bf16[96,3200]{1,0:T(8,128)(2,1)S(1)}, u32[]{:S(2)}, u32[]{:S(2)}) %collective-permute-start.5) | collective-permute-done | bytes 614432 | tf_op jit(solution)/shard_map/ppermute | solution.py:1040
  61.2 12.3 %collective-permute-done.7.refs_8_.refs_2_ = bf16[96,3200]{1,0:T(8,128)(2,1)S(1)} collective-permute-done((bf16[96,3200]{1,0:T(8,128)(2,1)}, bf16[96,3200]{1,0:T(8,128)(2,1)S(1)}, u32[]{:S(2)}, u32[]{:S(2)}) %collective-permute-start.7) | collective-permute-done | bytes 614432 | tf_op jit(solution)/shard_map/ppermute | solution.py:1040
  75.3 2.4 begin.1
  79.5 1.1 collective-permute-done.4.refs_5_
  80.6 7.2 %collective-permute-start.13 = (bf16[384,768]{1,0:T(8,128)(2,1)}, bf16[384,768]{1,0:T(8,128)(2,1)S(1)}, u32[]{:S(2)}, u32[]{:S(2)}) collective-permute-start(bf16[384,768]{1,0:T(8,128)(2,1)} %get-tuple-element.75), channel_id=1, source_target_pairs={{0,1},{1,2},{2,3},{4,5},{5,6},{6,7},{8,9},{9,10},{10,11},{12,13},{... | collective-permute-start | bytes 1769480 | tf_op jit(solution)/shard_map/ppermute | solution.py:1044
  88.4 1.9 slice.97.refs_2_
  91.4 11.2 %project_own.1 = (bf16[768,3072]{1,0:T(8,128)(2,1)}, f32[8,768]{1,0:T(8,128)}, bf16[896,768]{1,0:T(8,128)(2,1)}, bf16[896,768]{1,0:T(8,128)(2,1)}, bf16[896,768]{1,0:T(8,128)(2,1)}, /*index=5*/bf16[896,768]{1,0:T(8,128)(2,1)}) custom-call(s32[2]{0:T(128)} %pad_add_fusion.refs_0_.at_ref.refs_1_.refs_3_, bf16[896,768]{1,0:T(8,128)(2,1)} %refs_4_.3, ...), custom_call_target="tpu_custom_call" | custom-call | flops 300000000 | tf_op jit(solution)/shard_map/project_own/pallas_call | solution.py:339
  103.5 2.0 join.2
  105.5 10.1 %collective-permute-start.14 = (bf16[384,768]{1,0:T(8,128)(2,1)}, bf16[384,768]{1,0:T(8,128)(2,1)S(1)}, u32[]{:S(2)}, u32[]{:S(2)}) collective-permute-start(bf16[384,768]{1,0:T(8,128)(2,1)} %join.2), channel_id=1, source_target_pairs={{0,2},{1,3},{4,6},{5,7},{8,10},{9,11},{12,14},{13,15},{16,18},{17,... | collective-permute-start | bytes 1769480 | tf_op jit(solution)/shard_map/ppermute | solution.py:1044
  115.6 3.2 collective-permute-start.15
  118.8 2.2 plan.1
  121.8 7.4 %project_near.1 = (bf16[640,768]{1,0:T(8,128)(2,1)}, bf16[640,768]{1,0:T(8,128)(2,1)}, bf16[640,768]{1,0:T(8,128)(2,1)}, bf16[640,768]{1,0:T(8,128)(2,1)}) custom-call(s32[2]{0:T(128)} %pad_add_fusion.refs_0_.at_ref.refs_1_.refs_3_, bf16[896,768]{1,0:T(8,128)(2,1)} %refs_4_.3, bf16[512,768]{1,0:T(8,128)(2,1)} %copy-done.3, bf16[512,768]{1,0:T(8,128)(2,1)} %copy-done.1, ...), custom_call_target="tpu_custom_call" | custom-call | flops 150000000 | tf_op jit(solution)/shard_map/project_near/pallas_call | solution.py:385
  129.3 22.3 %attend_near.1 = (f32[768,896]{1,0:T(8,128)}, f32[6,8,896]{2,1,0:T(8,128)}) custom-call(s32[8,8]{1,0:T(8,128)} %get-tuple-element.72.meta_ref.refs_1_, bf16[896,768]{1,0:T(8,128)(2,1)} %get-tuple-element.73.q_ref.refs_2_, bf16[640,768]{1,0:T(8,128)(2,1)} %get-tuple-element.81.kn_ref.refs_6_, bf16[640,768]{1,0:T(8,128)(2,1)} %get-tuple-element.82.vn_ref.refs_7_, ...), custom_call_target="tpu_custom_call" | custom-call | flops 600000000 | tf_op jit(solution)/shard_map/attend_near/pallas_call | solution.py:555
  152.6 10.4 %project_far.1 = (bf16[1024,768]{1,0:T(8,128)(2,1)}, bf16[1024,768]{1,0:T(8,128)(2,1)}, bf16[1024,768]{1,0:T(8,128)(2,1)}, bf16[1024,768]{1,0:T(8,128)(2,1)}) custom-call(s32[8,8]{1,0:T(8,128)} %get-tuple-element.72.meta_ref.refs_1_, s32[8,8]{1,0:T(8,128)} %get-tuple-element.74.slot_ref, bf16[896,768]{1,0:T(8,128)(2,1)} %refs_4_.3, ...), custom_call_target="tpu_custom_call" | custom-call | flops 210000000 | tf_op jit(solution)/shard_map/project_far/pallas_call | solution.py:436
  163.0 15.8 %attend_far.1 = (bf16[896,768]{1,0:T(8,128)(2,1)}, f32[6,8,896]{2,1,0:T(8,128)}) custom-call(s32[8,8]{1,0:T(8,128)} %get-tuple-element.72.meta_ref.refs_1_, bf16[896,768]{1,0:T(8,128)(2,1)} %get-tuple-element.73.q_ref.refs_2_, bf16[1024,768]{1,0:T(8,128)(2,1)} %get-tuple-element.79.ks_ref, bf16[1024,768]{1,0:T(8,128)(2,1)} %get-tuple-element.80.vs_ref, ...), custom_call_target="tpu_custom_call" | custom-call | flops 270000000 | tf_op jit(solution)/shard_map/attend_far/pallas_call | solution.py:596
  178.8 15.1 %all-gather.3.cloned.1.call-done = bf16[3072,1536]{1,0:T(8,128)(2,1)} async-done(((bf16[96,1536]{1,0:T(8,128)(2,1)}), bf16[3072,1536]{1,0:T(8,128)(2,1)}) %all-gather.3.cloned.1.call-update) | async-done | bytes 9437200 | tf_op jit(solution)/shard_map/all_gather | solution.py:1111
  193.9 45.7 %feed_forward.1 = (bf16[896,768]{1,0:T(8,128)(2,1)}, bf16[896,768]{1,0:T(8,128)(2,1)}, bf16[896,768]{1,0:T(8,128)(2,1)}, f32[896,768]{1,0:T(8,128)}, f32[8,768]{...) custom-call(s32[2]{0:T(128)} %pad_add_fusion.refs_0_.at_ref.refs_1_.refs_3_, ...), custom_call_target="tpu_custom_call" | custom-call | flops 1200000000 | tf_op jit(solution)/shard_map/feed_forward/pallas_call | solution.py:696
  240.0 27.3 %back_far.1 = (f32[768,896]{1,0:T(8,128)}, bf16[1536,768]{1,0:T(8,128)(2,1)}, bf16[1536,768]{1,0:T(8,128)(2,1)}) custom-call(s32[8,8]{1,0:T(8,128)} %get-tuple-element.72.meta_ref.refs_1_, s32[8,8]{1,0:T(8,128)} %get-tuple-element.74.slot_ref, bf16[896,768]{1,0:T(8,128)(2,1)} %get-tuple-element.73.q_ref.refs_2_, ...), custom_call_target="tpu_custom_call" | custom-call | flops 1500000000 | tf_op jit(solution)/shard_map/back_far/pallas_call | solution.py:782
  267.3 6.4 %meet_rest.1 = (bf16[4,96,1536]{2,1,0:T(8,128)(2,1)}, bf16[4,96,1536]{2,1,0:T(8,128)(2,1)}, bf16[4,96,1536]{2,1,0:T(8,128)(2,1)}, bf16[4,96,1536]{2,1,0:T(8,128)(2,1)}) custom-call(s32[2]{0:T(128)} %pad_add_fusion.refs_0_.at_ref.refs_1_.refs_3_, bf16[4,4,96,1536]{3,2,1,0:T(8,128)(2,1)} %get-tuple-element.89.kept_ref, ...), custom_call_target="tpu_custom_call" | custom-call | flops 150000000 | tf_op jit(solution)/shard_map/meet_rest/pallas_call | solution.py:219
  273.7 10.2 %spread.1 = (bf16[768,768]{1,0:T(8,128)(2,1)}, bf16[768,768]{1,0:T(8,128)(2,1)}, f32[8,768]{1,0:T(8,128)}) custom-call(bf16[4,96,1536]{2,1,0:T(8,128)(2,1)} %get-tuple-element.91.refs_0_, bf16[1536,768]{1,0:T(8,128)(2,1)} %get-tuple-element.94.refs_1_.refs_9_, bf16[1536,768]{1,0:T(8,128)(2,1)} %get-tuple-element.95.refs_2_.refs_10_, ...), custom_call_target="tpu_custom_call" | custom-call | flops 180000000 | tf_op jit(solution)/shard_map/spread/pallas_call | solution.py:883
  283.8 1.3 collective-permute-start.22
  285.1 1.5 collective-permute-start.19
  287.3 1.4 collective-permute-start.21
  288.7 14.4 %back_near.1 = (bf16[896,768]{1,0:T(8,128)(2,1)}, bf16[896,768]{1,0:T(8,128)(2,1)}, bf16[896,768]{1,0:T(8,128)(2,1)}, bf16[128,768]{1,0:T(8,128)(2,1)}, bf16[128,768]{1,0:T(8,128)(2,1)}) custom-call(bf16[768,768]{1,0:T(8,128)(2,1)} %get-tuple-element.98.refs_0_.refs_1_, s32[8,8]{1,0:T(8,128)} %get-tuple-element.72.meta_ref.refs_1_, ...), custom_call_target="tpu_custom_call" | custom-call | flops 750000000 | tf_op jit(solution)/shard_map/back_near/pallas_call | solution.py:843
  303.1 2.4 join.3
  305.4 1.7 collective-permute-start.17
  307.1 11.7 %collective-permute-done.22.refs_2_ = bf16[768,768]{1,0:T(8,128)(2,1)S(1)} collective-permute-done((bf16[768,768]{1,0:T(8,128)(2,1)}, bf16[768,768]{1,0:T(8,128)(2,1)S(1)}, u32[]{:S(2)}, u32[]{:S(2)}) %collective-permute-start.22) | collective-permute-done | bytes 1179680 | tf_op jit(solution)/shard_map/ppermute | solution.py:1044
  319.8 3.0 total.4.refs_0_.refs_6_
  322.8 1.3 collective-permute-start.23
  324.1 15.9 %collective-permute-done.20.refs_2_ = bf16[4,96,1536]{2,1,0:T(8,128)(2,1)S(1)} collective-permute-done((bf16[4,96,1536]{2,1,0:T(8,128)(2,1)}, bf16[4,96,1536]{2,1,0:T(8,128)(2,1)S(1)}, u32[]{:S(2)}, u32[]{:S(2)}) %collective-permute-start.20) | collective-permute-done | bytes 1179680 | tf_op jit(solution)/shard_map/ppermute | solution.py:1040
  340.0 1.0 copy-done.12
  341.1 3.9 fold.1
  344.9 9.7 %own_back.1 = (f32[896,768]{1,0:T(8,128)}, bf16[128,768]{1,0:T(8,128)(2,1)}, f32[8,768]{1,0:T(8,128)}) custom-call(bf16[768,768]{1,0:T(8,128)(2,1)} %total.4.refs_0_.refs_6_, bf16[896,768]{1,0:T(8,128)(2,1)} %refs_4_.3, bf16[640,768]{1,0:T(8,128)(2,1)} %get-tuple-element.96.refs_3_.refs_2_, bf16[896,768]{1,0:T(8,128)(2,1)} %get-tuple-element.100.refs_0_.refs_3_.refs_6_, ...), custom_call_target="tpu_custom_call" | custom-call | flops 180000000 | tf_op jit(solution)/shard_map/own_back/pallas_call | solution.py:920
  354.6 7.1 %weight_sums.2 = (bf16[4,96,1536]{2,1,0:T(8,128)(2,1)}, bf16[4,96,1536]{2,1,0:T(8,128)(2,1)}, bf16[4,96,128]{2,1,0:T(8,128)(2,1)}, bf16[4,96,128]{2,1,0:T(8,128)(2,1)}) custom-call(bf16[2,96,1536]{2,1,0:T(8,128)(2,1)} %get-tuple-element.105.refs_0_.refs_1_, s32[2]{0:T(128)} %pad_add_fusion.refs_0_.at_ref.refs_1_.refs_3_, ...), custom_call_target="tpu_custom_call" | custom-call | flops 240000000 | tf_op jit(solution)/shard_map/weight_sums/pallas_call | solution.py:977
  361.7 2.5 pad_maximum_fusion.1
  364.2 2.9 total.3.refs_1_.refs_7_
  368.1 13.0 %weight_sums.3 = (bf16[4,96,1536]{2,1,0:T(8,128)(2,1)}, bf16[4,96,1536]{2,1,0:T(8,128)(2,1)}) custom-call(bf16[2,96,1536]{2,1,0:T(8,128)(2,1)} %get-tuple-element.105.refs_0_.refs_1_, bf16[768,768]{1,0:T(8,128)(2,1)} %total.3.refs_1_.refs_7_, bf16[768,768]{1,0:T(8,128)(2,1)} %copy-done.5, s32[2]{0:T(128)} %pad_add_fusion.refs_0_.at_ref.refs_1_.refs_3_, ...), custom_call_target="tpu_custom_call" | custom-call | flops 240000000 | tf_op jit(solution)/shard_map/weight_sums/pallas_call | solution.py:977
  382.6 2.5 pad_maximum_fusion.refs_1_
  386.1 4.0 meet.1
  390.7 1.5 collective-permute-start.27
  392.2 1.4 collective-permute-start.28
  393.6 1.2 slice.98
  395.4 9.9 %collective-permute-start.33 = (bf16[2,96,1536]{2,1,0:T(8,128)(2,1)}, bf16[2,96,1536]{2,1,0:T(8,128)(2,1)}, u32[]{:S(2)}, u32[]{:S(2)}) collective-permute-start(bf16[2,96,1536]{2,1,0:T(8,128)(2,1)} %get-tuple-element.130), channel_id=1, source_target_pairs={{0,2},{1,3},{2,0},{3,1},{4,6},{5,7},{6,4},{7,5},{8,10},{9,11},{10,... | collective-permute-start | bytes 1769480 | tf_op jit(solution)/shard_map/ppermute | solution.py:1040
  405.3 1.1 fusion.2
  406.5 1.3 collective-permute-start.29
  407.8 11.9 %collective-permute-done.27.refs_3_ = bf16[96,3200]{1,0:T(8,128)(2,1)} collective-permute-done((bf16[96,3200]{1,0:T(8,128)(2,1)}, bf16[96,3200]{1,0:T(8,128)(2,1)}, u32[]{:S(2)}, u32[]{:S(2)}) %collective-permute-start.27) | collective-permute-done | bytes 614432 | tf_op jit(solution)/shard_map/ppermute | solution.py:1040
  419.7 2.8 total.5.refs_0_
  422.5 1.4 fusion.11
  424.8 15.7 %collective-permute-start.30 = (bf16[96,896]{1,0:T(8,128)(2,1)S(1)}, bf16[96,896]{1,0:T(8,128)(2,1)S(1)}, u32[]{:S(2)}, u32[]{:S(2)}) collective-permute-start(bf16[96,896]{1,0:T(8,128)(2,1)S(1)} %concatenate.29), channel_id=1, source_target_pairs={{0,1},{1,0},{2,3},{3,2},{4,5},{5,4},{6,7},{7,6},{8,9},{9,8},{10,11... | collective-permute-start | bytes 516104 | tf_op jit(solution)/shard_map/ppermute | solution.py:1040
  440.6 1.7 collective-permute-start.31
  443.3 5.8 %collective-permute-done.33.refs_2_ = bf16[2,96,1536]{2,1,0:T(8,128)(2,1)} collective-permute-done((bf16[2,96,1536]{2,1,0:T(8,128)(2,1)}, bf16[2,96,1536]{2,1,0:T(8,128)(2,1)}, u32[]{:S(2)}, u32[]{:S(2)}) %collective-permute-start.33) | collective-permute-done | bytes 589856 | tf_op jit(solution)/shard_map/ppermute | solution.py:1040
  449.0 2.1 middle.1
  451.3 3.1 collective-permute-done.29.refs_10_
  455.2 8.3 %finish.1 = f32[896,768]{1,0:T(8,128)} custom-call(bf16[96,3200]{1,0:T(8,128)(2,1)} %total.5.refs_0_, s32[8,8]{1,0:T(8,128)} %get-tuple-element.72.meta_ref.refs_1_, f32[896,768]{1,0:T(8,128)} %get-tuple-element.127.refs_2_, f32[896,768]{1,0:T(8,128)} %get-tuple-element.128.refs_3_, bf16[896,768]{1,0:T(8,128)(2,1)} %refs_4_.3, ...), custom_call_target="tpu_custom_call" | custom-call | flops 180000000 | tf_op jit(solution)/shard_map/finish/pallas_call | solution.py:1019
  (132 shorter events, 23.9 us)
Async XLA Ops:
  7.2 6.3 %copy-start.32 = (f32[24]{0:T(128)S(1)}, f32[24]{0:T(128)}, u32[]{:S(2)}) copy-start(f32[24]{0:T(128)} %param.15) | copy-start | bytes 292
  7.2 6.3 %copy-start.33 = (f32[24]{0:T(128)S(1)}, f32[24]{0:T(128)}, u32[]{:S(2)}) copy-start(f32[24]{0:T(128)} %param.20) | copy-start | bytes 292
  7.2 6.5 %copy-start.30 = (bf16[192,96]{1,0:T(8,128)(2,1)S(1)}, bf16[192,96]{1,0:T(8,128)(2,1)}, u32[]{:S(2)}) copy-start(bf16[192,96]{1,0:T(8,128)(2,1)} %param.19) | copy-start | bytes 110596
  7.2 7.0 %copy-start.27 = (bf16[96,192]{1,0:T(8,128)(2,1)S(1)}, bf16[96,192]{1,0:T(8,128)(2,1)}, u32[]{:S(2)}) copy-start(bf16[96,192]{1,0:T(8,128)(2,1)} %param.16) | copy-start | bytes 110596
  7.2 7.0 %copy-start.28 = (bf16[96,192]{1,0:T(8,128)(2,1)S(1)}, bf16[96,192]{1,0:T(8,128)(2,1)}, u32[]{:S(2)}) copy-start(bf16[96,192]{1,0:T(8,128)(2,1)} %param.17) | copy-start | bytes 110596
  7.2 7.0 %copy-start.29 = (bf16[96,192]{1,0:T(8,128)(2,1)S(1)}, bf16[96,192]{1,0:T(8,128)(2,1)}, u32[]{:S(2)}) copy-start(bf16[96,192]{1,0:T(8,128)(2,1)} %param.18) | copy-start | bytes 110596
  7.2 11.6 %copy-start.31 = (s32[3584]{0:T(1024)S(1)}, s32[3584]{0:T(1024)}, u32[]{:S(2)}) copy-start(s32[3584]{0:T(1024)} %param.26) | copy-start | bytes 43012
  7.2 186.7 %all-gather.3.cloned.1.call-start = ((), (), s32[]{:S(2)}) async-start(), calls=%async_computation | async-start | bytes 9732096 | tf_op jit(solution)/shard_map/all_gather | solution.py:1111
  8.5 22.9 %collective-permute-start = (bf16[512,768]{1,0:T(8,128)(2,1)S(1)}, bf16[512,768]{1,0:T(8,128)(2,1)S(1)}, u32[]{:S(2)}, u32[]{:S(2)}) collective-permute-start(bf16[512,768]{1,0:T(8,128)(2,1)S(1)} %slice.96), channel_id=1, source_target_pairs={{0,1},{1,2},{2,3},{4,5},{5,6},{6,7},{8,9},{9,10},{10,11},{12,13},{... | collective-permute-start | bytes 2359304 | tf_op jit(solution)/shard_map/ppermute | solution.py:1044
  14.4 25.9 %copy-start.15 = (bf16[96,896]{1,0:T(8,128)(2,1)}, bf16[96,896]{1,0:T(8,128)(2,1)S(1)}, u32[]{:S(2)}) copy-start(bf16[96,896]{1,0:T(8,128)(2,1)S(1)} %concatenate.25.refs_3_) | copy-start | bytes 516100
  14.4 25.9 %collective-permute-start.1 = (bf16[96,896]{1,0:T(8,128)(2,1)S(1)}, bf16[96,896]{1,0:T(8,128)(2,1)S(1)}, u32[]{:S(2)}, u32[]{:S(2)}) collective-permute-start(bf16[96,896]{1,0:T(8,128)(2,1)S(1)} %concatenate.25.refs_3_), channel_id=1, source_target_pairs={{0,1},{1,0},{2,3},{3,2},{4,5},{5,4},{6,7},{7,6},{8,9},{9,8},{10,11... | collective-permute-start | bytes 516104 | tf_op jit(solution)/shard_map/ppermute | solution.py:1040
  16.0 24.4 %collective-permute-start.2 = (bf16[96,896]{1,0:T(8,128)(2,1)S(1)}, bf16[96,896]{1,0:T(8,128)(2,1)S(1)}, u32[]{:S(2)}, u32[]{:S(2)}) collective-permute-start(bf16[96,896]{1,0:T(8,128)(2,1)S(1)} %concatenate.25.refs_3_), channel_id=1, source_target_pairs={{0,2},{1,3},{2,0},{3,1},{4,6},{5,7},{6,4},{7,5},{8,10},{9,11},{10,... | collective-permute-start | bytes 516104 | tf_op jit(solution)/shard_map/ppermute | solution.py:1040
  17.1 24.3 %collective-permute-start.3 = (bf16[96,896]{1,0:T(8,128)(2,1)S(1)}, bf16[96,896]{1,0:T(8,128)(2,1)S(1)}, u32[]{:S(2)}, u32[]{:S(2)}) collective-permute-start(bf16[96,896]{1,0:T(8,128)(2,1)S(1)} %concatenate.25.refs_3_), channel_id=1, source_target_pairs={{0,3},{1,2},{2,1},{3,0},{4,7},{5,6},{6,5},{7,4},{8,11},{9,10},{10,... | collective-permute-start | bytes 516104 | tf_op jit(solution)/shard_map/ppermute | solution.py:1040
  31.4 9.0 %copy-start.3 = (bf16[512,768]{1,0:T(8,128)(2,1)}, bf16[512,768]{1,0:T(8,128)(2,1)S(1)}, u32[]{:S(2)}) copy-start(bf16[512,768]{1,0:T(8,128)(2,1)S(1)} %collective-permute-done.refs_0_.a1_ref.r1_ref) | copy-start | bytes 2359300
  31.4 42.1 %collective-permute-start.11 = (bf16[512,768]{1,0:T(8,128)(2,1)S(1)}, bf16[512,768]{1,0:T(8,128)(2,1)S(1)}, u32[]{:S(2)}, u32[]{:S(2)}) collective-permute-start(bf16[512,768]{1,0:T(8,128)(2,1)S(1)} %collective-permute-done.refs_0_.a1_ref.r1_ref), channel_id=1, source_target_pairs={{1,2},{2,3},{5,6},{6,7},{9,10},{10,11},{13,14},{14,15},{17,18},{18... | collective-permute-start | bytes 2359304 | tf_op jit(solution)/shard_map/ppermute | solution.py:1044
  40.4 1.0 copy-start.24
  40.4 1.0 copy-start.25
  44.2 17.0 %collective-permute-start.5 = (bf16[96,3200]{1,0:T(8,128)(2,1)}, bf16[96,3200]{1,0:T(8,128)(2,1)S(1)}, u32[]{:S(2)}, u32[]{:S(2)}) collective-permute-start(bf16[96,3200]{1,0:T(8,128)(2,1)} %line.1.refs_4_), channel_id=1, source_target_pairs={{0,8},{4,12},{8,0},{12,4},{16,24},{20,28},{24,16},{28,20},{1,9},{5... | collective-permute-start | bytes 1843208 | tf_op jit(solution)/shard_map/ppermute | solution.py:1040
  45.7 27.8 %collective-permute-start.7 = (bf16[96,3200]{1,0:T(8,128)(2,1)}, bf16[96,3200]{1,0:T(8,128)(2,1)S(1)}, u32[]{:S(2)}, u32[]{:S(2)}) collective-permute-start(bf16[96,3200]{1,0:T(8,128)(2,1)} %line.1.refs_4_), channel_id=1, source_target_pairs={{0,16},{4,20},{8,24},{12,28},{16,0},{20,4},{24,8},{28,12},{1,17},{... | collective-permute-start | bytes 1843208 | tf_op jit(solution)/shard_map/ppermute | solution.py:1040
  47.2 26.3 %collective-permute-start.9 = (bf16[96,3200]{1,0:T(8,128)(2,1)}, bf16[96,3200]{1,0:T(8,128)(2,1)S(1)}, u32[]{:S(2)}, u32[]{:S(2)}) collective-permute-start(bf16[96,3200]{1,0:T(8,128)(2,1)} %line.1.refs_4_), channel_id=1, source_target_pairs={{0,24},{4,28},{8,16},{12,20},{16,8},{20,12},{24,0},{28,4},{1,25},{... | collective-permute-start | bytes 1843208 | tf_op jit(solution)/shard_map/ppermute | solution.py:1040
  61.2 13.1 %copy-start.7 = (bf16[96,3200]{1,0:T(8,128)(2,1)}, bf16[96,3200]{1,0:T(8,128)(2,1)S(1)}, u32[]{:S(2)}) copy-start(bf16[96,3200]{1,0:T(8,128)(2,1)S(1)} %collective-permute-done.5.refs_6_.refs_1_) | copy-start | bytes 1843204
  73.5 1.0 copy-start.8
  74.3 0.9 copy-start.1
  75.3 3.2 copy-start.6
  77.7 24.9 %collective-permute-start.12 = (bf16[512,768]{1,0:T(8,128)(2,1)}, bf16[512,768]{1,0:T(8,128)(2,1)S(1)}, u32[]{:S(2)}, u32[]{:S(2)}) collective-permute-start(bf16[512,768]{1,0:T(8,128)(2,1)} %copy-done.1), channel_id=1, source_target_pairs={{2,3},{6,7},{10,11},{14,15},{18,19},{22,23},{26,27},{30,31}} | collective-permute-start | bytes 2359304 | tf_op jit(solution)/shard_map/ppermute | solution.py:1044
  78.4 2.2 collective-permute-start.4
  78.5 11.9 %collective-permute-start.10 = (bf16[96,3200]{1,0:T(8,128)(2,1)}, bf16[96,3200]{1,0:T(8,128)(2,1)S(1)}, u32[]{:S(2)}, u32[]{:S(2)}) collective-permute-start(bf16[96,3200]{1,0:T(8,128)(2,1)} %copy-done.9), channel_id=1, source_target_pairs={{0,4},{4,0},{8,12},{12,8},{16,20},{20,16},{24,28},{28,24},{1,5},{5... | collective-permute-start | bytes 1843208 | tf_op jit(solution)/shard_map/ppermute | solution.py:1040
  79.0 11.4 %collective-permute-start.6 = (bf16[96,3200]{1,0:T(8,128)(2,1)}, bf16[96,3200]{1,0:T(8,128)(2,1)S(1)}, u32[]{:S(2)}, u32[]{:S(2)}) collective-permute-start(bf16[96,3200]{1,0:T(8,128)(2,1)} %copy-done.7), channel_id=1, source_target_pairs={{0,4},{4,0},{8,12},{12,8},{16,20},{20,16},{24,28},{28,24},{1,5},{5... | collective-permute-start | bytes 1843208 | tf_op jit(solution)/shard_map/ppermute | solution.py:1040
  79.1 11.3 %collective-permute-start.8 = (bf16[96,3200]{1,0:T(8,128)(2,1)}, bf16[96,3200]{1,0:T(8,128)(2,1)}, u32[]{:S(2)}, u32[]{:S(2)}) collective-permute-start(bf16[96,3200]{1,0:T(8,128)(2,1)} %copy-done.8), channel_id=1, source_target_pairs={{0,4},{4,0},{8,12},{12,8},{16,20},{20,16},{24,28},{28,24},{1,5},{5... | collective-permute-start | bytes 1843208 | tf_op jit(solution)/shard_map/ppermute | solution.py:1040
  80.6 9.8 %copy-start.16 = (bf16[96,3200]{1,0:T(8,128)(2,1)}, bf16[96,3200]{1,0:T(8,128)(2,1)S(1)}, u32[]{:S(2)}) copy-start(bf16[96,3200]{1,0:T(8,128)(2,1)S(1)} %collective-permute-done.4.refs_5_) | copy-start | bytes 1843204
  80.6 40.4 %collective-permute-start.13 = (bf16[384,768]{1,0:T(8,128)(2,1)}, bf16[384,768]{1,0:T(8,128)(2,1)S(1)}, u32[]{:S(2)}, u32[]{:S(2)}) collective-permute-start(bf16[384,768]{1,0:T(8,128)(2,1)} %get-tuple-element.75), channel_id=1, source_target_pairs={{0,1},{1,2},{2,3},{4,5},{5,6},{6,7},{8,9},{9,10},{10,11},{12,13},{... | collective-permute-start | bytes 1769480 | tf_op jit(solution)/shard_map/ppermute | solution.py:1044
  90.4 1.0 copy-start.18
  102.6 0.9 copy-start.2
  105.5 46.1 %collective-permute-start.14 = (bf16[384,768]{1,0:T(8,128)(2,1)}, bf16[384,768]{1,0:T(8,128)(2,1)S(1)}, u32[]{:S(2)}, u32[]{:S(2)}) collective-permute-start(bf16[384,768]{1,0:T(8,128)(2,1)} %join.2), channel_id=1, source_target_pairs={{0,2},{1,3},{4,6},{5,7},{8,10},{9,11},{12,14},{13,15},{16,18},{17,... | collective-permute-start | bytes 1769480 | tf_op jit(solution)/shard_map/ppermute | solution.py:1044
  115.6 36.0 %collective-permute-start.15 = (bf16[384,768]{1,0:T(8,128)(2,1)}, bf16[384,768]{1,0:T(8,128)(2,1)S(1)}, u32[]{:S(2)}, u32[]{:S(2)}) collective-permute-start(bf16[384,768]{1,0:T(8,128)(2,1)} %join.2), channel_id=1, source_target_pairs={{0,3},{4,7},{8,11},{12,15},{16,19},{20,23},{24,27},{28,31}} | collective-permute-start | bytes 1769480 | tf_op jit(solution)/shard_map/ppermute | solution.py:1044
  151.6 1.0 copy-start.21
  239.6 27.6 %collective-permute-start.16 = (bf16[4,4,96,1536]{3,2,1,0:T(8,128)(2,1)}, bf16[4,4,96,1536]{3,2,1,0:T(8,128)(2,1)}, u32[]{:S(2)}, u32[]{:S(2)}) collective-permute-start(bf16[4,4,96,1536]{3,2,1,0:T(8,128)(2,1)} %get-tuple-element.90), channel_id=1, source_target_pairs={{0,4},{4,0},{8,12},{12,8},{16,20},{20,16},{24,28},{28,24},{1,5},{5... | collective-permute-start | bytes 14155784 | tf_op jit(solution)/shard_map/ppermute | solution.py:1040
  283.8 34.9 %collective-permute-start.22 = (bf16[768,768]{1,0:T(8,128)(2,1)}, bf16[768,768]{1,0:T(8,128)(2,1)S(1)}, u32[]{:S(2)}, u32[]{:S(2)}) collective-permute-start(bf16[768,768]{1,0:T(8,128)(2,1)} %get-tuple-element.98.refs_0_.refs_1_), channel_id=1, source_target_pairs={{3,2},{1,0},{7,6},{5,4},{11,10},{9,8},{15,14},{13,12},{19,18},{17,... | collective-permute-start | bytes 3538952 | tf_op jit(solution)/shard_map/ppermute | solution.py:1044
  285.1 38.9 %collective-permute-start.19 = (bf16[4,96,1536]{2,1,0:T(8,128)(2,1)}, bf16[4,96,1536]{2,1,0:T(8,128)(2,1)S(1)}, u32[]{:S(2)}, u32[]{:S(2)}) collective-permute-start(bf16[4,96,1536]{2,1,0:T(8,128)(2,1)} %get-tuple-element.102), channel_id=1, source_target_pairs={{0,8},{4,12},{8,0},{12,4},{16,24},{20,28},{24,16},{28,20},{1,9},{5... | collective-permute-start | bytes 3538952 | tf_op jit(solution)/shard_map/ppermute | solution.py:1040
  286.6 53.4 %collective-permute-start.20 = (bf16[4,96,1536]{2,1,0:T(8,128)(2,1)}, bf16[4,96,1536]{2,1,0:T(8,128)(2,1)S(1)}, u32[]{:S(2)}, u32[]{:S(2)}) collective-permute-start(bf16[4,96,1536]{2,1,0:T(8,128)(2,1)} %get-tuple-element.103), channel_id=1, source_target_pairs={{0,16},{4,20},{8,24},{12,28},{16,0},{20,4},{24,8},{28,12},{1,17},{... | collective-permute-start | bytes 3538952 | tf_op jit(solution)/shard_map/ppermute | solution.py:1040
  287.3 52.7 %collective-permute-start.21 = (bf16[4,96,1536]{2,1,0:T(8,128)(2,1)}, bf16[4,96,1536]{2,1,0:T(8,128)(2,1)}, u32[]{:S(2)}, u32[]{:S(2)}) collective-permute-start(bf16[4,96,1536]{2,1,0:T(8,128)(2,1)} %get-tuple-element.104), channel_id=1, source_target_pairs={{0,24},{4,28},{8,16},{12,20},{16,8},{20,12},{24,0},{28,4},{1,25},{... | collective-permute-start | bytes 3538952 | tf_op jit(solution)/shard_map/ppermute | solution.py:1040
  305.4 58.7 %collective-permute-start.17 = (bf16[768,768]{1,0:T(8,128)(2,1)}, bf16[768,768]{1,0:T(8,128)(2,1)}, u32[]{:S(2)}, u32[]{:S(2)}) collective-permute-start(bf16[768,768]{1,0:T(8,128)(2,1)} %join.3), channel_id=1, source_target_pairs={{3,2},{7,6},{11,10},{15,14},{19,18},{23,22},{27,26},{31,30}} | collective-permute-start | bytes 3538952 | tf_op jit(solution)/shard_map/ppermute | solution.py:1044
  318.8 1.0 copy-start.14
  322.8 44.3 %collective-permute-start.23 = (bf16[768,768]{1,0:T(8,128)(2,1)}, bf16[768,768]{1,0:T(8,128)(2,1)S(1)}, u32[]{:S(2)}, u32[]{:S(2)}) collective-permute-start(bf16[768,768]{1,0:T(8,128)(2,1)} %total.4.refs_0_.refs_6_), channel_id=1, source_target_pairs={{2,0},{6,4},{10,8},{14,12},{18,16},{22,20},{26,24},{30,28}} | collective-permute-start | bytes 3538952 | tf_op jit(solution)/shard_map/ppermute | solution.py:1044
  324.1 16.0 %copy-start.11 = (bf16[4,96,1536]{2,1,0:T(8,128)(2,1)}, bf16[4,96,1536]{2,1,0:T(8,128)(2,1)S(1)}, u32[]{:S(2)}) copy-start(bf16[4,96,1536]{2,1,0:T(8,128)(2,1)S(1)} %collective-permute-done.19.refs_1_) | copy-start | bytes 3538948
  340.0 1.1 copy-start.12
  364.2 20.9 %collective-permute-start.24 = (bf16[4,96,1664]{2,1,0:T(8,128)(2,1)}, bf16[4,96,1664]{2,1,0:T(8,128)(2,1)}, u32[]{:S(2)}, u32[]{:S(2)}) collective-permute-start(bf16[4,96,1664]{2,1,0:T(8,128)(2,1)} %pad_maximum_fusion.1), channel_id=1, source_target_pairs={{0,4},{4,0},{8,12},{12,8},{16,20},{20,16},{24,28},{28,24},{1,5},{5... | collective-permute-start | bytes 3833864 | tf_op jit(solution)/shard_map/ppermute | solution.py:1040
  367.1 1.0 copy-start.5
  368.1 13.5 %copy-start = (bf16[768,768]{1,0:T(8,128)(2,1)S(1)}, bf16[768,768]{1,0:T(8,128)(2,1)}, u32[]{:S(2)}) copy-start(bf16[768,768]{1,0:T(8,128)(2,1)} %total.3.refs_1_.refs_7_) | copy-start | bytes 3538948
  381.1 4.0 collective-permute-start.25
  381.6 23.7 %collective-permute-start.18 = (bf16[768,768]{1,0:T(8,128)(2,1)S(1)}, bf16[768,768]{1,0:T(8,128)(2,1)S(1)}, u32[]{:S(2)}, u32[]{:S(2)}) collective-permute-start(bf16[768,768]{1,0:T(8,128)(2,1)S(1)} %copy-done), channel_id=1, source_target_pairs={{2,1},{6,5},{10,9},{14,13},{18,17},{22,21},{26,25},{30,29}} | collective-permute-start | bytes 3538952 | tf_op jit(solution)/shard_map/ppermute | solution.py:1044
  385.1 1.0 copy-start.13
  390.1 17.7 %collective-permute-start.26 = (bf16[96,3200]{1,0:T(8,128)(2,1)}, bf16[96,3200]{1,0:T(8,128)(2,1)S(1)}, u32[]{:S(2)}, u32[]{:S(2)}) collective-permute-start(bf16[96,3200]{1,0:T(8,128)(2,1)} %get-tuple-element.124), channel_id=1, source_target_pairs={{0,8},{4,12},{8,0},{12,4},{16,24},{20,28},{24,16},{28,20},{1,9},{5... | collective-permute-start | bytes 1843208 | tf_op jit(solution)/shard_map/ppermute | solution.py:1040
  390.7 29.0 %collective-permute-start.27 = (bf16[96,3200]{1,0:T(8,128)(2,1)}, bf16[96,3200]{1,0:T(8,128)(2,1)}, u32[]{:S(2)}, u32[]{:S(2)}) collective-permute-start(bf16[96,3200]{1,0:T(8,128)(2,1)} %get-tuple-element.125), channel_id=1, source_target_pairs={{0,16},{4,20},{8,24},{12,28},{16,0},{20,4},{24,8},{28,12},{1,17},{... | collective-permute-start | bytes 1843208 | tf_op jit(solution)/shard_map/ppermute | solution.py:1040
  392.2 27.5 %collective-permute-start.28 = (bf16[96,3200]{1,0:T(8,128)(2,1)}, bf16[96,3200]{1,0:T(8,128)(2,1)}, u32[]{:S(2)}, u32[]{:S(2)}) collective-permute-start(bf16[96,3200]{1,0:T(8,128)(2,1)} %get-tuple-element.126), channel_id=1, source_target_pairs={{0,24},{4,28},{8,16},{12,20},{16,8},{20,12},{24,0},{28,4},{1,25},{... | collective-permute-start | bytes 1843208 | tf_op jit(solution)/shard_map/ppermute | solution.py:1040
  395.4 53.6 %collective-permute-start.33 = (bf16[2,96,1536]{2,1,0:T(8,128)(2,1)}, bf16[2,96,1536]{2,1,0:T(8,128)(2,1)}, u32[]{:S(2)}, u32[]{:S(2)}) collective-permute-start(bf16[2,96,1536]{2,1,0:T(8,128)(2,1)} %get-tuple-element.130), channel_id=1, source_target_pairs={{0,2},{1,3},{2,0},{3,1},{4,6},{5,7},{6,4},{7,5},{8,10},{9,11},{10,... | collective-permute-start | bytes 1769480 | tf_op jit(solution)/shard_map/ppermute | solution.py:1040
  405.3 14.4 %copy-start.4 = (bf16[768,768]{1,0:T(8,128)(2,1)}, bf16[768,768]{1,0:T(8,128)(2,1)S(1)}, u32[]{:S(2)}) copy-start(bf16[768,768]{1,0:T(8,128)(2,1)S(1)} %collective-permute-done.18.refs_0_.refs_9_) | copy-start | bytes 3538948
  406.5 48.0 %collective-permute-start.29 = (bf16[128,768]{1,0:T(8,128)(2,1)S(1)}, bf16[128,768]{1,0:T(8,128)(2,1)S(1)}, u32[]{:S(2)}, u32[]{:S(2)}) collective-permute-start(bf16[128,768]{1,0:T(8,128)(2,1)S(1)} %fusion.2), channel_id=1, source_target_pairs={{1,0},{3,2},{5,4},{7,6},{9,8},{11,10},{13,12},{15,14},{17,16},{19,... | collective-permute-start | bytes 589832 | tf_op jit(solution)/shard_map/ppermute | solution.py:1044
  407.8 11.9 %copy-start.19 = (bf16[96,3200]{1,0:T(8,128)(2,1)}, bf16[96,3200]{1,0:T(8,128)(2,1)S(1)}, u32[]{:S(2)}) copy-start(bf16[96,3200]{1,0:T(8,128)(2,1)S(1)} %collective-permute-done.26.refs_2_) | copy-start | bytes 1843204
  424.8 38.7 %collective-permute-start.30 = (bf16[96,896]{1,0:T(8,128)(2,1)S(1)}, bf16[96,896]{1,0:T(8,128)(2,1)S(1)}, u32[]{:S(2)}, u32[]{:S(2)}) collective-permute-start(bf16[96,896]{1,0:T(8,128)(2,1)S(1)} %concatenate.29), channel_id=1, source_target_pairs={{0,1},{1,0},{2,3},{3,2},{4,5},{5,4},{6,7},{7,6},{8,9},{9,8},{10,11... | collective-permute-start | bytes 516104 | tf_op jit(solution)/shard_map/ppermute | solution.py:1040
  440.6 22.9 %collective-permute-start.31 = (bf16[96,896]{1,0:T(8,128)(2,1)S(1)}, bf16[96,896]{1,0:T(8,128)(2,1)S(1)}, u32[]{:S(2)}, u32[]{:S(2)}) collective-permute-start(bf16[96,896]{1,0:T(8,128)(2,1)S(1)} %concatenate.30), channel_id=1, source_target_pairs={{0,2},{1,3},{2,0},{3,1},{4,6},{5,7},{6,4},{7,5},{8,10},{9,11},{10,... | collective-permute-start | bytes 516104 | tf_op jit(solution)/shard_map/ppermute | solution.py:1040
  442.5 21.1 %collective-permute-start.32 = (bf16[96,896]{1,0:T(8,128)(2,1)S(1)}, bf16[96,896]{1,0:T(8,128)(2,1)S(1)}, u32[]{:S(2)}, u32[]{:S(2)}) collective-permute-start(bf16[96,896]{1,0:T(8,128)(2,1)S(1)} %concatenate.31), channel_id=1, source_target_pairs={{0,3},{1,2},{2,1},{3,0},{4,7},{5,6},{6,5},{7,4},{8,11},{9,10},{10,... | collective-permute-start | bytes 516104 | tf_op jit(solution)/shard_map/ppermute | solution.py:1040
  451.2 14.6 %collective-permute-start.34 = (bf16[96,1536]{1,0:T(8,128)(2,1)}, bf16[96,1536]{1,0:T(8,128)(2,1)S(1)}, u32[]{:S(2)}, u32[]{:S(2)}) collective-permute-start(bf16[96,1536]{1,0:T(8,128)(2,1)} %get-tuple-element.132), channel_id=1, source_target_pairs={{0,1},{1,0},{2,3},{3,2},{4,5},{5,4},{6,7},{7,6},{8,9},{9,8},{10,11... | collective-permute-start | bytes 884744 | tf_op jit(solution)/shard_map/ppermute | solution.py:1040
  463.5 2.3 copy-start.22
  (6 other events, 4.7 us)
Sparse Core Ops, SparseCore 0:
  77.8 116.0 all-gather.2

commit v4 on v3

--- a/solution.py
+++ b/solution.py
@@ -267,19 +267,19 @@
             send_ref[r - half] = got
 
 
-def fold(at, *blocks):
+def fold(deps, at, *blocks):
     parts, rows, wide = blocks[0].shape
     out = (parts // 2, rows, wide)
     return pl.pallas_call(
-        fold_kernel,
+        after(len(deps), fold_kernel),
         grid=(1,),
-        in_specs=[SMEM] + [fixed(one.shape) for one in blocks],
+        in_specs=[ANY] * len(deps) + [SMEM] + [fixed(one.shape) for one in blocks],
         out_specs=[fixed(out)] * 2,
         out_shape=[jax.ShapeDtypeStruct(out, BF16)] * 2,
         compiler_params=params(),
         cost_estimate=cost(4),
         name="fold",
-    )(at, *blocks)
+    )(*deps, at, *blocks)
 
 
 def middle_kernel(keep_ref, got_ref, mine_ref, send_ref):
@@ -859,34 +859,31 @@
     step = pl.program_id(0)
     da = dot(dk_ref[...], wk_ref[...], COLS) + dot(dv_ref[...], wv_ref[...], COLS)
 
-    @pl.when(step < EARLY // BLOCK)
+    def gain_part(part, x):
+        x = x.astype(F32)
+        return jnp.sum(part * (x * inv_rms(x)), axis=0, keepdims=True)
+
+    @pl.when(step == 0)
     def _():
         early_ref[...] = da.astype(BF16)
-
-    @pl.when(step >= EARLY // BLOCK)
+        sum_ref[...] = jnp.zeros_like(sum_ref)
+        sum_ref[0:1, :] = gain_part(da[:ROOT], xn_ref[pl.ds(0, ROOT), :]) + gain_part(da[ROOT:], xs_ref[pl.ds(0, BLOCK), :])
+
+    @pl.when(step == 1)
     def _():
         late_ref[...] = da.astype(BF16)
-
-    x = jnp.where(step < ROOT // BLOCK, xn_ref[...], xs_ref[...]).astype(F32)
-
-    @pl.when(step == 0)
-    def _():
-        sum_ref[...] = jnp.zeros_like(sum_ref)
-
-    sum_ref[0:1, :] += jnp.sum(da * (x * inv_rms(x)), axis=0, keepdims=True)
+        sum_ref[0:1, :] += gain_part(da, xs_ref[pl.ds(BLOCK, FAR - EARLY), :])
 
 
 def spread(deps, dk, dv, x_near, x_slot, w):
     d = w.shape[0]
-    near, early = ROOT // BLOCK, EARLY // BLOCK
-    at = lambda f: pl.BlockSpec((BLOCK, d), lambda i: (f(i), 0))
+    once = pl.BlockSpec((EARLY, d), lambda i: (0, 0))
     return pl.pallas_call(
         after(len(deps), spread_kernel),
-        grid=(FAR // BLOCK,),
-        in_specs=[ANY] * len(deps) + [at(lambda i: i), at(lambda i: i), at(lambda i: jnp.minimum(i, near - 1)), at(lambda i: jnp.maximum(i - near, 0)),
-                  weight(d, 1), weight(d, 2)],
-        out_specs=[at(lambda i: jnp.minimum(i, early - 1)), at(lambda i: jnp.maximum(i - early, 0)),
-                   pl.BlockSpec((8, d), lambda i: (0, 0))],
+        grid=(2,),
+        in_specs=[ANY] * len(deps) + [tiled(EARLY, d), tiled(EARLY, d), fixed(x_near.shape), fixed(x_slot.shape),
+                                      weight(d, 1), weight(d, 2)],
+        out_specs=[once, once, pl.BlockSpec((8, d), lambda i: (0, 0))],
         out_shape=[shape(EARLY, d, BF16), shape(FAR - EARLY, d, BF16), shape(8, d, F32)],
         compiler_params=params(),
         cost_estimate=cost(6),
@@ -930,9 +927,10 @@
     )(*deps, x, x_near, dq, dk, dv, dke, dve, w, w, w)
 
 
-def spill(core, got, kept_ref, away_ref):
+def spill(core, got, kept_ref, away_ref, at=0):
     chips, rows, _ = kept_ref.shape
-    split_cores(core, got.astype(BF16).reshape(chips, 2, rows, got.shape[1]), kept_ref, away_ref, (slice(None),) * 3)
+    split_cores(core, got.astype(BF16).reshape(chips, 2, rows, got.shape[1]), kept_ref, away_ref,
+                (slice(None), slice(None), slice(at, at + got.shape[1])))
 
 
 def keyed(a_ref, an_ref, as_ref, own, far, edge):
@@ -941,19 +939,13 @@
             + dot(as_ref[...], far[pl.ds(ROOT, SLOTS), :], ROWS) + dot(an_ref[tail, :], edge[...], ROWS))
 
 
-def first_kernel(at_ref, s1_ref, s2_ref, s3_ref, a_ref, dq_ref, dhb_ref, o_ref, kept_ref, away_ref, kept_gain, away_gain):
-    step, core = pl.program_id(0), at_ref[1] % 2
-
-    @pl.when(step == 0)
-    def _():
-        line = lax.broadcasted_iota(jnp.int32, (GAIN_LANES, a_ref.shape[1]), 0)
-        table = jnp.where(line == 0, s1_ref[0:1, :] + s2_ref[0:1, :], jnp.where(line == 1, s3_ref[0:1, :], 0.0))
-        spill(core, table.T, kept_gain, away_gain)
-        spill(core, dot(a_ref[...], dq_ref[...], ROWS), kept_ref, away_ref)
-
-    @pl.when(step == 1)
-    def _():
-        spill(core, dot(dhb_ref[...], o_ref[...], ROWS), kept_ref, away_ref)
+def first_kernel(at_ref, s1_ref, s2_ref, s3_ref, a_ref, dq_ref, dhb_ref, o_ref, kept_ref, away_ref):
+    core, d = at_ref[1] % 2, a_ref.shape[1]
+    line = lax.broadcasted_iota(jnp.int32, (GAIN_LANES, d), 0)
+    table = jnp.where(line == 0, s1_ref[0:1, :] + s2_ref[0:1, :], jnp.where(line == 1, s3_ref[0:1, :], 0.0))
+    spill(core, dot(a_ref[...], dq_ref[...], ROWS), kept_ref, away_ref)
+    spill(core, dot(dhb_ref[...], o_ref[...], ROWS), kept_ref, away_ref, d)
+    spill(core, table.T, kept_ref, away_ref, 2 * d)
 
 
 def second_kernel(at_ref, a_ref, an_ref, as_ref, dk_ref, dv_ref, dkf_ref, dvf_ref, dke_ref, dve_ref, kept_ref, away_ref):
@@ -968,18 +960,17 @@
         spill(core, keyed(a_ref, an_ref, as_ref, dv_ref, dvf_ref, dve_ref), kept_ref, away_ref)
 
 
-def weight_sums(kernel, deps, at, arrays, dp, gains):
+def weight_sums(kernel, deps, at, arrays, dp, extra):
     d = arrays[-1].shape[1]
-    chips, rows = dp // 2, d // dp
-    widths = [(2 * d, pl.BlockSpec((chips, rows, d), lambda i: (0, 0, i)))] * 2
-    if gains:
-        widths += [(GAIN_LANES, pl.BlockSpec((chips, rows, GAIN_LANES), lambda i: (0, 0, 0)))] * 2
+    chips, rows, wide = dp // 2, d // dp, 2 * d + extra
+    steps = 1 if extra else 2
+    spec = pl.BlockSpec((chips, rows, wide // steps), lambda i: (0, 0, i))
     return pl.pallas_call(
         after(len(deps), kernel),
-        grid=(2,),
+        grid=(steps,),
         in_specs=[ANY] * len(deps) + [SMEM] + [fixed(one.shape) for one in arrays],
-        out_specs=[spec for _, spec in widths],
-        out_shape=[jax.ShapeDtypeStruct((chips, rows, wide), BF16) for wide, _ in widths],
+        out_specs=[spec, spec],
+        out_shape=[jax.ShapeDtypeStruct((chips, rows, wide), BF16)] * 2,
         compiler_params=params(),
         cost_estimate=cost(8),
         name="weight_sums",
@@ -1125,23 +1116,23 @@
     dq_part, dk_far, dv_far = back_far(meta, slots, q, do, o, logs, near, far, tab)
     rest_blocks = meet_rest(at, kept, away)
     early, late, far_sum = spread((rest_blocks[0],), dk_far, dv_far, x_near, x_slot, w)
-    keep, away = fold(at, rest_blocks[0], *(swap(block, "dp", 2 * m) for m, block in enumerate(rest_blocks) if m))
+    moved = [swap(block, "dp", 2 * m) for m, block in enumerate(rest_blocks) if m]
     early_in = send(early, (3, 2), (1, 0))
     dq, dk, dv, dke, dve = back_near((early,), meta, q, do, o, logs, near, own, tab, dq_part)
     late_in = send(join((dq,), late), (3, 2))
     early = total((dq,), early, early_in)
     early_in = send(early, (2, 0))
-    da, edge, own_sum = own_back((early,), tokens, x_near, dq, dk, dv, dke, dve, w)
-    kept_a, away_a, kept_gain, away_gain = weight_sums(
-        first_kernel, (keep,), at, (far_sum, own_sum, ffn_sum, a_own, dq, dhb, o), d_size, True)
-    away_a = swap(jnp.concatenate([away_a, away_gain], axis=2), "dp", 1)
-    late = total((dq,), late, late_in)
+    da, edge, own_sum = own_back((early, moved[-1]), tokens, x_near, dq, dk, dv, dke, dve, w)
+    kept_b, away_b = weight_sums(
+        second_kernel, (da,), at, (a_own, a_near, a_slot, dk, dv, dk_far, dv_far, dke, dve), d_size, 0)
+    away_b = swap(away_b, "dp", 1)
+    keep, away = fold((kept_b,), at, rest_blocks[0], *moved)
+    away = swap(away, "tensor", 2)
+    late = total((kept_b,), late, late_in)
     late_in = send(late, (2, 1))
-    kept_b, away_b = weight_sums(
-        second_kernel, (keep, late, early_in), at, (a_own, a_near, a_slot, dk, dv, dk_far, dv_far, dke, dve), d_size, False)
-    away = swap(away, "tensor", 2)
-    away_b = swap(away_b, "dp", 1)
-    kept_a = jnp.concatenate([kept_a, kept_gain], axis=2)
+    kept_a, away_a = weight_sums(
+        first_kernel, (keep, late, early_in), at, (far_sum, own_sum, ffn_sum, a_own, dq, dhb, o), d_size, GAIN_LANES)
+    away_a = swap(away_a, "dp", 1)
     blocks = meet((), at, (kept_a, kept_b), (away_a, away_b))
     summed = meet_chips((late_in,), blocks)
     mine, away = middle((summed,), keep, away)

time: 481 us -> 459 us (0.954)
  starting transfers between devices: 78.4 us -> 64.7 us
  other arithmetic: 15.2 us -> 10.2 us
    ppermute x24, starting transfers between devices: 45 us -> 31.5 us  [swap(): lax.ppermute(x, axis, [(i, i ^ mask) for i in range(lax.axis_size(axis))])]
    ppermute x24, waiting for transfers between devices: 61.5 us -> 53.5 us  [swap(): lax.ppermute(x, axis, [(i, i ^ mask) for i in range(lax.axis_size(axis))])]
    concatenate x2 -> x0, other arithmetic: 4.93 us -> none  [the longest x1 2.47 us: per_device(): kept_a = jnp.concatenate([kept_a, kept_gain], axis=2)]
  transfers between devices with their start and end apart: 36 -> 36, of which waited for: 11 -> 13; matrix products, arithmetic and copies ran while one was open for 5% -> 4% of each run, Pallas kernels for 37% -> 37%
where the time goes in v4:
time: 459 us; the launch traced here: 453 us
  Pallas kernels  240 us (52%)
  waiting for transfers between devices  99.4 us (22%)
  starting transfers between devices  64.7 us (14%)
  local copies, waits for them, and re-layouts  22.6 us (5%)
  between operations  15.7 us (3%)
  other arithmetic  10.2 us (2%)
    ppermute x24, waiting for transfers between devices, swap(): lax.ppermute(x, axis, [(i, i ^ mask) for i in range(lax.axis_size(axis))])  53.5 us
    pallas_call x1, Pallas kernels, feed_forward(): pl.pallas_call(ffn_kernel, grid=(steps + parts,), in_specs=[SMEM, tile, t...  45.7 us
    ppermute x11, starting transfers between devices, send(): return lax.ppermute(x, 'tensor', list(pairs))  33.2 us
    ppermute x24, starting transfers between devices, swap(): lax.ppermute(x, axis, [(i, i ^ mask) for i in range(lax.axis_size(axis))])  31.5 us
    ppermute x11, waiting for transfers between devices, send(): return lax.ppermute(x, 'tensor', list(pairs))  30.8 us
    pallas_call x1, Pallas kernels, back_far(): pl.pallas_call(back_far_kernel, grid=(d // 128,), in_specs=[SMEM, SMEM, p...  27.3 us
    pallas_call x1, Pallas kernels, attend_near(): pl.pallas_call(attend_near_kernel, grid=(d // 128,), in_specs=[SMEM, pair...  22.3 us
    pallas_call x2, Pallas kernels, weight_sums(): pl.pallas_call(after(len(deps), kernel), grid=(steps,), in_specs=[ANY] *...  21.4 us
  transfers between devices with their start and end apart: 36, of which 13 were waited for; matrix products, arithmetic and copies ran while one was open for 4% of the time, Pallas kernels for 37%

profile of v4, /device:TPU:0, one launch (start us, length us, event | category | flops | bytes accessed | tf_op | source)
XLA Modules:
  0.0 452.5 jit_solution(11977601315553189035)
XLA Ops:
  7.3 1.2 slice.96
  8.5 5.0 %collective-permute-start = (bf16[512,768]{1,0:T(8,128)(2,1)S(1)}, bf16[512,768]{1,0:T(8,128)(2,1)S(1)}, u32[]{:S(2)}, u32[]{:S(2)}) collective-permute-start(bf16[512,768]{1,0:T(8,128)(2,1)S(1)} %slice.96), channel_id=1, source_target_pairs={{0,1},{1,2},{2,3},{4,5},{5,6},{6,7},{8,9},{9,10},{10,11},{12,13},{... | collective-permute-start | bytes 2359304 | tf_op jit(solution)/shard_map/ppermute | solution.py:1035
  14.4 1.6 collective-permute-start.1
  16.0 1.1 collective-permute-start.2
  17.1 1.8 collective-permute-start.3
  19.0 12.4 %collective-permute-done.refs_0_.a1_ref.r1_ref = bf16[512,768]{1,0:T(8,128)(2,1)S(1)} collective-permute-done((bf16[512,768]{1,0:T(8,128)(2,1)S(1)}, bf16[512,768]{1,0:T(8,128)(2,1)S(1)}, u32[]{:S(2)}, u32[]{:S(2)}) %collective-permute-start) | collective-permute-done | bytes 786464 | tf_op jit(solution)/shard_map/ppermute | solution.py:1035
  32.1 8.3 %fusion = (f32[3584,128]{1,0:T(8,128)}, f32[3584,128]{1,0:T(8,128)}) fusion(f32[128]{0:T(128)S(1)} %get-tuple-element.195, f32[128]{0:T(128)S(1)} %get-tuple-element.196, f32[3584]{0:T(1024)S(1)} %convert_element_type.39), kind=kLoop, calls=%fused_computation.2 | loop fusion | flops 917504 | bytes 3685376 | tf_op jit(solution)/shard_map/mul | solution.py:1027
  42.0 2.2 line.1.refs_4_
  44.2 1.5 collective-permute-start.5
  45.7 1.5 collective-permute-start.7
  47.7 13.5 %collective-permute-done.5.refs_6_.refs_1_ = bf16[96,3200]{1,0:T(8,128)(2,1)S(1)} collective-permute-done((bf16[96,3200]{1,0:T(8,128)(2,1)}, bf16[96,3200]{1,0:T(8,128)(2,1)S(1)}, u32[]{:S(2)}, u32[]{:S(2)}) %collective-permute-start.5) | collective-permute-done | bytes 614432 | tf_op jit(solution)/shard_map/ppermute | solution.py:1031
  61.2 12.3 %collective-permute-done.7.refs_8_.refs_2_ = bf16[96,3200]{1,0:T(8,128)(2,1)S(1)} collective-permute-done((bf16[96,3200]{1,0:T(8,128)(2,1)}, bf16[96,3200]{1,0:T(8,128)(2,1)S(1)}, u32[]{:S(2)}, u32[]{:S(2)}) %collective-permute-start.7) | collective-permute-done | bytes 614432 | tf_op jit(solution)/shard_map/ppermute | solution.py:1031
  75.2 2.4 begin.1
  79.4 1.1 collective-permute-done.4.refs_5_
  80.6 7.2 %collective-permute-start.13 = (bf16[384,768]{1,0:T(8,128)(2,1)}, bf16[384,768]{1,0:T(8,128)(2,1)S(1)}, u32[]{:S(2)}, u32[]{:S(2)}) collective-permute-start(bf16[384,768]{1,0:T(8,128)(2,1)} %get-tuple-element.73), channel_id=1, source_target_pairs={{0,1},{1,2},{2,3},{4,5},{5,6},{6,7},{8,9},{9,10},{10,11},{12,13},{... | collective-permute-start | bytes 1769480 | tf_op jit(solution)/shard_map/ppermute | solution.py:1035
  88.4 1.9 slice.97.refs_2_
  91.4 11.2 %project_own.1 = (bf16[768,3072]{1,0:T(8,128)(2,1)}, f32[8,768]{1,0:T(8,128)}, bf16[896,768]{1,0:T(8,128)(2,1)}, bf16[896,768]{1,0:T(8,128)(2,1)}, bf16[896,768]{1,0:T(8,128)(2,1)}, /*index=5*/bf16[896,768]{1,0:T(8,128)(2,1)}) custom-call(s32[2]{0:T(128)} %pad_add_fusion.refs_0_.at_ref.refs_1_.refs_3_, bf16[896,768]{1,0:T(8,128)(2,1)} %refs_4_.3, ...), custom_call_target="tpu_custom_call" | custom-call | flops 300000000 | tf_op jit(solution)/shard_map/project_own/pallas_call | solution.py:339
  103.5 1.9 join.2
  105.4 10.1 %collective-permute-start.14 = (bf16[384,768]{1,0:T(8,128)(2,1)}, bf16[384,768]{1,0:T(8,128)(2,1)S(1)}, u32[]{:S(2)}, u32[]{:S(2)}) collective-permute-start(bf16[384,768]{1,0:T(8,128)(2,1)} %join.2), channel_id=1, source_target_pairs={{0,2},{1,3},{4,6},{5,7},{8,10},{9,11},{12,14},{13,15},{16,18},{17,... | collective-permute-start | bytes 1769480 | tf_op jit(solution)/shard_map/ppermute | solution.py:1035
  115.5 3.1 collective-permute-start.15
  118.7 2.2 plan.1
  121.7 7.5 %project_near.1 = (bf16[640,768]{1,0:T(8,128)(2,1)}, bf16[640,768]{1,0:T(8,128)(2,1)}, bf16[640,768]{1,0:T(8,128)(2,1)}, bf16[640,768]{1,0:T(8,128)(2,1)}) custom-call(s32[2]{0:T(128)} %pad_add_fusion.refs_0_.at_ref.refs_1_.refs_3_, bf16[896,768]{1,0:T(8,128)(2,1)} %refs_4_.3, bf16[512,768]{1,0:T(8,128)(2,1)} %copy-done.3, bf16[512,768]{1,0:T(8,128)(2,1)} %copy-done.1, ...), custom_call_target="tpu_custom_call" | custom-call | flops 150000000 | tf_op jit(solution)/shard_map/project_near/pallas_call | solution.py:385
  129.2 22.3 %attend_near.1 = (f32[768,896]{1,0:T(8,128)}, f32[6,8,896]{2,1,0:T(8,128)}) custom-call(s32[8,8]{1,0:T(8,128)} %get-tuple-element.70.meta_ref.refs_1_, bf16[896,768]{1,0:T(8,128)(2,1)} %get-tuple-element.71.q_ref.refs_2_, bf16[640,768]{1,0:T(8,128)(2,1)} %get-tuple-element.79.kn_ref.refs_6_, bf16[640,768]{1,0:T(8,128)(2,1)} %get-tuple-element.80.vn_ref.refs_7_, ...), custom_call_target="tpu_custom_call" | custom-call | flops 600000000 | tf_op jit(solution)/shard_map/attend_near/pallas_call | solution.py:555
  152.5 10.5 %project_far.1 = (bf16[1024,768]{1,0:T(8,128)(2,1)}, bf16[1024,768]{1,0:T(8,128)(2,1)}, bf16[1024,768]{1,0:T(8,128)(2,1)}, bf16[1024,768]{1,0:T(8,128)(2,1)}) custom-call(s32[8,8]{1,0:T(8,128)} %get-tuple-element.70.meta_ref.refs_1_, s32[8,8]{1,0:T(8,128)} %get-tuple-element.72.slot_ref, bf16[896,768]{1,0:T(8,128)(2,1)} %refs_4_.3, ...), custom_call_target="tpu_custom_call" | custom-call | flops 210000000 | tf_op jit(solution)/shard_map/project_far/pallas_call | solution.py:436
  163.0 15.7 %attend_far.1 = (bf16[896,768]{1,0:T(8,128)(2,1)}, f32[6,8,896]{2,1,0:T(8,128)}) custom-call(s32[8,8]{1,0:T(8,128)} %get-tuple-element.70.meta_ref.refs_1_, bf16[896,768]{1,0:T(8,128)(2,1)} %get-tuple-element.71.q_ref.refs_2_, bf16[1024,768]{1,0:T(8,128)(2,1)} %get-tuple-element.77.ks_ref, bf16[1024,768]{1,0:T(8,128)(2,1)} %get-tuple-element.78.vs_ref, ...), custom_call_target="tpu_custom_call" | custom-call | flops 270000000 | tf_op jit(solution)/shard_map/attend_far/pallas_call | solution.py:596
  178.7 15.1 %all-gather.3.cloned.1.call-done = bf16[3072,1536]{1,0:T(8,128)(2,1)} async-done(((bf16[96,1536]{1,0:T(8,128)(2,1)}), bf16[3072,1536]{1,0:T(8,128)(2,1)}) %all-gather.3.cloned.1.call-update) | async-done | bytes 9437200 | tf_op jit(solution)/shard_map/all_gather | solution.py:1102
  193.8 45.7 %feed_forward.1 = (bf16[896,768]{1,0:T(8,128)(2,1)}, bf16[896,768]{1,0:T(8,128)(2,1)}, bf16[896,768]{1,0:T(8,128)(2,1)}, f32[896,768]{1,0:T(8,128)}, f32[8,768]{...) custom-call(s32[2]{0:T(128)} %pad_add_fusion.refs_0_.at_ref.refs_1_.refs_3_, ...), custom_call_target="tpu_custom_call" | custom-call | flops 1200000000 | tf_op jit(solution)/shard_map/feed_forward/pallas_call | solution.py:696
  239.8 27.3 %back_far.1 = (f32[768,896]{1,0:T(8,128)}, bf16[1536,768]{1,0:T(8,128)(2,1)}, bf16[1536,768]{1,0:T(8,128)(2,1)}) custom-call(s32[8,8]{1,0:T(8,128)} %get-tuple-element.70.meta_ref.refs_1_, s32[8,8]{1,0:T(8,128)} %get-tuple-element.72.slot_ref, bf16[896,768]{1,0:T(8,128)(2,1)} %get-tuple-element.71.q_ref.refs_2_, ...), custom_call_target="tpu_custom_call" | custom-call | flops 1500000000 | tf_op jit(solution)/shard_map/back_far/pallas_call | solution.py:782
  267.1 6.4 %meet_rest.1 = (bf16[4,96,1536]{2,1,0:T(8,128)(2,1)}, bf16[4,96,1536]{2,1,0:T(8,128)(2,1)}, bf16[4,96,1536]{2,1,0:T(8,128)(2,1)}, bf16[4,96,1536]{2,1,0:T(8,128)(2,1)}) custom-call(s32[2]{0:T(128)} %pad_add_fusion.refs_0_.at_ref.refs_1_.refs_3_, bf16[4,4,96,1536]{3,2,1,0:T(8,128)(2,1)} %get-tuple-element.87.kept_ref, ...), custom_call_target="tpu_custom_call" | custom-call | flops 150000000 | tf_op jit(solution)/shard_map/meet_rest/pallas_call | solution.py:219
  273.5 9.8 %spread.1 = (bf16[768,768]{1,0:T(8,128)(2,1)}, bf16[768,768]{1,0:T(8,128)(2,1)}, f32[8,768]{1,0:T(8,128)}) custom-call(bf16[4,96,1536]{2,1,0:T(8,128)(2,1)} %get-tuple-element.89.refs_0_.refs_2_, bf16[1536,768]{1,0:T(8,128)(2,1)} %get-tuple-element.92.refs_1_.refs_7_, bf16[1536,768]{1,0:T(8,128)(2,1)} %get-tuple-element.93.refs_2_.refs_8_, ...), custom_call_target="tpu_custom_call" | custom-call | flops 180000000 | tf_op jit(solution)/shard_map/spread/pallas_call | solution.py:881
  283.3 1.3 collective-permute-start.17
  284.6 1.5 collective-permute-start.18
  286.2 14.4 %back_near.1 = (bf16[896,768]{1,0:T(8,128)(2,1)}, bf16[896,768]{1,0:T(8,128)(2,1)}, bf16[896,768]{1,0:T(8,128)(2,1)}, bf16[128,768]{1,0:T(8,128)(2,1)}, bf16[128,768]{1,0:T(8,128)(2,1)}) custom-call(bf16[768,768]{1,0:T(8,128)(2,1)} %get-tuple-element.96.refs_0_.refs_1_, s32[8,8]{1,0:T(8,128)} %get-tuple-element.70.meta_ref.refs_1_, ...), custom_call_target="tpu_custom_call" | custom-call | flops 750000000 | tf_op jit(solution)/shard_map/back_near/pallas_call | solution.py:843
  300.6 2.4 join.3
  303.0 1.7 collective-permute-start.19
  304.7 1.5 collective-permute-start.21
  306.7 11.6 %collective-permute-done.17.refs_2_ = bf16[768,768]{1,0:T(8,128)(2,1)S(1)} collective-permute-done((bf16[768,768]{1,0:T(8,128)(2,1)}, bf16[768,768]{1,0:T(8,128)(2,1)S(1)}, u32[]{:S(2)}, u32[]{:S(2)}) %collective-permute-start.17) | collective-permute-done | bytes 1179680 | tf_op jit(solution)/shard_map/ppermute | solution.py:1035
  319.3 2.9 total.3.refs_0_.refs_6_
  322.3 1.3 collective-permute-start.23
  324.6 9.6 %own_back.1 = (f32[896,768]{1,0:T(8,128)}, bf16[128,768]{1,0:T(8,128)(2,1)}, f32[8,768]{1,0:T(8,128)}) custom-call(bf16[768,768]{1,0:T(8,128)(2,1)} %total.3.refs_0_.refs_6_, bf16[4,96,1536]{2,1,0:T(8,128)(2,1)} %copy-done.6, bf16[896,768]{1,0:T(8,128)(2,1)} %refs_4_.3, bf16[640,768]{1,0:T(8,128)(2,1)} %get-tuple-element.94.refs_3_, ...), custom_call_target="tpu_custom_call" | custom-call | flops 180000000 | tf_op jit(solution)/shard_map/own_back/pallas_call | solution.py:917
  334.2 13.0 %weight_sums.2 = (bf16[4,96,1536]{2,1,0:T(8,128)(2,1)}, bf16[4,96,1536]{2,1,0:T(8,128)(2,1)}) custom-call(f32[896,768]{1,0:T(8,128)} %get-tuple-element.104.refs_0_.refs_2_, s32[2]{0:T(128)} %pad_add_fusion.refs_0_.at_ref.refs_1_.refs_3_, bf16[896,768]{1,0:T(8,128)(2,1)} %get-tuple-element.105.refs_2_.refs_7_, bf16[640,768]{1,0:T(8,128)(2,1)} %get-tuple-element.106.refs_3_, ...), custom_call_target="tpu_custom_call" | custom-call | flops 240000000 | tf_op jit(solution)/shard_map/weight_sums/pallas_call | solution.py:968
  347.2 2.9 total.4.refs_1_.refs_7_
  350.1 1.0 copy-done.13
  351.1 3.9 fold.1
  355.0 1.1 copy-done.5
  356.1 8.4 %weight_sums.3 = (bf16[4,96,1664]{2,1,0:T(8,128)(2,1)}, bf16[4,96,1664]{2,1,0:T(8,128)(2,1)}) custom-call(bf16[2,96,1536]{2,1,0:T(8,128)(2,1)} %get-tuple-element.112.refs_0_.refs_1_, bf16[768,768]{1,0:T(8,128)(2,1)} %total.4.refs_1_.refs_7_, bf16[768,768]{1,0:T(8,128)(2,1)} %copy-done.5, s32[2]{0:T(128)} %pad_add_fusion.refs_0_.at_ref.refs_1_.refs_3_, ...), custom_call_target="tpu_custom_call" | custom-call | flops 240000000 | tf_op jit(solution)/shard_map/weight_sums/pallas_call | solution.py:968
  365.8 3.5 collective-permute-done.25.refs_4_
  370.4 4.0 meet.1
  374.4 1.4 collective-permute-start.26
  376.4 1.4 collective-permute-start.28
  377.9 1.2 slice.98
  379.7 3.7 collective-permute-start.33
  383.4 1.1 fusion.2
  384.5 1.3 collective-permute-start.29
  385.8 5.4 %collective-permute-done.26.refs_2_ = bf16[96,3200]{1,0:T(8,128)(2,1)S(1)} collective-permute-done((bf16[96,3200]{1,0:T(8,128)(2,1)}, bf16[96,3200]{1,0:T(8,128)(2,1)S(1)}, u32[]{:S(2)}, u32[]{:S(2)}) %collective-permute-start.26) | collective-permute-done | bytes 614432 | tf_op jit(solution)/shard_map/ppermute | solution.py:1031
  391.3 13.6 %collective-permute-done.27.refs_3_ = bf16[96,3200]{1,0:T(8,128)(2,1)} collective-permute-done((bf16[96,3200]{1,0:T(8,128)(2,1)}, bf16[96,3200]{1,0:T(8,128)(2,1)}, u32[]{:S(2)}, u32[]{:S(2)}) %collective-permute-start.27) | collective-permute-done | bytes 614432 | tf_op jit(solution)/shard_map/ppermute | solution.py:1031
  404.9 2.8 total.5.refs_0_
  407.7 1.4 fusion.11
  410.0 8.4 %collective-permute-start.30 = (bf16[96,896]{1,0:T(8,128)(2,1)S(1)}, bf16[96,896]{1,0:T(8,128)(2,1)S(1)}, u32[]{:S(2)}, u32[]{:S(2)}) collective-permute-start(bf16[96,896]{1,0:T(8,128)(2,1)S(1)} %concatenate.21), channel_id=1, source_target_pairs={{0,1},{1,0},{2,3},{3,2},{4,5},{5,4},{6,7},{7,6},{8,9},{9,8},{10,11... | collective-permute-start | bytes 516104 | tf_op jit(solution)/shard_map/ppermute | solution.py:1031
  418.5 1.7 collective-permute-start.31
  421.1 2.7 collective-permute-done.33.refs_2_
  423.9 2.2 middle.1
  426.2 6.8 %collective-permute-done.29.refs_10_ = bf16[128,768]{1,0:T(8,128)(2,1)S(1)} collective-permute-done((bf16[128,768]{1,0:T(8,128)(2,1)S(1)}, bf16[128,768]{1,0:T(8,128)(2,1)S(1)}, u32[]{:S(2)}, u32[]{:S(2)}) %collective-permute-start.29) | collective-permute-done | bytes 196640 | tf_op jit(solution)/shard_map/ppermute | solution.py:1035
  433.6 8.4 %finish.1 = f32[896,768]{1,0:T(8,128)} custom-call(bf16[96,3200]{1,0:T(8,128)(2,1)} %total.5.refs_0_, s32[8,8]{1,0:T(8,128)} %get-tuple-element.70.meta_ref.refs_1_, f32[896,768]{1,0:T(8,128)} %get-tuple-element.104.refs_0_.refs_2_, f32[896,768]{1,0:T(8,128)} %get-tuple-element.124.refs_3_, bf16[896,768]{1,0:T(8,128)(2,1)} %refs_4_.3, ...), custom_call_target="tpu_custom_call" | custom-call | flops 180000000 | tf_op jit(solution)/shard_map/finish/pallas_call | solution.py:1010
  (130 shorter events, 23.4 us)
Async XLA Ops:
  7.2 6.3 %copy-start.32 = (f32[24]{0:T(128)S(1)}, f32[24]{0:T(128)}, u32[]{:S(2)}) copy-start(f32[24]{0:T(128)} %param.15) | copy-start | bytes 292
  7.2 6.3 %copy-start.33 = (f32[24]{0:T(128)S(1)}, f32[24]{0:T(128)}, u32[]{:S(2)}) copy-start(f32[24]{0:T(128)} %param.20) | copy-start | bytes 292
  7.2 6.5 %copy-start.30 = (bf16[192,96]{1,0:T(8,128)(2,1)S(1)}, bf16[192,96]{1,0:T(8,128)(2,1)}, u32[]{:S(2)}) copy-start(bf16[192,96]{1,0:T(8,128)(2,1)} %param.19) | copy-start | bytes 110596
  7.2 7.0 %copy-start.27 = (bf16[96,192]{1,0:T(8,128)(2,1)S(1)}, bf16[96,192]{1,0:T(8,128)(2,1)}, u32[]{:S(2)}) copy-start(bf16[96,192]{1,0:T(8,128)(2,1)} %param.16) | copy-start | bytes 110596
  7.2 7.0 %copy-start.28 = (bf16[96,192]{1,0:T(8,128)(2,1)S(1)}, bf16[96,192]{1,0:T(8,128)(2,1)}, u32[]{:S(2)}) copy-start(bf16[96,192]{1,0:T(8,128)(2,1)} %param.17) | copy-start | bytes 110596
  7.2 7.0 %copy-start.29 = (bf16[96,192]{1,0:T(8,128)(2,1)S(1)}, bf16[96,192]{1,0:T(8,128)(2,1)}, u32[]{:S(2)}) copy-start(bf16[96,192]{1,0:T(8,128)(2,1)} %param.18) | copy-start | bytes 110596
  7.2 11.6 %copy-start.31 = (s32[3584]{0:T(1024)S(1)}, s32[3584]{0:T(1024)}, u32[]{:S(2)}) copy-start(s32[3584]{0:T(1024)} %param.26) | copy-start | bytes 43012
  7.2 186.6 %all-gather.3.cloned.1.call-start = ((), (), s32[]{:S(2)}) async-start(), calls=%async_computation | async-start | bytes 9732096 | tf_op jit(solution)/shard_map/all_gather | solution.py:1102
  8.5 22.9 %collective-permute-start = (bf16[512,768]{1,0:T(8,128)(2,1)S(1)}, bf16[512,768]{1,0:T(8,128)(2,1)S(1)}, u32[]{:S(2)}, u32[]{:S(2)}) collective-permute-start(bf16[512,768]{1,0:T(8,128)(2,1)S(1)} %slice.96), channel_id=1, source_target_pairs={{0,1},{1,2},{2,3},{4,5},{5,6},{6,7},{8,9},{9,10},{10,11},{12,13},{... | collective-permute-start | bytes 2359304 | tf_op jit(solution)/shard_map/ppermute | solution.py:1035
  14.4 25.9 %copy-start.15 = (bf16[96,896]{1,0:T(8,128)(2,1)}, bf16[96,896]{1,0:T(8,128)(2,1)S(1)}, u32[]{:S(2)}) copy-start(bf16[96,896]{1,0:T(8,128)(2,1)S(1)} %concatenate.19.refs_3_) | copy-start | bytes 516100
  14.4 25.9 %collective-permute-start.1 = (bf16[96,896]{1,0:T(8,128)(2,1)S(1)}, bf16[96,896]{1,0:T(8,128)(2,1)S(1)}, u32[]{:S(2)}, u32[]{:S(2)}) collective-permute-start(bf16[96,896]{1,0:T(8,128)(2,1)S(1)} %concatenate.19.refs_3_), channel_id=1, source_target_pairs={{0,1},{1,0},{2,3},{3,2},{4,5},{5,4},{6,7},{7,6},{8,9},{9,8},{10,11... | collective-permute-start | bytes 516104 | tf_op jit(solution)/shard_map/ppermute | solution.py:1031
  16.0 24.4 %collective-permute-start.2 = (bf16[96,896]{1,0:T(8,128)(2,1)S(1)}, bf16[96,896]{1,0:T(8,128)(2,1)S(1)}, u32[]{:S(2)}, u32[]{:S(2)}) collective-permute-start(bf16[96,896]{1,0:T(8,128)(2,1)S(1)} %concatenate.19.refs_3_), channel_id=1, source_target_pairs={{0,2},{1,3},{2,0},{3,1},{4,6},{5,7},{6,4},{7,5},{8,10},{9,11},{10,... | collective-permute-start | bytes 516104 | tf_op jit(solution)/shard_map/ppermute | solution.py:1031
  17.1 24.3 %collective-permute-start.3 = (bf16[96,896]{1,0:T(8,128)(2,1)S(1)}, bf16[96,896]{1,0:T(8,128)(2,1)S(1)}, u32[]{:S(2)}, u32[]{:S(2)}) collective-permute-start(bf16[96,896]{1,0:T(8,128)(2,1)S(1)} %concatenate.19.refs_3_), channel_id=1, source_target_pairs={{0,3},{1,2},{2,1},{3,0},{4,7},{5,6},{6,5},{7,4},{8,11},{9,10},{10,... | collective-permute-start | bytes 516104 | tf_op jit(solution)/shard_map/ppermute | solution.py:1031
  31.4 9.0 %copy-start.3 = (bf16[512,768]{1,0:T(8,128)(2,1)}, bf16[512,768]{1,0:T(8,128)(2,1)S(1)}, u32[]{:S(2)}) copy-start(bf16[512,768]{1,0:T(8,128)(2,1)S(1)} %collective-permute-done.refs_0_.a1_ref.r1_ref) | copy-start | bytes 2359300
  31.4 42.1 %collective-permute-start.11 = (bf16[512,768]{1,0:T(8,128)(2,1)S(1)}, bf16[512,768]{1,0:T(8,128)(2,1)S(1)}, u32[]{:S(2)}, u32[]{:S(2)}) collective-permute-start(bf16[512,768]{1,0:T(8,128)(2,1)S(1)} %collective-permute-done.refs_0_.a1_ref.r1_ref), channel_id=1, source_target_pairs={{1,2},{2,3},{5,6},{6,7},{9,10},{10,11},{13,14},{14,15},{17,18},{18... | collective-permute-start | bytes 2359304 | tf_op jit(solution)/shard_map/ppermute | solution.py:1035
  40.4 1.0 copy-start.24
  40.4 1.0 copy-start.25
  44.2 17.0 %collective-permute-start.5 = (bf16[96,3200]{1,0:T(8,128)(2,1)}, bf16[96,3200]{1,0:T(8,128)(2,1)S(1)}, u32[]{:S(2)}, u32[]{:S(2)}) collective-permute-start(bf16[96,3200]{1,0:T(8,128)(2,1)} %line.1.refs_4_), channel_id=1, source_target_pairs={{0,8},{4,12},{8,0},{12,4},{16,24},{20,28},{24,16},{28,20},{1,9},{5... | collective-permute-start | bytes 1843208 | tf_op jit(solution)/shard_map/ppermute | solution.py:1031
  45.7 27.8 %collective-permute-start.7 = (bf16[96,3200]{1,0:T(8,128)(2,1)}, bf16[96,3200]{1,0:T(8,128)(2,1)S(1)}, u32[]{:S(2)}, u32[]{:S(2)}) collective-permute-start(bf16[96,3200]{1,0:T(8,128)(2,1)} %line.1.refs_4_), channel_id=1, source_target_pairs={{0,16},{4,20},{8,24},{12,28},{16,0},{20,4},{24,8},{28,12},{1,17},{... | collective-permute-start | bytes 1843208 | tf_op jit(solution)/shard_map/ppermute | solution.py:1031
  47.2 26.3 %collective-permute-start.9 = (bf16[96,3200]{1,0:T(8,128)(2,1)}, bf16[96,3200]{1,0:T(8,128)(2,1)S(1)}, u32[]{:S(2)}, u32[]{:S(2)}) collective-permute-start(bf16[96,3200]{1,0:T(8,128)(2,1)} %line.1.refs_4_), channel_id=1, source_target_pairs={{0,24},{4,28},{8,16},{12,20},{16,8},{20,12},{24,0},{28,4},{1,25},{... | collective-permute-start | bytes 1843208 | tf_op jit(solution)/shard_map/ppermute | solution.py:1031
  61.2 13.1 %copy-start.8 = (bf16[96,3200]{1,0:T(8,128)(2,1)}, bf16[96,3200]{1,0:T(8,128)(2,1)S(1)}, u32[]{:S(2)}) copy-start(bf16[96,3200]{1,0:T(8,128)(2,1)S(1)} %collective-permute-done.5.refs_6_.refs_1_) | copy-start | bytes 1843204
  73.5 1.0 copy-start.9
  73.5 0.9 copy-start.10
  75.2 3.2 copy-start.7
  77.6 24.9 %collective-permute-start.12 = (bf16[512,768]{1,0:T(8,128)(2,1)}, bf16[512,768]{1,0:T(8,128)(2,1)S(1)}, u32[]{:S(2)}, u32[]{:S(2)}) collective-permute-start(bf16[512,768]{1,0:T(8,128)(2,1)} %copy-done.1), channel_id=1, source_target_pairs={{2,3},{6,7},{10,11},{14,15},{18,19},{22,23},{26,27},{30,31}} | collective-permute-start | bytes 2359304 | tf_op jit(solution)/shard_map/ppermute | solution.py:1035
  78.4 2.2 collective-permute-start.4
  78.4 11.9 %collective-permute-start.10 = (bf16[96,3200]{1,0:T(8,128)(2,1)}, bf16[96,3200]{1,0:T(8,128)(2,1)S(1)}, u32[]{:S(2)}, u32[]{:S(2)}) collective-permute-start(bf16[96,3200]{1,0:T(8,128)(2,1)} %copy-done.10), channel_id=1, source_target_pairs={{0,4},{4,0},{8,12},{12,8},{16,20},{20,16},{24,28},{28,24},{1,5},{5... | collective-permute-start | bytes 1843208 | tf_op jit(solution)/shard_map/ppermute | solution.py:1031
  78.9 11.4 %collective-permute-start.6 = (bf16[96,3200]{1,0:T(8,128)(2,1)}, bf16[96,3200]{1,0:T(8,128)(2,1)S(1)}, u32[]{:S(2)}, u32[]{:S(2)}) collective-permute-start(bf16[96,3200]{1,0:T(8,128)(2,1)} %copy-done.8), channel_id=1, source_target_pairs={{0,4},{4,0},{8,12},{12,8},{16,20},{20,16},{24,28},{28,24},{1,5},{5... | collective-permute-start | bytes 1843208 | tf_op jit(solution)/shard_map/ppermute | solution.py:1031
  79.0 11.3 %collective-permute-start.8 = (bf16[96,3200]{1,0:T(8,128)(2,1)}, bf16[96,3200]{1,0:T(8,128)(2,1)}, u32[]{:S(2)}, u32[]{:S(2)}) collective-permute-start(bf16[96,3200]{1,0:T(8,128)(2,1)} %copy-done.9), channel_id=1, source_target_pairs={{0,4},{4,0},{8,12},{12,8},{16,20},{20,16},{24,28},{28,24},{1,5},{5... | collective-permute-start | bytes 1843208 | tf_op jit(solution)/shard_map/ppermute | solution.py:1031
  80.6 9.8 %copy-start.16 = (bf16[96,3200]{1,0:T(8,128)(2,1)}, bf16[96,3200]{1,0:T(8,128)(2,1)S(1)}, u32[]{:S(2)}) copy-start(bf16[96,3200]{1,0:T(8,128)(2,1)S(1)} %collective-permute-done.4.refs_5_) | copy-start | bytes 1843204
  80.6 40.3 %collective-permute-start.13 = (bf16[384,768]{1,0:T(8,128)(2,1)}, bf16[384,768]{1,0:T(8,128)(2,1)S(1)}, u32[]{:S(2)}, u32[]{:S(2)}) collective-permute-start(bf16[384,768]{1,0:T(8,128)(2,1)} %get-tuple-element.73), channel_id=1, source_target_pairs={{0,1},{1,2},{2,3},{4,5},{5,6},{6,7},{8,9},{9,10},{10,11},{12,13},{... | collective-permute-start | bytes 1769480 | tf_op jit(solution)/shard_map/ppermute | solution.py:1035
  90.3 1.0 copy-start.18
  102.6 0.9 copy-start.2
  105.4 46.1 %collective-permute-start.14 = (bf16[384,768]{1,0:T(8,128)(2,1)}, bf16[384,768]{1,0:T(8,128)(2,1)S(1)}, u32[]{:S(2)}, u32[]{:S(2)}) collective-permute-start(bf16[384,768]{1,0:T(8,128)(2,1)} %join.2), channel_id=1, source_target_pairs={{0,2},{1,3},{4,6},{5,7},{8,10},{9,11},{12,14},{13,15},{16,18},{17,... | collective-permute-start | bytes 1769480 | tf_op jit(solution)/shard_map/ppermute | solution.py:1035
  115.5 36.0 %collective-permute-start.15 = (bf16[384,768]{1,0:T(8,128)(2,1)}, bf16[384,768]{1,0:T(8,128)(2,1)S(1)}, u32[]{:S(2)}, u32[]{:S(2)}) collective-permute-start(bf16[384,768]{1,0:T(8,128)(2,1)} %join.2), channel_id=1, source_target_pairs={{0,3},{4,7},{8,11},{12,15},{16,19},{20,23},{24,27},{28,31}} | collective-permute-start | bytes 1769480 | tf_op jit(solution)/shard_map/ppermute | solution.py:1035
  151.5 1.0 copy-start.21
  239.5 27.6 %collective-permute-start.16 = (bf16[4,4,96,1536]{3,2,1,0:T(8,128)(2,1)}, bf16[4,4,96,1536]{3,2,1,0:T(8,128)(2,1)}, u32[]{:S(2)}, u32[]{:S(2)}) collective-permute-start(bf16[4,4,96,1536]{3,2,1,0:T(8,128)(2,1)} %get-tuple-element.88), channel_id=1, source_target_pairs={{0,4},{4,0},{8,12},{12,8},{16,20},{20,16},{24,28},{28,24},{1,5},{5... | collective-permute-start | bytes 14155784 | tf_op jit(solution)/shard_map/ppermute | solution.py:1031
  283.3 35.0 %collective-permute-start.17 = (bf16[768,768]{1,0:T(8,128)(2,1)}, bf16[768,768]{1,0:T(8,128)(2,1)S(1)}, u32[]{:S(2)}, u32[]{:S(2)}) collective-permute-start(bf16[768,768]{1,0:T(8,128)(2,1)} %get-tuple-element.96.refs_0_.refs_1_), channel_id=1, source_target_pairs={{3,2},{1,0},{7,6},{5,4},{11,10},{9,8},{15,14},{13,12},{19,18},{17,... | collective-permute-start | bytes 3538952 | tf_op jit(solution)/shard_map/ppermute | solution.py:1035
  284.6 38.9 %collective-permute-start.18 = (bf16[4,96,1536]{2,1,0:T(8,128)(2,1)}, bf16[4,96,1536]{2,1,0:T(8,128)(2,1)S(1)}, u32[]{:S(2)}, u32[]{:S(2)}) collective-permute-start(bf16[4,96,1536]{2,1,0:T(8,128)(2,1)} %get-tuple-element.99), channel_id=1, source_target_pairs={{0,24},{4,28},{8,16},{12,20},{16,8},{20,12},{24,0},{28,4},{1,25},{... | collective-permute-start | bytes 3538952 | tf_op jit(solution)/shard_map/ppermute | solution.py:1031
  303.0 44.2 %collective-permute-start.19 = (bf16[768,768]{1,0:T(8,128)(2,1)}, bf16[768,768]{1,0:T(8,128)(2,1)}, u32[]{:S(2)}, u32[]{:S(2)}) collective-permute-start(bf16[768,768]{1,0:T(8,128)(2,1)} %join.3), channel_id=1, source_target_pairs={{3,2},{7,6},{11,10},{15,14},{19,18},{23,22},{27,26},{31,30}} | collective-permute-start | bytes 3538952 | tf_op jit(solution)/shard_map/ppermute | solution.py:1035
  304.7 45.4 %collective-permute-start.21 = (bf16[4,96,1536]{2,1,0:T(8,128)(2,1)}, bf16[4,96,1536]{2,1,0:T(8,128)(2,1)S(1)}, u32[]{:S(2)}, u32[]{:S(2)}) collective-permute-start(bf16[4,96,1536]{2,1,0:T(8,128)(2,1)} %get-tuple-element.110), channel_id=1, source_target_pairs={{0,8},{4,12},{8,0},{12,4},{16,24},{20,28},{24,16},{28,20},{1,9},{5... | collective-permute-start | bytes 3538952 | tf_op jit(solution)/shard_map/ppermute | solution.py:1031
  306.2 43.9 %collective-permute-start.22 = (bf16[4,96,1536]{2,1,0:T(8,128)(2,1)}, bf16[4,96,1536]{2,1,0:T(8,128)(2,1)}, u32[]{:S(2)}, u32[]{:S(2)}) collective-permute-start(bf16[4,96,1536]{2,1,0:T(8,128)(2,1)} %get-tuple-element.111), channel_id=1, source_target_pairs={{0,16},{4,20},{8,24},{12,28},{16,0},{20,4},{24,8},{28,12},{1,17},{... | collective-permute-start | bytes 3538952 | tf_op jit(solution)/shard_map/ppermute | solution.py:1031
  318.3 1.0 copy-start.14
  322.3 32.8 %collective-permute-start.23 = (bf16[768,768]{1,0:T(8,128)(2,1)}, bf16[768,768]{1,0:T(8,128)(2,1)S(1)}, u32[]{:S(2)}, u32[]{:S(2)}) collective-permute-start(bf16[768,768]{1,0:T(8,128)(2,1)} %total.3.refs_0_.refs_6_), channel_id=1, source_target_pairs={{2,0},{6,4},{10,8},{14,12},{18,16},{22,20},{26,24},{30,28}} | collective-permute-start | bytes 3538952 | tf_op jit(solution)/shard_map/ppermute | solution.py:1035
  323.5 1.0 copy-start.6
  350.1 1.0 copy-start.13
  355.0 1.1 copy-start.5
  356.1 9.0 %copy-start = (bf16[768,768]{1,0:T(8,128)(2,1)S(1)}, bf16[768,768]{1,0:T(8,128)(2,1)}, u32[]{:S(2)}) copy-start(bf16[768,768]{1,0:T(8,128)(2,1)} %total.4.refs_1_.refs_7_) | copy-start | bytes 3538948
  364.5 5.0 %collective-permute-start.24 = (bf16[4,96,1664]{2,1,0:T(8,128)(2,1)}, bf16[4,96,1664]{2,1,0:T(8,128)(2,1)}, u32[]{:S(2)}, u32[]{:S(2)}) collective-permute-start(bf16[4,96,1664]{2,1,0:T(8,128)(2,1)} %get-tuple-element.118), channel_id=1, source_target_pairs={{0,4},{4,0},{8,12},{12,8},{16,20},{20,16},{24,28},{28,24},{1,5},{5... | collective-permute-start | bytes 3833864 | tf_op jit(solution)/shard_map/ppermute | solution.py:1031
  364.5 4.8 %collective-permute-start.25 = (bf16[4,96,1536]{2,1,0:T(8,128)(2,1)}, bf16[4,96,1536]{2,1,0:T(8,128)(2,1)S(1)}, u32[]{:S(2)}, u32[]{:S(2)}) collective-permute-start(bf16[4,96,1536]{2,1,0:T(8,128)(2,1)} %get-tuple-element.119), channel_id=1, source_target_pairs={{0,4},{4,0},{8,12},{12,8},{16,20},{20,16},{24,28},{28,24},{1,5},{5... | collective-permute-start | bytes 3538952 | tf_op jit(solution)/shard_map/ppermute | solution.py:1031
  365.1 18.3 %collective-permute-start.20 = (bf16[768,768]{1,0:T(8,128)(2,1)S(1)}, bf16[768,768]{1,0:T(8,128)(2,1)S(1)}, u32[]{:S(2)}, u32[]{:S(2)}) collective-permute-start(bf16[768,768]{1,0:T(8,128)(2,1)S(1)} %copy-done), channel_id=1, source_target_pairs={{2,1},{6,5},{10,9},{14,13},{18,17},{22,21},{26,25},{30,29}} | collective-permute-start | bytes 3538952 | tf_op jit(solution)/shard_map/ppermute | solution.py:1035
  369.3 1.1 copy-start.12
  374.4 16.9 %collective-permute-start.26 = (bf16[96,3200]{1,0:T(8,128)(2,1)}, bf16[96,3200]{1,0:T(8,128)(2,1)S(1)}, u32[]{:S(2)}, u32[]{:S(2)}) collective-permute-start(bf16[96,3200]{1,0:T(8,128)(2,1)} %get-tuple-element.121), channel_id=1, source_target_pairs={{0,8},{4,12},{8,0},{12,4},{16,24},{20,28},{24,16},{28,20},{1,9},{5... | collective-permute-start | bytes 1843208 | tf_op jit(solution)/shard_map/ppermute | solution.py:1031
  375.8 29.1 %collective-permute-start.27 = (bf16[96,3200]{1,0:T(8,128)(2,1)}, bf16[96,3200]{1,0:T(8,128)(2,1)}, u32[]{:S(2)}, u32[]{:S(2)}) collective-permute-start(bf16[96,3200]{1,0:T(8,128)(2,1)} %get-tuple-element.122), channel_id=1, source_target_pairs={{0,16},{4,20},{8,24},{12,28},{16,0},{20,4},{24,8},{28,12},{1,17},{... | collective-permute-start | bytes 1843208 | tf_op jit(solution)/shard_map/ppermute | solution.py:1031
  376.4 28.5 %collective-permute-start.28 = (bf16[96,3200]{1,0:T(8,128)(2,1)}, bf16[96,3200]{1,0:T(8,128)(2,1)}, u32[]{:S(2)}, u32[]{:S(2)}) collective-permute-start(bf16[96,3200]{1,0:T(8,128)(2,1)} %get-tuple-element.123), channel_id=1, source_target_pairs={{0,24},{4,28},{8,16},{12,20},{16,8},{20,12},{24,0},{28,4},{1,25},{... | collective-permute-start | bytes 1843208 | tf_op jit(solution)/shard_map/ppermute | solution.py:1031
  379.7 44.2 %collective-permute-start.33 = (bf16[2,96,1536]{2,1,0:T(8,128)(2,1)}, bf16[2,96,1536]{2,1,0:T(8,128)(2,1)}, u32[]{:S(2)}, u32[]{:S(2)}) collective-permute-start(bf16[2,96,1536]{2,1,0:T(8,128)(2,1)} %get-tuple-element.126), channel_id=1, source_target_pairs={{0,2},{1,3},{2,0},{3,1},{4,6},{5,7},{6,4},{7,5},{8,10},{9,11},{10,... | collective-permute-start | bytes 1769480 | tf_op jit(solution)/shard_map/ppermute | solution.py:1031
  383.4 21.5 %copy-start.4 = (bf16[768,768]{1,0:T(8,128)(2,1)}, bf16[768,768]{1,0:T(8,128)(2,1)S(1)}, u32[]{:S(2)}) copy-start(bf16[768,768]{1,0:T(8,128)(2,1)S(1)} %collective-permute-done.20.refs_0_.refs_9_) | copy-start | bytes 3538948
  384.5 48.4 %collective-permute-start.29 = (bf16[128,768]{1,0:T(8,128)(2,1)S(1)}, bf16[128,768]{1,0:T(8,128)(2,1)S(1)}, u32[]{:S(2)}, u32[]{:S(2)}) collective-permute-start(bf16[128,768]{1,0:T(8,128)(2,1)S(1)} %fusion.2), channel_id=1, source_target_pairs={{1,0},{3,2},{5,4},{7,6},{9,8},{11,10},{13,12},{15,14},{17,16},{19,... | collective-permute-start | bytes 589832 | tf_op jit(solution)/shard_map/ppermute | solution.py:1035
  391.3 13.6 %copy-start.19 = (bf16[96,3200]{1,0:T(8,128)(2,1)}, bf16[96,3200]{1,0:T(8,128)(2,1)S(1)}, u32[]{:S(2)}) copy-start(bf16[96,3200]{1,0:T(8,128)(2,1)S(1)} %collective-permute-done.26.refs_2_) | copy-start | bytes 1843204
  410.0 32.0 %collective-permute-start.30 = (bf16[96,896]{1,0:T(8,128)(2,1)S(1)}, bf16[96,896]{1,0:T(8,128)(2,1)S(1)}, u32[]{:S(2)}, u32[]{:S(2)}) collective-permute-start(bf16[96,896]{1,0:T(8,128)(2,1)S(1)} %concatenate.21), channel_id=1, source_target_pairs={{0,1},{1,0},{2,3},{3,2},{4,5},{5,4},{6,7},{7,6},{8,9},{9,8},{10,11... | collective-permute-start | bytes 516104 | tf_op jit(solution)/shard_map/ppermute | solution.py:1031
  418.5 23.6 %collective-permute-start.31 = (bf16[96,896]{1,0:T(8,128)(2,1)S(1)}, bf16[96,896]{1,0:T(8,128)(2,1)S(1)}, u32[]{:S(2)}, u32[]{:S(2)}) collective-permute-start(bf16[96,896]{1,0:T(8,128)(2,1)S(1)} %concatenate.22), channel_id=1, source_target_pairs={{0,2},{1,3},{2,0},{3,1},{4,6},{5,7},{6,4},{7,5},{8,10},{9,11},{10,... | collective-permute-start | bytes 516104 | tf_op jit(solution)/shard_map/ppermute | solution.py:1031
  420.3 21.7 %collective-permute-start.32 = (bf16[96,896]{1,0:T(8,128)(2,1)S(1)}, bf16[96,896]{1,0:T(8,128)(2,1)S(1)}, u32[]{:S(2)}, u32[]{:S(2)}) collective-permute-start(bf16[96,896]{1,0:T(8,128)(2,1)S(1)} %concatenate.23), channel_id=1, source_target_pairs={{0,3},{1,2},{2,1},{3,0},{4,7},{5,6},{6,5},{7,4},{8,11},{9,10},{10,... | collective-permute-start | bytes 516104 | tf_op jit(solution)/shard_map/ppermute | solution.py:1031
  426.0 18.3 %collective-permute-start.34 = (bf16[96,1536]{1,0:T(8,128)(2,1)}, bf16[96,1536]{1,0:T(8,128)(2,1)S(1)}, u32[]{:S(2)}, u32[]{:S(2)}) collective-permute-start(bf16[96,1536]{1,0:T(8,128)(2,1)} %get-tuple-element.128), channel_id=1, source_target_pairs={{0,1},{1,0},{2,3},{3,2},{4,5},{5,4},{6,7},{7,6},{8,9},{9,8},{10,11... | collective-permute-start | bytes 884744 | tf_op jit(solution)/shard_map/ppermute | solution.py:1031
  442.0 2.3 copy-start.22
  (6 other events, 4.7 us)
Sparse Core Ops, SparseCore 0:
  77.8 116.0 all-gather.2

commit v5 on v4

--- a/solution.py
+++ b/solution.py
@@ -206,28 +206,6 @@
     )(*deps, x, *parts)
 
 
-def cores_kernel(at_ref, kept_ref, away_ref, *outs):
-    chip = at_ref[1] // 2
-    for m, out_ref in enumerate(outs):
-        out_ref[0] = (kept_ref[chip ^ m, 0].astype(F32) + away_ref[chip ^ m, 0].astype(F32)).astype(BF16)
-
-
-def meet_rest(at, kept, away):
-    chips, parts, rows, wide = kept.shape
-    block = pl.BlockSpec((chips, 1, rows, wide), lambda i: (0, i, 0, 0))
-    out = pl.BlockSpec((1, rows, wide), lambda i: (i, 0, 0))
-    return pl.pallas_call(
-        cores_kernel,
-        grid=(parts,),
-        in_specs=[SMEM, block, block],
-        out_specs=[out] * chips,
-        out_shape=[jax.ShapeDtypeStruct((parts, rows, wide), BF16)] * chips,
-        compiler_params=params(),
-        cost_estimate=cost(5),
-        name="meet_rest",
-    )(at, kept, away)
-
-
 def meet_kernel(count, at_ref, *refs):
     ins, outs = refs[:2 * count], refs[2 * count:]
     chip = at_ref[1] // 2
@@ -255,10 +233,11 @@
     )(*deps, at, *ins)
 
 
-def fold_kernel(at_ref, *refs):
-    ins, (keep_ref, send_ref) = refs[:-2], refs[-2:]
+def fold_kernel(at_ref, late_ref, in_ref, *refs):
+    ins, (keep_ref, send_ref, late_out) = refs[:-3], refs[-3:]
     t = at_ref[0]
     half = keep_ref.shape[0]
+    late_out[...] = (late_ref[...].astype(F32) + in_ref[...].astype(F32)).astype(BF16)
     for r in range(2 * half):
         got = sum((one[t ^ r].astype(F32) for one in ins[1:]), ins[0][t ^ r].astype(F32)).astype(BF16)
         if r < half:
@@ -267,19 +246,19 @@
             send_ref[r - half] = got
 
 
-def fold(deps, at, *blocks):
+def fold(deps, at, late, late_in, *blocks):
     parts, rows, wide = blocks[0].shape
     out = (parts // 2, rows, wide)
     return pl.pallas_call(
         after(len(deps), fold_kernel),
         grid=(1,),
-        in_specs=[ANY] * len(deps) + [SMEM] + [fixed(one.shape) for one in blocks],
-        out_specs=[fixed(out)] * 2,
-        out_shape=[jax.ShapeDtypeStruct(out, BF16)] * 2,
+        in_specs=[ANY] * len(deps) + [SMEM] + [fixed(one.shape) for one in (late, late_in, *blocks)],
+        out_specs=[fixed(out), fixed(out), fixed(late.shape)],
+        out_shape=[jax.ShapeDtypeStruct(out, BF16)] * 2 + [jax.ShapeDtypeStruct(late.shape, BF16)],
         compiler_params=params(),
         cost_estimate=cost(4),
         name="fold",
-    )(*deps, at, *blocks)
+    )(*deps, at, late, late_in, *blocks)
 
 
 def middle_kernel(keep_ref, got_ref, mine_ref, send_ref):
@@ -794,12 +773,13 @@
     )(meta, slots, q, do, o, logs, *near, *far, *tab)
 
 
-def back_near_kernel(meta_ref, q_ref, do_ref, o_ref, l_ref, kn_ref, vn_ref, k_ref, v_ref, cos_ref, sin_ref, part_ref,
-                     dq_ref, dk_ref, dv_ref, dke_ref, dve_ref, own_ref, ko_ref, vo_ref, kt_ref, dk_acc, dv_acc):
+def back_near_kernel(meta_ref, q_ref, do_ref, o_ref, l_ref, kn_ref, vn_ref, k_ref, v_ref, cos_ref, sin_ref, part_ref, late_ref,
+                     dq_ref, dk_ref, dv_ref, dke_ref, dve_ref, copy_ref, own_ref, ko_ref, vo_ref, kt_ref, dk_acc, dv_acc):
     @pl.when(pl.program_id(0) == 0)
     def _():
         fill_bias(None, own_ref, 0)
 
+    copy_ref[...] = late_ref[...]
     line_up(ko_ref, kn_ref, k_ref)
     line_up(vo_ref, vn_ref, v_ref)
     kt_ref[...] = ko_ref[...].T
@@ -837,27 +817,31 @@
     dv_ref[...] = dv_acc[mine, :].astype(BF16)
 
 
-def back_near(deps, meta, q, do, o, logs, near, own, tab, dq_part):
+def back_near(deps, meta, q, do, o, logs, near, own, tab, dq_part, late):
     loc, d = do.shape
     n = ROOT + TILE
     return pl.pallas_call(
         after(len(deps), back_near_kernel),
         grid=(d // 128,),
         in_specs=[ANY] * len(deps) + [SMEM, pair(loc), pair(loc), pair(loc), log_spec(loc), pair(n), pair(n), pair(loc), pair(loc)]
-        + [fixed(one.shape) for one in tab] + [turned(loc)],
-        out_specs=[pair(loc)] * 3 + [pair(TILE)] * 2,
-        out_shape=[shape(loc, d, BF16)] * 3 + [shape(TILE, d, BF16)] * 2,
+        + [fixed(one.shape) for one in tab] + [turned(loc), pair(late.shape[0])],
+        out_specs=[pair(loc)] * 3 + [pair(TILE)] * 2 + [pair(late.shape[0])],
+        out_shape=[shape(loc, d, BF16)] * 3 + [shape(TILE, d, BF16)] * 2 + [shape(late.shape[0], d, BF16)],
         scratch_shapes=[bias_scratch(0)[1], line_scratch(loc, BF16), line_scratch(loc, BF16),
                         pltpu.VMEM((128, loc + 2 * TILE), BF16), line_scratch(loc, F32), line_scratch(loc, F32)],
         compiler_params=params(),
         cost_estimate=cost(25),
         name="back_near",
-    )(*deps, meta, q, do, o, logs, *near, *own, *tab, dq_part)
-
-
-def spread_kernel(dk_ref, dv_ref, xn_ref, xs_ref, wk_ref, wv_ref, early_ref, late_ref, sum_ref):
+    )(*deps, meta, q, do, o, logs, *near, *own, *tab, dq_part, late)
+
+
+def spread_kernel(at_ref, kept_ref, away_ref, dk_ref, dv_ref, xn_ref, xs_ref, wk_ref, wv_ref, early_ref, late_ref, sum_ref, *outs):
     step = pl.program_id(0)
+    chip = at_ref[1] // 2
+    for m, out_ref in enumerate(outs):
+        out_ref[0] = (kept_ref[chip ^ m, 0].astype(F32) + away_ref[chip ^ m, 0].astype(F32)).astype(BF16)
     da = dot(dk_ref[...], wk_ref[...], COLS) + dot(dv_ref[...], wv_ref[...], COLS)
+    n = da.shape[0]
 
     def gain_part(part, x):
         x = x.astype(F32)
@@ -865,30 +849,44 @@
 
     @pl.when(step == 0)
     def _():
-        early_ref[...] = da.astype(BF16)
         sum_ref[...] = jnp.zeros_like(sum_ref)
-        sum_ref[0:1, :] = gain_part(da[:ROOT], xn_ref[pl.ds(0, ROOT), :]) + gain_part(da[ROOT:], xs_ref[pl.ds(0, BLOCK), :])
-
-    @pl.when(step == 1)
-    def _():
-        late_ref[...] = da.astype(BF16)
-        sum_ref[0:1, :] += gain_part(da, xs_ref[pl.ds(BLOCK, FAR - EARLY), :])
-
-
-def spread(deps, dk, dv, x_near, x_slot, w):
+
+    for i in range(FAR // n):
+        @pl.when(step == i)
+        def _():
+            near = max(min(ROOT - i * n, n), 0)
+            got = jnp.zeros((1, da.shape[1]), F32)
+            if near:
+                got = got + gain_part(da[:near], xn_ref[pl.ds(i * n, near), :])
+            if near < n:
+                got = got + gain_part(da[near:], xs_ref[pl.ds(i * n + near - ROOT, n - near), :])
+            sum_ref[0:1, :] += got
+            if i * n < EARLY:
+                early_ref[...] = da.astype(BF16)
+            else:
+                late_ref[...] = da.astype(BF16)
+
+
+def spread(at, kept, away, dk, dv, x_near, x_slot, w):
     d = w.shape[0]
-    once = pl.BlockSpec((EARLY, d), lambda i: (0, 0))
-    return pl.pallas_call(
-        after(len(deps), spread_kernel),
-        grid=(2,),
-        in_specs=[ANY] * len(deps) + [tiled(EARLY, d), tiled(EARLY, d), fixed(x_near.shape), fixed(x_slot.shape),
-                                      weight(d, 1), weight(d, 2)],
-        out_specs=[once, once, pl.BlockSpec((8, d), lambda i: (0, 0))],
-        out_shape=[shape(EARLY, d, BF16), shape(FAR - EARLY, d, BF16), shape(8, d, F32)],
-        compiler_params=params(),
-        cost_estimate=cost(6),
+    chips, parts, rows, wide = kept.shape
+    n = FAR // parts
+    half = EARLY // n
+    block = pl.BlockSpec((chips, 1, rows, wide), lambda i: (0, i, 0, 0))
+    out = pl.BlockSpec((1, rows, wide), lambda i: (i, 0, 0))
+    got = pl.pallas_call(
+        spread_kernel,
+        grid=(parts,),
+        in_specs=[SMEM, block, block, tiled(n, d), tiled(n, d), fixed(x_near.shape), fixed(x_slot.shape), weight(d, 1), weight(d, 2)],
+        out_specs=[pl.BlockSpec((n, d), lambda i: (jnp.minimum(i, half - 1), 0)), pl.BlockSpec((n, d), lambda i: (jnp.maximum(i - half, 0), 0)),
+                   pl.BlockSpec((8, d), lambda i: (0, 0))] + [out] * chips,
+        out_shape=[shape(EARLY, d, BF16), shape(FAR - EARLY, d, BF16), shape(8, d, F32)]
+        + [jax.ShapeDtypeStruct((parts, rows, wide), BF16)] * chips,
+        compiler_params=params(),
+        cost_estimate=cost(9),
         name="spread",
-    )(*deps, dk, dv, x_near, x_slot, w, w)
+    )(at, kept, away, dk, dv, x_near, x_slot, w, w)
+    return got[0], got[1], got[2], got[3:]
 
 
 def own_back_kernel(x_ref, xe_ref, dq_ref, dk_ref, dv_ref, dke_ref, dve_ref, wq_ref, wk_ref, wv_ref, da_ref, edge_ref, sum_ref):
@@ -1088,9 +1086,8 @@
     pieces = [None] * d_size
     for m in range(0, d_size, 2):
         pieces[m] = swap(lined, "dp", m) if m else lined
-    ready = (a2, *(pieces[m] for m in range(2, d_size, 2)))
-    rest, front = begin(ready, tokens, w_gate, w_up, w_down.T)
-    b1 = send(front, *up)
+    b1 = send(join((lined,), tokens[ROOT:]), *up)
+    rest = join((a2, b1, *(pieces[m] for m in range(2, d_size, 2))), w_gate, w_up, w_down.T)
     a3 = send(a2, *up[2:])
     for m in range(0, d_size, 2):
         pieces[m + 1] = swap(pieces[m], "dp", 1)
@@ -1101,8 +1098,8 @@
         pieces = [whole]
     rest = lax.all_gather(rest, ("dp", "tensor"), axis=0, tiled=False).reshape(d_size, t_size, rows, 3 * hid)
     w, gains, a_own, q, k_own, v_own = project_own((), at, tokens, tab, pieces)
-    front = join((a3, k_own), tokens[ROOT:])
-    b2 = send(front, (0, 2), (1, 3))
+    again, front = begin((a3, k_own), tokens, b1)
+    b2 = send(again, *up[1:])
     b3 = send(front, (0, 3))
     x_near, a_near, k_near, v_near = project_near(at, tokens, a1, a2, a3, b1, gains, w, tab)
     near, own = (k_near, v_near), (k_own, v_own)
@@ -1114,21 +1111,19 @@
     mixed, do, dhb, dh, ffn_sum, kept, away = feed_forward(at, tokens, o, cotangent, gains, w, rest)
     away = swap(away, "dp", 1)
     dq_part, dk_far, dv_far = back_far(meta, slots, q, do, o, logs, near, far, tab)
-    rest_blocks = meet_rest(at, kept, away)
-    early, late, far_sum = spread((rest_blocks[0],), dk_far, dv_far, x_near, x_slot, w)
+    early, late, far_sum, rest_blocks = spread(at, kept, away, dk_far, dv_far, x_near, x_slot, w)
     moved = [swap(block, "dp", 2 * m) for m, block in enumerate(rest_blocks) if m]
     early_in = send(early, (3, 2), (1, 0))
-    dq, dk, dv, dke, dve = back_near((early,), meta, q, do, o, logs, near, own, tab, dq_part)
-    late_in = send(join((dq,), late), (3, 2))
+    dq, dk, dv, dke, dve, late = back_near((early,), meta, q, do, o, logs, near, own, tab, dq_part, late)
+    late_in = send(late, (3, 2))
     early = total((dq,), early, early_in)
     early_in = send(early, (2, 0))
     da, edge, own_sum = own_back((early, moved[-1]), tokens, x_near, dq, dk, dv, dke, dve, w)
     kept_b, away_b = weight_sums(
         second_kernel, (da,), at, (a_own, a_near, a_slot, dk, dv, dk_far, dv_far, dke, dve), d_size, 0)
     away_b = swap(away_b, "dp", 1)
-    keep, away = fold((kept_b,), at, rest_blocks[0], *moved)
+    keep, away, late = fold((kept_b,), at, late, late_in, rest_blocks[0], *moved)
     away = swap(away, "tensor", 2)
-    late = total((kept_b,), late, late_in)
     late_in = send(late, (2, 1))
     kept_a, away_a = weight_sums(
         first_kernel, (keep, late, early_in), at, (far_sum, own_sum, ffn_sum, a_own, dq, dhb, o), d_size, GAIN_LANES)

time: 459 us -> 440 us (0.959)
  waiting for transfers between devices: 99.4 us -> 73.4 us
  starting transfers between devices: 64.7 us -> 78.4 us
  Pallas kernels: 240 us -> 234 us
    ppermute x24, waiting for transfers between devices: 53.5 us -> 30.2 us  [swap(): lax.ppermute(x, axis, [(i, i ^ mask) for i in range(lax.axis_size(axis))])]
    ppermute x11, starting transfers between devices: 33.2 us -> 46.9 us  [send(): return lax.ppermute(x, 'tensor', list(pairs))]
    all_gather x1, waiting for transfers between devices: 15.1 us -> 1.66 us  [per_device(): lax.all_gather(rest, ('dp', 'tensor'), axis=0, tiled=False)]
    ppermute x11, waiting for transfers between devices: 30.8 us -> 41.6 us  [send(): return lax.ppermute(x, 'tensor', list(pairs))]
    pallas_call x2 -> x1, Pallas kernels: 16.2 us -> 12.8 us  [spread(): pl.pallas_call(spread_kernel, grid=(parts,), in_specs=[SMEM, block, block...]
    unnamed x70 -> x68, local copies, waits for them, and re-layouts: 12.6 us -> 11 us
  transfers between devices with their start and end apart: 36 -> 36, of which waited for: 13 -> 16; matrix products, arithmetic and copies ran while one was open for 4% -> 4% of each run, Pallas kernels for 37% -> 38%
where the time goes in v5:
time: 440 us; the launch traced here: 433 us
  Pallas kernels  234 us (53%)
  starting transfers between devices  78.4 us (18%)
  waiting for transfers between devices  73.4 us (17%)
  local copies, waits for them, and re-layouts  20.9 us (5%)
  between operations  15.7 us (4%)
  other arithmetic  10.3 us (2%)
    ppermute x11, starting transfers between devices, send(): return lax.ppermute(x, 'tensor', list(pairs))  46.9 us
    pallas_call x1, Pallas kernels, feed_forward(): pl.pallas_call(ffn_kernel, grid=(steps + parts,), in_specs=[SMEM, tile, t...  45.7 us
    ppermute x11, waiting for transfers between devices, send(): return lax.ppermute(x, 'tensor', list(pairs))  41.6 us
    ppermute x24, starting transfers between devices, swap(): lax.ppermute(x, axis, [(i, i ^ mask) for i in range(lax.axis_size(axis))])  31.5 us
    ppermute x24, waiting for transfers between devices, swap(): lax.ppermute(x, axis, [(i, i ^ mask) for i in range(lax.axis_size(axis))])  30.2 us
    pallas_call x1, Pallas kernels, back_far(): pl.pallas_call(back_far_kernel, grid=(d // 128,), in_specs=[SMEM, SMEM, p...  27.3 us
    pallas_call x1, Pallas kernels, attend_near(): pl.pallas_call(attend_near_kernel, grid=(d // 128,), in_specs=[SMEM, pair...  22.3 us
    pallas_call x2, Pallas kernels, weight_sums(): pl.pallas_call(after(len(deps), kernel), grid=(steps,), in_specs=[ANY] *...  21.4 us
  transfers between devices with their start and end apart: 36, of which 16 were waited for; matrix products, arithmetic and copies ran while one was open for 4% of the time, Pallas kernels for 38%

profile of v5, /device:TPU:0, one launch (start us, length us, event | category | flops | bytes accessed | tf_op | source)
XLA Modules:
  0.0 432.9 jit_solution(10195954905091714352)
XLA Ops:
  7.3 1.2 slice.96
  8.5 5.0 %collective-permute-start = (bf16[512,768]{1,0:T(8,128)(2,1)S(1)}, bf16[512,768]{1,0:T(8,128)(2,1)S(1)}, u32[]{:S(2)}, u32[]{:S(2)}) collective-permute-start(bf16[512,768]{1,0:T(8,128)(2,1)S(1)} %slice.96), channel_id=1, source_target_pairs={{0,1},{1,2},{2,3},{4,5},{5,6},{6,7},{8,9},{9,10},{10,11},{12,13},{... | collective-permute-start | bytes 2359304 | tf_op jit(solution)/shard_map/ppermute | solution.py:1033
  14.4 1.4 collective-permute-start.3
  15.8 1.7 collective-permute-start.2
  17.5 1.4 collective-permute-start.1
  19.0 12.4 %collective-permute-done.refs_0_.a1_ref.r1_ref = bf16[512,768]{1,0:T(8,128)(2,1)S(1)} collective-permute-done((bf16[512,768]{1,0:T(8,128)(2,1)S(1)}, bf16[512,768]{1,0:T(8,128)(2,1)S(1)}, u32[]{:S(2)}, u32[]{:S(2)}) %collective-permute-start) | collective-permute-done | bytes 786464 | tf_op jit(solution)/shard_map/ppermute | solution.py:1033
  32.1 8.3 %fusion = (f32[3584,128]{1,0:T(8,128)}, f32[3584,128]{1,0:T(8,128)}) fusion(f32[128]{0:T(128)S(1)} %get-tuple-element.199, f32[128]{0:T(128)S(1)} %get-tuple-element.200, f32[3584]{0:T(1024)S(1)} %convert_element_type.39), kind=kLoop, calls=%fused_computation.2 | loop fusion | flops 917504 | bytes 3685376 | tf_op jit(solution)/shard_map/mul | solution.py:1025
  40.4 0.9 collective-permute-done.1.refs_4_
  42.0 2.2 line.1.refs_4_.refs_0_
  44.2 2.4 collective-permute-start.9
  47.6 1.9 slice.97.refs_1_
  49.6 1.9 join.2
  51.5 13.7 %collective-permute-start.13 = (bf16[384,768]{1,0:T(8,128)(2,1)}, bf16[384,768]{1,0:T(8,128)(2,1)S(1)}, u32[]{:S(2)}, u32[]{:S(2)}) collective-permute-start(bf16[384,768]{1,0:T(8,128)(2,1)} %join.2), channel_id=1, source_target_pairs={{0,1},{1,2},{2,3},{4,5},{5,6},{6,7},{8,9},{9,10},{10,11},{12,13},{... | collective-permute-start | bytes 1769480 | tf_op jit(solution)/shard_map/ppermute | solution.py:1033
  65.3 7.7 %collective-permute-done.13.refs_3_.b1_ref.f1_ref.refs_1_ = bf16[384,768]{1,0:T(8,128)(2,1)S(1)} collective-permute-done((bf16[384,768]{1,0:T(8,128)(2,1)}, bf16[384,768]{1,0:T(8,128)(2,1)S(1)}, u32[]{:S(2)}, u32[]{:S(2)}) %collective-permute-start.13) | collective-permute-done | bytes 589856 | tf_op jit(solution)/shard_map/ppermute | solution.py:1033
  74.4 1.8 join.3
  79.2 1.8 collective-permute-done.10.refs_11_
  81.0 1.0 collective-permute-done.8.refs_9_
  82.8 11.2 %project_own.1 = (bf16[768,3072]{1,0:T(8,128)(2,1)}, f32[8,768]{1,0:T(8,128)}, bf16[896,768]{1,0:T(8,128)(2,1)}, bf16[896,768]{1,0:T(8,128)(2,1)}, bf16[896,768]{1,0:T(8,128)(2,1)}, /*index=5*/bf16[896,768]{1,0:T(8,128)(2,1)}) custom-call(s32[2]{0:T(128)} %pad_add_fusion.refs_0_.at_ref.refs_1_.refs_3_, bf16[896,768]{1,0:T(8,128)(2,1)} %refs_4_.1, ...), custom_call_target="tpu_custom_call" | custom-call | flops 300000000 | tf_op jit(solution)/shard_map/project_own/pallas_call | solution.py:318
  93.9 0.9 copy-done.3
  94.8 2.6 begin.1
  98.1 20.8 %collective-permute-start.15 = (bf16[384,768]{1,0:T(8,128)(2,1)}, bf16[384,768]{1,0:T(8,128)(2,1)S(1)}, u32[]{:S(2)}, u32[]{:S(2)}) collective-permute-start(bf16[384,768]{1,0:T(8,128)(2,1)} %get-tuple-element.77), channel_id=1, source_target_pairs={{0,3},{4,7},{8,11},{12,15},{16,19},{20,23},{24,27},{28,31}} | collective-permute-start | bytes 1769480 | tf_op jit(solution)/shard_map/ppermute | solution.py:1033
  118.8 2.2 plan.1
  121.0 7.6 %project_near.1 = (bf16[640,768]{1,0:T(8,128)(2,1)}, bf16[640,768]{1,0:T(8,128)(2,1)}, bf16[640,768]{1,0:T(8,128)(2,1)}, bf16[640,768]{1,0:T(8,128)(2,1)}) custom-call(s32[2]{0:T(128)} %pad_add_fusion.refs_0_.at_ref.refs_1_.refs_3_, bf16[896,768]{1,0:T(8,128)(2,1)} %refs_4_.1, bf16[512,768]{1,0:T(8,128)(2,1)} %copy-done.1, bf16[512,768]{1,0:T(8,128)(2,1)} %copy-done.2, ...), custom_call_target="tpu_custom_call" | custom-call | flops 150000000 | tf_op jit(solution)/shard_map/project_near/pallas_call | solution.py:364
  128.6 22.3 %attend_near.1 = (f32[768,896]{1,0:T(8,128)}, f32[6,8,896]{2,1,0:T(8,128)}) custom-call(s32[8,8]{1,0:T(8,128)} %get-tuple-element.72.meta_ref.refs_1_, bf16[896,768]{1,0:T(8,128)(2,1)} %get-tuple-element.73.q_ref.refs_2_, bf16[640,768]{1,0:T(8,128)(2,1)} %get-tuple-element.82.kn_ref.refs_6_, bf16[640,768]{1,0:T(8,128)(2,1)} %get-tuple-element.83.vn_ref.refs_7_, ...), custom_call_target="tpu_custom_call" | custom-call | flops 600000000 | tf_op jit(solution)/shard_map/attend_near/pallas_call | solution.py:534
  152.0 10.0 %project_far.1 = (bf16[1024,768]{1,0:T(8,128)(2,1)}, bf16[1024,768]{1,0:T(8,128)(2,1)}, bf16[1024,768]{1,0:T(8,128)(2,1)}, bf16[1024,768]{1,0:T(8,128)(2,1)}) custom-call(s32[8,8]{1,0:T(8,128)} %get-tuple-element.72.meta_ref.refs_1_, s32[8,8]{1,0:T(8,128)} %get-tuple-element.74.slot_ref, bf16[896,768]{1,0:T(8,128)(2,1)} %refs_4_.1, ...), custom_call_target="tpu_custom_call" | custom-call | flops 210000000 | tf_op jit(solution)/shard_map/project_far/pallas_call | solution.py:415
  161.9 15.8 %attend_far.1 = (bf16[896,768]{1,0:T(8,128)(2,1)}, f32[6,8,896]{2,1,0:T(8,128)}) custom-call(s32[8,8]{1,0:T(8,128)} %get-tuple-element.72.meta_ref.refs_1_, bf16[896,768]{1,0:T(8,128)(2,1)} %get-tuple-element.73.q_ref.refs_2_, bf16[1024,768]{1,0:T(8,128)(2,1)} %get-tuple-element.80.ks_ref, bf16[1024,768]{1,0:T(8,128)(2,1)} %get-tuple-element.81.vs_ref, ...), custom_call_target="tpu_custom_call" | custom-call | flops 270000000 | tf_op jit(solution)/shard_map/attend_far/pallas_call | solution.py:575
  177.7 1.7 all-gather.3.cloned.1.call-done
  179.4 45.7 %feed_forward.1 = (bf16[896,768]{1,0:T(8,128)(2,1)}, bf16[896,768]{1,0:T(8,128)(2,1)}, bf16[896,768]{1,0:T(8,128)(2,1)}, f32[896,768]{1,0:T(8,128)}, f32[8,768]{...) custom-call(s32[2]{0:T(128)} %pad_add_fusion.refs_0_.at_ref.refs_1_.refs_3_, ...), custom_call_target="tpu_custom_call" | custom-call | flops 1200000000 | tf_op jit(solution)/shard_map/feed_forward/pallas_call | solution.py:675
  225.4 27.3 %back_far.1 = (f32[768,896]{1,0:T(8,128)}, bf16[1536,768]{1,0:T(8,128)(2,1)}, bf16[1536,768]{1,0:T(8,128)(2,1)}) custom-call(s32[8,8]{1,0:T(8,128)} %get-tuple-element.72.meta_ref.refs_1_, s32[8,8]{1,0:T(8,128)} %get-tuple-element.74.slot_ref, bf16[896,768]{1,0:T(8,128)(2,1)} %get-tuple-element.73.q_ref.refs_2_, ...), custom_call_target="tpu_custom_call" | custom-call | flops 1500000000 | tf_op jit(solution)/shard_map/back_far/pallas_call | solution.py:761
  252.7 12.8 %spread.1 = (bf16[768,768]{1,0:T(8,128)(2,1)}, bf16[768,768]{1,0:T(8,128)(2,1)}, f32[8,768]{1,0:T(8,128)}, bf16[4,96,1536]{2,1,0:T(8,128)(2,1)}, bf16[4,96,1536]...) custom-call(s32[2]{0:T(128)} %pad_add_fusion.refs_0_.at_ref.refs_1_.refs_3_, ...), custom_call_target="tpu_custom_call" | custom-call | flops 270000000 | tf_op jit(solution)/shard_map/spread/pallas_call | solution.py:877
  265.5 1.3 collective-permute-start.17
  266.8 1.5 collective-permute-start.18
  268.4 14.6 %back_near.1 = (bf16[896,768]{1,0:T(8,128)(2,1)}, bf16[896,768]{1,0:T(8,128)(2,1)}, bf16[896,768]{1,0:T(8,128)(2,1)}, bf16[128,768]{1,0:T(8,128)(2,1)}, bf16[128...) custom-call(bf16[768,768]{1,0:T(8,128)(2,1)} %get-tuple-element.97.refs_0_.refs_1_, ...), custom_call_target="tpu_custom_call" | custom-call | flops 750000000 | tf_op jit(solution)/shard_map/back_near/pallas_call | solution.py:823
  283.7 1.5 collective-permute-start.20
  285.8 14.7 %collective-permute-done.17.refs_2_ = bf16[768,768]{1,0:T(8,128)(2,1)S(1)} collective-permute-done((bf16[768,768]{1,0:T(8,128)(2,1)}, bf16[768,768]{1,0:T(8,128)(2,1)S(1)}, u32[]{:S(2)}, u32[]{:S(2)}) %collective-permute-start.17) | collective-permute-done | bytes 1179680 | tf_op jit(solution)/shard_map/ppermute | solution.py:1033
  300.5 1.0 copy-done.13
  301.5 2.9 total.2.refs_0_.refs_6_
  304.4 1.3 collective-permute-start.23
  305.7 1.0 copy-done.8
  306.7 9.6 %own_back.1 = (f32[896,768]{1,0:T(8,128)}, bf16[128,768]{1,0:T(8,128)(2,1)}, f32[8,768]{1,0:T(8,128)}) custom-call(bf16[768,768]{1,0:T(8,128)(2,1)} %total.2.refs_0_.refs_6_, bf16[4,96,1536]{2,1,0:T(8,128)(2,1)} %copy-done.8, bf16[896,768]{1,0:T(8,128)(2,1)} %refs_4_.1, bf16[640,768]{1,0:T(8,128)(2,1)} %get-tuple-element.95.xn_ref.refs_3_, ...), custom_call_target="tpu_custom_call" | custom-call | flops 180000000 | tf_op jit(solution)/shard_map/own_back/pallas_call | solution.py:915
  316.4 13.0 %weight_sums.2 = (bf16[4,96,1536]{2,1,0:T(8,128)(2,1)}, bf16[4,96,1536]{2,1,0:T(8,128)(2,1)}) custom-call(f32[896,768]{1,0:T(8,128)} %get-tuple-element.106.refs_0_.refs_2_, s32[2]{0:T(128)} %pad_add_fusion.refs_0_.at_ref.refs_1_.refs_3_, bf16[896,768]{1,0:T(8,128)(2,1)} %get-tuple-element.107.refs_2_.refs_7_, bf16[640,768]{1,0:T(8,128)(2,1)} %get-tuple-element.108.refs_3_, ...), custom_call_target="tpu_custom_call" | custom-call | flops 240000000 | tf_op jit(solution)/shard_map/weight_sums/pallas_call | solution.py:966
  329.4 1.0 copy-done.12
  330.4 5.0 %fold.1 = (bf16[2,96,1536]{2,1,0:T(8,128)(2,1)}, bf16[2,96,1536]{2,1,0:T(8,128)(2,1)}, bf16[768,768]{1,0:T(8,128)(2,1)}) custom-call(bf16[4,96,1536]{2,1,0:T(8,128)(2,1)} %get-tuple-element.110.refs_0_.refs_2_, s32[2]{0:T(128)} %pad_add_fusion.refs_0_.at_ref.refs_1_.refs_3_, bf16[768,768]{1,0:T(8,128)(2,1)} %get-tuple-element.111.refs_2_, ...), custom_call_target="tpu_custom_call" | custom-call | flops 120000000 | tf_op jit(solution)/shard_map/fold/pallas_call | solution.py:252
  335.4 1.1 copy-done.7
  336.5 8.4 %weight_sums.3 = (bf16[4,96,1664]{2,1,0:T(8,128)(2,1)}, bf16[4,96,1664]{2,1,0:T(8,128)(2,1)}) custom-call(bf16[2,96,1536]{2,1,0:T(8,128)(2,1)} %get-tuple-element.116.refs_0_.refs_1_, bf16[768,768]{1,0:T(8,128)(2,1)} %get-tuple-element.115.refs_1_.refs_7_, bf16[768,768]{1,0:T(8,128)(2,1)} %copy-done.7, s32[2]{0:T(128)} %pad_add_fusion.refs_0_.at_ref.refs_1_.refs_3_, ...), custom_call_target="tpu_custom_call" | custom-call | flops 240000000 | tf_op jit(solution)/shard_map/weight_sums/pallas_call | solution.py:966
  346.2 3.5 collective-permute-done.25.refs_4_
  350.0 0.8 copy-done.11
  350.8 4.0 meet.1
  354.8 1.4 collective-permute-start.26
  356.8 1.5 collective-permute-start.28
  358.3 1.2 slice.98
  360.1 3.7 collective-permute-start.33
  363.8 1.1 fusion.2
  365.0 1.3 collective-permute-start.29
  366.3 5.4 %collective-permute-done.26.refs_2_ = bf16[96,3200]{1,0:T(8,128)(2,1)S(1)} collective-permute-done((bf16[96,3200]{1,0:T(8,128)(2,1)}, bf16[96,3200]{1,0:T(8,128)(2,1)S(1)}, u32[]{:S(2)}, u32[]{:S(2)}) %collective-permute-start.26) | collective-permute-done | bytes 614432 | tf_op jit(solution)/shard_map/ppermute | solution.py:1029
  371.7 13.6 %collective-permute-done.27.refs_3_ = bf16[96,3200]{1,0:T(8,128)(2,1)} collective-permute-done((bf16[96,3200]{1,0:T(8,128)(2,1)}, bf16[96,3200]{1,0:T(8,128)(2,1)}, u32[]{:S(2)}, u32[]{:S(2)}) %collective-permute-start.27) | collective-permute-done | bytes 614432 | tf_op jit(solution)/shard_map/ppermute | solution.py:1029
  385.3 2.8 total.3.refs_0_
  388.1 1.4 fusion.11
  390.4 8.3 %collective-permute-start.30 = (bf16[96,896]{1,0:T(8,128)(2,1)S(1)}, bf16[96,896]{1,0:T(8,128)(2,1)S(1)}, u32[]{:S(2)}, u32[]{:S(2)}) collective-permute-start(bf16[96,896]{1,0:T(8,128)(2,1)S(1)} %concatenate.21), channel_id=1, source_target_pairs={{0,1},{1,0},{2,3},{3,2},{4,5},{5,4},{6,7},{7,6},{8,9},{9,8},{10,11... | collective-permute-start | bytes 516104 | tf_op jit(solution)/shard_map/ppermute | solution.py:1029
  398.9 1.7 collective-permute-start.31
  401.5 2.8 collective-permute-done.33.refs_2_
  404.3 2.2 middle.1
  406.6 6.8 %collective-permute-done.29.refs_10_ = bf16[128,768]{1,0:T(8,128)(2,1)S(1)} collective-permute-done((bf16[128,768]{1,0:T(8,128)(2,1)S(1)}, bf16[128,768]{1,0:T(8,128)(2,1)S(1)}, u32[]{:S(2)}, u32[]{:S(2)}) %collective-permute-start.29) | collective-permute-done | bytes 196640 | tf_op jit(solution)/shard_map/ppermute | solution.py:1033
  414.0 8.4 %finish.1 = f32[896,768]{1,0:T(8,128)} custom-call(bf16[96,3200]{1,0:T(8,128)(2,1)} %total.3.refs_0_, s32[8,8]{1,0:T(8,128)} %get-tuple-element.72.meta_ref.refs_1_, f32[896,768]{1,0:T(8,128)} %get-tuple-element.106.refs_0_.refs_2_, f32[896,768]{1,0:T(8,128)} %get-tuple-element.128.refs_3_, bf16[896,768]{1,0:T(8,128)(2,1)} %refs_4_.1, ...), custom_call_target="tpu_custom_call" | custom-call | flops 180000000 | tf_op jit(solution)/shard_map/finish/pallas_call | solution.py:1008
  (126 shorter events, 20.0 us)
Async XLA Ops:
  7.2 6.3 %copy-start.32 = (f32[24]{0:T(128)S(1)}, f32[24]{0:T(128)}, u32[]{:S(2)}) copy-start(f32[24]{0:T(128)} %param.20) | copy-start | bytes 292
  7.2 6.3 %copy-start.31 = (f32[24]{0:T(128)S(1)}, f32[24]{0:T(128)}, u32[]{:S(2)}) copy-start(f32[24]{0:T(128)} %param.15) | copy-start | bytes 292
  7.2 6.5 %copy-start.29 = (bf16[192,96]{1,0:T(8,128)(2,1)S(1)}, bf16[192,96]{1,0:T(8,128)(2,1)}, u32[]{:S(2)}) copy-start(bf16[192,96]{1,0:T(8,128)(2,1)} %param.19) | copy-start | bytes 110596
  7.2 7.0 %copy-start.28 = (bf16[96,192]{1,0:T(8,128)(2,1)S(1)}, bf16[96,192]{1,0:T(8,128)(2,1)}, u32[]{:S(2)}) copy-start(bf16[96,192]{1,0:T(8,128)(2,1)} %param.18) | copy-start | bytes 110596
  7.2 7.0 %copy-start.27 = (bf16[96,192]{1,0:T(8,128)(2,1)S(1)}, bf16[96,192]{1,0:T(8,128)(2,1)}, u32[]{:S(2)}) copy-start(bf16[96,192]{1,0:T(8,128)(2,1)} %param.17) | copy-start | bytes 110596
  7.2 7.0 %copy-start.26 = (bf16[96,192]{1,0:T(8,128)(2,1)S(1)}, bf16[96,192]{1,0:T(8,128)(2,1)}, u32[]{:S(2)}) copy-start(bf16[96,192]{1,0:T(8,128)(2,1)} %param.16) | copy-start | bytes 110596
  7.2 11.6 %copy-start.30 = (s32[3584]{0:T(1024)S(1)}, s32[3584]{0:T(1024)}, u32[]{:S(2)}) copy-start(s32[3584]{0:T(1024)} %param.26) | copy-start | bytes 43012
  7.2 172.1 %all-gather.3.cloned.1.call-start = ((), (), s32[]{:S(2)}) async-start(), calls=%async_computation | async-start | bytes 9732096 | tf_op jit(solution)/shard_map/all_gather | solution.py:1099
  8.5 22.9 %collective-permute-start = (bf16[512,768]{1,0:T(8,128)(2,1)S(1)}, bf16[512,768]{1,0:T(8,128)(2,1)S(1)}, u32[]{:S(2)}, u32[]{:S(2)}) collective-permute-start(bf16[512,768]{1,0:T(8,128)(2,1)S(1)} %slice.96), channel_id=1, source_target_pairs={{0,1},{1,2},{2,3},{4,5},{5,6},{6,7},{8,9},{9,10},{10,11},{12,13},{... | collective-permute-start | bytes 2359304 | tf_op jit(solution)/shard_map/ppermute | solution.py:1033
  14.4 26.0 %copy-start.14 = (bf16[96,896]{1,0:T(8,128)(2,1)}, bf16[96,896]{1,0:T(8,128)(2,1)S(1)}, u32[]{:S(2)}) copy-start(bf16[96,896]{1,0:T(8,128)(2,1)S(1)} %concatenate.19.refs_3_) | copy-start | bytes 516100
  14.4 25.9 %collective-permute-start.3 = (bf16[96,896]{1,0:T(8,128)(2,1)S(1)}, bf16[96,896]{1,0:T(8,128)(2,1)S(1)}, u32[]{:S(2)}, u32[]{:S(2)}) collective-permute-start(bf16[96,896]{1,0:T(8,128)(2,1)S(1)} %concatenate.19.refs_3_), channel_id=1, source_target_pairs={{0,3},{1,2},{2,1},{3,0},{4,7},{5,6},{6,5},{7,4},{8,11},{9,10},{10,... | collective-permute-start | bytes 516104 | tf_op jit(solution)/shard_map/ppermute | solution.py:1029
  15.8 24.6 %collective-permute-start.2 = (bf16[96,896]{1,0:T(8,128)(2,1)S(1)}, bf16[96,896]{1,0:T(8,128)(2,1)S(1)}, u32[]{:S(2)}, u32[]{:S(2)}) collective-permute-start(bf16[96,896]{1,0:T(8,128)(2,1)S(1)} %concatenate.19.refs_3_), channel_id=1, source_target_pairs={{0,2},{1,3},{2,0},{3,1},{4,6},{5,7},{6,4},{7,5},{8,10},{9,11},{10,... | collective-permute-start | bytes 516104 | tf_op jit(solution)/shard_map/ppermute | solution.py:1029
  17.5 23.9 %collective-permute-start.1 = (bf16[96,896]{1,0:T(8,128)(2,1)S(1)}, bf16[96,896]{1,0:T(8,128)(2,1)S(1)}, u32[]{:S(2)}, u32[]{:S(2)}) collective-permute-start(bf16[96,896]{1,0:T(8,128)(2,1)S(1)} %concatenate.19.refs_3_), channel_id=1, source_target_pairs={{0,1},{1,0},{2,3},{3,2},{4,5},{5,4},{6,7},{7,6},{8,9},{9,8},{10,11... | collective-permute-start | bytes 516104 | tf_op jit(solution)/shard_map/ppermute | solution.py:1029
  31.4 9.0 %copy-start.1 = (bf16[512,768]{1,0:T(8,128)(2,1)}, bf16[512,768]{1,0:T(8,128)(2,1)S(1)}, u32[]{:S(2)}) copy-start(bf16[512,768]{1,0:T(8,128)(2,1)S(1)} %collective-permute-done.refs_0_.a1_ref.r1_ref) | copy-start | bytes 2359300
  31.4 42.0 %collective-permute-start.11 = (bf16[512,768]{1,0:T(8,128)(2,1)S(1)}, bf16[512,768]{1,0:T(8,128)(2,1)S(1)}, u32[]{:S(2)}, u32[]{:S(2)}) collective-permute-start(bf16[512,768]{1,0:T(8,128)(2,1)S(1)} %collective-permute-done.refs_0_.a1_ref.r1_ref), channel_id=1, source_target_pairs={{1,2},{2,3},{5,6},{6,7},{9,10},{10,11},{13,14},{14,15},{17,18},{18... | collective-permute-start | bytes 2359304 | tf_op jit(solution)/shard_map/ppermute | solution.py:1033
  40.4 1.0 copy-start.23
  40.4 1.0 copy-start.24
  44.2 28.8 %collective-permute-start.9 = (bf16[96,3200]{1,0:T(8,128)(2,1)}, bf16[96,3200]{1,0:T(8,128)(2,1)S(1)}, u32[]{:S(2)}, u32[]{:S(2)}) collective-permute-start(bf16[96,3200]{1,0:T(8,128)(2,1)} %line.1.refs_4_.refs_0_), channel_id=1, source_target_pairs={{0,24},{4,28},{8,16},{12,20},{16,8},{20,12},{24,0},{28,4},{1,25},{... | collective-permute-start | bytes 1843208 | tf_op jit(solution)/shard_map/ppermute | solution.py:1029
  46.6 26.6 %collective-permute-start.7 = (bf16[96,3200]{1,0:T(8,128)(2,1)}, bf16[96,3200]{1,0:T(8,128)(2,1)S(1)}, u32[]{:S(2)}, u32[]{:S(2)}) collective-permute-start(bf16[96,3200]{1,0:T(8,128)(2,1)} %line.1.refs_4_.refs_0_), channel_id=1, source_target_pairs={{0,16},{4,20},{8,24},{12,28},{16,0},{20,4},{24,8},{28,12},{1,17},{... | collective-permute-start | bytes 1843208 | tf_op jit(solution)/shard_map/ppermute | solution.py:1029
  47.1 26.3 %collective-permute-start.5 = (bf16[96,3200]{1,0:T(8,128)(2,1)}, bf16[96,3200]{1,0:T(8,128)(2,1)}, u32[]{:S(2)}, u32[]{:S(2)}) collective-permute-start(bf16[96,3200]{1,0:T(8,128)(2,1)} %line.1.refs_4_.refs_0_), channel_id=1, source_target_pairs={{0,8},{4,12},{8,0},{12,4},{16,24},{20,28},{24,16},{28,20},{1,9},{5... | collective-permute-start | bytes 1843208 | tf_op jit(solution)/shard_map/ppermute | solution.py:1029
  51.5 21.4 %collective-permute-start.13 = (bf16[384,768]{1,0:T(8,128)(2,1)}, bf16[384,768]{1,0:T(8,128)(2,1)S(1)}, u32[]{:S(2)}, u32[]{:S(2)}) collective-permute-start(bf16[384,768]{1,0:T(8,128)(2,1)} %join.2), channel_id=1, source_target_pairs={{0,1},{1,2},{2,3},{4,5},{5,6},{6,7},{8,9},{9,10},{10,11},{12,13},{... | collective-permute-start | bytes 1769480 | tf_op jit(solution)/shard_map/ppermute | solution.py:1033
  72.9 1.0 copy-start.9
  73.2 1.0 copy-start.10
  73.4 1.1 copy-start.2
  74.4 2.5 copy-start.6
  76.2 17.7 %collective-permute-start.12 = (bf16[512,768]{1,0:T(8,128)(2,1)}, bf16[512,768]{1,0:T(8,128)(2,1)S(1)}, u32[]{:S(2)}, u32[]{:S(2)}) collective-permute-start(bf16[512,768]{1,0:T(8,128)(2,1)} %copy-done.2), channel_id=1, source_target_pairs={{2,3},{6,7},{10,11},{14,15},{18,19},{22,23},{26,27},{30,31}} | collective-permute-start | bytes 2359304 | tf_op jit(solution)/shard_map/ppermute | solution.py:1033
  77.0 2.2 collective-permute-start.4
  77.1 3.9 collective-permute-start.10
  77.6 4.4 %collective-permute-start.8 = (bf16[96,3200]{1,0:T(8,128)(2,1)}, bf16[96,3200]{1,0:T(8,128)(2,1)S(1)}, u32[]{:S(2)}, u32[]{:S(2)}) collective-permute-start(bf16[96,3200]{1,0:T(8,128)(2,1)} %copy-done.10), channel_id=1, source_target_pairs={{0,4},{4,0},{8,12},{12,8},{16,20},{20,16},{24,28},{28,24},{1,5},{5... | collective-permute-start | bytes 1843208 | tf_op jit(solution)/shard_map/ppermute | solution.py:1029
  77.6 4.3 collective-permute-start.6
  79.2 2.8 copy-start.15
  81.0 1.0 copy-start.16
  93.9 0.9 copy-start.3
  97.4 53.6 %collective-permute-start.14 = (bf16[384,768]{1,0:T(8,128)(2,1)}, bf16[384,768]{1,0:T(8,128)(2,1)S(1)}, u32[]{:S(2)}, u32[]{:S(2)}) collective-permute-start(bf16[384,768]{1,0:T(8,128)(2,1)} %get-tuple-element.76), channel_id=1, source_target_pairs={{1,2},{2,3},{5,6},{6,7},{9,10},{10,11},{13,14},{14,15},{17,18},{18... | collective-permute-start | bytes 1769480 | tf_op jit(solution)/shard_map/ppermute | solution.py:1033
  98.1 52.9 %collective-permute-start.15 = (bf16[384,768]{1,0:T(8,128)(2,1)}, bf16[384,768]{1,0:T(8,128)(2,1)S(1)}, u32[]{:S(2)}, u32[]{:S(2)}) collective-permute-start(bf16[384,768]{1,0:T(8,128)(2,1)} %get-tuple-element.77), channel_id=1, source_target_pairs={{0,3},{4,7},{8,11},{12,15},{16,19},{20,23},{24,27},{28,31}} | collective-permute-start | bytes 1769480 | tf_op jit(solution)/shard_map/ppermute | solution.py:1033
  151.0 1.0 copy-start.20
  225.1 27.6 %collective-permute-start.16 = (bf16[4,4,96,1536]{3,2,1,0:T(8,128)(2,1)}, bf16[4,4,96,1536]{3,2,1,0:T(8,128)(2,1)}, u32[]{:S(2)}, u32[]{:S(2)}) collective-permute-start(bf16[4,4,96,1536]{3,2,1,0:T(8,128)(2,1)} %get-tuple-element.90), channel_id=1, source_target_pairs={{0,4},{4,0},{8,12},{12,8},{16,20},{20,16},{24,28},{28,24},{1,5},{5... | collective-permute-start | bytes 14155784 | tf_op jit(solution)/shard_map/ppermute | solution.py:1029
  265.5 35.0 %collective-permute-start.17 = (bf16[768,768]{1,0:T(8,128)(2,1)}, bf16[768,768]{1,0:T(8,128)(2,1)S(1)}, u32[]{:S(2)}, u32[]{:S(2)}) collective-permute-start(bf16[768,768]{1,0:T(8,128)(2,1)} %get-tuple-element.97.refs_0_.refs_1_), channel_id=1, source_target_pairs={{3,2},{1,0},{7,6},{5,4},{11,10},{9,8},{15,14},{13,12},{19,18},{17,... | collective-permute-start | bytes 3538952 | tf_op jit(solution)/shard_map/ppermute | solution.py:1033
  266.8 38.9 %collective-permute-start.18 = (bf16[4,96,1536]{2,1,0:T(8,128)(2,1)}, bf16[4,96,1536]{2,1,0:T(8,128)(2,1)S(1)}, u32[]{:S(2)}, u32[]{:S(2)}) collective-permute-start(bf16[4,96,1536]{2,1,0:T(8,128)(2,1)} %get-tuple-element.101), channel_id=1, source_target_pairs={{0,24},{4,28},{8,16},{12,20},{16,8},{20,12},{24,0},{28,4},{1,25},{... | collective-permute-start | bytes 3538952 | tf_op jit(solution)/shard_map/ppermute | solution.py:1029
  283.0 46.4 %collective-permute-start.19 = (bf16[768,768]{1,0:T(8,128)(2,1)}, bf16[768,768]{1,0:T(8,128)(2,1)S(1)}, u32[]{:S(2)}, u32[]{:S(2)}) collective-permute-start(bf16[768,768]{1,0:T(8,128)(2,1)} %get-tuple-element.111.refs_2_), channel_id=1, source_target_pairs={{3,2},{7,6},{11,10},{15,14},{19,18},{23,22},{27,26},{31,30}} | collective-permute-start | bytes 3538952 | tf_op jit(solution)/shard_map/ppermute | solution.py:1033
  283.7 45.6 %collective-permute-start.20 = (bf16[4,96,1536]{2,1,0:T(8,128)(2,1)}, bf16[4,96,1536]{2,1,0:T(8,128)(2,1)}, u32[]{:S(2)}, u32[]{:S(2)}) collective-permute-start(bf16[4,96,1536]{2,1,0:T(8,128)(2,1)} %get-tuple-element.113), channel_id=1, source_target_pairs={{0,8},{4,12},{8,0},{12,4},{16,24},{20,28},{24,16},{28,20},{1,9},{5... | collective-permute-start | bytes 3538952 | tf_op jit(solution)/shard_map/ppermute | solution.py:1029
  285.3 44.1 %collective-permute-start.21 = (bf16[4,96,1536]{2,1,0:T(8,128)(2,1)}, bf16[4,96,1536]{2,1,0:T(8,128)(2,1)}, u32[]{:S(2)}, u32[]{:S(2)}) collective-permute-start(bf16[4,96,1536]{2,1,0:T(8,128)(2,1)} %get-tuple-element.114), channel_id=1, source_target_pairs={{0,16},{4,20},{8,24},{12,28},{16,0},{20,4},{24,8},{28,12},{1,17},{... | collective-permute-start | bytes 3538952 | tf_op jit(solution)/shard_map/ppermute | solution.py:1029
  300.5 1.0 copy-start.13
  304.4 31.0 %collective-permute-start.23 = (bf16[768,768]{1,0:T(8,128)(2,1)}, bf16[768,768]{1,0:T(8,128)(2,1)S(1)}, u32[]{:S(2)}, u32[]{:S(2)}) collective-permute-start(bf16[768,768]{1,0:T(8,128)(2,1)} %total.2.refs_0_.refs_6_), channel_id=1, source_target_pairs={{2,0},{6,4},{10,8},{14,12},{18,16},{22,20},{26,24},{30,28}} | collective-permute-start | bytes 3538952 | tf_op jit(solution)/shard_map/ppermute | solution.py:1033
  305.7 1.0 copy-start.8
  329.3 1.1 copy-start.12
  335.4 1.1 copy-start.7
  336.5 9.0 %copy-start.4 = (bf16[768,768]{1,0:T(8,128)(2,1)S(1)}, bf16[768,768]{1,0:T(8,128)(2,1)}, u32[]{:S(2)}) copy-start(bf16[768,768]{1,0:T(8,128)(2,1)} %get-tuple-element.115.refs_1_.refs_7_) | copy-start | bytes 3538948
  344.9 5.0 %collective-permute-start.24 = (bf16[4,96,1664]{2,1,0:T(8,128)(2,1)}, bf16[4,96,1664]{2,1,0:T(8,128)(2,1)}, u32[]{:S(2)}, u32[]{:S(2)}) collective-permute-start(bf16[4,96,1664]{2,1,0:T(8,128)(2,1)} %get-tuple-element.122), channel_id=1, source_target_pairs={{0,4},{4,0},{8,12},{12,8},{16,20},{20,16},{24,28},{28,24},{1,5},{5... | collective-permute-start | bytes 3833864 | tf_op jit(solution)/shard_map/ppermute | solution.py:1029
  344.9 4.8 %collective-permute-start.25 = (bf16[4,96,1536]{2,1,0:T(8,128)(2,1)}, bf16[4,96,1536]{2,1,0:T(8,128)(2,1)S(1)}, u32[]{:S(2)}, u32[]{:S(2)}) collective-permute-start(bf16[4,96,1536]{2,1,0:T(8,128)(2,1)} %get-tuple-element.123), channel_id=1, source_target_pairs={{0,4},{4,0},{8,12},{12,8},{16,20},{20,16},{24,28},{28,24},{1,5},{5... | collective-permute-start | bytes 3538952 | tf_op jit(solution)/shard_map/ppermute | solution.py:1029
  345.5 18.4 %collective-permute-start.22 = (bf16[768,768]{1,0:T(8,128)(2,1)S(1)}, bf16[768,768]{1,0:T(8,128)(2,1)S(1)}, u32[]{:S(2)}, u32[]{:S(2)}) collective-permute-start(bf16[768,768]{1,0:T(8,128)(2,1)S(1)} %copy-done.4), channel_id=1, source_target_pairs={{2,1},{6,5},{10,9},{14,13},{18,17},{22,21},{26,25},{30,29}} | collective-permute-start | bytes 3538952 | tf_op jit(solution)/shard_map/ppermute | solution.py:1033
  349.7 1.1 copy-start.11
  354.8 16.9 %collective-permute-start.26 = (bf16[96,3200]{1,0:T(8,128)(2,1)}, bf16[96,3200]{1,0:T(8,128)(2,1)S(1)}, u32[]{:S(2)}, u32[]{:S(2)}) collective-permute-start(bf16[96,3200]{1,0:T(8,128)(2,1)} %get-tuple-element.125), channel_id=1, source_target_pairs={{0,8},{4,12},{8,0},{12,4},{16,24},{20,28},{24,16},{28,20},{1,9},{5... | collective-permute-start | bytes 1843208 | tf_op jit(solution)/shard_map/ppermute | solution.py:1029
  356.2 29.1 %collective-permute-start.27 = (bf16[96,3200]{1,0:T(8,128)(2,1)}, bf16[96,3200]{1,0:T(8,128)(2,1)}, u32[]{:S(2)}, u32[]{:S(2)}) collective-permute-start(bf16[96,3200]{1,0:T(8,128)(2,1)} %get-tuple-element.126), channel_id=1, source_target_pairs={{0,16},{4,20},{8,24},{12,28},{16,0},{20,4},{24,8},{28,12},{1,17},{... | collective-permute-start | bytes 1843208 | tf_op jit(solution)/shard_map/ppermute | solution.py:1029
  356.8 28.5 %collective-permute-start.28 = (bf16[96,3200]{1,0:T(8,128)(2,1)}, bf16[96,3200]{1,0:T(8,128)(2,1)}, u32[]{:S(2)}, u32[]{:S(2)}) collective-permute-start(bf16[96,3200]{1,0:T(8,128)(2,1)} %get-tuple-element.127), channel_id=1, source_target_pairs={{0,24},{4,28},{8,16},{12,20},{16,8},{20,12},{24,0},{28,4},{1,25},{... | collective-permute-start | bytes 1843208 | tf_op jit(solution)/shard_map/ppermute | solution.py:1029
  360.1 44.2 %collective-permute-start.33 = (bf16[2,96,1536]{2,1,0:T(8,128)(2,1)}, bf16[2,96,1536]{2,1,0:T(8,128)(2,1)}, u32[]{:S(2)}, u32[]{:S(2)}) collective-permute-start(bf16[2,96,1536]{2,1,0:T(8,128)(2,1)} %get-tuple-element.130), channel_id=1, source_target_pairs={{0,2},{1,3},{2,0},{3,1},{4,6},{5,7},{6,4},{7,5},{8,10},{9,11},{10,... | collective-permute-start | bytes 1769480 | tf_op jit(solution)/shard_map/ppermute | solution.py:1029
  363.8 21.5 %copy-start.5 = (bf16[768,768]{1,0:T(8,128)(2,1)}, bf16[768,768]{1,0:T(8,128)(2,1)S(1)}, u32[]{:S(2)}) copy-start(bf16[768,768]{1,0:T(8,128)(2,1)S(1)} %collective-permute-done.22.refs_0_.refs_9_) | copy-start | bytes 3538948
  365.0 48.4 %collective-permute-start.29 = (bf16[128,768]{1,0:T(8,128)(2,1)S(1)}, bf16[128,768]{1,0:T(8,128)(2,1)S(1)}, u32[]{:S(2)}, u32[]{:S(2)}) collective-permute-start(bf16[128,768]{1,0:T(8,128)(2,1)S(1)} %fusion.2), channel_id=1, source_target_pairs={{1,0},{3,2},{5,4},{7,6},{9,8},{11,10},{13,12},{15,14},{17,16},{19,... | collective-permute-start | bytes 589832 | tf_op jit(solution)/shard_map/ppermute | solution.py:1033
  371.7 13.6 %copy-start.18 = (bf16[96,3200]{1,0:T(8,128)(2,1)}, bf16[96,3200]{1,0:T(8,128)(2,1)S(1)}, u32[]{:S(2)}) copy-start(bf16[96,3200]{1,0:T(8,128)(2,1)S(1)} %collective-permute-done.26.refs_2_) | copy-start | bytes 1843204
  390.4 32.0 %collective-permute-start.30 = (bf16[96,896]{1,0:T(8,128)(2,1)S(1)}, bf16[96,896]{1,0:T(8,128)(2,1)S(1)}, u32[]{:S(2)}, u32[]{:S(2)}) collective-permute-start(bf16[96,896]{1,0:T(8,128)(2,1)S(1)} %concatenate.21), channel_id=1, source_target_pairs={{0,1},{1,0},{2,3},{3,2},{4,5},{5,4},{6,7},{7,6},{8,9},{9,8},{10,11... | collective-permute-start | bytes 516104 | tf_op jit(solution)/shard_map/ppermute | solution.py:1029
  398.9 23.5 %collective-permute-start.31 = (bf16[96,896]{1,0:T(8,128)(2,1)S(1)}, bf16[96,896]{1,0:T(8,128)(2,1)S(1)}, u32[]{:S(2)}, u32[]{:S(2)}) collective-permute-start(bf16[96,896]{1,0:T(8,128)(2,1)S(1)} %concatenate.22), channel_id=1, source_target_pairs={{0,2},{1,3},{2,0},{3,1},{4,6},{5,7},{6,4},{7,5},{8,10},{9,11},{10,... | collective-permute-start | bytes 516104 | tf_op jit(solution)/shard_map/ppermute | solution.py:1029
  400.7 21.7 %collective-permute-start.32 = (bf16[96,896]{1,0:T(8,128)(2,1)S(1)}, bf16[96,896]{1,0:T(8,128)(2,1)S(1)}, u32[]{:S(2)}, u32[]{:S(2)}) collective-permute-start(bf16[96,896]{1,0:T(8,128)(2,1)S(1)} %concatenate.23), channel_id=1, source_target_pairs={{0,3},{1,2},{2,1},{3,0},{4,7},{5,6},{6,5},{7,4},{8,11},{9,10},{10,... | collective-permute-start | bytes 516104 | tf_op jit(solution)/shard_map/ppermute | solution.py:1029
  406.4 18.3 %collective-permute-start.34 = (bf16[96,1536]{1,0:T(8,128)(2,1)}, bf16[96,1536]{1,0:T(8,128)(2,1)S(1)}, u32[]{:S(2)}, u32[]{:S(2)}) collective-permute-start(bf16[96,1536]{1,0:T(8,128)(2,1)} %get-tuple-element.132), channel_id=1, source_target_pairs={{0,1},{1,0},{2,3},{3,2},{4,5},{5,4},{6,7},{7,6},{8,9},{9,8},{10,11... | collective-permute-start | bytes 884744 | tf_op jit(solution)/shard_map/ppermute | solution.py:1029
  422.4 2.3 copy-start.21
  (5 other events, 3.8 us)
Sparse Core Ops, SparseCore 0:
  76.4 102.9 all-gather.2

commit v6 on v5

--- a/solution.py
+++ b/solution.py
@@ -1081,13 +1081,13 @@
     others = [pack] + [swap(pack, "tensor", m) for m in range(1, t_size)]
     meta, slots = plan(at[:1], segment_ids, parent_ids, tiles)
     tab = tables(positions)
-    lined = line((a1, *tab), others)
+    lined = line((a1,), others)
     a2 = send(a1, *up[1:])
     pieces = [None] * d_size
     for m in range(0, d_size, 2):
         pieces[m] = swap(lined, "dp", m) if m else lined
     b1 = send(join((lined,), tokens[ROOT:]), *up)
-    rest = join((a2, b1, *(pieces[m] for m in range(2, d_size, 2))), w_gate, w_up, w_down.T)
+    rest = join((a2, b1, *tab, *(pieces[m] for m in range(2, d_size, 2))), w_gate, w_up, w_down.T)
     a3 = send(a2, *up[2:])
     for m in range(0, d_size, 2):
         pieces[m + 1] = swap(pieces[m], "dp", 1)

time: 440 us -> 451 us (1.025)
  waiting for transfers between devices: 73.4 us -> 84.8 us
    ppermute x24, waiting for transfers between devices: 30.2 us -> 54.7 us  [swap(): lax.ppermute(x, axis, [(i, i ^ mask) for i in range(lax.axis_size(axis))])]
    ppermute x11, waiting for transfers between devices: 41.6 us -> 23.6 us  [send(): return lax.ppermute(x, 'tensor', list(pairs))]
    all_gather x1, waiting for transfers between devices: 1.66 us -> 6.41 us  [per_device(): lax.all_gather(rest, ('dp', 'tensor'), axis=0, tiled=False)]
    unnamed x68 -> x70, local copies, waits for them, and re-layouts: 11 us -> 11.6 us
  transfers between devices with their start and end apart: 36 -> 36, of which waited for: 16 -> 17; matrix products, arithmetic and copies ran while one was open for 4% -> 4% of each run, Pallas kernels for 38% -> 37%
where the time goes in v6:
time: 451 us; the launch traced here: 444 us
  Pallas kernels  234 us (52%)
  waiting for transfers between devices  84.8 us (19%)
  starting transfers between devices  77.6 us (17%)
  local copies, waits for them, and re-layouts  21.6 us (5%)
  between operations  15.7 us (3%)
  other arithmetic  10.3 us (2%)
    ppermute x24, waiting for transfers between devices, swap(): lax.ppermute(x, axis, [(i, i ^ mask) for i in range(lax.axis_size(axis))])  54.7 us
    ppermute x11, starting transfers between devices, send(): return lax.ppermute(x, 'tensor', list(pairs))  46.1 us
    pallas_call x1, Pallas kernels, feed_forward(): pl.pallas_call(ffn_kernel, grid=(steps + parts,), in_specs=[SMEM, tile, t...  45.7 us
    ppermute x24, starting transfers between devices, swap(): lax.ppermute(x, axis, [(i, i ^ mask) for i in range(lax.axis_size(axis))])  31.5 us
    pallas_call x1, Pallas kernels, back_far(): pl.pallas_call(back_far_kernel, grid=(d // 128,), in_specs=[SMEM, SMEM, p...  27.2 us
    ppermute x11, waiting for transfers between devices, send(): return lax.ppermute(x, 'tensor', list(pairs))  23.6 us
    pallas_call x1, Pallas kernels, attend_near(): pl.pallas_call(attend_near_kernel, grid=(d // 128,), in_specs=[SMEM, pair...  22.3 us
    pallas_call x2, Pallas kernels, weight_sums(): pl.pallas_call(after(len(deps), kernel), grid=(steps,), in_specs=[ANY] *...  21.4 us
  transfers between devices with their start and end apart: 36, of which 17 were waited for; matrix products, arithmetic and copies ran while one was open for 4% of the time, Pallas kernels for 37%

profile of v6, /device:TPU:0, one launch (start us, length us, event | category | flops | bytes accessed | tf_op | source)
XLA Modules:
  0.0 444.3 jit_solution(4762533018183932142)
XLA Ops:
  7.3 1.2 slice.96
  8.5 5.0 %collective-permute-start = (bf16[512,768]{1,0:T(8,128)(2,1)S(1)}, bf16[512,768]{1,0:T(8,128)(2,1)S(1)}, u32[]{:S(2)}, u32[]{:S(2)}) collective-permute-start(bf16[512,768]{1,0:T(8,128)(2,1)S(1)} %slice.96), channel_id=1, source_target_pairs={{0,1},{1,2},{2,3},{4,5},{5,6},{6,7},{8,9},{9,10},{10,11},{12,13},{... | collective-permute-start | bytes 2359304 | tf_op jit(solution)/shard_map/ppermute | solution.py:1033
  14.4 1.4 collective-permute-start.3
  15.8 1.7 collective-permute-start.2
  17.5 1.4 collective-permute-start.1
  18.9 2.0 slice.97.refs_1_
  20.9 14.2 %collective-permute-done.3.refs_4_ = bf16[96,896]{1,0:T(8,128)(2,1)S(1)} collective-permute-done((bf16[96,896]{1,0:T(8,128)(2,1)S(1)}, bf16[96,896]{1,0:T(8,128)(2,1)S(1)}, u32[]{:S(2)}, u32[]{:S(2)}) %collective-permute-start.3) | collective-permute-done | bytes 172064 | tf_op jit(solution)/shard_map/ppermute | solution.py:1029
  35.1 3.7 collective-permute-done.2.refs_3_
  38.8 2.5 collective-permute-done.1.refs_2_
  42.0 0.9 copy-done.1
  42.9 2.2 line.1.refs_4_.refs_0_
  45.0 2.4 collective-permute-start.9
  48.5 1.9 join.2
  50.4 7.2 %collective-permute-start.13 = (bf16[384,768]{1,0:T(8,128)(2,1)}, bf16[384,768]{1,0:T(8,128)(2,1)S(1)}, u32[]{:S(2)}, u32[]{:S(2)}) collective-permute-start(bf16[384,768]{1,0:T(8,128)(2,1)} %join.2), channel_id=1, source_target_pairs={{0,1},{1,2},{2,3},{4,5},{5,6},{6,7},{8,9},{9,10},{10,11},{12,13},{... | collective-permute-start | bytes 1769480 | tf_op jit(solution)/shard_map/ppermute | solution.py:1033
  58.4 8.3 %fusion = (f32[3584,128]{1,0:T(8,128)}, f32[3584,128]{1,0:T(8,128)}) fusion(f32[128]{0:T(128)S(1)} %get-tuple-element.199, f32[128]{0:T(128)S(1)} %get-tuple-element.200, f32[3584]{0:T(1024)S(1)} %convert_element_type.39), kind=kLoop, calls=%fused_computation.2 | loop fusion | flops 917504 | bytes 3685376 | tf_op jit(solution)/shard_map/mul | solution.py:1025
  66.7 2.1 collective-permute-done.13.refs_3_.b1_ref.f1_ref.refs_1_
  68.8 5.2 %collective-permute-done.7.refs_8_.refs_5_ = bf16[96,3200]{1,0:T(8,128)(2,1)S(1)} collective-permute-done((bf16[96,3200]{1,0:T(8,128)(2,1)}, bf16[96,3200]{1,0:T(8,128)(2,1)S(1)}, u32[]{:S(2)}, u32[]{:S(2)}) %collective-permute-start.7) | collective-permute-done | bytes 614432 | tf_op jit(solution)/shard_map/ppermute | solution.py:1029
  75.1 1.8 join.3
  79.8 2.0 collective-permute-done.10.refs_11_
  83.4 11.2 %project_own.1 = (bf16[768,3072]{1,0:T(8,128)(2,1)}, f32[8,768]{1,0:T(8,128)}, bf16[896,768]{1,0:T(8,128)(2,1)}, bf16[896,768]{1,0:T(8,128)(2,1)}, bf16[896,768]{1,0:T(8,128)(2,1)}, /*index=5*/bf16[896,768]{1,0:T(8,128)(2,1)}) custom-call(s32[2]{0:T(128)} %pad_add_fusion.refs_0_.at_ref.refs_1_.refs_3_, bf16[896,768]{1,0:T(8,128)(2,1)} %refs_4_.1, ...), custom_call_target="tpu_custom_call" | custom-call | flops 300000000 | tf_op jit(solution)/shard_map/project_own/pallas_call | solution.py:318
  95.5 2.5 begin.1
  98.7 26.5 %collective-permute-start.15 = (bf16[384,768]{1,0:T(8,128)(2,1)}, bf16[384,768]{1,0:T(8,128)(2,1)S(1)}, u32[]{:S(2)}, u32[]{:S(2)}) collective-permute-start(bf16[384,768]{1,0:T(8,128)(2,1)} %get-tuple-element.77), channel_id=1, source_target_pairs={{0,3},{4,7},{8,11},{12,15},{16,19},{20,23},{24,27},{28,31}} | collective-permute-start | bytes 1769480 | tf_op jit(solution)/shard_map/ppermute | solution.py:1033
  125.2 2.2 plan.1
  127.4 7.5 %project_near.1 = (bf16[640,768]{1,0:T(8,128)(2,1)}, bf16[640,768]{1,0:T(8,128)(2,1)}, bf16[640,768]{1,0:T(8,128)(2,1)}, bf16[640,768]{1,0:T(8,128)(2,1)}) custom-call(s32[2]{0:T(128)} %pad_add_fusion.refs_0_.at_ref.refs_1_.refs_3_, bf16[896,768]{1,0:T(8,128)(2,1)} %refs_4_.1, bf16[512,768]{1,0:T(8,128)(2,1)} %copy-done.1, bf16[512,768]{1,0:T(8,128)(2,1)} %copy-done.3, ...), custom_call_target="tpu_custom_call" | custom-call | flops 150000000 | tf_op jit(solution)/shard_map/project_near/pallas_call | solution.py:364
  134.9 22.3 %attend_near.1 = (f32[768,896]{1,0:T(8,128)}, f32[6,8,896]{2,1,0:T(8,128)}) custom-call(s32[8,8]{1,0:T(8,128)} %get-tuple-element.72.meta_ref.refs_1_, bf16[896,768]{1,0:T(8,128)(2,1)} %get-tuple-element.73.q_ref.refs_2_, bf16[640,768]{1,0:T(8,128)(2,1)} %get-tuple-element.82.kn_ref.refs_6_, bf16[640,768]{1,0:T(8,128)(2,1)} %get-tuple-element.83.vn_ref.refs_7_, ...), custom_call_target="tpu_custom_call" | custom-call | flops 600000000 | tf_op jit(solution)/shard_map/attend_near/pallas_call | solution.py:534
  158.2 10.4 %project_far.1 = (bf16[1024,768]{1,0:T(8,128)(2,1)}, bf16[1024,768]{1,0:T(8,128)(2,1)}, bf16[1024,768]{1,0:T(8,128)(2,1)}, bf16[1024,768]{1,0:T(8,128)(2,1)}) custom-call(s32[8,8]{1,0:T(8,128)} %get-tuple-element.72.meta_ref.refs_1_, s32[8,8]{1,0:T(8,128)} %get-tuple-element.74.slot_ref, bf16[896,768]{1,0:T(8,128)(2,1)} %refs_4_.1, ...), custom_call_target="tpu_custom_call" | custom-call | flops 210000000 | tf_op jit(solution)/shard_map/project_far/pallas_call | solution.py:415
  168.6 15.7 %attend_far.1 = (bf16[896,768]{1,0:T(8,128)(2,1)}, f32[6,8,896]{2,1,0:T(8,128)}) custom-call(s32[8,8]{1,0:T(8,128)} %get-tuple-element.72.meta_ref.refs_1_, bf16[896,768]{1,0:T(8,128)(2,1)} %get-tuple-element.73.q_ref.refs_2_, bf16[1024,768]{1,0:T(8,128)(2,1)} %get-tuple-element.80.ks_ref, bf16[1024,768]{1,0:T(8,128)(2,1)} %get-tuple-element.81.vs_ref, ...), custom_call_target="tpu_custom_call" | custom-call | flops 270000000 | tf_op jit(solution)/shard_map/attend_far/pallas_call | solution.py:575
  184.3 6.4 %all-gather.3.cloned.1.call-done = bf16[3072,1536]{1,0:T(8,128)(2,1)} async-done(((bf16[96,1536]{1,0:T(8,128)(2,1)}), bf16[3072,1536]{1,0:T(8,128)(2,1)}) %all-gather.3.cloned.1.call-update) | async-done | bytes 9437200 | tf_op jit(solution)/shard_map/all_gather | solution.py:1099
  190.8 45.7 %feed_forward.1 = (bf16[896,768]{1,0:T(8,128)(2,1)}, bf16[896,768]{1,0:T(8,128)(2,1)}, bf16[896,768]{1,0:T(8,128)(2,1)}, f32[896,768]{1,0:T(8,128)}, f32[8,768]{...) custom-call(s32[2]{0:T(128)} %pad_add_fusion.refs_0_.at_ref.refs_1_.refs_3_, ...), custom_call_target="tpu_custom_call" | custom-call | flops 1200000000 | tf_op jit(solution)/shard_map/feed_forward/pallas_call | solution.py:675
  236.8 27.2 %back_far.1 = (f32[768,896]{1,0:T(8,128)}, bf16[1536,768]{1,0:T(8,128)(2,1)}, bf16[1536,768]{1,0:T(8,128)(2,1)}) custom-call(s32[8,8]{1,0:T(8,128)} %get-tuple-element.72.meta_ref.refs_1_, s32[8,8]{1,0:T(8,128)} %get-tuple-element.74.slot_ref, bf16[896,768]{1,0:T(8,128)(2,1)} %get-tuple-element.73.q_ref.refs_2_, ...), custom_call_target="tpu_custom_call" | custom-call | flops 1500000000 | tf_op jit(solution)/shard_map/back_far/pallas_call | solution.py:761
  264.0 12.8 %spread.1 = (bf16[768,768]{1,0:T(8,128)(2,1)}, bf16[768,768]{1,0:T(8,128)(2,1)}, f32[8,768]{1,0:T(8,128)}, bf16[4,96,1536]{2,1,0:T(8,128)(2,1)}, bf16[4,96,1536]...) custom-call(s32[2]{0:T(128)} %pad_add_fusion.refs_0_.at_ref.refs_1_.refs_3_, ...), custom_call_target="tpu_custom_call" | custom-call | flops 270000000 | tf_op jit(solution)/shard_map/spread/pallas_call | solution.py:877
  276.9 1.3 collective-permute-start.17
  278.2 1.5 collective-permute-start.18
  279.7 14.6 %back_near.1 = (bf16[896,768]{1,0:T(8,128)(2,1)}, bf16[896,768]{1,0:T(8,128)(2,1)}, bf16[896,768]{1,0:T(8,128)(2,1)}, bf16[128,768]{1,0:T(8,128)(2,1)}, bf16[128...) custom-call(bf16[768,768]{1,0:T(8,128)(2,1)} %get-tuple-element.97.refs_0_.refs_1_, ...), custom_call_target="tpu_custom_call" | custom-call | flops 750000000 | tf_op jit(solution)/shard_map/back_near/pallas_call | solution.py:823
  295.0 1.5 collective-permute-start.20
  297.1 14.7 %collective-permute-done.17.refs_2_ = bf16[768,768]{1,0:T(8,128)(2,1)S(1)} collective-permute-done((bf16[768,768]{1,0:T(8,128)(2,1)}, bf16[768,768]{1,0:T(8,128)(2,1)S(1)}, u32[]{:S(2)}, u32[]{:S(2)}) %collective-permute-start.17) | collective-permute-done | bytes 1179680 | tf_op jit(solution)/shard_map/ppermute | solution.py:1033
  311.9 1.0 copy-done.14
  312.9 2.9 total.2.refs_0_.refs_6_
  315.8 1.3 collective-permute-start.23
  317.1 1.0 copy-done.9
  318.1 9.6 %own_back.1 = (f32[896,768]{1,0:T(8,128)}, bf16[128,768]{1,0:T(8,128)(2,1)}, f32[8,768]{1,0:T(8,128)}) custom-call(bf16[768,768]{1,0:T(8,128)(2,1)} %total.2.refs_0_.refs_6_, bf16[4,96,1536]{2,1,0:T(8,128)(2,1)} %copy-done.9, bf16[896,768]{1,0:T(8,128)(2,1)} %refs_4_.1, bf16[640,768]{1,0:T(8,128)(2,1)} %get-tuple-element.95.xn_ref.refs_3_, ...), custom_call_target="tpu_custom_call" | custom-call | flops 180000000 | tf_op jit(solution)/shard_map/own_back/pallas_call | solution.py:915
  327.7 12.9 %weight_sums.2 = (bf16[4,96,1536]{2,1,0:T(8,128)(2,1)}, bf16[4,96,1536]{2,1,0:T(8,128)(2,1)}) custom-call(f32[896,768]{1,0:T(8,128)} %get-tuple-element.106.refs_0_.refs_2_, s32[2]{0:T(128)} %pad_add_fusion.refs_0_.at_ref.refs_1_.refs_3_, bf16[896,768]{1,0:T(8,128)(2,1)} %get-tuple-element.107.refs_2_.refs_7_, bf16[640,768]{1,0:T(8,128)(2,1)} %get-tuple-element.108.refs_3_, ...), custom_call_target="tpu_custom_call" | custom-call | flops 240000000 | tf_op jit(solution)/shard_map/weight_sums/pallas_call | solution.py:966
  340.7 1.1 copy-done.13
  341.8 5.0 %fold.1 = (bf16[2,96,1536]{2,1,0:T(8,128)(2,1)}, bf16[2,96,1536]{2,1,0:T(8,128)(2,1)}, bf16[768,768]{1,0:T(8,128)(2,1)}) custom-call(bf16[4,96,1536]{2,1,0:T(8,128)(2,1)} %get-tuple-element.110.refs_0_.refs_2_, s32[2]{0:T(128)} %pad_add_fusion.refs_0_.at_ref.refs_1_.refs_3_, bf16[768,768]{1,0:T(8,128)(2,1)} %get-tuple-element.111.refs_2_, ...), custom_call_target="tpu_custom_call" | custom-call | flops 120000000 | tf_op jit(solution)/shard_map/fold/pallas_call | solution.py:252
  346.8 1.1 copy-done.8
  347.9 8.4 %weight_sums.3 = (bf16[4,96,1664]{2,1,0:T(8,128)(2,1)}, bf16[4,96,1664]{2,1,0:T(8,128)(2,1)}) custom-call(bf16[2,96,1536]{2,1,0:T(8,128)(2,1)} %get-tuple-element.116.refs_0_.refs_1_, bf16[768,768]{1,0:T(8,128)(2,1)} %get-tuple-element.115.refs_1_.refs_7_, bf16[768,768]{1,0:T(8,128)(2,1)} %copy-done.8, s32[2]{0:T(128)} %pad_add_fusion.refs_0_.at_ref.refs_1_.refs_3_, ...), custom_call_target="tpu_custom_call" | custom-call | flops 240000000 | tf_op jit(solution)/shard_map/weight_sums/pallas_call | solution.py:966
  357.6 3.5 collective-permute-done.25.refs_4_
  362.2 4.0 meet.1
  366.2 1.4 collective-permute-start.26
  368.2 1.5 collective-permute-start.28
  369.7 1.2 slice.98
  371.5 3.7 collective-permute-start.33
  375.2 1.1 fusion.2
  376.3 1.3 collective-permute-start.29
  377.6 5.4 %collective-permute-done.26.refs_2_ = bf16[96,3200]{1,0:T(8,128)(2,1)S(1)} collective-permute-done((bf16[96,3200]{1,0:T(8,128)(2,1)}, bf16[96,3200]{1,0:T(8,128)(2,1)S(1)}, u32[]{:S(2)}, u32[]{:S(2)}) %collective-permute-start.26) | collective-permute-done | bytes 614432 | tf_op jit(solution)/shard_map/ppermute | solution.py:1029
  383.1 13.6 %collective-permute-done.27.refs_3_ = bf16[96,3200]{1,0:T(8,128)(2,1)} collective-permute-done((bf16[96,3200]{1,0:T(8,128)(2,1)}, bf16[96,3200]{1,0:T(8,128)(2,1)}, u32[]{:S(2)}, u32[]{:S(2)}) %collective-permute-start.27) | collective-permute-done | bytes 614432 | tf_op jit(solution)/shard_map/ppermute | solution.py:1029
  396.7 2.8 total.3.refs_0_
  399.5 1.4 fusion.11
  401.8 8.3 %collective-permute-start.30 = (bf16[96,896]{1,0:T(8,128)(2,1)S(1)}, bf16[96,896]{1,0:T(8,128)(2,1)S(1)}, u32[]{:S(2)}, u32[]{:S(2)}) collective-permute-start(bf16[96,896]{1,0:T(8,128)(2,1)S(1)} %concatenate.21), channel_id=1, source_target_pairs={{0,1},{1,0},{2,3},{3,2},{4,5},{5,4},{6,7},{7,6},{8,9},{9,8},{10,11... | collective-permute-start | bytes 516104 | tf_op jit(solution)/shard_map/ppermute | solution.py:1029
  410.3 1.7 collective-permute-start.31
  412.9 2.8 collective-permute-done.33.refs_2_
  415.7 2.2 middle.1
  418.0 6.8 %collective-permute-done.29.refs_10_ = bf16[128,768]{1,0:T(8,128)(2,1)S(1)} collective-permute-done((bf16[128,768]{1,0:T(8,128)(2,1)S(1)}, bf16[128,768]{1,0:T(8,128)(2,1)S(1)}, u32[]{:S(2)}, u32[]{:S(2)}) %collective-permute-start.29) | collective-permute-done | bytes 196640 | tf_op jit(solution)/shard_map/ppermute | solution.py:1033
  425.4 8.4 %finish.1 = f32[896,768]{1,0:T(8,128)} custom-call(bf16[96,3200]{1,0:T(8,128)(2,1)} %total.3.refs_0_, s32[8,8]{1,0:T(8,128)} %get-tuple-element.72.meta_ref.refs_1_, f32[896,768]{1,0:T(8,128)} %get-tuple-element.106.refs_0_.refs_2_, f32[896,768]{1,0:T(8,128)} %get-tuple-element.128.refs_3_, bf16[896,768]{1,0:T(8,128)(2,1)} %refs_4_.1, ...), custom_call_target="tpu_custom_call" | custom-call | flops 180000000 | tf_op jit(solution)/shard_map/finish/pallas_call | solution.py:1008
  (128 shorter events, 22.0 us)
Async XLA Ops:
  7.2 6.3 %copy-start.33 = (f32[24]{0:T(128)S(1)}, f32[24]{0:T(128)}, u32[]{:S(2)}) copy-start(f32[24]{0:T(128)} %param.20) | copy-start | bytes 292
  7.2 6.3 %copy-start.32 = (f32[24]{0:T(128)S(1)}, f32[24]{0:T(128)}, u32[]{:S(2)}) copy-start(f32[24]{0:T(128)} %param.15) | copy-start | bytes 292
  7.2 6.5 %copy-start.30 = (bf16[192,96]{1,0:T(8,128)(2,1)S(1)}, bf16[192,96]{1,0:T(8,128)(2,1)}, u32[]{:S(2)}) copy-start(bf16[192,96]{1,0:T(8,128)(2,1)} %param.19) | copy-start | bytes 110596
  7.2 7.0 %copy-start.29 = (bf16[96,192]{1,0:T(8,128)(2,1)S(1)}, bf16[96,192]{1,0:T(8,128)(2,1)}, u32[]{:S(2)}) copy-start(bf16[96,192]{1,0:T(8,128)(2,1)} %param.18) | copy-start | bytes 110596
  7.2 7.0 %copy-start.28 = (bf16[96,192]{1,0:T(8,128)(2,1)S(1)}, bf16[96,192]{1,0:T(8,128)(2,1)}, u32[]{:S(2)}) copy-start(bf16[96,192]{1,0:T(8,128)(2,1)} %param.17) | copy-start | bytes 110596
  7.2 7.0 %copy-start.27 = (bf16[96,192]{1,0:T(8,128)(2,1)S(1)}, bf16[96,192]{1,0:T(8,128)(2,1)}, u32[]{:S(2)}) copy-start(bf16[96,192]{1,0:T(8,128)(2,1)} %param.16) | copy-start | bytes 110596
  7.2 13.6 %copy-start.31 = (s32[3584]{0:T(1024)S(1)}, s32[3584]{0:T(1024)}, u32[]{:S(2)}) copy-start(s32[3584]{0:T(1024)} %param.26) | copy-start | bytes 43012
  7.2 183.5 %all-gather.3.cloned.1.call-start = ((), (), s32[]{:S(2)}) async-start(), calls=%async_computation | async-start | bytes 9732096 | tf_op jit(solution)/shard_map/all_gather | solution.py:1099
  8.5 32.8 %collective-permute-start = (bf16[512,768]{1,0:T(8,128)(2,1)S(1)}, bf16[512,768]{1,0:T(8,128)(2,1)S(1)}, u32[]{:S(2)}, u32[]{:S(2)}) collective-permute-start(bf16[512,768]{1,0:T(8,128)(2,1)S(1)} %slice.96), channel_id=1, source_target_pairs={{0,1},{1,2},{2,3},{4,5},{5,6},{6,7},{8,9},{9,10},{10,11},{12,13},{... | collective-permute-start | bytes 2359304 | tf_op jit(solution)/shard_map/ppermute | solution.py:1033
  14.4 26.9 %copy-start.15 = (bf16[96,896]{1,0:T(8,128)(2,1)}, bf16[96,896]{1,0:T(8,128)(2,1)S(1)}, u32[]{:S(2)}) copy-start(bf16[96,896]{1,0:T(8,128)(2,1)S(1)} %concatenate.19.refs_1_) | copy-start | bytes 516100
  14.4 20.7 %collective-permute-start.3 = (bf16[96,896]{1,0:T(8,128)(2,1)S(1)}, bf16[96,896]{1,0:T(8,128)(2,1)S(1)}, u32[]{:S(2)}, u32[]{:S(2)}) collective-permute-start(bf16[96,896]{1,0:T(8,128)(2,1)S(1)} %concatenate.19.refs_1_), channel_id=1, source_target_pairs={{0,3},{1,2},{2,1},{3,0},{4,7},{5,6},{6,5},{7,4},{8,11},{9,10},{10,... | collective-permute-start | bytes 516104 | tf_op jit(solution)/shard_map/ppermute | solution.py:1029
  15.8 23.0 %collective-permute-start.2 = (bf16[96,896]{1,0:T(8,128)(2,1)S(1)}, bf16[96,896]{1,0:T(8,128)(2,1)S(1)}, u32[]{:S(2)}, u32[]{:S(2)}) collective-permute-start(bf16[96,896]{1,0:T(8,128)(2,1)S(1)} %concatenate.19.refs_1_), channel_id=1, source_target_pairs={{0,2},{1,3},{2,0},{3,1},{4,6},{5,7},{6,4},{7,5},{8,10},{9,11},{10,... | collective-permute-start | bytes 516104 | tf_op jit(solution)/shard_map/ppermute | solution.py:1029
  17.5 23.9 %collective-permute-start.1 = (bf16[96,896]{1,0:T(8,128)(2,1)S(1)}, bf16[96,896]{1,0:T(8,128)(2,1)S(1)}, u32[]{:S(2)}, u32[]{:S(2)}) collective-permute-start(bf16[96,896]{1,0:T(8,128)(2,1)S(1)} %concatenate.19.refs_1_), channel_id=1, source_target_pairs={{0,1},{1,0},{2,3},{3,2},{4,5},{5,4},{6,7},{7,6},{8,9},{9,8},{10,11... | collective-permute-start | bytes 516104 | tf_op jit(solution)/shard_map/ppermute | solution.py:1029
  35.1 6.2 %copy-start.24 = (bf16[96,896]{1,0:T(8,128)(2,1)}, bf16[96,896]{1,0:T(8,128)(2,1)S(1)}, u32[]{:S(2)}) copy-start(bf16[96,896]{1,0:T(8,128)(2,1)S(1)} %collective-permute-done.3.refs_4_) | copy-start | bytes 516100
  38.8 2.6 copy-start.25
  42.0 0.9 copy-start.1
  45.0 12.6 %copy-start.2 = (bf16[512,768]{1,0:T(8,128)(2,1)S(1)}, bf16[512,768]{1,0:T(8,128)(2,1)}, u32[]{:S(2)}) copy-start(bf16[512,768]{1,0:T(8,128)(2,1)} %copy-done.1) | copy-start | bytes 2359300
  45.0 23.8 %collective-permute-start.9 = (bf16[96,3200]{1,0:T(8,128)(2,1)}, bf16[96,3200]{1,0:T(8,128)(2,1)S(1)}, u32[]{:S(2)}, u32[]{:S(2)}) collective-permute-start(bf16[96,3200]{1,0:T(8,128)(2,1)} %line.1.refs_4_.refs_0_), channel_id=1, source_target_pairs={{0,24},{4,28},{8,16},{12,20},{16,8},{20,12},{24,0},{28,4},{1,25},{... | collective-permute-start | bytes 1843208 | tf_op jit(solution)/shard_map/ppermute | solution.py:1029
  47.5 26.6 %collective-permute-start.7 = (bf16[96,3200]{1,0:T(8,128)(2,1)}, bf16[96,3200]{1,0:T(8,128)(2,1)S(1)}, u32[]{:S(2)}, u32[]{:S(2)}) collective-permute-start(bf16[96,3200]{1,0:T(8,128)(2,1)} %line.1.refs_4_.refs_0_), channel_id=1, source_target_pairs={{0,16},{4,20},{8,24},{12,28},{16,0},{20,4},{24,8},{28,12},{1,17},{... | collective-permute-start | bytes 1843208 | tf_op jit(solution)/shard_map/ppermute | solution.py:1029
  48.0 26.3 %collective-permute-start.5 = (bf16[96,3200]{1,0:T(8,128)(2,1)}, bf16[96,3200]{1,0:T(8,128)(2,1)}, u32[]{:S(2)}, u32[]{:S(2)}) collective-permute-start(bf16[96,3200]{1,0:T(8,128)(2,1)} %line.1.refs_4_.refs_0_), channel_id=1, source_target_pairs={{0,8},{4,12},{8,0},{12,4},{16,24},{20,28},{24,16},{28,20},{1,9},{5... | collective-permute-start | bytes 1843208 | tf_op jit(solution)/shard_map/ppermute | solution.py:1029
  50.4 18.3 %collective-permute-start.13 = (bf16[384,768]{1,0:T(8,128)(2,1)}, bf16[384,768]{1,0:T(8,128)(2,1)S(1)}, u32[]{:S(2)}, u32[]{:S(2)}) collective-permute-start(bf16[384,768]{1,0:T(8,128)(2,1)} %join.2), channel_id=1, source_target_pairs={{0,1},{1,2},{2,3},{4,5},{5,6},{6,7},{8,9},{9,10},{10,11},{12,13},{... | collective-permute-start | bytes 1769480 | tf_op jit(solution)/shard_map/ppermute | solution.py:1033
  57.7 16.6 %collective-permute-start.11 = (bf16[512,768]{1,0:T(8,128)(2,1)S(1)}, bf16[512,768]{1,0:T(8,128)(2,1)S(1)}, u32[]{:S(2)}, u32[]{:S(2)}) collective-permute-start(bf16[512,768]{1,0:T(8,128)(2,1)S(1)} %copy-done.2), channel_id=1, source_target_pairs={{1,2},{2,3},{5,6},{6,7},{9,10},{10,11},{13,14},{14,15},{17,18},{18... | collective-permute-start | bytes 2359304 | tf_op jit(solution)/shard_map/ppermute | solution.py:1033
  68.8 5.5 %copy-start = (bf16[384,768]{1,0:T(8,128)(2,1)}, bf16[384,768]{1,0:T(8,128)(2,1)S(1)}, u32[]{:S(2)}) copy-start(bf16[384,768]{1,0:T(8,128)(2,1)S(1)} %collective-permute-done.13.refs_3_.b1_ref.f1_ref.refs_1_) | copy-start | bytes 1769476
  68.8 5.5 %copy-start.10 = (bf16[96,3200]{1,0:T(8,128)(2,1)}, bf16[96,3200]{1,0:T(8,128)(2,1)S(1)}, u32[]{:S(2)}) copy-start(bf16[96,3200]{1,0:T(8,128)(2,1)S(1)} %collective-permute-done.9.refs_10_.refs_6_) | copy-start | bytes 1843204
  75.1 2.5 copy-start.7
  76.9 17.7 %collective-permute-start.12 = (bf16[512,768]{1,0:T(8,128)(2,1)}, bf16[512,768]{1,0:T(8,128)(2,1)S(1)}, u32[]{:S(2)}, u32[]{:S(2)}) collective-permute-start(bf16[512,768]{1,0:T(8,128)(2,1)} %copy-done.3), channel_id=1, source_target_pairs={{2,3},{6,7},{10,11},{14,15},{18,19},{22,23},{26,27},{30,31}} | collective-permute-start | bytes 2359304 | tf_op jit(solution)/shard_map/ppermute | solution.py:1033
  77.7 2.1 collective-permute-start.4
  77.8 3.9 collective-permute-start.10
  78.2 4.4 collective-permute-start.8
  78.4 4.3 collective-permute-start.6
  79.8 2.9 copy-start.16
  81.7 0.9 copy-start.17
  94.6 0.9 copy-start.4
  98.0 59.2 %collective-permute-start.14 = (bf16[384,768]{1,0:T(8,128)(2,1)}, bf16[384,768]{1,0:T(8,128)(2,1)S(1)}, u32[]{:S(2)}, u32[]{:S(2)}) collective-permute-start(bf16[384,768]{1,0:T(8,128)(2,1)} %get-tuple-element.76), channel_id=1, source_target_pairs={{1,2},{2,3},{5,6},{6,7},{9,10},{10,11},{13,14},{14,15},{17,18},{18... | collective-permute-start | bytes 1769480 | tf_op jit(solution)/shard_map/ppermute | solution.py:1033
  98.7 58.5 %collective-permute-start.15 = (bf16[384,768]{1,0:T(8,128)(2,1)}, bf16[384,768]{1,0:T(8,128)(2,1)S(1)}, u32[]{:S(2)}, u32[]{:S(2)}) collective-permute-start(bf16[384,768]{1,0:T(8,128)(2,1)} %get-tuple-element.77), channel_id=1, source_target_pairs={{0,3},{4,7},{8,11},{12,15},{16,19},{20,23},{24,27},{28,31}} | collective-permute-start | bytes 1769480 | tf_op jit(solution)/shard_map/ppermute | solution.py:1033
  157.2 1.0 copy-start.21
  236.5 27.6 %collective-permute-start.16 = (bf16[4,4,96,1536]{3,2,1,0:T(8,128)(2,1)}, bf16[4,4,96,1536]{3,2,1,0:T(8,128)(2,1)}, u32[]{:S(2)}, u32[]{:S(2)}) collective-permute-start(bf16[4,4,96,1536]{3,2,1,0:T(8,128)(2,1)} %get-tuple-element.90), channel_id=1, source_target_pairs={{0,4},{4,0},{8,12},{12,8},{16,20},{20,16},{24,28},{28,24},{1,5},{5... | collective-permute-start | bytes 14155784 | tf_op jit(solution)/shard_map/ppermute | solution.py:1029
  276.9 35.0 %collective-permute-start.17 = (bf16[768,768]{1,0:T(8,128)(2,1)}, bf16[768,768]{1,0:T(8,128)(2,1)S(1)}, u32[]{:S(2)}, u32[]{:S(2)}) collective-permute-start(bf16[768,768]{1,0:T(8,128)(2,1)} %get-tuple-element.97.refs_0_.refs_1_), channel_id=1, source_target_pairs={{3,2},{1,0},{7,6},{5,4},{11,10},{9,8},{15,14},{13,12},{19,18},{17,... | collective-permute-start | bytes 3538952 | tf_op jit(solution)/shard_map/ppermute | solution.py:1033
  278.2 38.9 %collective-permute-start.18 = (bf16[4,96,1536]{2,1,0:T(8,128)(2,1)}, bf16[4,96,1536]{2,1,0:T(8,128)(2,1)S(1)}, u32[]{:S(2)}, u32[]{:S(2)}) collective-permute-start(bf16[4,96,1536]{2,1,0:T(8,128)(2,1)} %get-tuple-element.101), channel_id=1, source_target_pairs={{0,24},{4,28},{8,16},{12,20},{16,8},{20,12},{24,0},{28,4},{1,25},{... | collective-permute-start | bytes 3538952 | tf_op jit(solution)/shard_map/ppermute | solution.py:1029
  294.3 46.4 %collective-permute-start.19 = (bf16[768,768]{1,0:T(8,128)(2,1)}, bf16[768,768]{1,0:T(8,128)(2,1)S(1)}, u32[]{:S(2)}, u32[]{:S(2)}) collective-permute-start(bf16[768,768]{1,0:T(8,128)(2,1)} %get-tuple-element.111.refs_2_), channel_id=1, source_target_pairs={{3,2},{7,6},{11,10},{15,14},{19,18},{23,22},{27,26},{31,30}} | collective-permute-start | bytes 3538952 | tf_op jit(solution)/shard_map/ppermute | solution.py:1033
  295.0 45.6 %collective-permute-start.20 = (bf16[4,96,1536]{2,1,0:T(8,128)(2,1)}, bf16[4,96,1536]{2,1,0:T(8,128)(2,1)}, u32[]{:S(2)}, u32[]{:S(2)}) collective-permute-start(bf16[4,96,1536]{2,1,0:T(8,128)(2,1)} %get-tuple-element.113), channel_id=1, source_target_pairs={{0,8},{4,12},{8,0},{12,4},{16,24},{20,28},{24,16},{28,20},{1,9},{5... | collective-permute-start | bytes 3538952 | tf_op jit(solution)/shard_map/ppermute | solution.py:1029
  296.6 44.1 %collective-permute-start.21 = (bf16[4,96,1536]{2,1,0:T(8,128)(2,1)}, bf16[4,96,1536]{2,1,0:T(8,128)(2,1)}, u32[]{:S(2)}, u32[]{:S(2)}) collective-permute-start(bf16[4,96,1536]{2,1,0:T(8,128)(2,1)} %get-tuple-element.114), channel_id=1, source_target_pairs={{0,16},{4,20},{8,24},{12,28},{16,0},{20,4},{24,8},{28,12},{1,17},{... | collective-permute-start | bytes 3538952 | tf_op jit(solution)/shard_map/ppermute | solution.py:1029
  311.9 1.0 copy-start.14
  315.8 31.0 %collective-permute-start.23 = (bf16[768,768]{1,0:T(8,128)(2,1)}, bf16[768,768]{1,0:T(8,128)(2,1)S(1)}, u32[]{:S(2)}, u32[]{:S(2)}) collective-permute-start(bf16[768,768]{1,0:T(8,128)(2,1)} %total.2.refs_0_.refs_6_), channel_id=1, source_target_pairs={{2,0},{6,4},{10,8},{14,12},{18,16},{22,20},{26,24},{30,28}} | collective-permute-start | bytes 3538952 | tf_op jit(solution)/shard_map/ppermute | solution.py:1033
  317.1 1.0 copy-start.9
  340.7 1.1 copy-start.13
  346.8 1.1 copy-start.8
  347.9 9.0 %copy-start.5 = (bf16[768,768]{1,0:T(8,128)(2,1)S(1)}, bf16[768,768]{1,0:T(8,128)(2,1)}, u32[]{:S(2)}) copy-start(bf16[768,768]{1,0:T(8,128)(2,1)} %get-tuple-element.115.refs_1_.refs_7_) | copy-start | bytes 3538948
  356.3 5.0 %collective-permute-start.24 = (bf16[4,96,1664]{2,1,0:T(8,128)(2,1)}, bf16[4,96,1664]{2,1,0:T(8,128)(2,1)}, u32[]{:S(2)}, u32[]{:S(2)}) collective-permute-start(bf16[4,96,1664]{2,1,0:T(8,128)(2,1)} %get-tuple-element.122), channel_id=1, source_target_pairs={{0,4},{4,0},{8,12},{12,8},{16,20},{20,16},{24,28},{28,24},{1,5},{5... | collective-permute-start | bytes 3833864 | tf_op jit(solution)/shard_map/ppermute | solution.py:1029
  356.3 4.8 %collective-permute-start.25 = (bf16[4,96,1536]{2,1,0:T(8,128)(2,1)}, bf16[4,96,1536]{2,1,0:T(8,128)(2,1)S(1)}, u32[]{:S(2)}, u32[]{:S(2)}) collective-permute-start(bf16[4,96,1536]{2,1,0:T(8,128)(2,1)} %get-tuple-element.123), channel_id=1, source_target_pairs={{0,4},{4,0},{8,12},{12,8},{16,20},{20,16},{24,28},{28,24},{1,5},{5... | collective-permute-start | bytes 3538952 | tf_op jit(solution)/shard_map/ppermute | solution.py:1029
  356.8 18.3 %collective-permute-start.22 = (bf16[768,768]{1,0:T(8,128)(2,1)S(1)}, bf16[768,768]{1,0:T(8,128)(2,1)S(1)}, u32[]{:S(2)}, u32[]{:S(2)}) collective-permute-start(bf16[768,768]{1,0:T(8,128)(2,1)S(1)} %copy-done.5), channel_id=1, source_target_pairs={{2,1},{6,5},{10,9},{14,13},{18,17},{22,21},{26,25},{30,29}} | collective-permute-start | bytes 3538952 | tf_op jit(solution)/shard_map/ppermute | solution.py:1033
  361.1 1.1 copy-start.12
  366.2 16.9 %collective-permute-start.26 = (bf16[96,3200]{1,0:T(8,128)(2,1)}, bf16[96,3200]{1,0:T(8,128)(2,1)S(1)}, u32[]{:S(2)}, u32[]{:S(2)}) collective-permute-start(bf16[96,3200]{1,0:T(8,128)(2,1)} %get-tuple-element.125), channel_id=1, source_target_pairs={{0,8},{4,12},{8,0},{12,4},{16,24},{20,28},{24,16},{28,20},{1,9},{5... | collective-permute-start | bytes 1843208 | tf_op jit(solution)/shard_map/ppermute | solution.py:1029
  367.6 29.1 %collective-permute-start.27 = (bf16[96,3200]{1,0:T(8,128)(2,1)}, bf16[96,3200]{1,0:T(8,128)(2,1)}, u32[]{:S(2)}, u32[]{:S(2)}) collective-permute-start(bf16[96,3200]{1,0:T(8,128)(2,1)} %get-tuple-element.126), channel_id=1, source_target_pairs={{0,16},{4,20},{8,24},{12,28},{16,0},{20,4},{24,8},{28,12},{1,17},{... | collective-permute-start | bytes 1843208 | tf_op jit(solution)/shard_map/ppermute | solution.py:1029
  368.2 28.5 %collective-permute-start.28 = (bf16[96,3200]{1,0:T(8,128)(2,1)}, bf16[96,3200]{1,0:T(8,128)(2,1)}, u32[]{:S(2)}, u32[]{:S(2)}) collective-permute-start(bf16[96,3200]{1,0:T(8,128)(2,1)} %get-tuple-element.127), channel_id=1, source_target_pairs={{0,24},{4,28},{8,16},{12,20},{16,8},{20,12},{24,0},{28,4},{1,25},{... | collective-permute-start | bytes 1843208 | tf_op jit(solution)/shard_map/ppermute | solution.py:1029
  371.5 44.2 %collective-permute-start.33 = (bf16[2,96,1536]{2,1,0:T(8,128)(2,1)}, bf16[2,96,1536]{2,1,0:T(8,128)(2,1)}, u32[]{:S(2)}, u32[]{:S(2)}) collective-permute-start(bf16[2,96,1536]{2,1,0:T(8,128)(2,1)} %get-tuple-element.130), channel_id=1, source_target_pairs={{0,2},{1,3},{2,0},{3,1},{4,6},{5,7},{6,4},{7,5},{8,10},{9,11},{10,... | collective-permute-start | bytes 1769480 | tf_op jit(solution)/shard_map/ppermute | solution.py:1029
  375.2 21.5 %copy-start.6 = (bf16[768,768]{1,0:T(8,128)(2,1)}, bf16[768,768]{1,0:T(8,128)(2,1)S(1)}, u32[]{:S(2)}) copy-start(bf16[768,768]{1,0:T(8,128)(2,1)S(1)} %collective-permute-done.22.refs_0_.refs_9_) | copy-start | bytes 3538948
  376.3 48.4 %collective-permute-start.29 = (bf16[128,768]{1,0:T(8,128)(2,1)S(1)}, bf16[128,768]{1,0:T(8,128)(2,1)S(1)}, u32[]{:S(2)}, u32[]{:S(2)}) collective-permute-start(bf16[128,768]{1,0:T(8,128)(2,1)S(1)} %fusion.2), channel_id=1, source_target_pairs={{1,0},{3,2},{5,4},{7,6},{9,8},{11,10},{13,12},{15,14},{17,16},{19,... | collective-permute-start | bytes 589832 | tf_op jit(solution)/shard_map/ppermute | solution.py:1033
  383.1 13.6 %copy-start.19 = (bf16[96,3200]{1,0:T(8,128)(2,1)}, bf16[96,3200]{1,0:T(8,128)(2,1)S(1)}, u32[]{:S(2)}) copy-start(bf16[96,3200]{1,0:T(8,128)(2,1)S(1)} %collective-permute-done.26.refs_2_) | copy-start | bytes 1843204
  401.8 32.0 %collective-permute-start.30 = (bf16[96,896]{1,0:T(8,128)(2,1)S(1)}, bf16[96,896]{1,0:T(8,128)(2,1)S(1)}, u32[]{:S(2)}, u32[]{:S(2)}) collective-permute-start(bf16[96,896]{1,0:T(8,128)(2,1)S(1)} %concatenate.21), channel_id=1, source_target_pairs={{0,1},{1,0},{2,3},{3,2},{4,5},{5,4},{6,7},{7,6},{8,9},{9,8},{10,11... | collective-permute-start | bytes 516104 | tf_op jit(solution)/shard_map/ppermute | solution.py:1029
  410.3 23.5 %collective-permute-start.31 = (bf16[96,896]{1,0:T(8,128)(2,1)S(1)}, bf16[96,896]{1,0:T(8,128)(2,1)S(1)}, u32[]{:S(2)}, u32[]{:S(2)}) collective-permute-start(bf16[96,896]{1,0:T(8,128)(2,1)S(1)} %concatenate.22), channel_id=1, source_target_pairs={{0,2},{1,3},{2,0},{3,1},{4,6},{5,7},{6,4},{7,5},{8,10},{9,11},{10,... | collective-permute-start | bytes 516104 | tf_op jit(solution)/shard_map/ppermute | solution.py:1029
  412.1 21.7 %collective-permute-start.32 = (bf16[96,896]{1,0:T(8,128)(2,1)S(1)}, bf16[96,896]{1,0:T(8,128)(2,1)S(1)}, u32[]{:S(2)}, u32[]{:S(2)}) collective-permute-start(bf16[96,896]{1,0:T(8,128)(2,1)S(1)} %concatenate.23), channel_id=1, source_target_pairs={{0,3},{1,2},{2,1},{3,0},{4,7},{5,6},{6,5},{7,4},{8,11},{9,10},{10,... | collective-permute-start | bytes 516104 | tf_op jit(solution)/shard_map/ppermute | solution.py:1029
  417.8 18.3 %collective-permute-start.34 = (bf16[96,1536]{1,0:T(8,128)(2,1)}, bf16[96,1536]{1,0:T(8,128)(2,1)S(1)}, u32[]{:S(2)}, u32[]{:S(2)}) collective-permute-start(bf16[96,1536]{1,0:T(8,128)(2,1)} %get-tuple-element.132), channel_id=1, source_target_pairs={{0,1},{1,0},{2,3},{3,2},{4,5},{5,4},{6,7},{7,6},{8,9},{9,8},{10,11... | collective-permute-start | bytes 884744 | tf_op jit(solution)/shard_map/ppermute | solution.py:1029
  433.8 2.3 copy-start.22
  (6 other events, 4.7 us)
Sparse Core Ops, SparseCore 0:
  77.0 113.6 all-gather.2
